TPU v7x, 128 devices: a whole 4x4x4 slice. The times are simulated.
128 devices in a mesh: gx: 16 (over z_hi, x, core), gy: 8 (over y, z_lo).
Axes of the slice: x: 4, y: 4, z: 4 (z_hi: 2, z_lo: 2; z = z_hi * 2 + z_lo), core: 2. Of those that a mesh axis runs over, the one named last changes fastest.
Arguments:
- inputs: bfloat16 [1024, 512, 256], P('gx', 'gy'), may hold values from -6 to 6
- cotangent: bfloat16 [1024, 512, 256], P('gx', 'gy'), may hold values from -6 to 6
- wet_mask: int32 [1024, 512], P('gx', 'gy'), may hold values from 0 to 1, as said below
- kernel: bfloat16 [49, 256], replicated, may hold values from -0.875 to 0.875
- conv_bias: bfloat16 [256], replicated, may hold values from -3 to 3
- norm_gain: bfloat16 [256], replicated, may hold values from 0.25 to 1.75
- norm_shift: bfloat16 [256], replicated, may hold values from -3 to 3
- up_weight: bfloat16 [256, 512], replicated, may hold values from -0.375 to 0.375
- up_bias: bfloat16 [512], replicated, may hold values from -3 to 3
- down_weight: bfloat16 [512, 256], replicated, may hold values from -0.25 to 0.25
Outputs:
- input_grad: float32 [1024, 512, 256], P('gx', 'gy')
- kernel_grad: float32 [49, 256], replicated
- conv_bias_grad: float32 [256], replicated
- norm_gain_grad: float32 [256], replicated
- norm_shift_grad: float32 [256], replicated
- up_weight_grad: float32 [256, 512], replicated
- up_bias_grad: float32 [512], replicated
- down_weight_grad: float32 [512, 256], replicated
Inputs may be any that keep to these rules, and one draw needn't show every extreme that they name: `wet_mask`: land fills whole aligned blocks of 32 by 32 cells; elsewhere single dry cells occur.
All inputs are finite; a program needn't handle non-finite values.
Results may differ from a plain program's by a relative error of at most 0.0075.
Values may be sent and summed in bfloat16 or wider, within the bound.
No kernel may reach another device: no remote copies, remote signals or barrier semaphores. Data moves between devices by JAX's collectives and lax.ppermute only.
A program may use at most 128 MiB of HBM per device.

v0:
```python
import jax
import jax.numpy as jnp
from jax import lax
from jax.sharding import PartitionSpec as P


def padded_2(x, sides, width):
    for axis, dim in sides:
        size, length = (lax.axis_size(axis), x.shape[dim])
        up = [(i, (i + 1) % size) for i in range(size)]
        down = [(j, i) for i, j in up]
        last = lax.slice_in_dim(x, length - width, length, axis=dim)
        first = lax.slice_in_dim(x, 0, width, axis=dim)
        before = lax.ppermute(last, axis, up)
        after = lax.ppermute(first, axis, down)
        x = jnp.concatenate([before, x, after], axis=dim)
    return x


def contract_rows(left, right):
    return lax.dot_general(
        left, right, (((0,), (0,)), ((), ())), preferred_element_type=jnp.float32
    )


def contract_cols(left, right):
    return lax.dot_general(
        left, right, (((1,), (1,)), ((), ())), preferred_element_type=jnp.float32
    )


def depthwise(padded, kernel, conv_bias, lon_count, lat_count):
    total = jnp.zeros((lon_count, lat_count, padded.shape[2]), jnp.float32) + conv_bias.astype(
        jnp.float32
    )
    for lon_off in range(7):
        for lat_off in range(7):
            window = padded[lon_off : lon_off + lon_count, lat_off : lat_off + lat_count]
            total = total + kernel[lon_off * 7 + lat_off].astype(jnp.float32) * window.astype(
                jnp.float32
            )
    return total


def spread_back(grad_pad, kernel, lon_count, lat_count):
    total = jnp.zeros((lon_count, lat_count, grad_pad.shape[2]), jnp.float32)
    for lon_off in range(7):
        for lat_off in range(7):
            window = grad_pad[
                6 - lon_off : 6 - lon_off + lon_count, 6 - lat_off : 6 - lat_off + lat_count
            ]
            total = total + kernel[lon_off * 7 + lat_off].astype(jnp.float32) * window.astype(
                jnp.float32
            )
    return total


def cell_grads(field, masked_grad, norm_gain, norm_shift, up_weight, up_bias, down_weight):
    average = jnp.mean(field, axis=-1, keepdims=True)
    centred = field - average
    variance = jnp.mean(centred * centred, axis=-1, keepdims=True)
    inv_std = 1.0 / jnp.sqrt(variance + 1e-06)
    normed = centred * inv_std
    gain = norm_gain.astype(jnp.float32)
    normed_out = (normed * gain + norm_shift.astype(jnp.float32)).astype(jnp.bfloat16)
    hidden = jnp.dot(normed_out, up_weight, preferred_element_type=jnp.float32) + up_bias.astype(
        jnp.float32
    )
    cumulative = 0.5 * (1.0 + lax.erf(hidden * 0.7071067811865476))
    activated = (hidden * cumulative).astype(jnp.bfloat16)
    down_sum = contract_rows(activated, masked_grad)
    act_grad = contract_cols(masked_grad, down_weight)
    density = jnp.exp(-0.5 * hidden * hidden) * 0.3989422804014327
    hidden_grad = (act_grad * (cumulative + hidden * density)).astype(jnp.bfloat16)
    up_sum = contract_rows(normed_out, hidden_grad)
    up_bias_sum = jnp.sum(hidden_grad.astype(jnp.float32), axis=0)
    normed_grad = contract_cols(hidden_grad, up_weight)
    gain_sum = jnp.sum(normed_grad * normed, axis=0)
    shift_sum = jnp.sum(normed_grad, axis=0)
    scaled = normed_grad * gain
    field_grad = inv_std * (
        scaled
        - jnp.mean(scaled, axis=-1, keepdims=True)
        - normed * jnp.mean(scaled * normed, axis=-1, keepdims=True)
    )
    return (field_grad.astype(jnp.bfloat16), (up_sum, up_bias_sum, down_sum, gain_sum, shift_sum))


def latitude_keep(lat_cells):
    first = lax.axis_index("gy") * lat_cells
    position = first + jnp.arange(lat_cells + 6, dtype=jnp.int32) - 3
    inside = (position >= 0) & (position < lat_cells * lax.axis_size("gy"))
    return inside.astype(jnp.bfloat16)[None, :, None]


def local(
    inputs,
    cotangent,
    wet_mask,
    kernel,
    conv_bias,
    norm_gain,
    norm_shift,
    up_weight,
    up_bias,
    down_weight,
):
    lon_cells, lat_cells, channels = inputs.shape
    hidden_units = up_weight.shape[1]
    cell_count = lon_cells * lat_cells
    wet = wet_mask.astype(jnp.bfloat16)[:, :, None]
    masked = inputs * wet
    masked_grad = cotangent * wet
    keep_lat = latitude_keep(lat_cells)
    padded = padded_2(masked, (("gx", 0), ("gy", 1)), 3) * keep_lat
    field = depthwise(padded, kernel, conv_bias, lon_cells, lat_cells)
    block_rows = max(1, min(lon_cells, 512 // lat_cells))
    block_count = lon_cells // block_rows
    block_cells = block_rows * lat_cells
    zero_parts = (
        jnp.zeros((channels, hidden_units), jnp.float32),
        jnp.zeros((hidden_units,), jnp.float32),
        jnp.zeros((hidden_units, channels), jnp.float32),
        jnp.zeros((channels,), jnp.float32),
        jnp.zeros((channels,), jnp.float32),
    )

    def compute_block(field_in, grad_in):
        return cell_grads(field_in, grad_in, norm_gain, norm_shift, up_weight, up_bias, down_weight)

    field_flat = field.reshape(cell_count, channels)
    grad_flat = masked_grad.reshape(cell_count, channels)
    field_blocks = field_flat.reshape(block_count, block_cells, channels)
    grad_blocks = grad_flat.reshape(block_count, block_cells, channels)
    active = jnp.any(grad_blocks != 0, axis=(1, 2))

    def advance(totals, blocks_in):
        field_in, grad_in, alive = blocks_in
        block_grad, parts = compute_block(field_in, grad_in)
        return (tuple((total + part for total, part in zip(totals, parts))), block_grad)

    totals, grad_out = lax.scan(advance, zero_parts, (field_blocks, grad_blocks, active))
    field_grad_flat, totals = (grad_out.reshape(cell_count, channels), totals)
    field_grad = field_grad_flat.reshape(lon_cells, lat_cells, channels)
    scale = float(lon_cells * lax.axis_size("gx") * lat_cells * lax.axis_size("gy")) ** (-0.5)
    up_sum, up_bias_sum, down_sum, gain_sum, shift_sum = [total * scale for total in totals]
    kernel_rows = []
    for lon_off in range(7):
        for lat_off in range(7):
            window = padded[lon_off : lon_off + lon_cells, lat_off : lat_off + lat_cells]
            kernel_rows.append(
                jnp.einsum("ijc,ijc->c", window, field_grad, preferred_element_type=jnp.float32)
            )
    kernel_sum = jnp.stack(kernel_rows, axis=0) * scale
    bias_sum = jnp.sum(field_grad.astype(jnp.float32), axis=(0, 1)) * scale
    grad_pad = padded_2(field_grad, (("gx", 0), ("gy", 1)), 3) * keep_lat
    spread = spread_back(grad_pad, kernel, lon_cells, lat_cells)
    input_grad = cotangent.astype(jnp.float32) + wet.astype(jnp.float32) * spread
    kernel_sum, bias_sum, gain_sum, shift_sum, up_sum, up_bias_sum, down_sum = lax.psum(
        (kernel_sum, bias_sum, gain_sum, shift_sum, up_sum, up_bias_sum, down_sum), ("gx", "gy")
    )
    return (input_grad, kernel_sum, bias_sum, gain_sum, shift_sum, up_sum, up_bias_sum, down_sum)


def solution(mesh):
    in_specs = (
        P("gx", "gy", None),
        P("gx", "gy", None),
        P("gx", "gy"),
        P(),
        P(),
        P(),
        P(),
        P(),
        P(),
        P(),
    )
    out_specs = (P("gx", "gy", None), P(), P(), P(), P(), P(), P(), P())
    return jax.shard_map(local, mesh=mesh, in_specs=in_specs, out_specs=out_specs, check_vma=False)
```

profile of v0, /device:TPU:1, one launch (start us, length us, event | category | flops | bytes accessed | tf_op | source)
XLA Modules:
  0.0 382.2 jit_solution(14918099358774612305)
XLA Ops:
  8.0 3.6 broadcast_multiply_fusion.3
  11.6 2.7 collective-permute-start
  16.3 2.3 collective-permute-done.1
  18.7 1.4 collective-permute-start.2
  20.1 2.7 collective-permute-start.3
  22.8 2.3 collective-permute-done.2
  25.6 2.8 maximum_multiply_fusion
  28.6 31.5 %multiply_add_fusion.1 = f32[64,64,256]{2,1,0:T(8,128)} fusion(f32[256]{0:T(256)S(1)} %bitcast.459, f32[256]{0:T(256)S(1)} %bitcast.461, f32[256]{0:T(256)S(1)} %bitcast.367, f32[256]{0:T(256)S(1)} %bitcast.369, f32[256]{0:T(256)S(1)} %bitcast.371, f32[256]{0:T(256)S(1)} %bitcast.373, f32[256]{0:T(256)S(1)} %bitcast.375, f32[256]{0:T(256)S(1)} %bitcast.377, ...), kind=kLoop, calls=%fused_computation.137 | loop fusion | flops 154140672 | bytes 107005952 | tf_op jit(solution)/shard_map/add | solution.py:39
  60.2 115.7 %while.21 = (s32[]{:T(128)}, f32[256,512]{1,0:T(8,128)S(1)}, f32[512]{0:T(512)S(1)}, f32[512,256]{1,0:T(8,128)}, f32[256]{0:T(256)S(1)}, /*index=5*/f32[256]{0:T...) while((s32[]{:T(128)}, f32[256,512]{1,0:T(8,128)S(1)}, ...), condition=%wide.region_8.9_spmd.clone, body=%wide.region_0.8_spmd.clone.sunk | while | flops 680397312 | bytes 13709542 | solution.py:142
  64.0 1.4 convolution_add_fusion.6
  65.5 2.1 convolution_add_fusion.8
  67.6 1.6 convert_reduce_fusion.3
  69.2 1.7 convolution_add_fusion.7
  70.9 1.5 multiply_reduce_fusion.7
  72.4 2.1 fusion.86
  79.8 2.3 convolution_add_fusion.8
  82.1 1.5 convert_reduce_fusion.3
  83.7 1.7 convolution_add_fusion.7
  85.4 1.5 multiply_reduce_fusion.7
  86.9 2.1 fusion.86
  94.3 2.3 convolution_add_fusion.8
  96.6 1.5 convert_reduce_fusion.3
  98.1 1.7 convolution_add_fusion.7
  99.8 1.5 multiply_reduce_fusion.7
  101.4 2.1 fusion.86
  108.7 2.3 convolution_add_fusion.8
  111.1 1.5 convert_reduce_fusion.3
  112.6 1.7 convolution_add_fusion.7
  114.3 1.5 multiply_reduce_fusion.7
  115.9 2.1 fusion.86
  121.8 1.4 convolution_add_fusion.6
  123.2 2.3 convolution_add_fusion.8
  125.6 1.6 convert_reduce_fusion.3
  127.1 1.7 convolution_add_fusion.7
  128.8 1.5 multiply_reduce_fusion.7
  130.4 2.1 fusion.86
  137.7 2.3 convolution_add_fusion.8
  140.1 1.5 convert_reduce_fusion.3
  141.6 1.7 convolution_add_fusion.7
  143.3 1.5 multiply_reduce_fusion.7
  144.9 2.1 fusion.86
  152.2 2.3 convolution_add_fusion.8
  154.5 1.5 convert_reduce_fusion.3
  156.1 1.7 convolution_add_fusion.7
  157.8 1.5 multiply_reduce_fusion.7
  159.3 2.1 fusion.86
  166.7 2.3 convolution_add_fusion.8
  169.0 1.6 convert_reduce_fusion.3
  170.6 1.7 convolution_add_fusion.7
  172.3 1.5 multiply_reduce_fusion.7
  173.8 2.1 fusion.86
  175.9 8.4 %fusion.62 = (f32[256]{0:T(256)S(1)}, f32[256]{0:T(256)S(1)}, f32[256]{0:T(256)S(1)}, f32[256]{0:T(256)S(1)}, f32[256]{0:T(256)S(1)}, /*index=5*/f32[256]{0:T(25...) fusion(bf16[256,64,64]{0,2,1:T(8,128)(2,1)} %bitcast.357, ...), kind=kLoop, calls=%fused_computation.132 | loop fusion | flops 41939712 | bytes 29373440 | tf_op jit(solution)/shard_map/ijc,ijc->c/dot_general | solution.py:152
  184.4 10.9 %fusion.63 = (f32[256]{0:T(256)S(1)}, f32[256]{0:T(256)S(1)}, f32[256]{0:T(256)S(1)}, f32[256]{0:T(256)S(1)}, f32[256]{0:T(256)S(1)}, /*index=5*/f32[256]{0:T(25...) fusion(bf16[256,64,64]{0,2,1:T(8,128)(2,1)S(1)} %bitcast.359, ...), kind=kLoop, calls=%fused_computation.133 | loop fusion | flops 57667072 | bytes 39864320 | tf_op jit(solution)/shard_map/ijc,ijc->c/dot_general | solution.py:152
  195.3 10.7 %fusion.64 = (f32[256]{0:T(256)S(1)}, f32[256]{0:T(256)S(1)}, f32[256]{0:T(256)S(1)}, f32[256]{0:T(256)S(1)}, f32[256]{0:T(256)S(1)}, /*index=5*/f32[256]{0:T(25...) fusion(bf16[256,64,64]{0,2,1:T(8,128)(2,1)S(1)} %bitcast.360, ...), kind=kLoop, calls=%fused_computation.134 | loop fusion | flops 57667072 | bytes 39864320 | tf_op jit(solution)/shard_map/ijc,ijc->c/dot_general | solution.py:152
  208.0 4.3 %collective-permute-start.4 = (bf16[3,64,256]{2,1,0:T(8,128)(2,1)S(1)}, bf16[3,64,256]{2,1,0:T(8,128)(2,1)S(1)}, u32[]{:S(2)}, u32[]{:S(2)}) collective-permute-start(bf16[3,64,256]{2,1,0:T(8,128)(2,1)S(1)} %get-tuple-element.237), channel_id=1, source_target_pairs={{0,8},{8,16},{16,24},{24,32},{32,40},{40,48},{48,56},{56,64},{64,7... | collective-permute-start | bytes 294920 | tf_op jit(solution)/shard_map/ppermute | solution.py:14
  212.3 1.9 broadcast_multiply_fusion.5
  214.9 1.4 collective-permute-done.5
  216.6 3.6 collective-permute-start.7
  220.2 72.7 %all-reduce = (f32[49,256]{1,0:T(8,128)}, f32[256]{0:T(256)}, f32[256]{0:T(256)}, f32[256]{0:T(256)}, f32[512]{0:T(512)}) all-reduce(f32[49,256]{1,0:T(8,128)S(1)} %broadcast_multiply_fusion.7, f32[256]{0:T(256)S(1)} %broadcast_multiply_fusion.11, f32[256]{0:T(256)S(1)} %get-tuple-element.293, ...), channel_id=1, replica_groups=mesh['gx'=16,'gy'=8] {'gx','gy'}, use_global_device_ids=true, to_apply=%region_9.10 | all-reduce | flops 13824 | bytes 110592 | tf_op jit(solution)/shard_map/psum | solution.py:159
  292.9 1.7 maximum_multiply_fusion.1
  294.7 31.7 %multiply_add_fusion = f32[64,64,256]{2,1,0:T(8,128)} fusion(bf16[64,64,256]{2,1,0:T(8,128)(2,1)S(1)} %copy-done.3, bf16[70,70,256]{2,1,0:T(8,128)(2,1)S(1)} %maximum_multiply_fusion.1, f32[256]{0:T(256)S(1)} %bitcast.460, f32[256]{0:T(256)S(1)} %bitcast.462, f32[256]{0:T(256)S(1)} %bitcast.368, f32[256]{0:T(256)S(1)} %bitcast.370, f32[256]{0:T(256)S(1)} %bitcast.372, ...), kind=kLoop, calls=%fused_computation.136 | loop fusion | flops 156237824 | bytes 109118464 | tf_op jit(solution)/shard_map/add | solution.py:158
  326.4 45.2 %all-reduce.4.cloned.1.call-done = (f32[256,512]{1,0:T(8,128)}, f32[512,256]{1,0:T(8,128)}) async-done(((f32[256,512]{1,0:T(8,128)}, f32[512,256]{1,0:T(8,128)}), (f32[256,512]{1,0:T(8,128)}, f32[512,256]{1,0:T(8,128)})) %all-reduce.4.cloned.1.call-update) | async-done | bytes 1048592 | tf_op jit(solution)/shard_map/psum | solution.py:159
  371.6 1.9 copy.385
  373.5 1.9 copy.386
  (217 shorter events, 45.4 us)
Async XLA Ops:
  7.2 364.4 %all-reduce.4.cloned.1.call-start = ((), (), s32[]{:S(2)}) async-start(), calls=%async_computation | async-start | bytes 2097152 | tf_op jit(solution)/shard_map/psum | solution.py:159
  8.0 6.3 %copy-start.5 = (bf16[49,256]{1,0:T(8,128)(2,1)S(1)}, bf16[49,256]{1,0:T(8,128)(2,1)}, u32[]{:S(2)}) copy-start(bf16[49,256]{1,0:T(8,128)(2,1)} %param.15) | copy-start | bytes 75268
  8.0 7.6 %copy-start.41 = (bf16[256]{0:T(256)(128)(2,1)S(1)}, bf16[256]{0:T(256)(128)(2,1)}, u32[]{:S(2)}) copy-start(bf16[256]{0:T(256)(128)(2,1)} %param.16) | copy-start | bytes 1540
  11.6 13.6 %copy-start.2 = (bf16[64,64,256]{2,1,0:T(8,128)(2,1)}, bf16[64,64,256]{2,1,0:T(8,128)(2,1)S(1)}, u32[]{:S(2)}) copy-start(bf16[64,64,256]{2,1,0:T(8,128)(2,1)S(1)} %get-tuple-element.291) | copy-start | bytes 6291460
  11.6 4.7 %collective-permute-start = (bf16[3,64,256]{2,1,0:T(8,128)(2,1)S(1)}, bf16[3,64,256]{2,1,0:T(8,128)(2,1)S(1)}, u32[]{:S(2)}, u32[]{:S(2)}) collective-permute-start(bf16[3,64,256]{2,1,0:T(8,128)(2,1)S(1)} %get-tuple-element.239), channel_id=1, source_target_pairs={{0,8},{8,16},{16,24},{24,32},{32,40},{40,48},{48,56},{56,64},{64,7... | collective-permute-start | bytes 294920 | tf_op jit(solution)/shard_map/ppermute | solution.py:14
  14.3 4.3 %collective-permute-start.1 = (bf16[3,64,256]{2,1,0:T(8,128)(2,1)S(1)}, bf16[3,64,256]{2,1,0:T(8,128)(2,1)S(1)}, u32[]{:S(2)}, u32[]{:S(2)}) collective-permute-start(bf16[3,64,256]{2,1,0:T(8,128)(2,1)S(1)} %get-tuple-element.240), channel_id=1, source_target_pairs={{8,0},{16,8},{24,16},{32,24},{40,32},{48,40},{56,48},{64,56},{72,6... | collective-permute-start | bytes 294920 | tf_op jit(solution)/shard_map/ppermute | solution.py:15
  16.1 12.3 %copy-start.7 = (f32[1,256]{1,0:T(1,128)S(1)}, f32[1,256]{1,0:T(1,128)}, u32[]{:S(2)}) copy-start(f32[1,256]{1,0:T(1,128)} %get-tuple-element.275) | copy-start | bytes 3076
  16.1 12.3 %copy-start.9 = (f32[1,256]{1,0:T(1,128)S(1)}, f32[1,256]{1,0:T(1,128)}, u32[]{:S(2)}) copy-start(f32[1,256]{1,0:T(1,128)} %get-tuple-element.276) | copy-start | bytes 3076
  16.1 12.3 %copy-start.11 = (f32[1,256]{1,0:T(1,128)S(1)}, f32[1,256]{1,0:T(1,128)}, u32[]{:S(2)}) copy-start(f32[1,256]{1,0:T(1,128)} %get-tuple-element.277) | copy-start | bytes 3076
  16.1 12.3 %copy-start.13 = (f32[1,256]{1,0:T(1,128)S(1)}, f32[1,256]{1,0:T(1,128)}, u32[]{:S(2)}) copy-start(f32[1,256]{1,0:T(1,128)} %get-tuple-element.278) | copy-start | bytes 3076
  16.1 12.4 %copy-start.15 = (f32[1,256]{1,0:T(1,128)S(1)}, f32[1,256]{1,0:T(1,128)}, u32[]{:S(2)}) copy-start(f32[1,256]{1,0:T(1,128)} %get-tuple-element.279) | copy-start | bytes 3076
  16.2 12.4 %copy-start.17 = (f32[1,256]{1,0:T(1,128)S(1)}, f32[1,256]{1,0:T(1,128)}, u32[]{:S(2)}) copy-start(f32[1,256]{1,0:T(1,128)} %get-tuple-element.280) | copy-start | bytes 3076
  16.2 12.4 %copy-start.19 = (f32[1,256]{1,0:T(1,128)S(1)}, f32[1,256]{1,0:T(1,128)}, u32[]{:S(2)}) copy-start(f32[1,256]{1,0:T(1,128)} %get-tuple-element.281) | copy-start | bytes 3076
  16.2 12.4 %copy-start.21 = (f32[1,256]{1,0:T(1,128)S(1)}, f32[1,256]{1,0:T(1,128)}, u32[]{:S(2)}) copy-start(f32[1,256]{1,0:T(1,128)} %get-tuple-element.282) | copy-start | bytes 3076
  16.2 12.4 %copy-start.23 = (f32[1,256]{1,0:T(1,128)S(1)}, f32[1,256]{1,0:T(1,128)}, u32[]{:S(2)}) copy-start(f32[1,256]{1,0:T(1,128)} %get-tuple-element.283) | copy-start | bytes 3076
  16.2 12.4 %copy-start.25 = (f32[1,256]{1,0:T(1,128)S(1)}, f32[1,256]{1,0:T(1,128)}, u32[]{:S(2)}) copy-start(f32[1,256]{1,0:T(1,128)} %get-tuple-element.284) | copy-start | bytes 3076
  16.2 12.4 %copy-start.27 = (f32[1,256]{1,0:T(1,128)S(1)}, f32[1,256]{1,0:T(1,128)}, u32[]{:S(2)}) copy-start(f32[1,256]{1,0:T(1,128)} %get-tuple-element.285) | copy-start | bytes 3076
  16.2 12.4 %copy-start.29 = (f32[1,256]{1,0:T(1,128)S(1)}, f32[1,256]{1,0:T(1,128)}, u32[]{:S(2)}) copy-start(f32[1,256]{1,0:T(1,128)} %get-tuple-element.286) | copy-start | bytes 3076
  16.2 12.4 %copy-start.31 = (f32[1,256]{1,0:T(1,128)S(1)}, f32[1,256]{1,0:T(1,128)}, u32[]{:S(2)}) copy-start(f32[1,256]{1,0:T(1,128)} %get-tuple-element.287) | copy-start | bytes 3076
  16.2 12.4 %copy-start.33 = (f32[1,256]{1,0:T(1,128)S(1)}, f32[1,256]{1,0:T(1,128)}, u32[]{:S(2)}) copy-start(f32[1,256]{1,0:T(1,128)} %get-tuple-element.288) | copy-start | bytes 3076
  16.2 12.4 %copy-start.35 = (f32[1,256]{1,0:T(1,128)S(1)}, f32[1,256]{1,0:T(1,128)}, u32[]{:S(2)}) copy-start(f32[1,256]{1,0:T(1,128)} %get-tuple-element.289) | copy-start | bytes 3076
  16.3 12.4 %copy-start.39 = (f32[256]{0:T(256)S(1)}, f32[256]{0:T(256)}, u32[]{:S(2)}) copy-start(f32[256]{0:T(256)} %convert_element_type.898) | copy-start | bytes 3076
  18.7 6.5 %collective-permute-start.2 = (bf16[70,3,256]{2,1,0:T(4,128)(2,1)S(1)}, bf16[70,3,256]{2,1,0:T(4,128)(2,1)S(1)}, u32[]{:S(2)}, u32[]{:S(2)}) collective-permute-start(bf16[70,3,256]{2,1,0:T(4,128)(2,1)S(1)} %get-tuple-element.235), channel_id=1, source_target_pairs={{0,1},{1,2},{2,3},{3,4},{4,5},{5,6},{6,7},{7,0},{8,9},{9,10},{10,1... | collective-permute-start | bytes 322568 | tf_op jit(solution)/shard_map/ppermute | solution.py:14
  20.1 5.5 %collective-permute-start.3 = (bf16[70,3,256]{2,1,0:T(4,128)(2,1)S(1)}, bf16[70,3,256]{2,1,0:T(4,128)(2,1)S(1)}, u32[]{:S(2)}, u32[]{:S(2)}) collective-permute-start(bf16[70,3,256]{2,1,0:T(4,128)(2,1)S(1)} %get-tuple-element.236), channel_id=1, source_target_pairs={{1,0},{2,1},{3,2},{4,3},{5,4},{6,5},{7,6},{0,7},{9,8},{10,9},{11,1... | collective-permute-start | bytes 322568 | tf_op jit(solution)/shard_map/ppermute | solution.py:15
  22.8 5.6 %copy-start.37 = (bf16[70]{0:T(256)(128)(2,1)}, bf16[70]{0:T(256)(128)(2,1)S(1)}, u32[]{:S(2)}) copy-start(bf16[70]{0:T(256)(128)(2,1)S(1)} %and_convert_fusion) | copy-start | bytes 424
  28.6 31.6 %copy-start.4 = (bf16[256,512]{1,0:T(8,128)(2,1)S(1)}, bf16[256,512]{1,0:T(8,128)(2,1)}, u32[]{:S(2)}) copy-start(bf16[256,512]{1,0:T(8,128)(2,1)} %param.19) | copy-start | bytes 786436
  28.6 31.6 %copy-start.6 = (bf16[512]{0:T(512)(128)(2,1)S(1)}, bf16[512]{0:T(512)(128)(2,1)}, u32[]{:S(2)}) copy-start(bf16[512]{0:T(512)(128)(2,1)} %param.20) | copy-start | bytes 3076
  60.2 7.4 %copy-start.40 = (bf16[512,256]{1,0:T(8,128)(2,1)S(1)}, bf16[512,256]{1,0:T(8,128)(2,1)}, u32[]{:S(2)}) copy-start(bf16[512,256]{1,0:T(8,128)(2,1)} %get-tuple-element.444) | copy-start | bytes 786436 | tf_op jit(solution)/shard_map/while
  74.5 7.6 %copy-start.40 = (bf16[512,256]{1,0:T(8,128)(2,1)S(1)}, bf16[512,256]{1,0:T(8,128)(2,1)}, u32[]{:S(2)}) copy-start(bf16[512,256]{1,0:T(8,128)(2,1)} %get-tuple-element.444) | copy-start | bytes 786436 | tf_op jit(solution)/shard_map/while
  89.0 7.6 %copy-start.40 = (bf16[512,256]{1,0:T(8,128)(2,1)S(1)}, bf16[512,256]{1,0:T(8,128)(2,1)}, u32[]{:S(2)}) copy-start(bf16[512,256]{1,0:T(8,128)(2,1)} %get-tuple-element.444) | copy-start | bytes 786436 | tf_op jit(solution)/shard_map/while
  103.5 7.6 %copy-start.40 = (bf16[512,256]{1,0:T(8,128)(2,1)S(1)}, bf16[512,256]{1,0:T(8,128)(2,1)}, u32[]{:S(2)}) copy-start(bf16[512,256]{1,0:T(8,128)(2,1)} %get-tuple-element.444) | copy-start | bytes 786436 | tf_op jit(solution)/shard_map/while
  118.0 7.6 %copy-start.40 = (bf16[512,256]{1,0:T(8,128)(2,1)S(1)}, bf16[512,256]{1,0:T(8,128)(2,1)}, u32[]{:S(2)}) copy-start(bf16[512,256]{1,0:T(8,128)(2,1)} %get-tuple-element.444) | copy-start | bytes 786436 | tf_op jit(solution)/shard_map/while
  132.5 7.6 %copy-start.40 = (bf16[512,256]{1,0:T(8,128)(2,1)S(1)}, bf16[512,256]{1,0:T(8,128)(2,1)}, u32[]{:S(2)}) copy-start(bf16[512,256]{1,0:T(8,128)(2,1)} %get-tuple-element.444) | copy-start | bytes 786436 | tf_op jit(solution)/shard_map/while
  147.0 7.6 %copy-start.40 = (bf16[512,256]{1,0:T(8,128)(2,1)S(1)}, bf16[512,256]{1,0:T(8,128)(2,1)}, u32[]{:S(2)}) copy-start(bf16[512,256]{1,0:T(8,128)(2,1)} %get-tuple-element.444) | copy-start | bytes 786436 | tf_op jit(solution)/shard_map/while
  161.4 7.6 %copy-start.40 = (bf16[512,256]{1,0:T(8,128)(2,1)S(1)}, bf16[512,256]{1,0:T(8,128)(2,1)}, u32[]{:S(2)}) copy-start(bf16[512,256]{1,0:T(8,128)(2,1)} %get-tuple-element.444) | copy-start | bytes 786436 | tf_op jit(solution)/shard_map/while
  175.9 8.4 %copy-start = (bf16[8,512,256]{2,1,0:T(8,128)(2,1)S(1)}, bf16[8,512,256]{2,1,0:T(8,128)(2,1)}, u32[]{:S(2)}) copy-start(bf16[8,512,256]{2,1,0:T(8,128)(2,1)} %get-tuple-element.85) | copy-start | bytes 6291460
  206.0 8.2 %copy-start.1 = (bf16[8,512,256]{2,1,0:T(8,128)(2,1)S(1)}, bf16[8,512,256]{2,1,0:T(8,128)(2,1)}, u32[]{:S(2)}) copy-start(bf16[8,512,256]{2,1,0:T(8,128)(2,1)} %get-tuple-element.85) | copy-start | bytes 6291460
  206.0 86.8 %copy-start.38 = (bf16[70]{0:T(256)(128)(2,1)S(1)}, bf16[70]{0:T(256)(128)(2,1)}, u32[]{:S(2)}) copy-start(bf16[70]{0:T(256)(128)(2,1)} %copy-done.37) | copy-start | bytes 424
  208.0 6.9 %collective-permute-start.4 = (bf16[3,64,256]{2,1,0:T(8,128)(2,1)S(1)}, bf16[3,64,256]{2,1,0:T(8,128)(2,1)S(1)}, u32[]{:S(2)}, u32[]{:S(2)}) collective-permute-start(bf16[3,64,256]{2,1,0:T(8,128)(2,1)S(1)} %get-tuple-element.237), channel_id=1, source_target_pairs={{0,8},{8,16},{16,24},{24,32},{32,40},{40,48},{48,56},{56,64},{64,7... | collective-permute-start | bytes 294920 | tf_op jit(solution)/shard_map/ppermute | solution.py:14
  212.3 4.0 %collective-permute-start.5 = (bf16[3,64,256]{2,1,0:T(8,128)(2,1)S(1)}, bf16[3,64,256]{2,1,0:T(8,128)(2,1)S(1)}, u32[]{:S(2)}, u32[]{:S(2)}) collective-permute-start(bf16[3,64,256]{2,1,0:T(8,128)(2,1)S(1)} %get-tuple-element.238), channel_id=1, source_target_pairs={{8,0},{16,8},{24,16},{32,24},{40,32},{48,40},{56,48},{64,56},{72,6... | collective-permute-start | bytes 294920 | tf_op jit(solution)/shard_map/ppermute | solution.py:15
  214.8 79.8 %copy-start.8 = (f32[1,256]{1,0:T(1,128)S(1)}, f32[1,256]{1,0:T(1,128)}, u32[]{:S(2)}) copy-start(f32[1,256]{1,0:T(1,128)} %get-tuple-element.275) | copy-start | bytes 3076
  214.8 79.8 %copy-start.10 = (f32[1,256]{1,0:T(1,128)S(1)}, f32[1,256]{1,0:T(1,128)}, u32[]{:S(2)}) copy-start(f32[1,256]{1,0:T(1,128)} %get-tuple-element.276) | copy-start | bytes 3076
  214.8 79.8 %copy-start.12 = (f32[1,256]{1,0:T(1,128)S(1)}, f32[1,256]{1,0:T(1,128)}, u32[]{:S(2)}) copy-start(f32[1,256]{1,0:T(1,128)} %get-tuple-element.277) | copy-start | bytes 3076
  214.8 79.8 %copy-start.14 = (f32[1,256]{1,0:T(1,128)S(1)}, f32[1,256]{1,0:T(1,128)}, u32[]{:S(2)}) copy-start(f32[1,256]{1,0:T(1,128)} %get-tuple-element.278) | copy-start | bytes 3076
  214.8 79.8 %copy-start.16 = (f32[1,256]{1,0:T(1,128)S(1)}, f32[1,256]{1,0:T(1,128)}, u32[]{:S(2)}) copy-start(f32[1,256]{1,0:T(1,128)} %get-tuple-element.279) | copy-start | bytes 3076
  214.8 79.8 %copy-start.18 = (f32[1,256]{1,0:T(1,128)S(1)}, f32[1,256]{1,0:T(1,128)}, u32[]{:S(2)}) copy-start(f32[1,256]{1,0:T(1,128)} %get-tuple-element.280) | copy-start | bytes 3076
  214.8 79.8 %copy-start.20 = (f32[1,256]{1,0:T(1,128)S(1)}, f32[1,256]{1,0:T(1,128)}, u32[]{:S(2)}) copy-start(f32[1,256]{1,0:T(1,128)} %get-tuple-element.281) | copy-start | bytes 3076
  214.8 79.8 %copy-start.22 = (f32[1,256]{1,0:T(1,128)S(1)}, f32[1,256]{1,0:T(1,128)}, u32[]{:S(2)}) copy-start(f32[1,256]{1,0:T(1,128)} %get-tuple-element.282) | copy-start | bytes 3076
  214.8 79.8 %copy-start.24 = (f32[1,256]{1,0:T(1,128)S(1)}, f32[1,256]{1,0:T(1,128)}, u32[]{:S(2)}) copy-start(f32[1,256]{1,0:T(1,128)} %get-tuple-element.283) | copy-start | bytes 3076
  214.9 79.8 %copy-start.26 = (f32[1,256]{1,0:T(1,128)S(1)}, f32[1,256]{1,0:T(1,128)}, u32[]{:S(2)}) copy-start(f32[1,256]{1,0:T(1,128)} %get-tuple-element.284) | copy-start | bytes 3076
  214.9 79.8 %copy-start.28 = (f32[1,256]{1,0:T(1,128)S(1)}, f32[1,256]{1,0:T(1,128)}, u32[]{:S(2)}) copy-start(f32[1,256]{1,0:T(1,128)} %get-tuple-element.285) | copy-start | bytes 3076
  214.9 79.8 %copy-start.30 = (f32[1,256]{1,0:T(1,128)S(1)}, f32[1,256]{1,0:T(1,128)}, u32[]{:S(2)}) copy-start(f32[1,256]{1,0:T(1,128)} %get-tuple-element.286) | copy-start | bytes 3076
  214.9 79.8 %copy-start.32 = (f32[1,256]{1,0:T(1,128)S(1)}, f32[1,256]{1,0:T(1,128)}, u32[]{:S(2)}) copy-start(f32[1,256]{1,0:T(1,128)} %get-tuple-element.287) | copy-start | bytes 3076
  214.9 79.8 %copy-start.34 = (f32[1,256]{1,0:T(1,128)S(1)}, f32[1,256]{1,0:T(1,128)}, u32[]{:S(2)}) copy-start(f32[1,256]{1,0:T(1,128)} %get-tuple-element.288) | copy-start | bytes 3076
  214.9 79.8 %copy-start.36 = (f32[1,256]{1,0:T(1,128)S(1)}, f32[1,256]{1,0:T(1,128)}, u32[]{:S(2)}) copy-start(f32[1,256]{1,0:T(1,128)} %get-tuple-element.289) | copy-start | bytes 3076
  216.5 76.4 %collective-permute-start.6 = (bf16[70,3,256]{2,1,0:T(4,128)(2,1)S(1)}, bf16[70,3,256]{2,1,0:T(4,128)(2,1)S(1)}, u32[]{:S(2)}, u32[]{:S(2)}) collective-permute-start(bf16[70,3,256]{2,1,0:T(4,128)(2,1)S(1)} %get-tuple-element.233), channel_id=1, source_target_pairs={{0,1},{1,2},{2,3},{3,4},{4,5},{5,6},{6,7},{7,0},{8,9},{9,10},{10,1... | collective-permute-start | bytes 322568 | tf_op jit(solution)/shard_map/ppermute | solution.py:14
  216.6 76.3 %collective-permute-start.7 = (bf16[70,3,256]{2,1,0:T(4,128)(2,1)S(1)}, bf16[70,3,256]{2,1,0:T(4,128)(2,1)S(1)}, u32[]{:S(2)}, u32[]{:S(2)}) collective-permute-start(bf16[70,3,256]{2,1,0:T(4,128)(2,1)S(1)} %get-tuple-element.234), channel_id=1, source_target_pairs={{1,0},{2,1},{3,2},{4,3},{5,4},{6,5},{7,6},{0,7},{9,8},{10,9},{11,1... | collective-permute-start | bytes 322568 | tf_op jit(solution)/shard_map/ppermute | solution.py:15
  292.8 1.9 copy-start.3
Sparse Core Ops, SparseCore 0:
  220.3 151.2 all-reduce.3
where the time goes:
time: 386 us; the launch traced here: 382 us
  other arithmetic  155 us (40%)
  blocking collectives  72.7 us (19%)
  matrix products  67.6 us (18%)
  waiting for transfers between devices  51.7 us (13%)
  starting transfers between devices  14.8 us (4%)
  between operations  14.7 us (4%)
  local copies, waits for them, and re-layouts  5.07 us (1%)
    psum x1, blocking collectives, local(): lax.psum((kernel_sum, bias_sum, gain_sum, shift_sum, up_sum, up_bias_sum,...  72.7 us
    psum x1, waiting for transfers between devices, local(): lax.psum((kernel_sum, bias_sum, gain_sum, shift_sum, up_sum, up_bias_sum,...  45.2 us
    dot_general x16, matrix products, contract_rows(): lax.dot_general(left, right, (((0,), (0,)), ((), ())), preferred_element_...  31.9 us
    add x1, other arithmetic, local(): cotangent.astype(jnp.float32) + wet.astype(jnp.float32) * spread  31.7 us
    add x1, other arithmetic, depthwise(): total + kernel[lon_off * 7 + lat_off].astype(jnp.float32) * window.astype...  31.5 us
    dot_general x3, other arithmetic, local(): jnp.einsum('ijc,ijc->c', window, field_grad, preferred_element_type=jnp.f...  30.1 us
    dot_general x16, matrix products, contract_cols(): lax.dot_general(left, right, (((1,), (1,)), ((), ())), preferred_element_...  24.6 us
    dynamic_update_slice x8, other arithmetic, local(): lax.scan(advance, zero_parts, (field_blocks, grad_blocks, active))  16.8 us
  transfers between devices with their start and end apart: 9, of which 5 were waited for; matrix products, arithmetic and copies ran while one was open for 10% of the time, Pallas kernels for 0%

commit v1 on v0

v1 whole, which is shorter than its diff:
```python
import functools

import jax
import jax.numpy as jnp
import numpy as np
from jax import lax
from jax.experimental import pallas as pl
from jax.experimental.pallas import tpu as pltpu
from jax.sharding import PartitionSpec as P

F32 = jnp.float32
BF16 = jnp.bfloat16
TILE = 16
SPAN = TILE + 6
HALF = 256
AXES = ("gx", "gy")


def basis():
    pairs, alone, seen = [], [], set()
    for a in range(SPAN):
        for b in range(SPAN):
            other = ((-a) % SPAN, (-b) % SPAN)
            if other == (a, b):
                alone.append((a, b))
            elif other not in seen:
                seen.add((a, b))
                pairs.append((a, b))
    i, j = np.meshgrid(np.arange(SPAN), np.arange(SPAN), indexing="ij")

    def angle(f):
        return 2 * np.pi * ((f[0] * i + f[1] * j) % SPAN) / SPAN

    cos = np.zeros((HALF, SPAN, SPAN))
    sin = np.zeros((HALF, SPAN, SPAN))
    weight = np.zeros(HALF)
    paired = np.zeros(HALF)
    for n, (one, two) in enumerate(((alone[0], alone[1]), (alone[2], alone[3]))):
        cos[n], sin[n], weight[n] = np.cos(angle(one)), np.cos(angle(two)), 1
    for n, f in enumerate(pairs, start=2):
        cos[n], sin[n], weight[n], paired[n] = np.cos(angle(f)), -np.sin(angle(f)), 2, 1
    return cos, sin, weight / SPAN**2, paired


@functools.cache
def tables():
    cos, sin, weight, paired = basis()
    both = np.concatenate([cos, sin])
    place = np.zeros((2 * HALF, 2 * HALF))
    for i in range(20):
        place[:, 24 * i : 24 * i + 22] = both[:, i]
        if i < 6:
            at = 16 + 2 * (i % 3)
            place[:, 24 * i + 22 : 24 * i + 24] = both[:, 20 + i // 3, at : at + 2]
    for m in range(2):
        place[:, 480 + 16 * m : 496 + 16 * m] = both[:, 20 + m, :16]
    own = both[:, :TILE, :TILE].reshape(2 * HALF, TILE * TILE)
    back = own.T
    ct = (cos * weight[:, None, None])[:, :7, :7].reshape(HALF, 49)
    st = (sin * weight[:, None, None])[:, :7, :7].reshape(HALF, 49)
    pair = paired[:, None]
    taps = np.concatenate([ct, st * pair, ct * pair + st * (1 - pair)])
    flipped = taps[:, ::-1]
    collect = np.concatenate([ct, ct * pair + st * (1 - pair), st * pair]).T
    return dict(
        place=place.astype(jnp.bfloat16),
        own=own.astype(jnp.bfloat16),
        back=back.astype(jnp.bfloat16),
        taps=np.concatenate([taps, flipped]).astype(np.float32),
        collect=collect.astype(np.float32),
    )


def dot(a, b):
    return jnp.dot(a, b, preferred_element_type=F32)


def dot_cols(a, b):
    return lax.dot_general(a, b, (((1,), (1,)), ((), ())), preferred_element_type=F32)


def dot_rows(a, b):
    return lax.dot_general(a, b, (((0,), (0,)), ((), ())), preferred_element_type=F32)


def patch(ref, a, b):
    slabs = [
        ref[TILE * a + i, pl.ds(pl.multiple_of(TILE * b, TILE), 32), :].astype(F32)
        for i in range(SPAN)
    ]
    row = lax.broadcasted_iota(jnp.int32, (8, slabs[0].shape[1]), 0)
    parts = []
    for i in range(20):
        tail = slabs[i][16:24]
        if i < 6:
            spare = pltpu.roll(slabs[20 + i // 3][16:24], 6 - 2 * (i % 3), 0)
            tail = jnp.where(row < 6, tail, spare)
        parts += [slabs[i][:16], tail]
    parts += [slabs[20][:16], slabs[21][:16]]
    return jnp.concatenate(parts, axis=0).astype(BF16)


def filtered(wave, taps_ref, back_ref):
    real, imag = wave[:HALF], wave[HALF:]
    k_real, k_imag, k_last = taps_ref[:HALF], taps_ref[HALF : 2 * HALF], taps_ref[2 * HALF :]
    out_real = real * k_real + imag * k_imag
    out_imag = imag * k_last - real * k_imag
    return dot(back_ref[:, :HALF], out_real.astype(BF16)) + dot(
        back_ref[:, HALF:], out_imag.astype(BF16)
    )


def cell_kernel(
    pad_ref, cot_ref, wet_ref, place_ref, own_ref, back_ref, taps_ref, collect_ref,
    bias_ref, gain_ref, shift_ref, up_ref, up_bias_ref, down_ref,
    fg_ref, up_sum_ref, up_bias_sum_ref, down_sum_ref, small_ref,
    p1_ref, p2_ref, p3_ref,
):
    a, b = pl.program_id(0), pl.program_id(1)
    channels = pad_ref.shape[2]

    @pl.when((a == 0) & (b == 0))
    def _():
        for ref in (up_sum_ref, up_bias_sum_ref, down_sum_ref, small_ref, p1_ref, p2_ref, p3_ref):
            ref[...] = jnp.zeros_like(ref)

    wave = dot(place_ref[...], patch(pad_ref, a, b))
    field = filtered(wave, taps_ref, back_ref) + bias_ref[...]
    wet = wet_ref[...].reshape(TILE * TILE, 128)
    wet = jnp.concatenate([wet, wet], axis=1)
    masked_grad = cot_ref[...].reshape(TILE * TILE, channels) * wet
    average = jnp.mean(field, axis=-1, keepdims=True)
    centred = field - average
    variance = jnp.mean(centred * centred, axis=-1, keepdims=True)
    inv_std = lax.rsqrt(variance + 1e-06)
    normed = centred * inv_std
    gain = gain_ref[...]
    normed_out = (normed * gain + shift_ref[...]).astype(BF16)
    hidden = dot(normed_out, up_ref[...]) + up_bias_ref[...]
    bell = jnp.exp(-0.5 * hidden * hidden)
    t = pl.reciprocal(1.0 + (0.3275911 * 0.7071067811865476) * jnp.abs(hidden), approx=True)
    poly = 0.5 * 1.061405429
    for c in (-1.453152027, 1.421413741, -0.284496736, 0.254829592):
        poly = poly * t + 0.5 * c
    tail = poly * t * bell
    cumulative = jnp.where(hidden >= 0, 1.0 - tail, tail)
    activated = (hidden * cumulative).astype(BF16)
    act_grad = dot_cols(masked_grad, down_ref[...])
    hidden_grad = (act_grad * (cumulative + hidden * (bell * 0.3989422804014327))).astype(BF16)
    down_sum_ref[...] += dot_rows(activated, masked_grad)
    up_sum_ref[...] += dot_rows(normed_out, hidden_grad)
    up_bias_sum_ref[...] += jnp.sum(hidden_grad.astype(F32), axis=0, keepdims=True)
    normed_grad = dot_cols(hidden_grad, up_ref[...])
    product = normed_grad * normed
    small_ref[49:50, :] += jnp.sum(product, axis=0, keepdims=True)
    small_ref[50:51, :] += jnp.sum(normed_grad, axis=0, keepdims=True)
    scaled_mean = jnp.mean(normed_grad * gain, axis=-1, keepdims=True)
    product_mean = jnp.mean(product * gain, axis=-1, keepdims=True)
    field_grad = (inv_std * (normed_grad * gain - scaled_mean - normed * product_mean)).astype(BF16)
    fg_ref[...] = field_grad.reshape(TILE, TILE, channels)
    ripple = dot(own_ref[...], field_grad)
    g_real, g_imag = ripple[:HALF], ripple[HALF:]
    x_real, x_imag = wave[:HALF], wave[HALF:]
    p1_ref[...] += g_real * x_real
    p2_ref[...] += g_imag * x_imag
    p3_ref[...] += g_real * x_imag - g_imag * x_real
    small_ref[51:52, :] += g_real[0:1]

    @pl.when((a == pl.num_programs(0) - 1) & (b == pl.num_programs(1) - 1))
    def _():
        total = 0.0
        for n, ref in enumerate((p1_ref, p2_ref, p3_ref)):
            total += jnp.dot(
                collect_ref[:, n * HALF : (n + 1) * HALF],
                ref[...],
                precision=lax.Precision.HIGHEST,
                preferred_element_type=F32,
            )
        small_ref[:49, :] = total


def spread_kernel(pad_ref, cot_ref, wet_ref, place_ref, back_ref, taps_ref, out_ref):
    a, b = pl.program_id(0), pl.program_id(1)
    channels = pad_ref.shape[2]
    wave = dot(place_ref[...], patch(pad_ref, a, b))
    spread = filtered(wave, taps_ref, back_ref)
    wet = wet_ref[...].reshape(TILE * TILE, 128).astype(F32)
    wet = jnp.concatenate([wet, wet], axis=1)
    cot = cot_ref[...].reshape(TILE * TILE, channels).astype(F32)
    out_ref[...] = (cot + wet * spread).reshape(TILE, TILE, channels)


def whole(*shape):
    return pl.BlockSpec(shape, lambda a, b: (0,) * len(shape))


def tiled(depth):
    return pl.BlockSpec((TILE, TILE, depth), lambda a, b: (a, b, 0))


def shape_of(shape, dtype=F32):
    return jax.ShapeDtypeStruct(shape, dtype)


def cell_pass(padded, cotangent, wet, taps, conv_bias, gain, shift, up, up_bias, down):
    table = tables()
    lon, lat, channels = cotangent.shape
    units = up.shape[1]
    return pl.pallas_call(
        cell_kernel,
        grid=(lon // TILE, lat // TILE),
        in_specs=[
            whole(*padded.shape), tiled(channels), tiled(128),
            whole(2 * HALF, 2 * HALF), whole(2 * HALF, HALF), whole(HALF, 2 * HALF),
            whole(3 * HALF, channels), whole(49, 3 * HALF),
            whole(1, channels), whole(1, channels), whole(1, channels),
            whole(channels, units), whole(1, units), whole(units, channels),
        ],
        out_specs=[
            tiled(channels), whole(channels, units), whole(1, units), whole(units, channels),
            whole(56, channels),
        ],
        out_shape=[
            shape_of((lon, lat, channels), BF16), shape_of((channels, units)),
            shape_of((1, units)), shape_of((units, channels)), shape_of((56, channels)),
        ],
        scratch_shapes=[pltpu.VMEM((HALF, channels), F32)] * 3,
        compiler_params=pltpu.CompilerParams(vmem_limit_bytes=40 * 2**20),
        name="cell_pass",
    )(
        padded, cotangent, wet, table["place"], table["own"], table["back"], taps,
        table["collect"], conv_bias, gain, shift, up, up_bias, down,
    )


def spread_pass(padded, cotangent, wet, taps):
    table = tables()
    lon, lat, channels = cotangent.shape
    return pl.pallas_call(
        spread_kernel,
        grid=(lon // TILE, lat // TILE),
        in_specs=[
            whole(*padded.shape), tiled(channels), tiled(128),
            whole(2 * HALF, 2 * HALF), whole(HALF, 2 * HALF), whole(3 * HALF, channels),
        ],
        out_specs=tiled(channels),
        out_shape=shape_of((lon, lat, channels)),
        compiler_params=pltpu.CompilerParams(vmem_limit_bytes=40 * 2**20),
        name="spread_pass",
    )(padded, cotangent, wet, table["place"], table["back"], taps)


def ring(axis, step):
    size = lax.axis_size(axis)
    return [(i, (i + step) % size) for i in range(size)]


def line(axis, step):
    size = lax.axis_size(axis)
    return [(i, i + step) for i in range(size) if 0 <= i + step < size]


def padded_2(x):
    before = lax.ppermute(x[-3:], "gx", ring("gx", 1))
    after = lax.ppermute(x[:3], "gx", ring("gx", -1))
    x = jnp.concatenate([before, x, after], axis=0)
    before = lax.ppermute(x[:, -3:], "gy", line("gy", 1))
    after = lax.ppermute(x[:, :3], "gy", line("gy", -1))
    zeros = jnp.zeros((x.shape[0], 10, x.shape[2]), x.dtype)
    return jnp.concatenate([before, x, after, zeros], axis=1)


def local(
    inputs, cotangent, wet_mask, kernel, conv_bias, norm_gain, norm_shift, up_weight, up_bias,
    down_weight,
):
    lon, lat, channels = inputs.shape
    wet = wet_mask.astype(BF16)[:, :, None]
    padded = padded_2(inputs * wet)
    wet_wide = jnp.broadcast_to(wet, (lon, lat, 128))
    taps = jnp.dot(
        tables()["taps"], kernel.astype(F32), precision=lax.Precision.HIGHEST,
        preferred_element_type=F32,
    )

    def row(x):
        return x.astype(F32)[None, :]

    field_grad, up_sum, up_bias_sum, down_sum, small = cell_pass(
        padded, cotangent, wet_wide, taps[: 3 * HALF], row(conv_bias), row(norm_gain),
        row(norm_shift), up_weight, row(up_bias), down_weight,
    )
    cells = lon * lat * lax.axis_size("gx") * lax.axis_size("gy")
    scale = float(cells) ** -0.5
    up_sum, up_bias_sum, down_sum, small = lax.psum((up_sum, up_bias_sum, down_sum, small), AXES)
    input_grad = spread_pass(padded_2(field_grad), cotangent, wet_wide, taps[3 * HALF :])
    small = small * scale
    return (
        input_grad, small[:49], small[51], small[49], small[50], up_sum * scale,
        up_bias_sum[0] * scale, down_sum * scale,
    )


def solution(mesh):
    whole_in = (P(),) * 7
    in_specs = (P("gx", "gy", None), P("gx", "gy", None), P("gx", "gy")) + whole_in
    out_specs = (P("gx", "gy", None),) + whole_in
    return jax.shard_map(local, mesh=mesh, in_specs=in_specs, out_specs=out_specs, check_vma=False)
```

time: 386 us -> 299 us (0.77)
  other arithmetic: 155 us -> 10.8 us
  waiting for transfers between devices: 51.7 us -> 131 us
  matrix products: 67.6 us -> 0.76 us
  Pallas kernels: 0 us -> 47.3 us
  local copies, waits for them, and re-layouts: 5.07 us -> 9.61 us
    psum x1, waiting for transfers between devices: 45.2 us -> 119 us  [local(): lax.psum((up_sum, up_bias_sum, down_sum, small), AXES)]
    dot_general x40 -> x1, matrix products: 67.6 us -> 0.76 us  [local(): jnp.dot(tables()['taps'], kernel.astype(F32), precision=lax.Precision.HIG...]
    add x18 -> x0, other arithmetic: 63.4 us -> none  [the longest x1 31.7 us: local(): cotangent.astype(jnp.float32) + wet.astype(jnp.float32) * spread]
    pallas_call x0 -> x2, Pallas kernels: none -> 47.3 us  [the longest x1 35.5 us: cell_pass(): pl.pallas_call(cell_kernel, grid=(lon // TILE, lat // TILE), in_specs=[wh...]
    dot_general x3 -> x0, other arithmetic: 30.1 us -> none  [local(): jnp.einsum('ijc,ijc->c', window, field_grad, preferred_element_type=jnp.f...]
    reduce_sum x17 -> x0, other arithmetic: 20.2 us -> none  [the longest x8 10.2 us: cell_grads(): variance = jnp.mean(centred * centred, axis=-1, keepdims=True)]
    dynamic_update_slice x8 -> x0, other arithmetic: 16.8 us -> none  [local(): lax.scan(advance, zero_parts, (field_blocks, grad_blocks, active))]
    convert_element_type x30 -> x1, other arithmetic: 13.5 us -> 0.83 us  [local(): wet = wet_mask.astype(BF16)[:, :, None]]
  transfers between devices with their start and end apart: 9 -> 9, of which waited for: 5 -> 6; matrix products, arithmetic and copies ran while one was open for 10% -> 3% of each run, Pallas kernels for 0% -> 4%
where the time goes in v1:
time: 299 us
  waiting for transfers between devices  131 us (44%)
  blocking collectives  70.3 us (24%)
  Pallas kernels  47.3 us (16%)
  starting transfers between devices  14.9 us (5%)
  between operations  14.4 us (5%)
  other arithmetic  10.8 us (4%)
  local copies, waits for them, and re-layouts  9.61 us (3%)
    psum x1, waiting for transfers between devices, local(): lax.psum((up_sum, up_bias_sum, down_sum, small), AXES)  119 us
    psum x1, blocking collectives, local(): lax.psum((up_sum, up_bias_sum, down_sum, small), AXES)  70.3 us
    pallas_call x1, Pallas kernels, cell_pass(): pl.pallas_call(cell_kernel, grid=(lon // TILE, lat // TILE), in_specs=[wh...  35.5 us
    pallas_call x1, Pallas kernels, spread_pass(): pl.pallas_call(spread_kernel, grid=(lon // TILE, lat // TILE), in_specs=[...  11.8 us
    ppermute x2, waiting for transfers between devices, padded_2(): after = lax.ppermute(x[:, :3], 'gy', line('gy', -1))  8.26 us
  transfers between devices with their start and end apart: 9, of which 6 were waited for; matrix products, arithmetic and copies ran while one was open for 3% of the time, Pallas kernels for 4%

profile of v1, /device:TPU:1, one launch (start us, length us, event | category | flops | bytes accessed | tf_op | source)
XLA Modules:
  0.0 299.0 jit_solution(2280693991526022492)
XLA Ops:
  7.2 0.0 copy-start
  7.2 0.0 copy-start.13
  7.2 0.0 all-reduce.4.cloned.1.call-start
  7.2 0.8 convert_element_type.2
  8.1 1.9 broadcast_multiply_fusion
  10.0 2.7 collective-permute-start
  12.7 0.0 collective-permute-start.1
  12.7 0.0 copy-done
  12.7 0.0 copy-done.13
  12.7 0.8 fusion.5
  13.5 0.0 copy-start.18
  13.5 0.0 copy-start.19
  13.5 0.0 copy-start.20
  13.5 0.0 copy-start.21
  13.5 0.8 collective-permute-done
  14.3 2.7 collective-permute-done.1
  17.0 0.1 pad_maximum_fusion.2
  17.2 3.3 %collective-permute-start.2 = (bf16[70,3,256]{2,1,0:T(4,128)(2,1)S(1)}, bf16[70,3,256]{2,1,0:T(4,128)(2,1)S(1)}, u32[]{:S(2)}, u32[]{:S(2)}) collective-permute-start(bf16[70,3,256]{2,1,0:T(4,128)(2,1)S(1)} %get-tuple-element.24), channel_id=1, source_target_pairs={{0,1},{1,2},{2,3},{3,4},{4,5},{5,6},{6,7},{8,9},{9,10},{10,11},{11... | collective-permute-start | bytes 322568 | tf_op jit(solution)/shard_map/ppermute | solution.py:267
  20.4 1.3 collective-permute-start.3
  21.7 1.0 fusion.3
  22.7 0.0 copy-done.18
  22.7 0.0 copy-done.19
  22.7 0.0 copy-done.20
  22.7 0.0 copy-done.21
  22.8 0.1 pad.9.clone
  22.9 0.0 copy-start.9
  22.9 0.0 copy-start.10
  22.9 0.0 copy-start.11
  22.9 0.0 copy-start.12
  22.9 0.0 collective-permute-done.2
  22.9 3.3 %collective-permute-done.3 = bf16[70,3,256]{2,1,0:T(4,128)(2,1)S(1)} collective-permute-done((bf16[70,3,256]{2,1,0:T(4,128)(2,1)S(1)}, bf16[70,3,256]{2,1,0:T(4,128)(2,1)S(1)}, u32[]{:S(2)}, u32[]{:S(2)}) %collective-permute-start.3) | collective-permute-done | bytes 107552 | tf_op jit(solution)/shard_map/ppermute | solution.py:268
  26.3 1.8 maximum_maximum_fusion.pad_ref
  28.1 0.6 broadcast_in_dim.26.wet_ref
  28.8 35.5 %cell_pass.1 = (bf16[64,64,256]{2,1,0:T(8,128)(2,1)S(1)}, f32[256,512]{1,0:T(8,128)S(1)}, f32[1,512]{1,0:T(1,128)S(1)}, f32[512,256]{1,0:T(8,128)S(1)}, f32[56,256]{1,0:T(8,128)S(1)}) custom-call(bf16[70,80,256]{2,1,0:T(8,128)(2,1)S(1)} %maximum_maximum_fusion.pad_ref, bf16[64,64,256]{2,1,0:T(8,128)(2,1)S(1)} %copy-done.1, ...), custom_call_target="tpu_custom_call" | custom-call | tf_op jit(solution)/shard_map/cell_pass/pallas_call | solution.py:209
  64.2 0.0 copy-start.7
  64.3 0.8 copy-done.7
  65.0 0.8 copy-done.8
  65.8 1.3 copy-done.3
  67.2 0.7 fusion.1
  67.9 2.7 collective-permute-start.4
  70.6 1.2 collective-permute-start.5
  71.8 70.3 %all-reduce = (f32[56,256]{1,0:T(8,128)S(1)}, f32[1,512]{1,0:T(1,128)}) all-reduce(f32[56,256]{1,0:T(8,128)S(1)} %get-tuple-element.14, f32[1,512]{1,0:T(1,128)S(1)} %get-tuple-element.16), channel_id=1, replica_groups=mesh['gx'=16,'gy'=8] {'gx','gy'}, use_global_device_ids=true, to_apply=%region_0.0 | all-reduce | flops 14848 | bytes 118784 | tf_op jit(solution)/shard_map/psum | solution.py:295
  142.1 0.6 fusion.4
  142.7 0.0 all-reduce.4.cloned.1.call-update
  142.8 0.0 collective-permute-done.4
  142.8 0.9 constant_dynamic-update-slice_fusion.2
  143.7 1.7 constant_dynamic-update-slice_fusion.1
  145.4 0.0 collective-permute-done.5
  145.4 0.9 constant_dynamic-update-slice_fusion
  146.3 0.1 fusion
  146.4 0.0 copy-done.14
  146.4 0.0 copy-start.2
  146.4 0.0 copy-start.5
  146.5 2.4 collective-permute-start.6
  148.8 1.3 collective-permute-start.7
  150.2 0.6 broadcast_multiply_fusion.4
  150.7 0.1 collective-permute-done.6
  150.9 4.9 %collective-permute-done.7 = bf16[70,3,256]{2,1,0:T(4,128)(2,1)S(1)} collective-permute-done((bf16[70,3,256]{2,1,0:T(4,128)(2,1)S(1)}, bf16[70,3,256]{2,1,0:T(4,128)(2,1)S(1)}, u32[]{:S(2)}, u32[]{:S(2)}) %collective-permute-start.7) | collective-permute-done | bytes 107552 | tf_op jit(solution)/shard_map/ppermute | solution.py:268
  155.8 0.0 copy-done.16
  155.8 1.8 maximum_maximum_fusion.1.pad_ref
  157.6 11.8 %spread_pass.1 = f32[64,64,256]{2,1,0:T(8,128)} custom-call(bf16[70,80,256]{2,1,0:T(8,128)(2,1)S(1)} %maximum_maximum_fusion.1.pad_ref, bf16[64,64,256]{2,1,0:T(8,128)(2,1)S(1)} %copy-done.1, bf16[64,64,128]{2,1,0:T(8,128)(2,1)S(1)} %broadcast_in_dim.26.wet_ref, bf16[512,512]{1,0:T(8,128)(2,1)S(1)} %copy-done.5, bf16[256,512]{1,0:T(8,128)(2,1)S(1)} %copy-done.6, ...), custom_call_target="tpu_custom_call" | custom-call | tf_op jit(solution)/shard_map/spread_pass/pallas_call | solution.py:239
  169.4 119.0 %all-reduce.4.cloned.1.call-done = (f32[256,512]{1,0:T(8,128)}, f32[512,256]{1,0:T(8,128)}) async-done(((f32[256,512]{1,0:T(8,128)}, f32[512,256]{1,0:T(8,128)}), (f32[256,512]{1,0:T(8,128)}, f32[512,256]{1,0:T(8,128)})) %all-reduce.4.cloned.1.call-update) | async-done | bytes 1048592 | tf_op jit(solution)/shard_map/psum | solution.py:295
  288.4 1.9 broadcast_multiply_fusion.1
  290.3 1.9 broadcast_multiply_fusion.2
  (27 shorter events, 0.1 us)
Async XLA Ops:
  7.2 5.5 %copy-start = (bf16[49,256]{1,0:T(8,128)(2,1)S(1)}, bf16[49,256]{1,0:T(8,128)(2,1)}, u32[]{:S(2)}) copy-start(bf16[49,256]{1,0:T(8,128)(2,1)} %param.18) | copy-start | bytes 75268
  7.2 5.5 %copy-start.13 = (f32[1536,49]{1,0:T(8,128)S(1)}, f32[1536,49]{1,0:T(8,128)}, u32[]{:S(2)}) copy-start(f32[1536,49]{1,0:T(8,128)} %constant.9.clone) | copy-start | bytes 903172
  7.2 281.2 %all-reduce.4.cloned.1.call-start = ((), (), s32[]{:S(2)}) async-start(), calls=%async_computation | async-start | bytes 2097152 | tf_op jit(solution)/shard_map/psum | solution.py:295
  10.0 4.3 %collective-permute-start = (bf16[3,64,256]{2,1,0:T(8,128)(2,1)S(1)}, bf16[3,64,256]{2,1,0:T(8,128)(2,1)S(1)}, u32[]{:S(2)}, u32[]{:S(2)}) collective-permute-start(bf16[3,64,256]{2,1,0:T(8,128)(2,1)S(1)} %get-tuple-element.28), channel_id=1, source_target_pairs={{0,8},{8,16},{16,24},{24,32},{32,40},{40,48},{48,56},{56,64},{64,7... | collective-permute-start | bytes 294920 | tf_op jit(solution)/shard_map/ppermute | solution.py:264
  12.7 4.3 %collective-permute-start.1 = (bf16[3,64,256]{2,1,0:T(8,128)(2,1)S(1)}, bf16[3,64,256]{2,1,0:T(8,128)(2,1)S(1)}, u32[]{:S(2)}, u32[]{:S(2)}) collective-permute-start(bf16[3,64,256]{2,1,0:T(8,128)(2,1)S(1)} %get-tuple-element.29), channel_id=1, source_target_pairs={{0,120},{8,0},{16,8},{24,16},{32,24},{40,32},{48,40},{56,48},{64,5... | collective-permute-start | bytes 294920 | tf_op jit(solution)/shard_map/ppermute | solution.py:265
  13.5 9.2 %copy-start.18 = (bf16[512]{0:T(512)(128)(2,1)S(1)}, bf16[512]{0:T(512)(128)(2,1)}, u32[]{:S(2)}) copy-start(bf16[512]{0:T(512)(128)(2,1)} %param.23) | copy-start | bytes 3076
  13.5 9.2 %copy-start.19 = (bf16[256]{0:T(256)(128)(2,1)S(1)}, bf16[256]{0:T(256)(128)(2,1)}, u32[]{:S(2)}) copy-start(bf16[256]{0:T(256)(128)(2,1)} %param.19) | copy-start | bytes 1540
  13.5 9.2 %copy-start.20 = (bf16[256]{0:T(256)(128)(2,1)S(1)}, bf16[256]{0:T(256)(128)(2,1)}, u32[]{:S(2)}) copy-start(bf16[256]{0:T(256)(128)(2,1)} %param.20) | copy-start | bytes 1540
  13.5 9.2 %copy-start.21 = (bf16[256]{0:T(256)(128)(2,1)S(1)}, bf16[256]{0:T(256)(128)(2,1)}, u32[]{:S(2)}) copy-start(bf16[256]{0:T(256)(128)(2,1)} %param.21) | copy-start | bytes 1540
  17.2 5.8 %collective-permute-start.2 = (bf16[70,3,256]{2,1,0:T(4,128)(2,1)S(1)}, bf16[70,3,256]{2,1,0:T(4,128)(2,1)S(1)}, u32[]{:S(2)}, u32[]{:S(2)}) collective-permute-start(bf16[70,3,256]{2,1,0:T(4,128)(2,1)S(1)} %get-tuple-element.24), channel_id=1, source_target_pairs={{0,1},{1,2},{2,3},{3,4},{4,5},{5,6},{6,7},{8,9},{9,10},{10,11},{11... | collective-permute-start | bytes 322568 | tf_op jit(solution)/shard_map/ppermute | solution.py:267
  20.4 5.8 %collective-permute-start.3 = (bf16[70,3,256]{2,1,0:T(4,128)(2,1)S(1)}, bf16[70,3,256]{2,1,0:T(4,128)(2,1)S(1)}, u32[]{:S(2)}, u32[]{:S(2)}) collective-permute-start(bf16[70,3,256]{2,1,0:T(4,128)(2,1)S(1)} %get-tuple-element.25), channel_id=1, source_target_pairs={{1,0},{2,1},{3,2},{4,3},{5,4},{6,5},{7,6},{9,8},{10,9},{11,10},{12... | collective-permute-start | bytes 322568 | tf_op jit(solution)/shard_map/ppermute | solution.py:268
  22.8 5.8 %copy-start.15 = (bf16[80]{0:T(256)(128)(2,1)}, bf16[80]{0:T(256)(128)(2,1)S(1)}, u32[]{:S(2)}) copy-start(bf16[80]{0:T(256)(128)(2,1)S(1)} %pad.9.clone) | copy-start | bytes 484
  22.8 5.9 %copy-start.1 = (bf16[64,64,256]{2,1,0:T(8,128)(2,1)S(1)}, bf16[64,64,256]{2,1,0:T(8,128)(2,1)}, u32[]{:S(2)}) copy-start(bf16[64,64,256]{2,1,0:T(8,128)(2,1)} %cot_ref.3) | copy-start | bytes 6291460
  22.9 5.9 %copy-start.4 = (bf16[512,512]{1,0:T(8,128)(2,1)S(1)}, bf16[512,512]{1,0:T(8,128)(2,1)}, u32[]{:S(2)}) copy-start(bf16[512,512]{1,0:T(8,128)(2,1)} %constant.5.clone.place_ref) | copy-start | bytes 1572868
  22.9 5.9 %copy-start.6 = (bf16[256,512]{1,0:T(8,128)(2,1)S(1)}, bf16[256,512]{1,0:T(8,128)(2,1)}, u32[]{:S(2)}) copy-start(bf16[256,512]{1,0:T(8,128)(2,1)} %constant.20.clone.back_ref) | copy-start | bytes 786436
  22.9 5.9 %copy-start.9 = (bf16[256,512]{1,0:T(8,128)(2,1)S(1)}, bf16[256,512]{1,0:T(8,128)(2,1)}, u32[]{:S(2)}) copy-start(bf16[256,512]{1,0:T(8,128)(2,1)} %up_ref.1) | copy-start | bytes 786436
  22.9 5.9 %copy-start.10 = (bf16[512,256]{1,0:T(8,128)(2,1)S(1)}, bf16[512,256]{1,0:T(8,128)(2,1)}, u32[]{:S(2)}) copy-start(bf16[512,256]{1,0:T(8,128)(2,1)} %down_ref.1) | copy-start | bytes 786436
  22.9 5.9 %copy-start.11 = (bf16[512,256]{1,0:T(8,128)(2,1)S(1)}, bf16[512,256]{1,0:T(8,128)(2,1)}, u32[]{:S(2)}) copy-start(bf16[512,256]{1,0:T(8,128)(2,1)} %constant.6.clone.own_ref) | copy-start | bytes 786436
  22.9 5.9 %copy-start.12 = (f32[49,768]{1,0:T(8,128)S(1)}, f32[49,768]{1,0:T(8,128)}, u32[]{:S(2)}) copy-start(f32[49,768]{1,0:T(8,128)} %constant.21.clone.collect_ref) | copy-start | bytes 451588
  64.2 0.8 copy-start.7
  65.0 0.8 copy-start.8
  65.8 1.3 copy-start.3
  67.9 74.9 %collective-permute-start.4 = (bf16[3,64,256]{2,1,0:T(8,128)(2,1)}, bf16[3,64,256]{2,1,0:T(8,128)(2,1)}, u32[]{:S(2)}, u32[]{:S(2)}) collective-permute-start(bf16[3,64,256]{2,1,0:T(8,128)(2,1)} %get-tuple-element.27), channel_id=1, source_target_pairs={{0,8},{8,16},{16,24},{24,32},{32,40},{40,48},{48,56},{56,64},{64,7... | collective-permute-start | bytes 294920 | tf_op jit(solution)/shard_map/ppermute | solution.py:264
  70.6 74.8 %collective-permute-start.5 = (bf16[3,64,256]{2,1,0:T(8,128)(2,1)}, bf16[3,64,256]{2,1,0:T(8,128)(2,1)}, u32[]{:S(2)}, u32[]{:S(2)}) collective-permute-start(bf16[3,64,256]{2,1,0:T(8,128)(2,1)} %get-tuple-element.26), channel_id=1, source_target_pairs={{0,120},{8,0},{16,8},{24,16},{32,24},{40,32},{48,40},{56,48},{64,5... | collective-permute-start | bytes 294920 | tf_op jit(solution)/shard_map/ppermute | solution.py:265
  142.1 4.3 %copy-start.14 = (f32[56,256]{1,0:T(8,128)}, f32[56,256]{1,0:T(8,128)S(1)}, u32[]{:S(2)}) copy-start(f32[56,256]{1,0:T(8,128)S(1)} %broadcast_multiply_fusion.3) | copy-start | bytes 172036
  142.7 7.4 %copy-start.17 = (f32[1,512]{1,0:T(1,128)S(1)}, f32[1,512]{1,0:T(1,128)}, u32[]{:S(2)}) copy-start(f32[1,512]{1,0:T(1,128)} %get-tuple-element.19) | copy-start | bytes 6148
  142.7 13.1 %copy-start.16 = (bf16[80]{0:T(256)(128)(2,1)S(1)}, bf16[80]{0:T(256)(128)(2,1)}, u32[]{:S(2)}) copy-start(bf16[80]{0:T(256)(128)(2,1)} %copy-done.15) | copy-start | bytes 484
  146.4 11.2 %copy-start.2 = (f32[768,256]{1,0:T(8,128)S(1)}, f32[768,256]{1,0:T(8,128)}, u32[]{:S(2)}) copy-start(f32[768,256]{1,0:T(8,128)} %get-tuple-element.30.taps_ref) | copy-start | bytes 2359300
  146.4 11.2 %copy-start.5 = (bf16[512,512]{1,0:T(8,128)(2,1)S(1)}, bf16[512,512]{1,0:T(8,128)(2,1)}, u32[]{:S(2)}) copy-start(bf16[512,512]{1,0:T(8,128)(2,1)} %constant.5.clone.place_ref) | copy-start | bytes 1572868
  146.5 4.4 %collective-permute-start.6 = (bf16[70,3,256]{2,1,0:T(4,128)(2,1)S(1)}, bf16[70,3,256]{2,1,0:T(4,128)(2,1)S(1)}, u32[]{:S(2)}, u32[]{:S(2)}) collective-permute-start(bf16[70,3,256]{2,1,0:T(4,128)(2,1)S(1)} %get-tuple-element.22), channel_id=1, source_target_pairs={{0,1},{1,2},{2,3},{3,4},{4,5},{5,6},{6,7},{8,9},{9,10},{10,11},{11... | collective-permute-start | bytes 322568 | tf_op jit(solution)/shard_map/ppermute | solution.py:267
  148.8 7.0 %collective-permute-start.7 = (bf16[70,3,256]{2,1,0:T(4,128)(2,1)S(1)}, bf16[70,3,256]{2,1,0:T(4,128)(2,1)S(1)}, u32[]{:S(2)}, u32[]{:S(2)}) collective-permute-start(bf16[70,3,256]{2,1,0:T(4,128)(2,1)S(1)} %get-tuple-element.23), channel_id=1, source_target_pairs={{1,0},{2,1},{3,2},{4,3},{5,4},{6,5},{7,6},{9,8},{10,9},{11,10},{12... | collective-permute-start | bytes 322568 | tf_op jit(solution)/shard_map/ppermute | solution.py:268
Sparse Core Ops, SparseCore 0:
  142.9 145.4 all-reduce.3

commit v2 on v1

--- a/solution.py
+++ b/solution.py
@@ -14,6 +14,9 @@
 SPAN = TILE + 6
 HALF = 256
 AXES = ("gx", "gy")
+BLOCKS = 32
+BLOCK_ROWS = 72
+LANES = 128
 
 
 def basis():
@@ -110,23 +113,28 @@
     )
 
 
+def block_rows(place, k):
+    return pl.ds(pl.multiple_of((place ^ k) * BLOCK_ROWS, 8), BLOCK_ROWS)
+
+
 def cell_kernel(
-    pad_ref, cot_ref, wet_ref, place_ref, own_ref, back_ref, taps_ref, collect_ref,
+    who_ref, pad_ref, cot_ref, wet_ref, place_ref, own_ref, back_ref, taps_ref, collect_ref,
     bias_ref, gain_ref, shift_ref, up_ref, up_bias_ref, down_ref,
-    fg_ref, up_sum_ref, up_bias_sum_ref, down_sum_ref, small_ref,
-    p1_ref, p2_ref, p3_ref,
+    fg_ref, keep_ref, send_ref,
+    sum_ref, p1_ref, p2_ref, p3_ref, small_ref,
 ):
     a, b = pl.program_id(0), pl.program_id(1)
     channels = pad_ref.shape[2]
+    units = up_ref.shape[1]
 
     @pl.when((a == 0) & (b == 0))
     def _():
-        for ref in (up_sum_ref, up_bias_sum_ref, down_sum_ref, small_ref, p1_ref, p2_ref, p3_ref):
+        for ref in (sum_ref, p1_ref, p2_ref, p3_ref, small_ref):
             ref[...] = jnp.zeros_like(ref)
 
     wave = dot(place_ref[...], patch(pad_ref, a, b))
     field = filtered(wave, taps_ref, back_ref) + bias_ref[...]
-    wet = wet_ref[...].reshape(TILE * TILE, 128)
+    wet = wet_ref[...].reshape(TILE * TILE, LANES)
     wet = jnp.concatenate([wet, wet], axis=1)
     masked_grad = cot_ref[...].reshape(TILE * TILE, channels) * wet
     average = jnp.mean(field, axis=-1, keepdims=True)
@@ -147,16 +155,24 @@
     activated = (hidden * cumulative).astype(BF16)
     act_grad = dot_cols(masked_grad, down_ref[...])
     hidden_grad = (act_grad * (cumulative + hidden * (bell * 0.3989422804014327))).astype(BF16)
-    down_sum_ref[...] += dot_rows(activated, masked_grad)
-    up_sum_ref[...] += dot_rows(normed_out, hidden_grad)
-    up_bias_sum_ref[...] += jnp.sum(hidden_grad.astype(F32), axis=0, keepdims=True)
+    up_part = dot_rows(normed_out, hidden_grad)
+    down_part = dot_rows(activated, masked_grad)
+    at = 0
+    for part in (up_part, down_part):
+        for n in range(0, part.shape[1], LANES):
+            sum_ref[at : at + part.shape[0], :] += part[:, n : n + LANES]
+            at += part.shape[0]
+    bias_part = jnp.sum(hidden_grad.astype(F32), axis=0, keepdims=True)
+    for n in range(units // channels):
+        small_ref[52 + n : 53 + n, :] += bias_part[:, n * channels : (n + 1) * channels]
     normed_grad = dot_cols(hidden_grad, up_ref[...])
     product = normed_grad * normed
     small_ref[49:50, :] += jnp.sum(product, axis=0, keepdims=True)
     small_ref[50:51, :] += jnp.sum(normed_grad, axis=0, keepdims=True)
-    scaled_mean = jnp.mean(normed_grad * gain, axis=-1, keepdims=True)
+    scaled = normed_grad * gain
+    scaled_mean = jnp.mean(scaled, axis=-1, keepdims=True)
     product_mean = jnp.mean(product * gain, axis=-1, keepdims=True)
-    field_grad = (inv_std * (normed_grad * gain - scaled_mean - normed * product_mean)).astype(BF16)
+    field_grad = (inv_std * (scaled - scaled_mean - normed * product_mean)).astype(BF16)
     fg_ref[...] = field_grad.reshape(TILE, TILE, channels)
     ripple = dot(own_ref[...], field_grad)
     g_real, g_imag = ripple[:HALF], ripple[HALF:]
@@ -177,17 +193,36 @@
                 preferred_element_type=F32,
             )
         small_ref[:49, :] = total
-
-
-def spread_kernel(pad_ref, cot_ref, wet_ref, place_ref, back_ref, taps_ref, out_ref):
-    a, b = pl.program_id(0), pl.program_id(1)
+        start = 4 * units * channels // LANES // 2
+        for n in range(0, channels, LANES):
+            sum_ref[start : start + 64, :] = small_ref[:, n : n + LANES]
+            start += 64
+        for n, ref in enumerate((keep_ref, send_ref)):
+            for k in range(BLOCKS // 2):
+                ref[k] = sum_ref[block_rows(who_ref[n], k), :]
+
+
+def finish_kernel(scale, who_ref, in_ref, up_ref, down_ref, small_ref, sum_ref):
+    for n in range(2):
+        for k in range(BLOCKS // 2):
+            rows = block_rows(who_ref[n], k)
+            sum_ref[rows, :] = in_ref[n * (BLOCKS // 2) + k].astype(F32) * scale
+    at = 0
+    for ref in (up_ref, down_ref, small_ref):
+        for n in range(0, ref.shape[1], LANES):
+            ref[:, n : n + LANES] = sum_ref[at : at + ref.shape[0], :]
+            at += ref.shape[0]
+
+
+def spread_kernel(at, pad_ref, cot_ref, wet_ref, place_ref, back_ref, taps_ref, *out_refs):
+    b = pl.program_id(1)
     channels = pad_ref.shape[2]
-    wave = dot(place_ref[...], patch(pad_ref, a, b))
+    wave = dot(place_ref[...], patch(pad_ref, at, b))
     spread = filtered(wave, taps_ref, back_ref)
-    wet = wet_ref[...].reshape(TILE * TILE, 128).astype(F32)
+    wet = wet_ref[...].reshape(TILE * TILE, LANES).astype(F32)
     wet = jnp.concatenate([wet, wet], axis=1)
     cot = cot_ref[...].reshape(TILE * TILE, channels).astype(F32)
-    out_ref[...] = (cot + wet * spread).reshape(TILE, TILE, channels)
+    out_refs[-1][...] = (cot + wet * spread).reshape(TILE, TILE, channels)
 
 
 def whole(*shape):
@@ -202,52 +237,76 @@
     return jax.ShapeDtypeStruct(shape, dtype)
 
 
-def cell_pass(padded, cotangent, wet, taps, conv_bias, gain, shift, up, up_bias, down):
+def cell_pass(who, padded, cotangent, wet, taps, conv_bias, gain, shift, up, up_bias, down):
     table = tables()
     lon, lat, channels = cotangent.shape
     units = up.shape[1]
+    half = (BLOCKS // 2, BLOCK_ROWS, LANES)
     return pl.pallas_call(
         cell_kernel,
         grid=(lon // TILE, lat // TILE),
         in_specs=[
-            whole(*padded.shape), tiled(channels), tiled(128),
+            pl.BlockSpec(memory_space=pltpu.SMEM),
+            whole(*padded.shape), tiled(channels), tiled(LANES),
             whole(2 * HALF, 2 * HALF), whole(2 * HALF, HALF), whole(HALF, 2 * HALF),
             whole(3 * HALF, channels), whole(49, 3 * HALF),
             whole(1, channels), whole(1, channels), whole(1, channels),
             whole(channels, units), whole(1, units), whole(units, channels),
         ],
-        out_specs=[
-            tiled(channels), whole(channels, units), whole(1, units), whole(units, channels),
-            whole(56, channels),
-        ],
-        out_shape=[
-            shape_of((lon, lat, channels), BF16), shape_of((channels, units)),
-            shape_of((1, units)), shape_of((units, channels)), shape_of((56, channels)),
-        ],
-        scratch_shapes=[pltpu.VMEM((HALF, channels), F32)] * 3,
+        out_specs=[tiled(channels), whole(*half), whole(*half)],
+        out_shape=[shape_of((lon, lat, channels), BF16), shape_of(half), shape_of(half)],
+        scratch_shapes=[pltpu.VMEM((BLOCKS * BLOCK_ROWS, LANES), F32)]
+        + [pltpu.VMEM((HALF, channels), F32)] * 3
+        + [pltpu.VMEM((64, channels), F32)],
         compiler_params=pltpu.CompilerParams(vmem_limit_bytes=40 * 2**20),
+        cost_estimate=pl.CostEstimate(
+            flops=20 * 10**9, bytes_accessed=16 * 2**20, transcendentals=0
+        ),
         name="cell_pass",
     )(
-        padded, cotangent, wet, table["place"], table["own"], table["back"], taps,
+        who, padded, cotangent, wet, table["place"], table["own"], table["back"], taps,
         table["collect"], conv_bias, gain, shift, up, up_bias, down,
     )
 
 
-def spread_pass(padded, cotangent, wet, taps):
+def finish(who, summed, scale, channels, units):
+    return pl.pallas_call(
+        functools.partial(finish_kernel, scale),
+        in_specs=[
+            pl.BlockSpec(memory_space=pltpu.SMEM),
+            pl.BlockSpec(memory_space=pltpu.VMEM),
+        ],
+        out_specs=[pl.BlockSpec(memory_space=pltpu.VMEM)] * 3,
+        out_shape=[shape_of((channels, units)), shape_of((units, channels)), shape_of((64, channels))],
+        scratch_shapes=[pltpu.VMEM((BLOCKS * BLOCK_ROWS, LANES), F32)],
+        name="finish",
+    )(who, summed)
+
+
+def spread_pass(at, padded, cotangent, wet, taps, out):
     table = tables()
     lon, lat, channels = cotangent.shape
+
+    def row_of(depth):
+        return pl.BlockSpec((TILE, TILE, depth), lambda a, b: (at, b, 0))
+
     return pl.pallas_call(
-        spread_kernel,
-        grid=(lon // TILE, lat // TILE),
+        functools.partial(spread_kernel, at),
+        grid=(1, lat // TILE),
         in_specs=[
-            whole(*padded.shape), tiled(channels), tiled(128),
+            whole(*padded.shape), row_of(channels), row_of(LANES),
             whole(2 * HALF, 2 * HALF), whole(HALF, 2 * HALF), whole(3 * HALF, channels),
-        ],
-        out_specs=tiled(channels),
+        ]
+        + [pl.BlockSpec(memory_space=pl.ANY)] * (out is not None),
+        out_specs=row_of(channels),
         out_shape=shape_of((lon, lat, channels)),
+        input_output_aliases={} if out is None else {6: 0},
         compiler_params=pltpu.CompilerParams(vmem_limit_bytes=40 * 2**20),
+        cost_estimate=pl.CostEstimate(
+            flops=4 * 10**9, bytes_accessed=4 * 2**20, transcendentals=0
+        ),
         name="spread_pass",
-    )(padded, cotangent, wet, table["place"], table["back"], taps)
+    )(padded, cotangent, wet, table["place"], table["back"], taps, *([] if out is None else [out]))
 
 
 def ring(axis, step):
@@ -270,6 +329,51 @@
     return jnp.concatenate([before, x, after, zeros], axis=1)
 
 
+def swapped(mesh_shape, stage, step):
+    gx, gy = mesh_shape
+    pairs = []
+    for n in range(gx * gy):
+        i, j = divmod(n, gy)
+        core, x, y, z = i % 2, i // 2 % 4, j // 2, i // 8 * 2 + j % 2
+        if stage == "core":
+            core ^= step
+        else:
+            axis = "abc".index(stage) if core == 0 else ("abc".index(stage) + 1) % 3
+            place = [x, y, z]
+            place[axis] ^= step
+            x, y, z = place
+        pairs.append((n, (z // 2 * 8 + x * 2 + core) * gy + y * 2 + z % 2))
+    return pairs
+
+
+def places():
+    i, j = lax.axis_index("gx"), lax.axis_index("gy")
+    core, x, y, z = i % 2, i // 2 % 4, j // 2, i // 8 * 2 + j % 2
+    on_0, on_1 = x * 4 + y, 16 + y * 4 + z
+    own, other = jnp.where(core == 0, on_0, on_1), jnp.where(core == 0, on_1, on_0)
+    return jnp.stack([own, other]).astype(jnp.int32)
+
+
+def summed_blocks(keep, send):
+    mesh_shape = (lax.axis_size("gx"), lax.axis_size("gy"))
+
+    def move(x, stage, step):
+        return lax.ppermute(x, AXES, swapped(mesh_shape, stage, step))
+
+    held = keep + move(send, "core", 1)
+    for stage, size in (("a", 4), ("b", 1)):
+        parts = [held[:size]] + [
+            move(held[size * n : size * (n + 1)].astype(BF16), stage, n).astype(F32)
+            for n in range(1, 4)
+        ]
+        held = (parts[0] + parts[1]) + (parts[2] + parts[3])
+    parts = [held] + [move(held, "c", n) for n in range(1, 4)]
+    held = ((parts[0] + parts[1]) + (parts[2] + parts[3])).astype(BF16)
+    for stage in ("b", "a"):
+        held = jnp.concatenate([held] + [move(held, stage, n) for n in range(1, 4)], axis=0)
+    return jnp.concatenate([held, move(held, "core", 1)], axis=0)
+
+
 def local(
     inputs, cotangent, wet_mask, kernel, conv_bias, norm_gain, norm_shift, up_weight, up_bias,
     down_weight,
@@ -277,27 +381,31 @@
     lon, lat, channels = inputs.shape
     wet = wet_mask.astype(BF16)[:, :, None]
     padded = padded_2(inputs * wet)
-    wet_wide = jnp.broadcast_to(wet, (lon, lat, 128))
+    wet_wide = jnp.broadcast_to(wet, (lon, lat, LANES))
     taps = jnp.dot(
         tables()["taps"], kernel.astype(F32), precision=lax.Precision.HIGHEST,
         preferred_element_type=F32,
     )
+    who = places()
 
     def row(x):
         return x.astype(F32)[None, :]
 
-    field_grad, up_sum, up_bias_sum, down_sum, small = cell_pass(
-        padded, cotangent, wet_wide, taps[: 3 * HALF], row(conv_bias), row(norm_gain),
+    field_grad, keep, send = cell_pass(
+        who, padded, cotangent, wet_wide, taps[: 3 * HALF], row(conv_bias), row(norm_gain),
         row(norm_shift), up_weight, row(up_bias), down_weight,
     )
     cells = lon * lat * lax.axis_size("gx") * lax.axis_size("gy")
     scale = float(cells) ** -0.5
-    up_sum, up_bias_sum, down_sum, small = lax.psum((up_sum, up_bias_sum, down_sum, small), AXES)
-    input_grad = spread_pass(padded_2(field_grad), cotangent, wet_wide, taps[3 * HALF :])
-    small = small * scale
+    grad_pad = padded_2(field_grad)
+    summed = summed_blocks(keep, send)
+    input_grad = None
+    for at in range(lon // TILE):
+        input_grad = spread_pass(at, grad_pad, cotangent, wet_wide, taps[3 * HALF :], input_grad)
+    up_sum, down_sum, small = finish(who, summed, scale, channels, up_weight.shape[1])
     return (
-        input_grad, small[:49], small[51], small[49], small[50], up_sum * scale,
-        up_bias_sum[0] * scale, down_sum * scale,
+        input_grad, small[:49], small[51], small[49], small[50], up_sum,
+        small[52 : 52 + up_weight.shape[1] // channels].reshape(-1), down_sum,
     )
 
 

time: 299 us -> 135 us (0.45)
  waiting for transfers between devices: 131 us -> 18.8 us
  blocking collectives: 70.3 us -> 0 us
  starting transfers between devices: 14.9 us -> 48.6 us
  between operations: 14.4 us -> 1.22 us
  Pallas kernels: 47.3 us -> 51.5 us
  local copies, waits for them, and re-layouts: 9.61 us -> 6.41 us
  other arithmetic: 10.8 us -> 7.78 us
    psum x1 -> x0, waiting for transfers between devices: 119 us -> none  [local(): lax.psum((up_sum, up_bias_sum, down_sum, small), AXES)]
    psum x1 -> x0, blocking collectives: 70.3 us -> none  [local(): lax.psum((up_sum, up_bias_sum, down_sum, small), AXES)]
    ppermute x0 -> x17, starting transfers between devices: none -> 32.2 us  [move(): return lax.ppermute(x, AXES, swapped(mesh_shape, stage, step))]
    ppermute x0 -> x17, waiting for transfers between devices: none -> 6.72 us  [move(): return lax.ppermute(x, AXES, swapped(mesh_shape, stage, step))]
    mul x4 -> x0, other arithmetic: 4.35 us -> none  [the longest x1 1.88 us: local(): up_sum * scale]
    pallas_call x2 -> x6, Pallas kernels: 47.3 us -> 51.5 us  [the longest x1 35.5 us: cell_pass(): pl.pallas_call(cell_kernel, grid=(lon // TILE, lat // TILE), in_specs=[pl...]
    unnamed x46 -> x44, local copies, waits for them, and re-layouts: 5.63 us -> 2.55 us
  transfers between devices with their start and end apart: 9 -> 25, of which waited for: 6 -> 13; matrix products, arithmetic and copies ran while one was open for 3% -> 2% of each run, Pallas kernels for 4% -> 10%
where the time goes in v2:
time: 135 us
  Pallas kernels  51.5 us (38%)
  starting transfers between devices  48.6 us (36%)
  waiting for transfers between devices  18.8 us (14%)
  other arithmetic  7.78 us (6%)
  local copies, waits for them, and re-layouts  6.41 us (5%)
    pallas_call x1, Pallas kernels, cell_pass(): pl.pallas_call(cell_kernel, grid=(lon // TILE, lat // TILE), in_specs=[pl...  35.5 us
    ppermute x17, starting transfers between devices, move(): return lax.ppermute(x, AXES, swapped(mesh_shape, stage, step))  32.2 us
    pallas_call x4, Pallas kernels, spread_pass(): pl.pallas_call(functools.partial(spread_kernel, at), grid=(1, lat // TILE...  13.7 us
    ppermute x2, waiting for transfers between devices, padded_2(): after = lax.ppermute(x[:, :3], 'gy', line('gy', -1))  7.61 us
    ppermute x2, starting transfers between devices, padded_2(): before = lax.ppermute(x[:, -3:], 'gy', line('gy', 1))  7.06 us
    ppermute x17, waiting for transfers between devices, move(): return lax.ppermute(x, AXES, swapped(mesh_shape, stage, step))  6.72 us
    ppermute x2, starting transfers between devices, padded_2(): before = lax.ppermute(x[-3:], 'gx', ring('gx', 1))  5.45 us
    concatenate x2, other arithmetic, padded_2(): return jnp.concatenate([before, x, after, zeros], axis=1)  3.62 us
  transfers between devices with their start and end apart: 25, of which 13 were waited for; matrix products, arithmetic and copies ran while one was open for 2% of the time, Pallas kernels for 10%

profile of v2, /device:TPU:1, one launch (start us, length us, event | category | flops | bytes accessed | tf_op | source)
XLA Modules:
  0.0 135.1 jit_solution(14106314489657105813)
XLA Ops:
  0.6 0.0 copy-start
  0.6 0.0 copy-start.11
  0.7 0.8 convert_element_type.16
  1.5 1.9 %broadcast_multiply_fusion = bf16[64,64,256]{2,1,0:T(8,128)(2,1)S(1)} fusion(bf16[64,64,256]{2,1,0:T(8,128)(2,1)} %param.15, bf16[64,64]{1,0:T(8,128)(2,1)S(1)} %convert_element_type.16), kind=kLoop, calls=%fused_computation.2 | loop fusion | flops 1048576 | bytes 4202496 | tf_op jit(solution)/shard_map/mul | solution.py:383
  3.5 2.7 %collective-permute-start = (bf16[3,64,256]{2,1,0:T(8,128)(2,1)S(1)}, bf16[3,64,256]{2,1,0:T(8,128)(2,1)S(1)}, u32[]{:S(2)}, u32[]{:S(2)}) collective-permute-start(bf16[3,64,256]{2,1,0:T(8,128)(2,1)S(1)} %get-tuple-element.32), channel_id=1, source_target_pairs={{0,8},{8,16},{16,24},{24,32},{32,40},{40,48},{48,56},{56,64},{64,7... | collective-permute-start | bytes 294920 | tf_op jit(solution)/shard_map/ppermute | solution.py:323
  6.2 0.8 fusion.12
  7.0 0.1 fusion.8
  7.3 0.1 pad.13.clone
  7.3 0.5 collective-permute-done
  7.8 2.7 %collective-permute-done.1 = bf16[3,64,256]{2,1,0:T(8,128)(2,1)S(1)} collective-permute-done((bf16[3,64,256]{2,1,0:T(8,128)(2,1)S(1)}, bf16[3,64,256]{2,1,0:T(8,128)(2,1)S(1)}, u32[]{:S(2)}, u32[]{:S(2)}) %collective-permute-start.1) | collective-permute-done | bytes 98336 | tf_op jit(solution)/shard_map/ppermute | solution.py:324
  10.5 1.1 pad_maximum_fusion.2
  11.7 3.3 %collective-permute-start.2 = (bf16[70,3,256]{2,1,0:T(4,128)(2,1)S(1)}, bf16[70,3,256]{2,1,0:T(4,128)(2,1)S(1)}, u32[]{:S(2)}, u32[]{:S(2)}) collective-permute-start(bf16[70,3,256]{2,1,0:T(4,128)(2,1)S(1)} %get-tuple-element.28), channel_id=1, source_target_pairs={{0,1},{1,2},{2,3},{3,4},{4,5},{5,6},{6,7},{8,9},{9,10},{10,11},{11... | collective-permute-start | bytes 322568 | tf_op jit(solution)/shard_map/ppermute | solution.py:326
  14.9 1.3 collective-permute-start.3
  16.2 0.1 pad_add_fusion.who_ref
  16.4 0.0 copy-start.7
  16.4 0.0 copy-start.8
  16.4 0.6 collective-permute-done.2
  17.0 3.8 %collective-permute-done.3 = bf16[70,3,256]{2,1,0:T(4,128)(2,1)S(1)} collective-permute-done((bf16[70,3,256]{2,1,0:T(4,128)(2,1)S(1)}, bf16[70,3,256]{2,1,0:T(4,128)(2,1)S(1)}, u32[]{:S(2)}, u32[]{:S(2)}) %collective-permute-start.3) | collective-permute-done | bytes 107552 | tf_op jit(solution)/shard_map/ppermute | solution.py:327
  20.8 1.8 %maximum_maximum_fusion.pad_ref = bf16[70,80,256]{2,1,0:T(8,128)(2,1)S(1)} fusion(bf16[70,3,256]{2,1,0:T(4,128)(2,1)S(1)} %collective-permute-done.3, bf16[3,64,256]{2,1,0:T(8,128)(2,1)S(1)} %collective-permute-done.1, bf16[64,64,256]{2,1,0:T(8,128)(2,1)S(1)} %copy-done.10, bf16[3,64,256]{2,1,0:T(8,128)(2,1)S(1)} %collective-permute-done, ...), kind=kLoop, calls=%fused_computation | loop fusion | flops 17203200 | bytes 5376160 | tf_op jit(solution)/shard_map/concatenate | solution.py:329
  22.6 0.6 broadcast_in_dim.26.wet_ref
  23.3 35.5 %cell_pass.1 = (bf16[64,64,256]{2,1,0:T(8,128)(2,1)S(1)}, f32[16,72,128]{2,1,0:T(8,128)S(1)}, f32[16,72,128]{2,1,0:T(8,128)S(1)}) custom-call(s32[2]{0:T(128)S(1)} %pad_add_fusion.who_ref, bf16[70,80,256]{2,1,0:T(8,128)(2,1)S(1)} %maximum_maximum_fusion.pad_ref, bf16[64,64,256]{2,1,0:T(8,128)(2,1)S(1)} %copy-done.1, ...), custom_call_target="tpu_custom_call" | custom-call | flops 20000000000 | bytes 16777216 | tf_op jit(solution)/shard_map/cell_pass/pallas_call | solution.py:245
  58.9 2.8 %collective-permute-start.4 = (bf16[3,64,256]{2,1,0:T(8,128)(2,1)S(1)}, bf16[3,64,256]{2,1,0:T(8,128)(2,1)S(1)}, u32[]{:S(2)}, u32[]{:S(2)}) collective-permute-start(bf16[3,64,256]{2,1,0:T(8,128)(2,1)S(1)} %get-tuple-element.31), channel_id=1, source_target_pairs={{0,8},{8,16},{16,24},{24,32},{32,40},{40,48},{48,56},{56,64},{64,7... | collective-permute-start | bytes 294920 | tf_op jit(solution)/shard_map/ppermute | solution.py:323
  61.6 1.3 collective-permute-start.5
  63.0 5.3 %collective-permute-start.8 = (f32[16,72,128]{2,1,0:T(8,128)S(1)}, f32[16,72,128]{2,1,0:T(8,128)S(1)}, u32[]{:S(2)}, u32[]{:S(2)}) collective-permute-start(f32[16,72,128]{2,1,0:T(8,128)S(1)} %get-tuple-element.16), channel_id=1, source_target_pairs={{0,8},{1,9},{2,10},{3,11},{4,12},{5,13},{6,14},{7,15},{8,0},{9,1},... | collective-permute-start | bytes 1769480 | tf_op jit(solution)/shard_map/ppermute | solution.py:361
  68.3 0.2 constant_dynamic-update-slice_fusion.1
  68.5 0.1 fusion.5
  68.7 3.8 %collective-permute-start.6 = (bf16[70,3,256]{2,1,0:T(4,128)(2,1)S(1)}, bf16[70,3,256]{2,1,0:T(4,128)(2,1)S(1)}, u32[]{:S(2)}, u32[]{:S(2)}) collective-permute-start(bf16[70,3,256]{2,1,0:T(4,128)(2,1)S(1)} %get-tuple-element.26), channel_id=1, source_target_pairs={{0,1},{1,2},{2,3},{3,4},{4,5},{5,6},{6,7},{8,9},{9,10},{10,11},{11... | collective-permute-start | bytes 322568 | tf_op jit(solution)/shard_map/ppermute | solution.py:326
  72.5 1.3 collective-permute-start.7
  73.8 0.7 collective-permute-done.6
  74.5 3.8 %collective-permute-done.7 = bf16[70,3,256]{2,1,0:T(4,128)(2,1)S(1)} collective-permute-done((bf16[70,3,256]{2,1,0:T(4,128)(2,1)S(1)}, bf16[70,3,256]{2,1,0:T(4,128)(2,1)S(1)}, u32[]{:S(2)}, u32[]{:S(2)}) %collective-permute-start.7) | collective-permute-done | bytes 107552 | tf_op jit(solution)/shard_map/ppermute | solution.py:327
  78.3 1.8 %maximum_maximum_fusion.1.pad_ref = bf16[70,80,256]{2,1,0:T(8,128)(2,1)S(1)} fusion(bf16[70,3,256]{2,1,0:T(4,128)(2,1)S(1)} %collective-permute-done.7, bf16[70,64,256]{2,1,0:T(8,128)(2,1)S(1)} %constant_dynamic-update-slice_fusion, bf16[70,3,256]{2,1,0:T(4,128)(2,1)S(1)} %collective-permute-done.6, bf16[80]{0:T(256)(128)(2,1)S(1)} %pad.13.clone), kind=kLoop, calls=%fused_computation.1 | loop fusion | flops 11468800 | bytes 5376160 | tf_op jit(solution)/shard_map/concatenate | solution.py:329
  80.1 0.1 fusion.4
  80.3 2.7 %collective-permute-start.9 = (bf16[4,72,128]{2,1,0:T(8,128)(2,1)S(1)}, bf16[4,72,128]{2,1,0:T(8,128)(2,1)S(1)}, u32[]{:S(2)}, u32[]{:S(2)}) collective-permute-start(bf16[4,72,128]{2,1,0:T(8,128)(2,1)S(1)} %get-tuple-element.36), channel_id=1, source_target_pairs={{0,16},{1,17},{2,18},{3,19},{4,20},{5,21},{6,22},{7,23},{8,10},{9,... | collective-permute-start | bytes 221192 | tf_op jit(solution)/shard_map/ppermute | solution.py:361
  83.0 1.8 %collective-permute-start.11 = (bf16[4,72,128]{2,1,0:T(8,128)(2,1)S(1)}, bf16[4,72,128]{2,1,0:T(8,128)(2,1)S(1)}, u32[]{:S(2)}, u32[]{:S(2)}) collective-permute-start(bf16[4,72,128]{2,1,0:T(8,128)(2,1)S(1)} %get-tuple-element.37), channel_id=1, source_target_pairs={{0,48},{1,49},{2,50},{3,51},{4,52},{5,53},{6,54},{7,55},{8,14},{9,... | collective-permute-start | bytes 221192 | tf_op jit(solution)/shard_map/ppermute | solution.py:361
  84.8 0.1 collective-permute-start.10
  84.9 3.4 %spread_pass.4.out_refs_0_ = f32[64,64,256]{2,1,0:T(8,128)} custom-call(bf16[70,80,256]{2,1,0:T(8,128)(2,1)S(1)} %maximum_maximum_fusion.1.pad_ref, bf16[64,64,256]{2,1,0:T(8,128)(2,1)S(1)} %copy-done.1, bf16[64,64,128]{2,1,0:T(8,128)(2,1)S(1)} %broadcast_in_dim.26.wet_ref, bf16[512,512]{1,0:T(8,128)(2,1)S(1)} %copy-done.2, bf16[256,512]{1,0:T(8,128)(2,1)S(1)} %copy-done.3, ...), custom_call_target="tpu_custom_call" | custom-call | flops 4000000000 | bytes 4194304 | tf_op jit(solution)/shard_map/spread_pass/pallas_call | solution.py:293
  88.3 1.5 %collective-permute-done.10 = bf16[4,72,128]{2,1,0:T(8,128)(2,1)S(1)} collective-permute-done((bf16[4,72,128]{2,1,0:T(8,128)(2,1)S(1)}, bf16[4,72,128]{2,1,0:T(8,128)(2,1)S(1)}, u32[]{:S(2)}, u32[]{:S(2)}) %collective-permute-start.10) | collective-permute-done | bytes 73760 | tf_op jit(solution)/shard_map/ppermute | solution.py:361
  89.8 0.1 collective-permute-start.12
  89.9 3.7 %collective-permute-start.14 = (bf16[1,72,128]{2,1,0:T(8,128)(2,1)S(1)}, bf16[1,72,128]{2,1,0:T(8,128)(2,1)S(1)}, u32[]{:S(2)}, u32[]{:S(2)}) collective-permute-start(bf16[1,72,128]{2,1,0:T(8,128)(2,1)S(1)} %get-tuple-element.46), channel_id=1, source_target_pairs={{0,6},{1,7},{2,4},{3,5},{4,2},{5,3},{6,0},{7,1},{8,73},{9,72},{10,... | collective-permute-start | bytes 55304 | tf_op jit(solution)/shard_map/ppermute | solution.py:361
  93.6 0.1 collective-permute-start.13
  93.7 3.4 %spread_pass.5.out_refs_0_ = f32[64,64,256]{2,1,0:T(8,128)} custom-call(bf16[70,80,256]{2,1,0:T(8,128)(2,1)S(1)} %maximum_maximum_fusion.1.pad_ref, bf16[64,64,256]{2,1,0:T(8,128)(2,1)S(1)} %copy-done.1, bf16[64,64,128]{2,1,0:T(8,128)(2,1)S(1)} %broadcast_in_dim.26.wet_ref, bf16[512,512]{1,0:T(8,128)(2,1)S(1)} %copy-done.2, ...), custom_call_target="tpu_custom_call", output_to_operand_aliasing={{}: (6, {})} | custom-call | flops 4000000000 | bytes 4194304 | tf_op jit(solution)/shard_map/spread_pass/pallas_call | solution.py:293
  97.2 0.6 collective-permute-done.13
  97.8 5.6 %collective-permute-start.17 = (f32[1,72,128]{2,1,0:T(8,128)S(1)}, f32[1,72,128]{2,1,0:T(8,128)S(1)}, u32[]{:S(2)}, u32[]{:S(2)}) collective-permute-start(f32[1,72,128]{2,1,0:T(8,128)S(1)} %fusion.1), channel_id=1, source_target_pairs={{0,65},{1,64},{2,67},{3,66},{4,69},{5,68},{6,71},{7,70},{8,56},{9,... | collective-permute-start | bytes 110600 | tf_op jit(solution)/shard_map/ppermute | solution.py:361
  103.4 0.7 collective-permute-start.15
  104.0 3.4 %spread_pass.6.out_refs_0_ = f32[64,64,256]{2,1,0:T(8,128)} custom-call(bf16[70,80,256]{2,1,0:T(8,128)(2,1)S(1)} %maximum_maximum_fusion.1.pad_ref, bf16[64,64,256]{2,1,0:T(8,128)(2,1)S(1)} %copy-done.1, bf16[64,64,128]{2,1,0:T(8,128)(2,1)S(1)} %broadcast_in_dim.26.wet_ref, bf16[512,512]{1,0:T(8,128)(2,1)S(1)} %copy-done.2, ...), custom_call_target="tpu_custom_call", output_to_operand_aliasing={{}: (6, {})} | custom-call | flops 4000000000 | bytes 4194304 | tf_op jit(solution)/shard_map/spread_pass/pallas_call | solution.py:293
  107.5 0.2 collective-permute-done.16
  107.7 1.0 collective-permute-start.20
  108.7 1.7 %collective-permute-start.19 = (bf16[1,72,128]{2,1,0:T(8,128)(2,1)S(1)}, bf16[1,72,128]{2,1,0:T(8,128)(2,1)S(1)}, u32[]{:S(2)}, u32[]{:S(2)}) collective-permute-start(bf16[1,72,128]{2,1,0:T(8,128)(2,1)S(1)} %get-tuple-element.21), channel_id=1, source_target_pairs={{0,4},{1,5},{2,6},{3,7},{4,0},{5,1},{6,2},{7,3},{8,72},{9,73},{10,... | collective-permute-start | bytes 55304 | tf_op jit(solution)/shard_map/ppermute | solution.py:361
  110.4 0.6 collective-permute-start.18
  111.0 0.6 collective-permute-done.20
  111.6 1.2 collective-permute-done.19
  112.8 0.2 collective-permute-done.18
  113.0 1.1 collective-permute-start.23
  114.2 1.3 collective-permute-start.22
  115.5 0.9 collective-permute-start.21
  116.4 2.5 %collective-permute-done.21 = bf16[4,72,128]{2,1,0:T(8,128)(2,1)S(1)} collective-permute-done((bf16[4,72,128]{2,1,0:T(8,128)(2,1)S(1)}, bf16[4,72,128]{2,1,0:T(8,128)(2,1)S(1)}, u32[]{:S(2)}, u32[]{:S(2)}) %collective-permute-start.21) | collective-permute-done | bytes 73760 | tf_op jit(solution)/shard_map/ppermute | solution.py:361
  119.0 5.5 %collective-permute-start.24 = (bf16[16,72,128]{2,1,0:T(8,128)(2,1)S(1)}, bf16[16,72,128]{2,1,0:T(8,128)(2,1)S(1)}, u32[]{:S(2)}, u32[]{:S(2)}) collective-permute-start(bf16[16,72,128]{2,1,0:T(8,128)(2,1)S(1)} %get-tuple-element.39), channel_id=1, source_target_pairs={{0,8},{1,9},{2,10},{3,11},{4,12},{5,13},{6,14},{7,15},{8,0},{9,1},... | collective-permute-start | bytes 884744 | tf_op jit(solution)/shard_map/ppermute | solution.py:361
  124.5 3.4 %spread_pass.7 = f32[64,64,256]{2,1,0:T(8,128)} custom-call(bf16[70,80,256]{2,1,0:T(8,128)(2,1)S(1)} %maximum_maximum_fusion.1.pad_ref, bf16[64,64,256]{2,1,0:T(8,128)(2,1)S(1)} %copy-done.1, bf16[64,64,128]{2,1,0:T(8,128)(2,1)S(1)} %broadcast_in_dim.26.wet_ref, bf16[512,512]{1,0:T(8,128)(2,1)S(1)} %copy-done.2, ...), custom_call_target="tpu_custom_call", output_to_operand_aliasing={{}: (6, {})} | custom-call | flops 4000000000 | bytes 4194304 | tf_op jit(solution)/shard_map/spread_pass/pallas_call | solution.py:293
  128.0 0.8 copy-done.12
  128.8 2.2 %finish.1 = (f32[256,512]{1,0:T(8,128)}, f32[512,256]{1,0:T(8,128)}, f32[64,256]{1,0:T(8,128)}) custom-call(s32[2]{0:T(128)} %copy-done.4, bf16[32,72,128]{2,1,0:T(8,128)(2,1)} %copy-done.12), custom_call_target="tpu_custom_call" | custom-call | tf_op jit(solution)/shard_map/finish/pallas_call | solution.py:273
  131.0 0.7 slice_bitcast_fusion
  131.7 1.4 %fusion.11 = (f32[1,256]{1,0:T(1,128)}, f32[1,256]{1,0:T(1,128)}, f32[1,256]{1,0:T(1,128)}) fusion(f32[64,256]{1,0:T(8,128)} %get-tuple-element.17), kind=kLoop, calls=%fused_computation.40 | loop fusion | bytes 6144 | tf_op jit(solution)/shard_map/slice | solution.py:407
  133.1 1.4 %slice.96 = f32[49,256]{1,0:T(8,128)} slice(f32[64,256]{1,0:T(8,128)} %get-tuple-element.17), slice={[0:49], [0:256]} | slice | bytes 100352 | tf_op jit(solution)/shard_map/slice | solution.py:407
  134.5 0.6 copy.26
  (66 shorter events, 0.5 us)
Async XLA Ops:
  0.6 5.6 %copy-start = (bf16[49,256]{1,0:T(8,128)(2,1)S(1)}, bf16[49,256]{1,0:T(8,128)(2,1)}, u32[]{:S(2)}) copy-start(bf16[49,256]{1,0:T(8,128)(2,1)} %param.18) | copy-start | bytes 75268
  0.6 5.5 %copy-start.11 = (f32[1536,49]{1,0:T(8,128)S(1)}, f32[1536,49]{1,0:T(8,128)}, u32[]{:S(2)}) copy-start(f32[1536,49]{1,0:T(8,128)} %constant.79.clone) | copy-start | bytes 903172
  3.4 3.6 %copy-start.9 = (bf16[64,64,256]{2,1,0:T(8,128)(2,1)}, bf16[64,64,256]{2,1,0:T(8,128)(2,1)S(1)}, u32[]{:S(2)}) copy-start(bf16[64,64,256]{2,1,0:T(8,128)(2,1)S(1)} %broadcast_multiply_fusion) | copy-start | bytes 6291460
  3.5 3.7 %copy-start.14 = (bf16[256]{0:T(256)(128)(2,1)S(1)}, bf16[256]{0:T(256)(128)(2,1)}, u32[]{:S(2)}) copy-start(bf16[256]{0:T(256)(128)(2,1)} %param.19) | copy-start | bytes 1540
  3.5 3.7 %copy-start.15 = (bf16[256]{0:T(256)(128)(2,1)S(1)}, bf16[256]{0:T(256)(128)(2,1)}, u32[]{:S(2)}) copy-start(bf16[256]{0:T(256)(128)(2,1)} %param.20) | copy-start | bytes 1540
  3.5 3.7 %copy-start.16 = (bf16[256]{0:T(256)(128)(2,1)S(1)}, bf16[256]{0:T(256)(128)(2,1)}, u32[]{:S(2)}) copy-start(bf16[256]{0:T(256)(128)(2,1)} %param.21) | copy-start | bytes 1540
  3.5 3.7 %copy-start.13 = (bf16[512]{0:T(512)(128)(2,1)S(1)}, bf16[512]{0:T(512)(128)(2,1)}, u32[]{:S(2)}) copy-start(bf16[512]{0:T(512)(128)(2,1)} %param.23) | copy-start | bytes 3076
  3.5 4.3 %collective-permute-start = (bf16[3,64,256]{2,1,0:T(8,128)(2,1)S(1)}, bf16[3,64,256]{2,1,0:T(8,128)(2,1)S(1)}, u32[]{:S(2)}, u32[]{:S(2)}) collective-permute-start(bf16[3,64,256]{2,1,0:T(8,128)(2,1)S(1)} %get-tuple-element.32), channel_id=1, source_target_pairs={{0,8},{8,16},{16,24},{24,32},{32,40},{40,48},{48,56},{56,64},{64,7... | collective-permute-start | bytes 294920 | tf_op jit(solution)/shard_map/ppermute | solution.py:323
  6.2 4.3 %collective-permute-start.1 = (bf16[3,64,256]{2,1,0:T(8,128)(2,1)S(1)}, bf16[3,64,256]{2,1,0:T(8,128)(2,1)S(1)}, u32[]{:S(2)}, u32[]{:S(2)}) collective-permute-start(bf16[3,64,256]{2,1,0:T(8,128)(2,1)S(1)} %get-tuple-element.33), channel_id=1, source_target_pairs={{0,120},{8,0},{16,8},{24,16},{32,24},{40,32},{48,40},{56,48},{64,5... | collective-permute-start | bytes 294920 | tf_op jit(solution)/shard_map/ppermute | solution.py:324
  7.2 13.6 %copy-start.10 = (bf16[64,64,256]{2,1,0:T(8,128)(2,1)S(1)}, bf16[64,64,256]{2,1,0:T(8,128)(2,1)}, u32[]{:S(2)}) copy-start(bf16[64,64,256]{2,1,0:T(8,128)(2,1)} %copy-done.9) | copy-start | bytes 6291460
  11.7 5.3 %collective-permute-start.2 = (bf16[70,3,256]{2,1,0:T(4,128)(2,1)S(1)}, bf16[70,3,256]{2,1,0:T(4,128)(2,1)S(1)}, u32[]{:S(2)}, u32[]{:S(2)}) collective-permute-start(bf16[70,3,256]{2,1,0:T(4,128)(2,1)S(1)} %get-tuple-element.28), channel_id=1, source_target_pairs={{0,1},{1,2},{2,3},{3,4},{4,5},{5,6},{6,7},{8,9},{9,10},{10,11},{11... | collective-permute-start | bytes 322568 | tf_op jit(solution)/shard_map/ppermute | solution.py:326
  14.9 5.8 %collective-permute-start.3 = (bf16[70,3,256]{2,1,0:T(4,128)(2,1)S(1)}, bf16[70,3,256]{2,1,0:T(4,128)(2,1)S(1)}, u32[]{:S(2)}, u32[]{:S(2)}) collective-permute-start(bf16[70,3,256]{2,1,0:T(4,128)(2,1)S(1)} %get-tuple-element.29), channel_id=1, source_target_pairs={{1,0},{2,1},{3,2},{4,3},{5,4},{6,5},{7,6},{9,8},{10,9},{11,10},{12... | collective-permute-start | bytes 322568 | tf_op jit(solution)/shard_map/ppermute | solution.py:327
  16.3 6.9 %copy-start.4 = (s32[2]{0:T(128)}, s32[2]{0:T(128)S(1)}, u32[]{:S(2)}) copy-start(s32[2]{0:T(128)S(1)} %pad_add_fusion.who_ref) | copy-start | bytes 28
  16.3 6.9 %copy-start.1 = (bf16[64,64,256]{2,1,0:T(8,128)(2,1)S(1)}, bf16[64,64,256]{2,1,0:T(8,128)(2,1)}, u32[]{:S(2)}) copy-start(bf16[64,64,256]{2,1,0:T(8,128)(2,1)} %cot_ref.9) | copy-start | bytes 6291460
  16.3 6.9 %copy-start.2 = (bf16[512,512]{1,0:T(8,128)(2,1)S(1)}, bf16[512,512]{1,0:T(8,128)(2,1)}, u32[]{:S(2)}) copy-start(bf16[512,512]{1,0:T(8,128)(2,1)} %constant.80.clone.place_ref) | copy-start | bytes 1572868
  16.3 6.9 %copy-start.3 = (bf16[256,512]{1,0:T(8,128)(2,1)S(1)}, bf16[256,512]{1,0:T(8,128)(2,1)}, u32[]{:S(2)}) copy-start(bf16[256,512]{1,0:T(8,128)(2,1)} %constant.82.clone.back_ref) | copy-start | bytes 786436
  16.3 6.9 %copy-start.5 = (bf16[256,512]{1,0:T(8,128)(2,1)S(1)}, bf16[256,512]{1,0:T(8,128)(2,1)}, u32[]{:S(2)}) copy-start(bf16[256,512]{1,0:T(8,128)(2,1)} %up_ref.1) | copy-start | bytes 786436
  16.3 6.9 %copy-start.6 = (bf16[512,256]{1,0:T(8,128)(2,1)S(1)}, bf16[512,256]{1,0:T(8,128)(2,1)}, u32[]{:S(2)}) copy-start(bf16[512,256]{1,0:T(8,128)(2,1)} %down_ref.1) | copy-start | bytes 786436
  16.4 6.9 %copy-start.7 = (bf16[512,256]{1,0:T(8,128)(2,1)S(1)}, bf16[512,256]{1,0:T(8,128)(2,1)}, u32[]{:S(2)}) copy-start(bf16[512,256]{1,0:T(8,128)(2,1)} %constant.81.clone.own_ref) | copy-start | bytes 786436
  16.4 6.9 %copy-start.8 = (f32[49,768]{1,0:T(8,128)S(1)}, f32[49,768]{1,0:T(8,128)}, u32[]{:S(2)}) copy-start(f32[49,768]{1,0:T(8,128)} %constant.83.clone.collect_ref) | copy-start | bytes 451588
  58.9 9.4 %collective-permute-start.4 = (bf16[3,64,256]{2,1,0:T(8,128)(2,1)S(1)}, bf16[3,64,256]{2,1,0:T(8,128)(2,1)S(1)}, u32[]{:S(2)}, u32[]{:S(2)}) collective-permute-start(bf16[3,64,256]{2,1,0:T(8,128)(2,1)S(1)} %get-tuple-element.31), channel_id=1, source_target_pairs={{0,8},{8,16},{16,24},{24,32},{32,40},{40,48},{48,56},{56,64},{64,7... | collective-permute-start | bytes 294920 | tf_op jit(solution)/shard_map/ppermute | solution.py:323
  61.6 6.9 %collective-permute-start.5 = (bf16[3,64,256]{2,1,0:T(8,128)(2,1)S(1)}, bf16[3,64,256]{2,1,0:T(8,128)(2,1)S(1)}, u32[]{:S(2)}, u32[]{:S(2)}) collective-permute-start(bf16[3,64,256]{2,1,0:T(8,128)(2,1)S(1)} %get-tuple-element.30), channel_id=1, source_target_pairs={{0,120},{8,0},{16,8},{24,16},{32,24},{40,32},{48,40},{56,48},{64,5... | collective-permute-start | bytes 294920 | tf_op jit(solution)/shard_map/ppermute | solution.py:324
  63.0 17.2 %collective-permute-start.8 = (f32[16,72,128]{2,1,0:T(8,128)S(1)}, f32[16,72,128]{2,1,0:T(8,128)S(1)}, u32[]{:S(2)}, u32[]{:S(2)}) collective-permute-start(f32[16,72,128]{2,1,0:T(8,128)S(1)} %get-tuple-element.16), channel_id=1, source_target_pairs={{0,8},{1,9},{2,10},{3,11},{4,12},{5,13},{6,14},{7,15},{8,0},{9,1},... | collective-permute-start | bytes 1769480 | tf_op jit(solution)/shard_map/ppermute | solution.py:361
  68.7 5.9 %collective-permute-start.6 = (bf16[70,3,256]{2,1,0:T(4,128)(2,1)S(1)}, bf16[70,3,256]{2,1,0:T(4,128)(2,1)S(1)}, u32[]{:S(2)}, u32[]{:S(2)}) collective-permute-start(bf16[70,3,256]{2,1,0:T(4,128)(2,1)S(1)} %get-tuple-element.26), channel_id=1, source_target_pairs={{0,1},{1,2},{2,3},{3,4},{4,5},{5,6},{6,7},{8,9},{9,10},{10,11},{11... | collective-permute-start | bytes 322568 | tf_op jit(solution)/shard_map/ppermute | solution.py:326
  72.5 5.8 %collective-permute-start.7 = (bf16[70,3,256]{2,1,0:T(4,128)(2,1)S(1)}, bf16[70,3,256]{2,1,0:T(4,128)(2,1)S(1)}, u32[]{:S(2)}, u32[]{:S(2)}) collective-permute-start(bf16[70,3,256]{2,1,0:T(4,128)(2,1)S(1)} %get-tuple-element.27), channel_id=1, source_target_pairs={{1,0},{2,1},{3,2},{4,3},{5,4},{6,5},{7,6},{9,8},{10,9},{11,10},{12... | collective-permute-start | bytes 322568 | tf_op jit(solution)/shard_map/ppermute | solution.py:327
  80.3 8.1 %collective-permute-start.9 = (bf16[4,72,128]{2,1,0:T(8,128)(2,1)S(1)}, bf16[4,72,128]{2,1,0:T(8,128)(2,1)S(1)}, u32[]{:S(2)}, u32[]{:S(2)}) collective-permute-start(bf16[4,72,128]{2,1,0:T(8,128)(2,1)S(1)} %get-tuple-element.36), channel_id=1, source_target_pairs={{0,16},{1,17},{2,18},{3,19},{4,20},{5,21},{6,22},{7,23},{8,10},{9,... | collective-permute-start | bytes 221192 | tf_op jit(solution)/shard_map/ppermute | solution.py:361
  83.0 5.3 %collective-permute-start.11 = (bf16[4,72,128]{2,1,0:T(8,128)(2,1)S(1)}, bf16[4,72,128]{2,1,0:T(8,128)(2,1)S(1)}, u32[]{:S(2)}, u32[]{:S(2)}) collective-permute-start(bf16[4,72,128]{2,1,0:T(8,128)(2,1)S(1)} %get-tuple-element.37), channel_id=1, source_target_pairs={{0,48},{1,49},{2,50},{3,51},{4,52},{5,53},{6,54},{7,55},{8,14},{9,... | collective-permute-start | bytes 221192 | tf_op jit(solution)/shard_map/ppermute | solution.py:361
  84.8 5.0 %collective-permute-start.10 = (bf16[4,72,128]{2,1,0:T(8,128)(2,1)S(1)}, bf16[4,72,128]{2,1,0:T(8,128)(2,1)S(1)}, u32[]{:S(2)}, u32[]{:S(2)}) collective-permute-start(bf16[4,72,128]{2,1,0:T(8,128)(2,1)S(1)} %get-tuple-element.38), channel_id=1, source_target_pairs={{0,32},{1,33},{2,34},{3,35},{4,36},{5,37},{6,38},{7,39},{8,12},{9,... | collective-permute-start | bytes 221192 | tf_op jit(solution)/shard_map/ppermute | solution.py:361
  89.8 7.3 %collective-permute-start.12 = (bf16[1,72,128]{2,1,0:T(8,128)(2,1)S(1)}, bf16[1,72,128]{2,1,0:T(8,128)(2,1)S(1)}, u32[]{:S(2)}, u32[]{:S(2)}) collective-permute-start(bf16[1,72,128]{2,1,0:T(8,128)(2,1)S(1)} %get-tuple-element.45), channel_id=1, source_target_pairs={{0,2},{1,3},{2,0},{3,1},{4,6},{5,7},{6,4},{7,5},{8,9},{9,8},{10,11... | collective-permute-start | bytes 55304 | tf_op jit(solution)/shard_map/ppermute | solution.py:361
  89.9 7.2 %collective-permute-start.14 = (bf16[1,72,128]{2,1,0:T(8,128)(2,1)S(1)}, bf16[1,72,128]{2,1,0:T(8,128)(2,1)S(1)}, u32[]{:S(2)}, u32[]{:S(2)}) collective-permute-start(bf16[1,72,128]{2,1,0:T(8,128)(2,1)S(1)} %get-tuple-element.46), channel_id=1, source_target_pairs={{0,6},{1,7},{2,4},{3,5},{4,2},{5,3},{6,0},{7,1},{8,73},{9,72},{10,... | collective-permute-start | bytes 55304 | tf_op jit(solution)/shard_map/ppermute | solution.py:361
  93.6 4.1 %collective-permute-start.13 = (bf16[1,72,128]{2,1,0:T(8,128)(2,1)S(1)}, bf16[1,72,128]{2,1,0:T(8,128)(2,1)S(1)}, u32[]{:S(2)}, u32[]{:S(2)}) collective-permute-start(bf16[1,72,128]{2,1,0:T(8,128)(2,1)S(1)} %get-tuple-element.47), channel_id=1, source_target_pairs={{0,4},{1,5},{2,6},{3,7},{4,0},{5,1},{6,2},{7,3},{8,72},{9,73},{10,... | collective-permute-start | bytes 55304 | tf_op jit(solution)/shard_map/ppermute | solution.py:361
  97.8 9.7 %collective-permute-start.17 = (f32[1,72,128]{2,1,0:T(8,128)S(1)}, f32[1,72,128]{2,1,0:T(8,128)S(1)}, u32[]{:S(2)}, u32[]{:S(2)}) collective-permute-start(f32[1,72,128]{2,1,0:T(8,128)S(1)} %fusion.1), channel_id=1, source_target_pairs={{0,65},{1,64},{2,67},{3,66},{4,69},{5,68},{6,71},{7,70},{8,56},{9,... | collective-permute-start | bytes 110600 | tf_op jit(solution)/shard_map/ppermute | solution.py:361
  103.4 4.3 %collective-permute-start.16 = (f32[1,72,128]{2,1,0:T(8,128)S(1)}, f32[1,72,128]{2,1,0:T(8,128)S(1)}, u32[]{:S(2)}, u32[]{:S(2)}) collective-permute-start(f32[1,72,128]{2,1,0:T(8,128)S(1)} %fusion.1), channel_id=1, source_target_pairs={{0,64},{1,65},{2,66},{3,67},{4,68},{5,69},{6,70},{7,71},{8,40},{9,... | collective-permute-start | bytes 110600 | tf_op jit(solution)/shard_map/ppermute | solution.py:361
  103.4 4.3 %collective-permute-start.15 = (f32[1,72,128]{2,1,0:T(8,128)S(1)}, f32[1,72,128]{2,1,0:T(8,128)S(1)}, u32[]{:S(2)}, u32[]{:S(2)}) collective-permute-start(f32[1,72,128]{2,1,0:T(8,128)S(1)} %fusion.1), channel_id=1, source_target_pairs={{0,1},{1,0},{2,3},{3,2},{4,5},{5,4},{6,7},{7,6},{8,24},{9,25},{10,... | collective-permute-start | bytes 110600 | tf_op jit(solution)/shard_map/ppermute | solution.py:361
  107.7 3.9 %collective-permute-start.20 = (bf16[1,72,128]{2,1,0:T(8,128)(2,1)S(1)}, bf16[1,72,128]{2,1,0:T(8,128)(2,1)S(1)}, u32[]{:S(2)}, u32[]{:S(2)}) collective-permute-start(bf16[1,72,128]{2,1,0:T(8,128)(2,1)S(1)} %get-tuple-element.21), channel_id=1, source_target_pairs={{0,6},{1,7},{2,4},{3,5},{4,2},{5,3},{6,0},{7,1},{8,73},{9,72},{10,... | collective-permute-start | bytes 55304 | tf_op jit(solution)/shard_map/ppermute | solution.py:361
  108.7 4.1 %collective-permute-start.19 = (bf16[1,72,128]{2,1,0:T(8,128)(2,1)S(1)}, bf16[1,72,128]{2,1,0:T(8,128)(2,1)S(1)}, u32[]{:S(2)}, u32[]{:S(2)}) collective-permute-start(bf16[1,72,128]{2,1,0:T(8,128)(2,1)S(1)} %get-tuple-element.21), channel_id=1, source_target_pairs={{0,4},{1,5},{2,6},{3,7},{4,0},{5,1},{6,2},{7,3},{8,72},{9,73},{10,... | collective-permute-start | bytes 55304 | tf_op jit(solution)/shard_map/ppermute | solution.py:361
  110.4 2.6 %collective-permute-start.18 = (bf16[1,72,128]{2,1,0:T(8,128)(2,1)S(1)}, bf16[1,72,128]{2,1,0:T(8,128)(2,1)S(1)}, u32[]{:S(2)}, u32[]{:S(2)}) collective-permute-start(bf16[1,72,128]{2,1,0:T(8,128)(2,1)S(1)} %get-tuple-element.21), channel_id=1, source_target_pairs={{0,2},{1,3},{2,0},{3,1},{4,6},{5,7},{6,4},{7,5},{8,9},{9,8},{10,11... | collective-permute-start | bytes 55304 | tf_op jit(solution)/shard_map/ppermute | solution.py:361
  113.0 5.9 %collective-permute-start.23 = (bf16[4,72,128]{2,1,0:T(8,128)(2,1)S(1)}, bf16[4,72,128]{2,1,0:T(8,128)(2,1)S(1)}, u32[]{:S(2)}, u32[]{:S(2)}) collective-permute-start(bf16[4,72,128]{2,1,0:T(8,128)(2,1)S(1)} %pad_maximum_fusion.3), channel_id=1, source_target_pairs={{0,48},{1,49},{2,50},{3,51},{4,52},{5,53},{6,54},{7,55},{8,14},{9,... | collective-permute-start | bytes 221192 | tf_op jit(solution)/shard_map/ppermute | solution.py:361
  114.2 4.8 %collective-permute-start.22 = (bf16[4,72,128]{2,1,0:T(8,128)(2,1)S(1)}, bf16[4,72,128]{2,1,0:T(8,128)(2,1)S(1)}, u32[]{:S(2)}, u32[]{:S(2)}) collective-permute-start(bf16[4,72,128]{2,1,0:T(8,128)(2,1)S(1)} %pad_maximum_fusion.3), channel_id=1, source_target_pairs={{0,32},{1,33},{2,34},{3,35},{4,36},{5,37},{6,38},{7,39},{8,12},{9,... | collective-permute-start | bytes 221192 | tf_op jit(solution)/shard_map/ppermute | solution.py:361
  115.5 3.4 %collective-permute-start.21 = (bf16[4,72,128]{2,1,0:T(8,128)(2,1)S(1)}, bf16[4,72,128]{2,1,0:T(8,128)(2,1)S(1)}, u32[]{:S(2)}, u32[]{:S(2)}) collective-permute-start(bf16[4,72,128]{2,1,0:T(8,128)(2,1)S(1)} %pad_maximum_fusion.3), channel_id=1, source_target_pairs={{0,16},{1,17},{2,18},{3,19},{4,20},{5,21},{6,22},{7,23},{8,10},{9,... | collective-permute-start | bytes 221192 | tf_op jit(solution)/shard_map/ppermute | solution.py:361
  119.0 8.9 %collective-permute-start.24 = (bf16[16,72,128]{2,1,0:T(8,128)(2,1)S(1)}, bf16[16,72,128]{2,1,0:T(8,128)(2,1)S(1)}, u32[]{:S(2)}, u32[]{:S(2)}) collective-permute-start(bf16[16,72,128]{2,1,0:T(8,128)(2,1)S(1)} %get-tuple-element.39), channel_id=1, source_target_pairs={{0,8},{1,9},{2,10},{3,11},{4,12},{5,13},{6,14},{7,15},{8,0},{9,1},... | collective-permute-start | bytes 884744 | tf_op jit(solution)/shard_map/ppermute | solution.py:361
  128.0 0.8 copy-start.12

commit v3 on v2

--- a/solution.py
+++ b/solution.py
@@ -14,6 +14,8 @@
 SPAN = TILE + 6
 HALF = 256
 AXES = ("gx", "gy")
+SIDES = ("north", "south", "west", "east", "nw", "ne", "sw", "se")
+MOVES = ((3, ((3, 0), (4, 1))), (6, ((3, 5), (4, 6))), (1, ((3, 2),)), (5, ((4, 7),)))
 BLOCKS = 32
 BLOCK_ROWS = 72
 LANES = 128
@@ -50,13 +52,15 @@
     cos, sin, weight, paired = basis()
     both = np.concatenate([cos, sin])
     place = np.zeros((2 * HALF, 2 * HALF))
+    for i in range(SPAN):
+        place[:, TILE * i : TILE * (i + 1)] = both[:, i, 3:19]
     for i in range(20):
-        place[:, 24 * i : 24 * i + 22] = both[:, i]
-        if i < 6:
-            at = 16 + 2 * (i % 3)
-            place[:, 24 * i + 22 : 24 * i + 24] = both[:, 20 + i // 3, at : at + 2]
-    for m in range(2):
-        place[:, 480 + 16 * m : 496 + 16 * m] = both[:, 20 + m, :16]
+        at = TILE * SPAN + 8 * i
+        place[:, at : at + 3] = both[:, i, 19:]
+        place[:, at + 5 : at + 8] = both[:, i, :3]
+        if i < 8:
+            for to, of in MOVES[i % 4][1]:
+                place[:, at + to] = both[:, 20 + i // 4, (of + 19) % 24]
     own = both[:, :TILE, :TILE].reshape(2 * HALF, TILE * TILE)
     back = own.T
     ct = (cos * weight[:, None, None])[:, :7, :7].reshape(HALF, 49)
@@ -86,21 +90,76 @@
     return lax.dot_general(a, b, (((0,), (0,)), ((), ())), preferred_element_type=F32)
 
 
-def patch(ref, a, b):
-    slabs = [
-        ref[TILE * a + i, pl.ds(pl.multiple_of(TILE * b, TILE), 32), :].astype(F32)
-        for i in range(SPAN)
+def rows_of(channels):
+    return lax.broadcasted_iota(jnp.int32, (8, channels), 0)
+
+
+def patch(mains, lefts, rights):
+    row = rows_of(mains[0].shape[1])
+    tails = [jnp.where(row < 4, after, before) for before, after in zip(lefts, rights)]
+    for i in range(8):
+        spare = pltpu.roll(tails[20 + i // 4], MOVES[i % 4][0], 0)
+        tails[i] = jnp.where((row == 3) | (row == 4), spare, tails[i])
+    return jnp.concatenate(mains + [jnp.concatenate(tails[:20], axis=0).astype(BF16)], axis=0)
+
+
+def pack_low(groups):
+    row = rows_of(groups[0].shape[1])
+    return [
+        jnp.where(row < 4, groups[n], pltpu.roll(groups[n + 1], 5, 0))
+        for n in range(0, len(groups), 2)
     ]
-    row = lax.broadcasted_iota(jnp.int32, (8, slabs[0].shape[1]), 0)
-    parts = []
-    for i in range(20):
-        tail = slabs[i][16:24]
-        if i < 6:
-            spare = pltpu.roll(slabs[20 + i // 3][16:24], 6 - 2 * (i % 3), 0)
-            tail = jnp.where(row < 6, tail, spare)
-        parts += [slabs[i][:16], tail]
-    parts += [slabs[20][:16], slabs[21][:16]]
-    return jnp.concatenate(parts, axis=0).astype(BF16)
+
+
+def pack_high(groups):
+    row = rows_of(groups[0].shape[1])
+    return [
+        jnp.where(row < 4, pltpu.roll(groups[n], 3, 0), groups[n + 1])
+        for n in range(0, len(groups), 2)
+    ]
+
+
+def packed_tiles(groups):
+    return [jnp.concatenate(groups[n : n + 2], axis=0).astype(BF16) for n in range(0, len(groups), 2)]
+
+
+def side_group(ref, i, low):
+    group = ref[i // 4].astype(F32)[i % 4 // 2 * 8 :][:8]
+    if low:
+        return group if i % 2 == 0 else pltpu.roll(group, 3, 0)
+    return group if i % 2 == 1 else pltpu.roll(group, 5, 0)
+
+
+def edge_kernel(
+    top_ref, bottom_ref, left_ref, right_ref, wet_top_ref, wet_bottom_ref, wet_left_ref,
+    wet_right_ref, north_ref, south_ref, west_ref, east_ref, nw_ref, ne_ref, sw_ref, se_ref,
+):
+    def both(wet):
+        return jnp.concatenate([wet, wet], axis=-1)
+
+    lon = left_ref.shape[0]
+    north_ref[...] = top_ref[:3] * both(wet_top_ref[:3])
+    south_ref[...] = bottom_ref[1:] * both(wet_bottom_ref[1:])
+
+    def pack(start, count, west_out, east_out):
+        low = [
+            (left_ref[start + i] * both(wet_left_ref[start + i])).astype(F32)[:8]
+            for i in range(count)
+        ]
+        high = [
+            (right_ref[start + i] * both(wet_right_ref[start + i])).astype(F32)[8:]
+            for i in range(count)
+        ]
+        if count % 2:
+            low.append(low[-1])
+            high.append(high[-1])
+        for ref, groups in ((west_out, pack_low(low)), (east_out, pack_high(high))):
+            for n, tile in enumerate(packed_tiles(groups)):
+                ref[n] = tile
+
+    pack(0, lon, west_ref, east_ref)
+    pack(0, 3, nw_ref, ne_ref)
+    pack(lon - 3, 3, sw_ref, se_ref)
 
 
 def filtered(wave, taps_ref, back_ref):
@@ -117,22 +176,63 @@
     return pl.ds(pl.multiple_of((place ^ k) * BLOCK_ROWS, 8), BLOCK_ROWS)
 
 
+def build(pad_ref, x_ref, wets_ref, halos):
+    lon, lat, channels = x_ref.shape
+    zeros = jnp.zeros((8, channels), F32)
+
+    def row(i, _):
+        wet = wets_ref[i]
+        pad_ref[3 + i, TILE : TILE + lat, :] = x_ref[i] * jnp.concatenate([wet, wet], axis=-1)
+        return 0
+
+    lax.fori_loop(0, lon, row, 0, unroll=4)
+    pad_ref[:3, TILE : TILE + lat, :] = halos["north"][...]
+    pad_ref[3 + lon :, TILE : TILE + lat, :] = halos["south"][...]
+
+    def sides(start, count, west_ref, east_ref):
+        for i in range(count):
+            before = side_group(west_ref, i, False)
+            after = side_group(east_ref, i, True)
+            pad_ref[start + i, :TILE, :] = jnp.concatenate([zeros, before], axis=0).astype(BF16)
+            pad_ref[start + i, TILE + lat :, :] = jnp.concatenate([after, zeros], axis=0).astype(BF16)
+
+    sides(0, 3, halos["nw"], halos["ne"])
+    sides(3, lon, halos["west"], halos["east"])
+    sides(3 + lon, 3, halos["sw"], halos["se"])
+
+
+def patch_at(pad_ref, a, b):
+    def cells(i, n):
+        return pad_ref[TILE * a + i, pl.ds(pl.multiple_of(TILE * (b + n), TILE), TILE), :]
+
+    return patch(
+        [cells(i, 1) for i in range(SPAN)],
+        [cells(i, 0).astype(F32)[8:] for i in range(SPAN)],
+        [cells(i, 2).astype(F32)[:8] for i in range(SPAN)],
+    )
+
+
 def cell_kernel(
-    who_ref, pad_ref, cot_ref, wet_ref, place_ref, own_ref, back_ref, taps_ref, collect_ref,
+    who_ref, x_ref, wets_ref, north_ref, south_ref, west_ref, east_ref, nw_ref, ne_ref, sw_ref,
+    se_ref, cot_ref, wet_ref, place_ref, own_ref, back_ref, taps_ref, collect_ref,
     bias_ref, gain_ref, shift_ref, up_ref, up_bias_ref, down_ref,
-    fg_ref, keep_ref, send_ref,
-    sum_ref, p1_ref, p2_ref, p3_ref, small_ref,
+    fg_ref, keep_ref, send_ref, to_north_ref, to_south_ref, to_west_ref, to_east_ref, to_nw_ref,
+    to_ne_ref, to_sw_ref, to_se_ref,
+    pad_ref, sum_ref, p1_ref, p2_ref, p3_ref, small_ref,
 ):
     a, b = pl.program_id(0), pl.program_id(1)
-    channels = pad_ref.shape[2]
+    last_a, last_b = pl.num_programs(0) - 1, pl.num_programs(1) - 1
+    channels = x_ref.shape[2]
     units = up_ref.shape[1]
 
     @pl.when((a == 0) & (b == 0))
     def _():
         for ref in (sum_ref, p1_ref, p2_ref, p3_ref, small_ref):
             ref[...] = jnp.zeros_like(ref)
-
-    wave = dot(place_ref[...], patch(pad_ref, a, b))
+        refs = (north_ref, south_ref, west_ref, east_ref, nw_ref, ne_ref, sw_ref, se_ref)
+        build(pad_ref, x_ref, wets_ref, dict(zip(SIDES, refs)))
+
+    wave = dot(place_ref[...], patch_at(pad_ref, a, b))
     field = filtered(wave, taps_ref, back_ref) + bias_ref[...]
     wet = wet_ref[...].reshape(TILE * TILE, LANES)
     wet = jnp.concatenate([wet, wet], axis=1)
@@ -172,8 +272,36 @@
     scaled = normed_grad * gain
     scaled_mean = jnp.mean(scaled, axis=-1, keepdims=True)
     product_mean = jnp.mean(product * gain, axis=-1, keepdims=True)
-    field_grad = (inv_std * (scaled - scaled_mean - normed * product_mean)).astype(BF16)
-    fg_ref[...] = field_grad.reshape(TILE, TILE, channels)
+    wide_grad = inv_std * (scaled - scaled_mean - normed * product_mean)
+    field_grad = wide_grad.astype(BF16)
+    fg_tile = field_grad.reshape(TILE, TILE, channels)
+    fg_ref[...] = fg_tile
+    lows = [wide_grad[TILE * i : TILE * i + 8] for i in range(TILE)]
+    highs = [wide_grad[TILE * i + 8 : TILE * i + TILE] for i in range(TILE)]
+
+    def when(condition, packed, out_ref, start=0):
+        @pl.when(condition)
+        def _():
+            for n, tile in enumerate(packed_tiles(packed())):
+                out_ref[start + n] = tile
+
+    columns = pl.ds(pl.multiple_of(TILE * b, TILE), TILE)
+
+    @pl.when(a == 0)
+    def _():
+        to_north_ref[:, columns, :] = fg_tile[:3]
+
+    @pl.when(a == last_a)
+    def _():
+        to_south_ref[:, columns, :] = fg_tile[-3:]
+
+    ends = [0, 1, 2, 2], [-3, -2, -1, -1]
+    when(b == 0, lambda: pack_low(lows), to_west_ref, 4 * a)
+    when(b == last_b, lambda: pack_high(highs), to_east_ref, 4 * a)
+    when((a == 0) & (b == 0), lambda: pack_low([lows[i] for i in ends[0]]), to_nw_ref)
+    when((a == 0) & (b == last_b), lambda: pack_high([highs[i] for i in ends[0]]), to_ne_ref)
+    when((a == last_a) & (b == 0), lambda: pack_low([lows[i] for i in ends[1]]), to_sw_ref)
+    when((a == last_a) & (b == last_b), lambda: pack_high([highs[i] for i in ends[1]]), to_se_ref)
     ripple = dot(own_ref[...], field_grad)
     g_real, g_imag = ripple[:HALF], ripple[HALF:]
     x_real, x_imag = wave[:HALF], wave[HALF:]
@@ -182,7 +310,7 @@
     p3_ref[...] += g_real * x_imag - g_imag * x_real
     small_ref[51:52, :] += g_real[0:1]
 
-    @pl.when((a == pl.num_programs(0) - 1) & (b == pl.num_programs(1) - 1))
+    @pl.when((a == last_a) & (b == last_b))
     def _():
         total = 0.0
         for n, ref in enumerate((p1_ref, p2_ref, p3_ref)):
@@ -202,27 +330,69 @@
                 ref[k] = sum_ref[block_rows(who_ref[n], k), :]
 
 
-def finish_kernel(scale, who_ref, in_ref, up_ref, down_ref, small_ref, sum_ref):
+def finish_kernel(
+    scale, who_ref, in_ref, taps_ref, conv_bias_ref, gain_ref, shift_ref, up_ref, up_bias_ref,
+    down_ref, sum_ref,
+):
     for n in range(2):
         for k in range(BLOCKS // 2):
             rows = block_rows(who_ref[n], k)
             sum_ref[rows, :] = in_ref[n * (BLOCKS // 2) + k].astype(F32) * scale
     at = 0
-    for ref in (up_ref, down_ref, small_ref):
+    for ref in (up_ref, down_ref):
         for n in range(0, ref.shape[1], LANES):
             ref[:, n : n + LANES] = sum_ref[at : at + ref.shape[0], :]
             at += ref.shape[0]
-
-
-def spread_kernel(at, pad_ref, cot_ref, wet_ref, place_ref, back_ref, taps_ref, *out_refs):
-    b = pl.program_id(1)
-    channels = pad_ref.shape[2]
-    wave = dot(place_ref[...], patch(pad_ref, at, b))
-    spread = filtered(wave, taps_ref, back_ref)
-    wet = wet_ref[...].reshape(TILE * TILE, LANES).astype(F32)
-    wet = jnp.concatenate([wet, wet], axis=1)
-    cot = cot_ref[...].reshape(TILE * TILE, channels).astype(F32)
-    out_refs[-1][...] = (cot + wet * spread).reshape(TILE, TILE, channels)
+    small = jnp.concatenate([sum_ref[at : at + 64, :], sum_ref[at + 64 : at + 128, :]], axis=1)
+    taps_ref[...] = small[:49]
+    gain_ref[...] = small[49:50]
+    shift_ref[...] = small[50:51]
+    conv_bias_ref[...] = small[51:52]
+    channels = small.shape[1]
+    for n in range(up_bias_ref.shape[1] // channels):
+        up_bias_ref[:, n * channels : (n + 1) * channels] = small[52 + n : 53 + n]
+
+
+def spread_kernel(
+    at, rows, before_ref, fg_ref, after_ref, north_ref, south_ref, west_ref, east_ref, nw_ref,
+    ne_ref, sw_ref, se_ref, cot_ref, wet_ref, place_ref, back_ref, taps_ref, *out_refs,
+):
+    channels = fg_ref.shape[2]
+    lat = fg_ref.shape[1]
+    slabs = []
+    for i in range(-3, TILE + 3):
+        if i < 0:
+            if at > 0:
+                slab = (before_ref, i + 8, west_ref, east_ref, TILE * at + i)
+            else:
+                slab = (north_ref, i + 3, nw_ref, ne_ref, i + 3)
+        elif i < TILE:
+            slab = (fg_ref, i, west_ref, east_ref, TILE * at + i)
+        elif at < rows - 1:
+            slab = (after_ref, i - TILE, west_ref, east_ref, TILE * at + i)
+        else:
+            slab = (south_ref, i - TILE, sw_ref, se_ref, i - TILE)
+        slabs.append(slab)
+    count = lat // TILE
+    for b in range(count):
+        mains, lefts, rights = [], [], []
+        for ref, i, first_ref, last_ref, n in slabs:
+            mains.append(ref[i, TILE * b : TILE * (b + 1), :])
+            if b:
+                lefts.append(ref[i, TILE * (b - 1) : TILE * b, :].astype(F32)[8:])
+            else:
+                lefts.append(side_group(first_ref, n, False))
+            if b < count - 1:
+                rights.append(ref[i, TILE * (b + 1) : TILE * (b + 2), :].astype(F32)[:8])
+            else:
+                rights.append(side_group(last_ref, n, True))
+        wave = dot(place_ref[...], patch(mains, lefts, rights))
+        spread = filtered(wave, taps_ref, back_ref)
+        columns = slice(TILE * b, TILE * (b + 1))
+        wet = wet_ref[:, columns, :].reshape(TILE * TILE, LANES).astype(F32)
+        wet = jnp.concatenate([wet, wet], axis=1)
+        cot = cot_ref[:, columns, :].reshape(TILE * TILE, channels).astype(F32)
+        out_refs[-1][:, columns, :] = (cot + wet * spread).reshape(TILE, TILE, channels)
 
 
 def whole(*shape):
@@ -237,25 +407,58 @@
     return jax.ShapeDtypeStruct(shape, dtype)
 
 
-def cell_pass(who, padded, cotangent, wet, taps, conv_bias, gain, shift, up, up_bias, down):
+def halo_shapes(lon, lat, channels):
+    ends, sides = shape_of((3, lat, channels), BF16), shape_of((lon // 4, 16, channels), BF16)
+    return [ends] * 2 + [sides] * 2 + [shape_of((1, 16, channels), BF16)] * 4
+
+
+def edges(x, wet):
+    lon, lat, channels = x.shape
+
+    def specs(depth):
+        return [
+            pl.BlockSpec((4, lat, depth), lambda i: (0, 0, 0)),
+            pl.BlockSpec((4, lat, depth), lambda i: (lon // 4 - 1, 0, 0)),
+            pl.BlockSpec((lon, TILE, depth), lambda i: (0, 0, 0)),
+            pl.BlockSpec((lon, TILE, depth), lambda i: (0, lat // TILE - 1, 0)),
+        ]
+
+    shapes = halo_shapes(lon, lat, channels)
+    return pl.pallas_call(
+        edge_kernel,
+        grid=(1,),
+        in_specs=specs(channels) + specs(LANES),
+        out_specs=[pl.BlockSpec(s.shape, lambda i: (0, 0, 0)) for s in shapes],
+        out_shape=shapes,
+        compiler_params=pltpu.CompilerParams(vmem_limit_bytes=40 * 2**20),
+        name="edges",
+    )(x, x, x, x, wet, wet, wet, wet)
+
+
+def cell_pass(who, x, halos, cotangent, wet, taps, conv_bias, gain, shift, up, up_bias, down):
     table = tables()
     lon, lat, channels = cotangent.shape
     units = up.shape[1]
     half = (BLOCKS // 2, BLOCK_ROWS, LANES)
+    sides = halo_shapes(lon, lat, channels)
     return pl.pallas_call(
         cell_kernel,
         grid=(lon // TILE, lat // TILE),
-        in_specs=[
-            pl.BlockSpec(memory_space=pltpu.SMEM),
-            whole(*padded.shape), tiled(channels), tiled(LANES),
+        in_specs=[pl.BlockSpec(memory_space=pltpu.SMEM), whole(*x.shape), whole(*wet.shape)]
+        + [whole(*s.shape) for s in sides]
+        + [
+            tiled(channels), tiled(LANES),
             whole(2 * HALF, 2 * HALF), whole(2 * HALF, HALF), whole(HALF, 2 * HALF),
             whole(3 * HALF, channels), whole(49, 3 * HALF),
             whole(1, channels), whole(1, channels), whole(1, channels),
             whole(channels, units), whole(1, units), whole(units, channels),
         ],
-        out_specs=[tiled(channels), whole(*half), whole(*half)],
-        out_shape=[shape_of((lon, lat, channels), BF16), shape_of(half), shape_of(half)],
-        scratch_shapes=[pltpu.VMEM((BLOCKS * BLOCK_ROWS, LANES), F32)]
+        out_specs=[tiled(channels), whole(*half), whole(*half)] + [whole(*s.shape) for s in sides],
+        out_shape=[shape_of((lon, lat, channels), BF16), shape_of(half), shape_of(half)] + sides,
+        scratch_shapes=[
+            pltpu.VMEM((lon + 6, lat + 2 * TILE, channels), BF16),
+            pltpu.VMEM((BLOCKS * BLOCK_ROWS, LANES), F32),
+        ]
         + [pltpu.VMEM((HALF, channels), F32)] * 3
         + [pltpu.VMEM((64, channels), F32)],
         compiler_params=pltpu.CompilerParams(vmem_limit_bytes=40 * 2**20),
@@ -264,69 +467,77 @@
         ),
         name="cell_pass",
     )(
-        who, padded, cotangent, wet, table["place"], table["own"], table["back"], taps,
+        who, x, wet, *halos, cotangent, wet, table["place"], table["own"], table["back"], taps,
         table["collect"], conv_bias, gain, shift, up, up_bias, down,
     )
 
 
 def finish(who, summed, scale, channels, units):
+    shapes = [(49, channels)] + [(1, channels)] * 3 + [(channels, units), (1, units), (units, channels)]
     return pl.pallas_call(
         functools.partial(finish_kernel, scale),
         in_specs=[
             pl.BlockSpec(memory_space=pltpu.SMEM),
             pl.BlockSpec(memory_space=pltpu.VMEM),
         ],
-        out_specs=[pl.BlockSpec(memory_space=pltpu.VMEM)] * 3,
-        out_shape=[shape_of((channels, units)), shape_of((units, channels)), shape_of((64, channels))],
+        out_specs=[pl.BlockSpec(memory_space=pltpu.VMEM)] * len(shapes),
+        out_shape=[shape_of(s) for s in shapes],
         scratch_shapes=[pltpu.VMEM((BLOCKS * BLOCK_ROWS, LANES), F32)],
         name="finish",
     )(who, summed)
 
 
-def spread_pass(at, padded, cotangent, wet, taps, out):
+def spread_pass(at, field_grad, halos, cotangent, wet, taps, out):
     table = tables()
     lon, lat, channels = cotangent.shape
+    rows = lon // TILE
 
     def row_of(depth):
-        return pl.BlockSpec((TILE, TILE, depth), lambda a, b: (at, b, 0))
+        return pl.BlockSpec((TILE, lat, depth), lambda a, b: (at, 0, 0))
+
+    def near(n):
+        return pl.BlockSpec((8, lat, channels), lambda a, b: (n, 0, 0))
 
     return pl.pallas_call(
-        functools.partial(spread_kernel, at),
-        grid=(1, lat // TILE),
+        functools.partial(spread_kernel, at, rows),
+        grid=(1, 1),
         in_specs=[
-            whole(*padded.shape), row_of(channels), row_of(LANES),
+            near(max(2 * at - 1, 0)), row_of(channels), near(min(2 * at + 2, 2 * rows - 1))
+        ]
+        + [whole(*h.shape) for h in halos]
+        + [
+            row_of(channels), row_of(LANES),
             whole(2 * HALF, 2 * HALF), whole(HALF, 2 * HALF), whole(3 * HALF, channels),
         ]
         + [pl.BlockSpec(memory_space=pl.ANY)] * (out is not None),
         out_specs=row_of(channels),
         out_shape=shape_of((lon, lat, channels)),
-        input_output_aliases={} if out is None else {6: 0},
+        input_output_aliases={} if out is None else {16: 0},
         compiler_params=pltpu.CompilerParams(vmem_limit_bytes=40 * 2**20),
         cost_estimate=pl.CostEstimate(
             flops=4 * 10**9, bytes_accessed=4 * 2**20, transcendentals=0
         ),
         name="spread_pass",
-    )(padded, cotangent, wet, table["place"], table["back"], taps, *([] if out is None else [out]))
-
-
-def ring(axis, step):
-    size = lax.axis_size(axis)
-    return [(i, (i + step) % size) for i in range(size)]
-
-
-def line(axis, step):
-    size = lax.axis_size(axis)
-    return [(i, i + step) for i in range(size) if 0 <= i + step < size]
-
-
-def padded_2(x):
-    before = lax.ppermute(x[-3:], "gx", ring("gx", 1))
-    after = lax.ppermute(x[:3], "gx", ring("gx", -1))
-    x = jnp.concatenate([before, x, after], axis=0)
-    before = lax.ppermute(x[:, -3:], "gy", line("gy", 1))
-    after = lax.ppermute(x[:, :3], "gy", line("gy", -1))
-    zeros = jnp.zeros((x.shape[0], 10, x.shape[2]), x.dtype)
-    return jnp.concatenate([before, x, after, zeros], axis=1)
+    )(
+        field_grad, field_grad, field_grad, *halos, cotangent, wet, table["place"], table["back"],
+        taps, *([] if out is None else [out]),
+    )
+
+
+def exchanged(packed):
+    gx, gy = lax.axis_size("gx"), lax.axis_size("gy")
+    steps = ((-1, 0), (1, 0), (0, -1), (0, 1), (-1, -1), (-1, 1), (1, -1), (1, 1))
+    opposite = (1, 0, 3, 2, 7, 6, 5, 4)
+    halos = [None] * len(steps)
+    for n, (di, dj) in enumerate(steps):
+        pairs = [
+            (i * gy + j, (i + di) % gx * gy + j + dj)
+            for i in range(gx)
+            for j in range(gy)
+            if 0 <= j + dj < gy
+        ]
+        halos[opposite[n]] = lax.ppermute(packed[n], AXES, pairs)
+    return halos
 
 
 def swapped(mesh_shape, stage, step):
@@ -379,9 +590,9 @@
     down_weight,
 ):
     lon, lat, channels = inputs.shape
-    wet = wet_mask.astype(BF16)[:, :, None]
-    padded = padded_2(inputs * wet)
-    wet_wide = jnp.broadcast_to(wet, (lon, lat, LANES))
+    units = up_weight.shape[1]
+    wet = jnp.broadcast_to(wet_mask.astype(BF16)[:, :, None], (lon, lat, LANES))
+    halos = exchanged(edges(inputs, wet))
     taps = jnp.dot(
         tables()["taps"], kernel.astype(F32), precision=lax.Precision.HIGHEST,
         preferred_element_type=F32,
@@ -391,21 +602,23 @@
     def row(x):
         return x.astype(F32)[None, :]
 
-    field_grad, keep, send = cell_pass(
-        who, padded, cotangent, wet_wide, taps[: 3 * HALF], row(conv_bias), row(norm_gain),
+    field_grad, keep, send, *packed = cell_pass(
+        who, inputs, halos, cotangent, wet, taps[: 3 * HALF], row(conv_bias), row(norm_gain),
         row(norm_shift), up_weight, row(up_bias), down_weight,
     )
     cells = lon * lat * lax.axis_size("gx") * lax.axis_size("gy")
-    scale = float(cells) ** -0.5
-    grad_pad = padded_2(field_grad)
+    halos = exchanged(packed)
     summed = summed_blocks(keep, send)
     input_grad = None
     for at in range(lon // TILE):
-        input_grad = spread_pass(at, grad_pad, cotangent, wet_wide, taps[3 * HALF :], input_grad)
-    up_sum, down_sum, small = finish(who, summed, scale, channels, up_weight.shape[1])
+        input_grad = spread_pass(
+            at, field_grad, halos, cotangent, wet, taps[3 * HALF :], input_grad
+        )
+    grads = finish(who, summed, float(cells) ** -0.5, channels, units)
+    taps_grad, bias_grad, gain_grad, shift_grad, up_grad, up_bias_grad, down_grad = grads
     return (
-        input_grad, small[:49], small[51], small[49], small[50], up_sum,
-        small[52 : 52 + up_weight.shape[1] // channels].reshape(-1), down_sum,
+        input_grad, taps_grad, bias_grad[0], gain_grad[0], shift_grad[0], up_grad,
+        up_bias_grad[0], down_grad,
     )
 
 

time: 135 us -> 159 us (1.18)
  starting transfers between devices: 48.6 us -> 76.8 us
  waiting for transfers between devices: 18.8 us -> 7.3 us
  local copies, waits for them, and re-layouts: 6.41 us -> 16.2 us
  other arithmetic: 7.78 us -> 2.98 us
  Pallas kernels: 51.5 us -> 53.4 us
    ppermute x8 -> x16, starting transfers between devices: 16.4 us -> 42.9 us  [exchanged(): halos[opposite[n]] = lax.ppermute(packed[n], AXES, pairs)]
    unnamed x44 -> x42, local copies, waits for them, and re-layouts: 2.55 us -> 12.9 us
    ppermute x8 -> x16, waiting for transfers between devices: 12.1 us -> 1.92 us  [exchanged(): halos[opposite[n]] = lax.ppermute(packed[n], AXES, pairs)]
    concatenate x2 -> x0, other arithmetic: 3.62 us -> none  [padded_2(): return jnp.concatenate([before, x, after, zeros], axis=1)]
    slice x5 -> x0, local copies, waits for them, and re-layouts: 2.97 us -> none  [the longest x1 1.44 us: local(): small[:49]]
    broadcast_in_dim x4, other arithmetic: 0.01 us -> 1.97 us  [row(): return x.astype(F32)[None, :]]
    mul x1 -> x0, other arithmetic: 1.93 us -> none  [local(): padded = padded_2(inputs * wet)]
    ppermute x17, starting transfers between devices: 32.2 us -> 34 us  [move(): return lax.ppermute(x, AXES, swapped(mesh_shape, stage, step))]
  transfers between devices with their start and end apart: 25 -> 33, of which waited for: 13 -> 7; matrix products, arithmetic and copies ran while one was open for 2% -> 5% of each run, Pallas kernels for 10% -> 8%
where the time goes in v3:
time: 159 us; the launch traced here: 158 us
  starting transfers between devices  76.8 us (48%)
  Pallas kernels  53.4 us (34%)
  local copies, waits for them, and re-layouts  16.2 us (10%)
  waiting for transfers between devices  7.3 us (5%)
  other arithmetic  2.98 us (2%)
    ppermute x16, starting transfers between devices, exchanged(): halos[opposite[n]] = lax.ppermute(packed[n], AXES, pairs)  42.9 us
    pallas_call x1, Pallas kernels, cell_pass(): pl.pallas_call(cell_kernel, grid=(lon // TILE, lat // TILE), in_specs=[pl...  37.2 us
    ppermute x17, starting transfers between devices, move(): return lax.ppermute(x, AXES, swapped(mesh_shape, stage, step))  34 us
    pallas_call x4, Pallas kernels, spread_pass(): pl.pallas_call(functools.partial(spread_kernel, at, rows), grid=(1, 1), i...  13.1 us
    unnamed x42, local copies, waits for them, and re-layouts  12.9 us
    ppermute x17, waiting for transfers between devices, move(): return lax.ppermute(x, AXES, swapped(mesh_shape, stage, step))  5.38 us
  transfers between devices with their start and end apart: 33, of which 7 were waited for; matrix products, arithmetic and copies ran while one was open for 5% of the time, Pallas kernels for 8%

profile of v3, /device:TPU:1, one launch (start us, length us, event | category | flops | bytes accessed | tf_op | source)
XLA Modules:
  0.0 158.5 jit_solution(6124412976333219767)
XLA Ops:
  0.6 0.8 convert_element_type.16
  1.4 0.6 broadcast_in_dim.26.wet_top_ref.wet_bottom_ref.wet_left_ref.wet_right_ref.wets_ref.wet_ref
  2.0 1.6 copy-done.2
  3.6 0.9 edges.1
  4.5 5.8 %collective-permute-start.4 = (bf16[1,16,256]{2,1,0:T(8,128)(2,1)}, bf16[1,16,256]{2,1,0:T(8,128)(2,1)S(1)}, u32[]{:S(2)}, u32[]{:S(2)}) collective-permute-start(bf16[1,16,256]{2,1,0:T(8,128)(2,1)} %get-tuple-element.38), channel_id=1, source_target_pairs={{0,9},{1,10},{2,11},{3,12},{4,13},{5,14},{6,15},{8,17},{9,18},{10,... | collective-permute-start | bytes 24584 | tf_op jit(solution)/shard_map/ppermute | solution.py:539
  10.4 1.3 collective-permute-start.5
  11.7 4.9 %collective-permute-start.6 = (bf16[1,16,256]{2,1,0:T(8,128)(2,1)}, bf16[1,16,256]{2,1,0:T(8,128)(2,1)}, u32[]{:S(2)}, u32[]{:S(2)}) collective-permute-start(bf16[1,16,256]{2,1,0:T(8,128)(2,1)} %get-tuple-element.40), channel_id=1, source_target_pairs={{0,121},{1,122},{2,123},{3,124},{4,125},{5,126},{6,127},{8,1},{9,2... | collective-permute-start | bytes 24584 | tf_op jit(solution)/shard_map/ppermute | solution.py:539
  16.6 3.7 %collective-permute-start.2 = (bf16[16,16,256]{2,1,0:T(8,128)(2,1)}, bf16[16,16,256]{2,1,0:T(8,128)(2,1)}, u32[]{:S(2)}, u32[]{:S(2)}) collective-permute-start(bf16[16,16,256]{2,1,0:T(8,128)(2,1)} %get-tuple-element.36), channel_id=1, source_target_pairs={{0,1},{1,2},{2,3},{3,4},{4,5},{5,6},{6,7},{8,9},{9,10},{10,11},{11... | collective-permute-start | bytes 393224 | tf_op jit(solution)/shard_map/ppermute | solution.py:539
  20.3 1.3 collective-permute-start.3
  21.6 0.8 fusion.8
  22.4 1.3 fusion.5
  23.7 1.3 collective-permute-start.7
  25.0 1.2 collective-permute-start
  26.5 0.7 broadcast_in_dim.35
  27.2 0.7 broadcast_in_dim.36
  27.8 0.7 broadcast_in_dim.37
  28.5 1.9 %collective-permute-done.7.se_ref = bf16[1,16,256]{2,1,0:T(8,128)(2,1)S(1)} collective-permute-done((bf16[1,16,256]{2,1,0:T(8,128)(2,1)}, bf16[1,16,256]{2,1,0:T(8,128)(2,1)S(1)}, u32[]{:S(2)}, u32[]{:S(2)}) %collective-permute-start.7) | collective-permute-done | bytes 8224 | tf_op jit(solution)/shard_map/ppermute | solution.py:539
  30.5 1.6 copy-done.3
  32.0 1.0 copy-done.5
  33.1 1.1 copy-done.8
  34.2 0.9 copy-done.10
  35.2 0.9 copy-done.11
  36.1 0.9 copy-done.14
  37.1 0.9 copy-done.15
  38.0 37.2 %cell_pass.1 = (bf16[64,64,256]{2,1,0:T(8,128)(2,1)S(1)}, f32[16,72,128]{2,1,0:T(8,128)S(1)}, f32[16,72,128]{2,1,0:T(8,128)S(1)}, bf16[3,64,256]{2,1,0:T(8,128)(...) custom-call(s32[2]{0:T(128)S(1)} %pad_add_fusion.who_ref, ...), custom_call_target="tpu_custom_call" | custom-call | flops 20000000000 | bytes 16777216 | tf_op jit(solution)/shard_map/cell_pass/pallas_call | solution.py:444
  75.2 3.9 %collective-permute-start.16 = (f32[16,72,128]{2,1,0:T(8,128)S(1)}, f32[16,72,128]{2,1,0:T(8,128)S(1)}, u32[]{:S(2)}, u32[]{:S(2)}) collective-permute-start(f32[16,72,128]{2,1,0:T(8,128)S(1)} %get-tuple-element.52), channel_id=1, source_target_pairs={{0,8},{1,9},{2,10},{3,11},{4,12},{5,13},{6,14},{7,15},{8,0},{9,1},... | collective-permute-start | bytes 1769480 | tf_op jit(solution)/shard_map/ppermute | solution.py:572
  79.1 2.3 %collective-permute-start.12 = (bf16[1,16,256]{2,1,0:T(8,128)(2,1)S(1)}, bf16[1,16,256]{2,1,0:T(8,128)(2,1)S(1)}, u32[]{:S(2)}, u32[]{:S(2)}) collective-permute-start(bf16[1,16,256]{2,1,0:T(8,128)(2,1)S(1)} %get-tuple-element.47), channel_id=1, source_target_pairs={{0,9},{1,10},{2,11},{3,12},{4,13},{5,14},{6,15},{8,17},{9,18},{10,... | collective-permute-start | bytes 24584 | tf_op jit(solution)/shard_map/ppermute | solution.py:539
  81.4 1.3 collective-permute-start.13
  82.7 9.0 %collective-permute-start.14 = (bf16[1,16,256]{2,1,0:T(8,128)(2,1)S(1)}, bf16[1,16,256]{2,1,0:T(8,128)(2,1)S(1)}, u32[]{:S(2)}, u32[]{:S(2)}) collective-permute-start(bf16[1,16,256]{2,1,0:T(8,128)(2,1)S(1)} %get-tuple-element.49), channel_id=1, source_target_pairs={{0,121},{1,122},{2,123},{3,124},{4,125},{5,126},{6,127},{8,1},{9,2... | collective-permute-start | bytes 24584 | tf_op jit(solution)/shard_map/ppermute | solution.py:539
  91.7 1.3 collective-permute-start.15
  93.2 3.5 %collective-permute-start.9 = (bf16[3,64,256]{2,1,0:T(8,128)(2,1)S(1)}, bf16[3,64,256]{2,1,0:T(8,128)(2,1)S(1)}, u32[]{:S(2)}, u32[]{:S(2)}) collective-permute-start(bf16[3,64,256]{2,1,0:T(8,128)(2,1)S(1)} %get-tuple-element.44), channel_id=1, source_target_pairs={{0,120},{1,121},{2,122},{3,123},{4,124},{5,125},{6,126},{7,127},{8... | collective-permute-start | bytes 294920 | tf_op jit(solution)/shard_map/ppermute | solution.py:539
  96.7 4.4 %collective-permute-start.10 = (bf16[16,16,256]{2,1,0:T(8,128)(2,1)S(1)}, bf16[16,16,256]{2,1,0:T(8,128)(2,1)S(1)}, u32[]{:S(2)}, u32[]{:S(2)}) collective-permute-start(bf16[16,16,256]{2,1,0:T(8,128)(2,1)S(1)} %get-tuple-element.45), channel_id=1, source_target_pairs={{0,1},{1,2},{2,3},{3,4},{4,5},{5,6},{6,7},{8,9},{9,10},{10,11},{11... | collective-permute-start | bytes 393224 | tf_op jit(solution)/shard_map/ppermute | solution.py:539
  101.1 1.3 collective-permute-start.11
  102.5 5.0 %collective-permute-start.17 = (bf16[4,72,128]{2,1,0:T(8,128)(2,1)S(1)}, bf16[4,72,128]{2,1,0:T(8,128)(2,1)S(1)}, u32[]{:S(2)}, u32[]{:S(2)}) collective-permute-start(bf16[4,72,128]{2,1,0:T(8,128)(2,1)S(1)} %get-tuple-element.68), channel_id=1, source_target_pairs={{0,16},{1,17},{2,18},{3,19},{4,20},{5,21},{6,22},{7,23},{8,10},{9,... | collective-permute-start | bytes 221192 | tf_op jit(solution)/shard_map/ppermute | solution.py:572
  107.5 1.3 collective-permute-start.19
  108.8 0.8 collective-permute-start.18
  109.6 3.3 %spread_pass.4.out_refs_0_ = f32[64,64,256]{2,1,0:T(8,128)} custom-call(bf16[64,64,256]{2,1,0:T(8,128)(2,1)S(1)} %get-tuple-element.42.before_ref.fg_ref.after_ref, bf16[64,64,256]{2,1,0:T(8,128)(2,1)S(1)} %get-tuple-element.42.before_ref.fg_ref.after_ref, bf16[64,64,256]{2,1,0:T(8,128)(2,1)S(1)} %get-tuple-element.42.before_ref.fg_ref.after_ref, ...), custom_call_target="tpu_custom_call" | custom-call | flops 4000000000 | bytes 4194304 | tf_op jit(solution)/shard_map/spread_pass/pallas_call | solution.py:501
  112.9 0.9 collective-permute-done.18
  113.8 0.6 collective-permute-start.20
  114.4 2.2 %collective-permute-start.22 = (bf16[1,72,128]{2,1,0:T(8,128)(2,1)S(1)}, bf16[1,72,128]{2,1,0:T(8,128)(2,1)S(1)}, u32[]{:S(2)}, u32[]{:S(2)}) collective-permute-start(bf16[1,72,128]{2,1,0:T(8,128)(2,1)S(1)} %get-tuple-element.78), channel_id=1, source_target_pairs={{0,6},{1,7},{2,4},{3,5},{4,2},{5,3},{6,0},{7,1},{8,73},{9,72},{10,... | collective-permute-start | bytes 55304 | tf_op jit(solution)/shard_map/ppermute | solution.py:572
  116.6 0.5 collective-permute-start.21
  117.2 3.3 %spread_pass.5.out_refs_0_ = f32[64,64,256]{2,1,0:T(8,128)} custom-call(bf16[64,64,256]{2,1,0:T(8,128)(2,1)S(1)} %get-tuple-element.42.before_ref.fg_ref.after_ref, bf16[64,64,256]{2,1,0:T(8,128)(2,1)S(1)} %get-tuple-element.42.before_ref.fg_ref.after_ref, ...), custom_call_target="tpu_custom_call", output_to_operand_aliasing={{}: (16, {})} | custom-call | flops 4000000000 | bytes 4194304 | tf_op jit(solution)/shard_map/spread_pass/pallas_call | solution.py:501
  120.8 3.9 %collective-permute-start.25 = (f32[1,72,128]{2,1,0:T(8,128)S(1)}, f32[1,72,128]{2,1,0:T(8,128)S(1)}, u32[]{:S(2)}, u32[]{:S(2)}) collective-permute-start(f32[1,72,128]{2,1,0:T(8,128)S(1)} %fusion.1), channel_id=1, source_target_pairs={{0,65},{1,64},{2,67},{3,66},{4,69},{5,68},{6,71},{7,70},{8,56},{9,... | collective-permute-start | bytes 110600 | tf_op jit(solution)/shard_map/ppermute | solution.py:572
  124.7 0.7 collective-permute-start.23
  125.3 3.3 %spread_pass.6.out_refs_0_ = f32[64,64,256]{2,1,0:T(8,128)} custom-call(bf16[64,64,256]{2,1,0:T(8,128)(2,1)S(1)} %get-tuple-element.42.before_ref.fg_ref.after_ref, bf16[64,64,256]{2,1,0:T(8,128)(2,1)S(1)} %get-tuple-element.42.before_ref.fg_ref.after_ref, ...), custom_call_target="tpu_custom_call", output_to_operand_aliasing={{}: (16, {})} | custom-call | flops 4000000000 | bytes 4194304 | tf_op jit(solution)/shard_map/spread_pass/pallas_call | solution.py:501
  128.6 0.4 collective-permute-done.24
  129.0 2.1 %collective-permute-start.28 = (bf16[1,72,128]{2,1,0:T(8,128)(2,1)S(1)}, bf16[1,72,128]{2,1,0:T(8,128)(2,1)S(1)}, u32[]{:S(2)}, u32[]{:S(2)}) collective-permute-start(bf16[1,72,128]{2,1,0:T(8,128)(2,1)S(1)} %get-tuple-element.61), channel_id=1, source_target_pairs={{0,6},{1,7},{2,4},{3,5},{4,2},{5,3},{6,0},{7,1},{8,73},{9,72},{10,... | collective-permute-start | bytes 55304 | tf_op jit(solution)/shard_map/ppermute | solution.py:572
  131.4 1.0 collective-permute-start.26
  132.3 0.6 constant_dynamic-update-slice_fusion.14
  133.2 2.3 %collective-permute-done.27 = bf16[1,72,128]{2,1,0:T(8,128)(2,1)S(1)} collective-permute-done((bf16[1,72,128]{2,1,0:T(8,128)(2,1)S(1)}, bf16[1,72,128]{2,1,0:T(8,128)(2,1)S(1)}, u32[]{:S(2)}, u32[]{:S(2)}) %collective-permute-start.27) | collective-permute-done | bytes 18464 | tf_op jit(solution)/shard_map/ppermute | solution.py:572
  135.5 1.6 %collective-permute-start.31 = (bf16[4,72,128]{2,1,0:T(8,128)(2,1)S(1)}, bf16[4,72,128]{2,1,0:T(8,128)(2,1)S(1)}, u32[]{:S(2)}, u32[]{:S(2)}) collective-permute-start(bf16[4,72,128]{2,1,0:T(8,128)(2,1)S(1)} %pad_maximum_fusion), channel_id=1, source_target_pairs={{0,48},{1,49},{2,50},{3,51},{4,52},{5,53},{6,54},{7,55},{8,14},{9,... | collective-permute-start | bytes 221192 | tf_op jit(solution)/shard_map/ppermute | solution.py:572
  137.1 1.0 collective-permute-start.30
  138.1 0.7 collective-permute-start.29
  138.8 0.6 constant_dynamic-update-slice_fusion.5
  139.4 0.6 constant_dynamic-update-slice_fusion.4
  140.0 0.6 constant_dynamic-update-slice_fusion.3
  140.6 1.3 collective-permute-done.29
  141.9 0.7 constant_dynamic-update-slice_fusion.2
  142.6 0.7 constant_dynamic-update-slice_fusion.1
  143.2 0.6 constant_dynamic-update-slice_fusion
  143.9 8.4 %collective-permute-start.32 = (bf16[16,72,128]{2,1,0:T(8,128)(2,1)S(1)}, bf16[16,72,128]{2,1,0:T(8,128)(2,1)S(1)}, u32[]{:S(2)}, u32[]{:S(2)}) collective-permute-start(bf16[16,72,128]{2,1,0:T(8,128)(2,1)S(1)} %get-tuple-element.71), channel_id=1, source_target_pairs={{0,8},{1,9},{2,10},{3,11},{4,12},{5,13},{6,14},{7,15},{8,0},{9,1},... | collective-permute-start | bytes 884744 | tf_op jit(solution)/shard_map/ppermute | solution.py:572
  152.2 3.3 %spread_pass.7 = f32[64,64,256]{2,1,0:T(8,128)} custom-call(bf16[64,64,256]{2,1,0:T(8,128)(2,1)S(1)} %get-tuple-element.42.before_ref.fg_ref.after_ref, bf16[64,64,256]{2,1,0:T(8,128)(2,1)S(1)} %get-tuple-element.42.before_ref.fg_ref.after_ref, ...), custom_call_target="tpu_custom_call", output_to_operand_aliasing={{}: (16, {})} | custom-call | flops 4000000000 | bytes 4194304 | tf_op jit(solution)/shard_map/spread_pass/pallas_call | solution.py:501
  155.5 0.7 constant_dynamic-update-slice_fusion.7.in_ref
  156.2 2.2 %finish.1 = (f32[49,256]{1,0:T(8,128)}, f32[1,256]{1,0:T(1,128)}, f32[1,256]{1,0:T(1,128)}, f32[1,256]{1,0:T(1,128)}, f32[256,512]{1,0:T(8,128)}, /*index=5*/f32[1,512]{1,0:T(1,128)}, f32[512,256]{1,0:T(8,128)}) custom-call(s32[2]{0:T(128)} %copy-done.9, bf16[32,72,128]{2,1,0:T(8,128)(2,1)} %constant_dynamic-update-slice_fusion.7.in_ref), custom_call_target="tpu_custom_call" | custom-call | tf_op jit(solution)/shard_map/finish/pallas_call | solution.py:477
  (69 shorter events, 1.4 us)
Async XLA Ops:
  0.6 20.9 %copy-start = (bf16[49,256]{1,0:T(8,128)(2,1)S(1)}, bf16[49,256]{1,0:T(8,128)(2,1)}, u32[]{:S(2)}) copy-start(bf16[49,256]{1,0:T(8,128)(2,1)} %param.18) | copy-start | bytes 75268
  2.0 1.6 %copy-start.2 = (bf16[64,64,256]{2,1,0:T(8,128)(2,1)S(1)}, bf16[64,64,256]{2,1,0:T(8,128)(2,1)}, u32[]{:S(2)}) copy-start(bf16[64,64,256]{2,1,0:T(8,128)(2,1)} %x_ref.1) | copy-start | bytes 6291460
  3.6 18.0 %copy-start.16 = (f32[1536,49]{1,0:T(8,128)S(1)}, f32[1536,49]{1,0:T(8,128)}, u32[]{:S(2)}) copy-start(f32[1536,49]{1,0:T(8,128)} %constant.77.clone) | copy-start | bytes 903172
  4.5 19.1 %copy-start.12 = (bf16[3,64,256]{2,1,0:T(8,128)(2,1)}, bf16[3,64,256]{2,1,0:T(8,128)(2,1)S(1)}, u32[]{:S(2)}) copy-start(bf16[3,64,256]{2,1,0:T(8,128)(2,1)S(1)} %get-tuple-element.34) | copy-start | bytes 294916
  4.5 19.1 %copy-start.13 = (bf16[1,16,256]{2,1,0:T(8,128)(2,1)}, bf16[1,16,256]{2,1,0:T(8,128)(2,1)S(1)}, u32[]{:S(2)}) copy-start(bf16[1,16,256]{2,1,0:T(8,128)(2,1)S(1)} %get-tuple-element.41) | copy-start | bytes 24580
  4.5 19.1 %collective-permute-start.4 = (bf16[1,16,256]{2,1,0:T(8,128)(2,1)}, bf16[1,16,256]{2,1,0:T(8,128)(2,1)S(1)}, u32[]{:S(2)}, u32[]{:S(2)}) collective-permute-start(bf16[1,16,256]{2,1,0:T(8,128)(2,1)} %get-tuple-element.38), channel_id=1, source_target_pairs={{0,9},{1,10},{2,11},{3,12},{4,13},{5,14},{6,15},{8,17},{9,18},{10,... | collective-permute-start | bytes 24584 | tf_op jit(solution)/shard_map/ppermute | solution.py:539
  10.4 14.6 %collective-permute-start.5 = (bf16[1,16,256]{2,1,0:T(8,128)(2,1)}, bf16[1,16,256]{2,1,0:T(8,128)(2,1)S(1)}, u32[]{:S(2)}, u32[]{:S(2)}) collective-permute-start(bf16[1,16,256]{2,1,0:T(8,128)(2,1)} %get-tuple-element.39), channel_id=1, source_target_pairs={{1,8},{2,9},{3,10},{4,11},{5,12},{6,13},{7,14},{9,16},{10,17},{11,... | collective-permute-start | bytes 24584 | tf_op jit(solution)/shard_map/ppermute | solution.py:539
  11.7 14.5 %collective-permute-start.6 = (bf16[1,16,256]{2,1,0:T(8,128)(2,1)}, bf16[1,16,256]{2,1,0:T(8,128)(2,1)}, u32[]{:S(2)}, u32[]{:S(2)}) collective-permute-start(bf16[1,16,256]{2,1,0:T(8,128)(2,1)} %get-tuple-element.40), channel_id=1, source_target_pairs={{0,121},{1,122},{2,123},{3,124},{4,125},{5,126},{6,127},{8,1},{9,2... | collective-permute-start | bytes 24584 | tf_op jit(solution)/shard_map/ppermute | solution.py:539
  16.6 13.8 %collective-permute-start.2 = (bf16[16,16,256]{2,1,0:T(8,128)(2,1)}, bf16[16,16,256]{2,1,0:T(8,128)(2,1)}, u32[]{:S(2)}, u32[]{:S(2)}) collective-permute-start(bf16[16,16,256]{2,1,0:T(8,128)(2,1)} %get-tuple-element.36), channel_id=1, source_target_pairs={{0,1},{1,2},{2,3},{3,4},{4,5},{5,6},{6,7},{8,9},{9,10},{10,11},{11... | collective-permute-start | bytes 393224 | tf_op jit(solution)/shard_map/ppermute | solution.py:539
  20.3 10.1 %collective-permute-start.3 = (bf16[16,16,256]{2,1,0:T(8,128)(2,1)}, bf16[16,16,256]{2,1,0:T(8,128)(2,1)}, u32[]{:S(2)}, u32[]{:S(2)}) collective-permute-start(bf16[16,16,256]{2,1,0:T(8,128)(2,1)} %get-tuple-element.37), channel_id=1, source_target_pairs={{1,0},{2,1},{3,2},{4,3},{5,4},{6,5},{7,6},{9,8},{10,9},{11,10},{12... | collective-permute-start | bytes 393224 | tf_op jit(solution)/shard_map/ppermute | solution.py:539
  22.4 6.1 %copy-start.17 = (bf16[512]{0:T(512)(128)(2,1)S(1)}, bf16[512]{0:T(512)(128)(2,1)}, u32[]{:S(2)}) copy-start(bf16[512]{0:T(512)(128)(2,1)} %param.23) | copy-start | bytes 3076
  22.4 8.0 %copy-start.1 = (bf16[64,64,256]{2,1,0:T(8,128)(2,1)S(1)}, bf16[64,64,256]{2,1,0:T(8,128)(2,1)}, u32[]{:S(2)}) copy-start(bf16[64,64,256]{2,1,0:T(8,128)(2,1)} %cot_ref.9) | copy-start | bytes 6291460
  22.4 8.0 %copy-start.7 = (bf16[256,512]{1,0:T(8,128)(2,1)S(1)}, bf16[256,512]{1,0:T(8,128)(2,1)}, u32[]{:S(2)}) copy-start(bf16[256,512]{1,0:T(8,128)(2,1)} %constant.80.clone.back_ref) | copy-start | bytes 786436
  23.7 6.7 %collective-permute-start.7 = (bf16[1,16,256]{2,1,0:T(8,128)(2,1)}, bf16[1,16,256]{2,1,0:T(8,128)(2,1)S(1)}, u32[]{:S(2)}, u32[]{:S(2)}) collective-permute-start(bf16[1,16,256]{2,1,0:T(8,128)(2,1)} %copy-done.13), channel_id=1, source_target_pairs={{1,120},{2,121},{3,122},{4,123},{5,124},{6,125},{7,126},{9,0},{10,... | collective-permute-start | bytes 24584 | tf_op jit(solution)/shard_map/ppermute | solution.py:539
  25.0 5.4 %collective-permute-start = (bf16[3,64,256]{2,1,0:T(8,128)(2,1)}, bf16[3,64,256]{2,1,0:T(8,128)(2,1)S(1)}, u32[]{:S(2)}, u32[]{:S(2)}) collective-permute-start(bf16[3,64,256]{2,1,0:T(8,128)(2,1)} %copy-done.12), channel_id=1, source_target_pairs={{0,8},{1,9},{2,10},{3,11},{4,12},{5,13},{6,14},{7,15},{8,16},{9,17... | collective-permute-start | bytes 294920 | tf_op jit(solution)/shard_map/ppermute | solution.py:539
  26.2 4.2 %collective-permute-start.1 = (bf16[3,64,256]{2,1,0:T(8,128)(2,1)S(1)}, bf16[3,64,256]{2,1,0:T(8,128)(2,1)S(1)}, u32[]{:S(2)}, u32[]{:S(2)}) collective-permute-start(bf16[3,64,256]{2,1,0:T(8,128)(2,1)S(1)} %get-tuple-element.35), channel_id=1, source_target_pairs={{0,120},{1,121},{2,122},{3,123},{4,124},{5,125},{6,126},{7,127},{8... | collective-permute-start | bytes 294920 | tf_op jit(solution)/shard_map/ppermute | solution.py:539
  26.5 48.7 %copy-start.9 = (s32[2]{0:T(128)}, s32[2]{0:T(128)S(1)}, u32[]{:S(2)}) copy-start(s32[2]{0:T(128)S(1)} %pad_add_fusion.who_ref) | copy-start | bytes 28
  30.4 1.6 %copy-start.3 = (bf16[64,64,256]{2,1,0:T(8,128)(2,1)S(1)}, bf16[64,64,256]{2,1,0:T(8,128)(2,1)}, u32[]{:S(2)}) copy-start(bf16[64,64,256]{2,1,0:T(8,128)(2,1)} %x_ref.1) | copy-start | bytes 6291460
  32.0 1.0 copy-start.5
  33.1 1.1 copy-start.8
  34.2 0.9 copy-start.10
  35.2 0.9 copy-start.11
  36.1 0.9 copy-start.14
  37.1 0.9 copy-start.15
  75.2 34.4 %copy-start.4 = (f32[768,256]{1,0:T(8,128)S(1)}, f32[768,256]{1,0:T(8,128)}, u32[]{:S(2)}) copy-start(f32[768,256]{1,0:T(8,128)} %get-tuple-element.66.taps_ref) | copy-start | bytes 2359300
  75.2 34.4 %copy-start.6 = (bf16[512,512]{1,0:T(8,128)(2,1)S(1)}, bf16[512,512]{1,0:T(8,128)(2,1)}, u32[]{:S(2)}) copy-start(bf16[512,512]{1,0:T(8,128)(2,1)} %constant.78.clone.place_ref) | copy-start | bytes 1572868
  75.2 17.8 %collective-permute-start.16 = (f32[16,72,128]{2,1,0:T(8,128)S(1)}, f32[16,72,128]{2,1,0:T(8,128)S(1)}, u32[]{:S(2)}, u32[]{:S(2)}) collective-permute-start(f32[16,72,128]{2,1,0:T(8,128)S(1)} %get-tuple-element.52), channel_id=1, source_target_pairs={{0,8},{1,9},{2,10},{3,11},{4,12},{5,13},{6,14},{7,15},{8,0},{9,1},... | collective-permute-start | bytes 1769480 | tf_op jit(solution)/shard_map/ppermute | solution.py:572
  79.1 14.1 %collective-permute-start.12 = (bf16[1,16,256]{2,1,0:T(8,128)(2,1)S(1)}, bf16[1,16,256]{2,1,0:T(8,128)(2,1)S(1)}, u32[]{:S(2)}, u32[]{:S(2)}) collective-permute-start(bf16[1,16,256]{2,1,0:T(8,128)(2,1)S(1)} %get-tuple-element.47), channel_id=1, source_target_pairs={{0,9},{1,10},{2,11},{3,12},{4,13},{5,14},{6,15},{8,17},{9,18},{10,... | collective-permute-start | bytes 24584 | tf_op jit(solution)/shard_map/ppermute | solution.py:539
  81.4 15.4 %collective-permute-start.13 = (bf16[1,16,256]{2,1,0:T(8,128)(2,1)S(1)}, bf16[1,16,256]{2,1,0:T(8,128)(2,1)S(1)}, u32[]{:S(2)}, u32[]{:S(2)}) collective-permute-start(bf16[1,16,256]{2,1,0:T(8,128)(2,1)S(1)} %get-tuple-element.48), channel_id=1, source_target_pairs={{1,8},{2,9},{3,10},{4,11},{5,12},{6,13},{7,14},{9,16},{10,17},{11,... | collective-permute-start | bytes 24584 | tf_op jit(solution)/shard_map/ppermute | solution.py:539
  82.7 18.4 %collective-permute-start.14 = (bf16[1,16,256]{2,1,0:T(8,128)(2,1)S(1)}, bf16[1,16,256]{2,1,0:T(8,128)(2,1)S(1)}, u32[]{:S(2)}, u32[]{:S(2)}) collective-permute-start(bf16[1,16,256]{2,1,0:T(8,128)(2,1)S(1)} %get-tuple-element.49), channel_id=1, source_target_pairs={{0,121},{1,122},{2,123},{3,124},{4,125},{5,126},{6,127},{8,1},{9,2... | collective-permute-start | bytes 24584 | tf_op jit(solution)/shard_map/ppermute | solution.py:539
  91.7 10.8 %collective-permute-start.15 = (bf16[1,16,256]{2,1,0:T(8,128)(2,1)S(1)}, bf16[1,16,256]{2,1,0:T(8,128)(2,1)S(1)}, u32[]{:S(2)}, u32[]{:S(2)}) collective-permute-start(bf16[1,16,256]{2,1,0:T(8,128)(2,1)S(1)} %get-tuple-element.50), channel_id=1, source_target_pairs={{1,120},{2,121},{3,122},{4,123},{5,124},{6,125},{7,126},{9,0},{10,... | collective-permute-start | bytes 24584 | tf_op jit(solution)/shard_map/ppermute | solution.py:539
  93.0 14.5 %collective-permute-start.8 = (bf16[3,64,256]{2,1,0:T(8,128)(2,1)S(1)}, bf16[3,64,256]{2,1,0:T(8,128)(2,1)S(1)}, u32[]{:S(2)}, u32[]{:S(2)}) collective-permute-start(bf16[3,64,256]{2,1,0:T(8,128)(2,1)S(1)} %get-tuple-element.43), channel_id=1, source_target_pairs={{0,8},{1,9},{2,10},{3,11},{4,12},{5,13},{6,14},{7,15},{8,16},{9,17... | collective-permute-start | bytes 294920 | tf_op jit(solution)/shard_map/ppermute | solution.py:539
  93.2 15.6 %collective-permute-start.9 = (bf16[3,64,256]{2,1,0:T(8,128)(2,1)S(1)}, bf16[3,64,256]{2,1,0:T(8,128)(2,1)S(1)}, u32[]{:S(2)}, u32[]{:S(2)}) collective-permute-start(bf16[3,64,256]{2,1,0:T(8,128)(2,1)S(1)} %get-tuple-element.44), channel_id=1, source_target_pairs={{0,120},{1,121},{2,122},{3,123},{4,124},{5,125},{6,126},{7,127},{8... | collective-permute-start | bytes 294920 | tf_op jit(solution)/shard_map/ppermute | solution.py:539
  96.7 12.8 %collective-permute-start.10 = (bf16[16,16,256]{2,1,0:T(8,128)(2,1)S(1)}, bf16[16,16,256]{2,1,0:T(8,128)(2,1)S(1)}, u32[]{:S(2)}, u32[]{:S(2)}) collective-permute-start(bf16[16,16,256]{2,1,0:T(8,128)(2,1)S(1)} %get-tuple-element.45), channel_id=1, source_target_pairs={{0,1},{1,2},{2,3},{3,4},{4,5},{5,6},{6,7},{8,9},{9,10},{10,11},{11... | collective-permute-start | bytes 393224 | tf_op jit(solution)/shard_map/ppermute | solution.py:539
  101.1 8.5 %collective-permute-start.11 = (bf16[16,16,256]{2,1,0:T(8,128)(2,1)S(1)}, bf16[16,16,256]{2,1,0:T(8,128)(2,1)S(1)}, u32[]{:S(2)}, u32[]{:S(2)}) collective-permute-start(bf16[16,16,256]{2,1,0:T(8,128)(2,1)S(1)} %get-tuple-element.46), channel_id=1, source_target_pairs={{1,0},{2,1},{3,2},{4,3},{5,4},{6,5},{7,6},{9,8},{10,9},{11,10},{12... | collective-permute-start | bytes 393224 | tf_op jit(solution)/shard_map/ppermute | solution.py:539
  102.5 10.4 %collective-permute-start.17 = (bf16[4,72,128]{2,1,0:T(8,128)(2,1)S(1)}, bf16[4,72,128]{2,1,0:T(8,128)(2,1)S(1)}, u32[]{:S(2)}, u32[]{:S(2)}) collective-permute-start(bf16[4,72,128]{2,1,0:T(8,128)(2,1)S(1)} %get-tuple-element.68), channel_id=1, source_target_pairs={{0,16},{1,17},{2,18},{3,19},{4,20},{5,21},{6,22},{7,23},{8,10},{9,... | collective-permute-start | bytes 221192 | tf_op jit(solution)/shard_map/ppermute | solution.py:572
  107.5 5.4 %collective-permute-start.19 = (bf16[4,72,128]{2,1,0:T(8,128)(2,1)S(1)}, bf16[4,72,128]{2,1,0:T(8,128)(2,1)S(1)}, u32[]{:S(2)}, u32[]{:S(2)}) collective-permute-start(bf16[4,72,128]{2,1,0:T(8,128)(2,1)S(1)} %get-tuple-element.69), channel_id=1, source_target_pairs={{0,48},{1,49},{2,50},{3,51},{4,52},{5,53},{6,54},{7,55},{8,14},{9,... | collective-permute-start | bytes 221192 | tf_op jit(solution)/shard_map/ppermute | solution.py:572
  108.8 5.0 %collective-permute-start.18 = (bf16[4,72,128]{2,1,0:T(8,128)(2,1)S(1)}, bf16[4,72,128]{2,1,0:T(8,128)(2,1)S(1)}, u32[]{:S(2)}, u32[]{:S(2)}) collective-permute-start(bf16[4,72,128]{2,1,0:T(8,128)(2,1)S(1)} %get-tuple-element.70), channel_id=1, source_target_pairs={{0,32},{1,33},{2,34},{3,35},{4,36},{5,37},{6,38},{7,39},{8,12},{9,... | collective-permute-start | bytes 221192 | tf_op jit(solution)/shard_map/ppermute | solution.py:572
  113.8 6.6 %collective-permute-start.20 = (bf16[1,72,128]{2,1,0:T(8,128)(2,1)S(1)}, bf16[1,72,128]{2,1,0:T(8,128)(2,1)S(1)}, u32[]{:S(2)}, u32[]{:S(2)}) collective-permute-start(bf16[1,72,128]{2,1,0:T(8,128)(2,1)S(1)} %get-tuple-element.77), channel_id=1, source_target_pairs={{0,2},{1,3},{2,0},{3,1},{4,6},{5,7},{6,4},{7,5},{8,9},{9,8},{10,11... | collective-permute-start | bytes 55304 | tf_op jit(solution)/shard_map/ppermute | solution.py:572
  114.4 6.0 %collective-permute-start.22 = (bf16[1,72,128]{2,1,0:T(8,128)(2,1)S(1)}, bf16[1,72,128]{2,1,0:T(8,128)(2,1)S(1)}, u32[]{:S(2)}, u32[]{:S(2)}) collective-permute-start(bf16[1,72,128]{2,1,0:T(8,128)(2,1)S(1)} %get-tuple-element.78), channel_id=1, source_target_pairs={{0,6},{1,7},{2,4},{3,5},{4,2},{5,3},{6,0},{7,1},{8,73},{9,72},{10,... | collective-permute-start | bytes 55304 | tf_op jit(solution)/shard_map/ppermute | solution.py:572
  116.6 4.1 %collective-permute-start.21 = (bf16[1,72,128]{2,1,0:T(8,128)(2,1)S(1)}, bf16[1,72,128]{2,1,0:T(8,128)(2,1)S(1)}, u32[]{:S(2)}, u32[]{:S(2)}) collective-permute-start(bf16[1,72,128]{2,1,0:T(8,128)(2,1)S(1)} %get-tuple-element.79), channel_id=1, source_target_pairs={{0,4},{1,5},{2,6},{3,7},{4,0},{5,1},{6,2},{7,3},{8,72},{9,73},{10,... | collective-permute-start | bytes 55304 | tf_op jit(solution)/shard_map/ppermute | solution.py:572
  120.8 7.9 %collective-permute-start.25 = (f32[1,72,128]{2,1,0:T(8,128)S(1)}, f32[1,72,128]{2,1,0:T(8,128)S(1)}, u32[]{:S(2)}, u32[]{:S(2)}) collective-permute-start(f32[1,72,128]{2,1,0:T(8,128)S(1)} %fusion.1), channel_id=1, source_target_pairs={{0,65},{1,64},{2,67},{3,66},{4,69},{5,68},{6,71},{7,70},{8,56},{9,... | collective-permute-start | bytes 110600 | tf_op jit(solution)/shard_map/ppermute | solution.py:572
  124.7 4.3 %collective-permute-start.24 = (f32[1,72,128]{2,1,0:T(8,128)S(1)}, f32[1,72,128]{2,1,0:T(8,128)S(1)}, u32[]{:S(2)}, u32[]{:S(2)}) collective-permute-start(f32[1,72,128]{2,1,0:T(8,128)S(1)} %fusion.1), channel_id=1, source_target_pairs={{0,64},{1,65},{2,66},{3,67},{4,68},{5,69},{6,70},{7,71},{8,40},{9,... | collective-permute-start | bytes 110600 | tf_op jit(solution)/shard_map/ppermute | solution.py:572
  124.7 4.3 %collective-permute-start.23 = (f32[1,72,128]{2,1,0:T(8,128)S(1)}, f32[1,72,128]{2,1,0:T(8,128)S(1)}, u32[]{:S(2)}, u32[]{:S(2)}) collective-permute-start(f32[1,72,128]{2,1,0:T(8,128)S(1)} %fusion.1), channel_id=1, source_target_pairs={{0,1},{1,0},{2,3},{3,2},{4,5},{5,4},{6,7},{7,6},{8,24},{9,25},{10,... | collective-permute-start | bytes 110600 | tf_op jit(solution)/shard_map/ppermute | solution.py:572
  129.0 4.2 %collective-permute-start.28 = (bf16[1,72,128]{2,1,0:T(8,128)(2,1)S(1)}, bf16[1,72,128]{2,1,0:T(8,128)(2,1)S(1)}, u32[]{:S(2)}, u32[]{:S(2)}) collective-permute-start(bf16[1,72,128]{2,1,0:T(8,128)(2,1)S(1)} %get-tuple-element.61), channel_id=1, source_target_pairs={{0,6},{1,7},{2,4},{3,5},{4,2},{5,3},{6,0},{7,1},{8,73},{9,72},{10,... | collective-permute-start | bytes 55304 | tf_op jit(solution)/shard_map/ppermute | solution.py:572
  131.2 4.3 %collective-permute-start.27 = (bf16[1,72,128]{2,1,0:T(8,128)(2,1)S(1)}, bf16[1,72,128]{2,1,0:T(8,128)(2,1)S(1)}, u32[]{:S(2)}, u32[]{:S(2)}) collective-permute-start(bf16[1,72,128]{2,1,0:T(8,128)(2,1)S(1)} %get-tuple-element.61), channel_id=1, source_target_pairs={{0,4},{1,5},{2,6},{3,7},{4,0},{5,1},{6,2},{7,3},{8,72},{9,73},{10,... | collective-permute-start | bytes 55304 | tf_op jit(solution)/shard_map/ppermute | solution.py:572
  131.4 4.1 %collective-permute-start.26 = (bf16[1,72,128]{2,1,0:T(8,128)(2,1)S(1)}, bf16[1,72,128]{2,1,0:T(8,128)(2,1)S(1)}, u32[]{:S(2)}, u32[]{:S(2)}) collective-permute-start(bf16[1,72,128]{2,1,0:T(8,128)(2,1)S(1)} %get-tuple-element.61), channel_id=1, source_target_pairs={{0,2},{1,3},{2,0},{3,1},{4,6},{5,7},{6,4},{7,5},{8,9},{9,8},{10,11... | collective-permute-start | bytes 55304 | tf_op jit(solution)/shard_map/ppermute | solution.py:572
  135.5 7.7 %collective-permute-start.31 = (bf16[4,72,128]{2,1,0:T(8,128)(2,1)S(1)}, bf16[4,72,128]{2,1,0:T(8,128)(2,1)S(1)}, u32[]{:S(2)}, u32[]{:S(2)}) collective-permute-start(bf16[4,72,128]{2,1,0:T(8,128)(2,1)S(1)} %pad_maximum_fusion), channel_id=1, source_target_pairs={{0,48},{1,49},{2,50},{3,51},{4,52},{5,53},{6,54},{7,55},{8,14},{9,... | collective-permute-start | bytes 221192 | tf_op jit(solution)/shard_map/ppermute | solution.py:572
  137.1 5.5 %collective-permute-start.30 = (bf16[4,72,128]{2,1,0:T(8,128)(2,1)S(1)}, bf16[4,72,128]{2,1,0:T(8,128)(2,1)S(1)}, u32[]{:S(2)}, u32[]{:S(2)}) collective-permute-start(bf16[4,72,128]{2,1,0:T(8,128)(2,1)S(1)} %pad_maximum_fusion), channel_id=1, source_target_pairs={{0,32},{1,33},{2,34},{3,35},{4,36},{5,37},{6,38},{7,39},{8,12},{9,... | collective-permute-start | bytes 221192 | tf_op jit(solution)/shard_map/ppermute | solution.py:572
  138.1 3.8 %collective-permute-start.29 = (bf16[4,72,128]{2,1,0:T(8,128)(2,1)S(1)}, bf16[4,72,128]{2,1,0:T(8,128)(2,1)S(1)}, u32[]{:S(2)}, u32[]{:S(2)}) collective-permute-start(bf16[4,72,128]{2,1,0:T(8,128)(2,1)S(1)} %pad_maximum_fusion), channel_id=1, source_target_pairs={{0,16},{1,17},{2,18},{3,19},{4,20},{5,21},{6,22},{7,23},{8,10},{9,... | collective-permute-start | bytes 221192 | tf_op jit(solution)/shard_map/ppermute | solution.py:572
  143.9 11.7 %collective-permute-start.32 = (bf16[16,72,128]{2,1,0:T(8,128)(2,1)S(1)}, bf16[16,72,128]{2,1,0:T(8,128)(2,1)S(1)}, u32[]{:S(2)}, u32[]{:S(2)}) collective-permute-start(bf16[16,72,128]{2,1,0:T(8,128)(2,1)S(1)} %get-tuple-element.71), channel_id=1, source_target_pairs={{0,8},{1,9},{2,10},{3,11},{4,12},{5,13},{6,14},{7,15},{8,0},{9,1},... | collective-permute-start | bytes 884744 | tf_op jit(solution)/shard_map/ppermute | solution.py:572

commit v4 on v2

v4 whole, which is shorter than its diff:
```python
import functools

import jax
import jax.numpy as jnp
import numpy as np
from jax import lax
from jax.experimental import pallas as pl
from jax.experimental.pallas import tpu as pltpu
from jax.sharding import PartitionSpec as P

F32 = jnp.float32
BF16 = jnp.bfloat16
TILE = 16
SPAN = TILE + 6
HALF = 256
AXES = ("gx", "gy")
MOVES = ((3, ((3, 0), (4, 1))), (6, ((3, 5), (4, 6))), (1, ((3, 2),)), (5, ((4, 7),)))
BLOCKS = 8
LANES = 128
CELLS = TILE * TILE


def basis():
    pairs, alone, seen = [], [], set()
    for a in range(SPAN):
        for b in range(SPAN):
            other = ((-a) % SPAN, (-b) % SPAN)
            if other == (a, b):
                alone.append((a, b))
            elif other not in seen:
                seen.add((a, b))
                pairs.append((a, b))
    i, j = np.meshgrid(np.arange(SPAN), np.arange(SPAN), indexing="ij")

    def angle(f):
        return 2 * np.pi * ((f[0] * i + f[1] * j) % SPAN) / SPAN

    cos = np.zeros((HALF, SPAN, SPAN))
    sin = np.zeros((HALF, SPAN, SPAN))
    weight = np.zeros(HALF)
    paired = np.zeros(HALF)
    for n, (one, two) in enumerate(((alone[0], alone[1]), (alone[2], alone[3]))):
        cos[n], sin[n], weight[n] = np.cos(angle(one)), np.cos(angle(two)), 1
    for n, f in enumerate(pairs, start=2):
        cos[n], sin[n], weight[n], paired[n] = np.cos(angle(f)), -np.sin(angle(f)), 2, 1
    return cos, sin, weight / SPAN**2, paired


@functools.cache
def tables():
    cos, sin, weight, paired = basis()
    both = np.concatenate([cos, sin])
    place = np.zeros((2 * HALF, 2 * HALF))
    for i in range(SPAN):
        place[:, TILE * i : TILE * (i + 1)] = both[:, i, 3:19]
    for i in range(20):
        at = TILE * SPAN + 8 * i
        place[:, at : at + 3] = both[:, i, 19:]
        place[:, at + 5 : at + 8] = both[:, i, :3]
        if i < 8:
            for to, of in MOVES[i % 4][1]:
                place[:, at + to] = both[:, 20 + i // 4, (of + 19) % 24]
    own = both[:, :TILE, :TILE].reshape(2 * HALF, TILE * TILE)
    back = own.T
    ct = (cos * weight[:, None, None])[:, :7, :7].reshape(HALF, 49)
    st = (sin * weight[:, None, None])[:, :7, :7].reshape(HALF, 49)
    pair = paired[:, None]
    taps = np.concatenate([ct, st * pair, ct * pair + st * (1 - pair)])
    flipped = taps[:, ::-1]
    collect = np.concatenate([ct, ct * pair + st * (1 - pair), st * pair]).T
    return dict(
        place=place.astype(jnp.bfloat16),
        own=own.astype(jnp.bfloat16),
        back=back.astype(jnp.bfloat16),
        taps=np.concatenate([taps, flipped]).astype(np.float32),
        collect=collect.astype(np.float32),
    )


def dot(a, b):
    return jnp.dot(a, b, preferred_element_type=F32)


def dot_cols(a, b):
    return lax.dot_general(a, b, (((1,), (1,)), ((), ())), preferred_element_type=F32)


def dot_rows(a, b):
    return lax.dot_general(a, b, (((0,), (0,)), ((), ())), preferred_element_type=F32)


def rows_of(channels):
    return lax.broadcasted_iota(jnp.int32, (8, channels), 0)


def patch(mains, lefts, rights):
    row = rows_of(mains[0].shape[1])
    tails = [jnp.where(row < 4, after, before) for before, after in zip(lefts, rights)]
    for i in range(8):
        spare = pltpu.roll(tails[20 + i // 4], MOVES[i % 4][0], 0)
        tails[i] = jnp.where((row == 3) | (row == 4), spare, tails[i])
    return jnp.concatenate(mains + [jnp.concatenate(tails[:20], axis=0).astype(BF16)], axis=0)


def pack_low(groups):
    row = rows_of(groups[0].shape[1])
    return [
        jnp.where(row < 4, groups[n], pltpu.roll(groups[n + 1], 5, 0))
        for n in range(0, len(groups), 2)
    ]


def pack_high(groups):
    row = rows_of(groups[0].shape[1])
    return [
        jnp.where(row < 4, pltpu.roll(groups[n], 3, 0), groups[n + 1])
        for n in range(0, len(groups), 2)
    ]


def packed_tiles(groups):
    return [jnp.concatenate(groups[n : n + 2], axis=0).astype(BF16) for n in range(0, len(groups), 2)]


def side_group(ref, tile, i, low):
    group = ref[tile + i // 4].astype(F32)[i % 4 // 2 * 8 :][:8]
    if low:
        return group if i % 2 == 0 else pltpu.roll(group, 3, 0)
    return group if i % 2 == 1 else pltpu.roll(group, 5, 0)


def outer(group, low):
    zeros = jnp.zeros_like(group)
    return jnp.concatenate([group, zeros] if low else [zeros, group], axis=0).astype(BF16)


def both(wet):
    return jnp.concatenate([wet, wet], axis=-1)


def side_kernel(left_ref, right_ref, wet_left_ref, wet_right_ref, west_ref, east_ref):
    lon = left_ref.shape[0]
    low = [(left_ref[i] * both(wet_left_ref[i])).astype(F32)[:8] for i in range(lon)]
    high = [(right_ref[i] * both(wet_right_ref[i])).astype(F32)[8:] for i in range(lon)]
    for ref, groups in ((west_ref, pack_low(low)), (east_ref, pack_high(high))):
        for n, tile in enumerate(packed_tiles(groups)):
            ref[n] = tile


def end_kernel(masks, top_ref, bottom_ref, *refs):
    west_ref, east_ref, north_ref, south_ref = refs[masks:]
    lat = top_ref.shape[1]
    tiles = west_ref.shape[0]
    for i in range(3):
        for out_ref, ref, n, tile, at in (
            (north_ref, top_ref, i, 0, i),
            (south_ref, bottom_ref, i + 1, tiles - 1, i + 1),
        ):
            cells = ref[n]
            if masks:
                cells = cells * both(refs[0 if ref is top_ref else 1][n])
            out_ref[i, :TILE, :] = outer(side_group(west_ref, tile, at, False), False)
            out_ref[i, TILE : TILE + lat, :] = cells
            out_ref[i, TILE + lat :, :] = outer(side_group(east_ref, tile, at, True), True)


def filtered(wave, taps_ref, back_ref):
    real, imag = wave[:HALF], wave[HALF:]
    k_real, k_imag, k_last = taps_ref[:HALF], taps_ref[HALF : 2 * HALF], taps_ref[2 * HALF :]
    out_real = real * k_real + imag * k_imag
    out_imag = imag * k_last - real * k_imag
    return dot(back_ref[:, :HALF], out_real.astype(BF16)) + dot(
        back_ref[:, HALF:], out_imag.astype(BF16)
    )


def block_rows(place, k, rows):
    return pl.ds(pl.multiple_of((place ^ k) * rows, 16), rows)


def row_of_step(ends, step, rows):
    return (rows - 1) * step if ends else 1 + step


def cell_kernel(ends, rows, *refs):
    (
        who_ref, before_ref, x_ref, after_ref, wet_before_ref, wet_ref, wet_after_ref,
        west_ref, east_ref, cot_ref, place_ref, own_ref, back_ref, taps_ref, collect_ref,
        bias_ref, gain_ref, shift_ref, up_ref, up_bias_ref, down_ref,
    ) = refs[:21]
    if ends:
        (
            north_ref, south_ref, _, _, _, sum_in_ref, p_in_ref, small_in_ref,
            fg_ref, to_west_ref, to_east_ref, keep_ref, send_ref,
            sum_ref, p_ref, small_ref, pad_ref,
        ) = refs[21:]
    else:
        fg_ref, to_west_ref, to_east_ref, sum_ref, p_ref, small_ref, pad_ref = refs[21:]
    step = pl.program_id(0)
    a = row_of_step(ends, step, rows)
    lat, channels = x_ref.shape[1:]
    units = up_ref.shape[1]
    count = lat // TILE

    @pl.when(step == 0)
    def _():
        if ends:
            sum_ref[...] = sum_in_ref[...]
            p_ref[...] = p_in_ref[...]
            small_ref[...] = small_in_ref[...]
        else:
            for ref in (sum_ref, p_ref, small_ref):
                ref[...] = jnp.zeros_like(ref)

    def fill(i):
        ref, wets, n = x_ref, wet_ref, i
        if i < 0:
            ref, wets, n = before_ref, wet_before_ref, i + 8
        elif i >= TILE:
            ref, wets, n = after_ref, wet_after_ref, i - TILE
        pad_ref[3 + i, :TILE, :] = outer(side_group(west_ref, 4 * a, i, False), False)
        pad_ref[3 + i, TILE : TILE + lat, :] = ref[n] * both(wets[n])
        pad_ref[3 + i, TILE + lat :, :] = outer(side_group(east_ref, 4 * a, i, True), True)

    for i in range(TILE):
        fill(i)
    if ends:

        @pl.when(step == 0)
        def _():
            pad_ref[:3] = north_ref[...]
            for i in range(TILE, TILE + 3):
                fill(i)

        @pl.when(step == 1)
        def _():
            pad_ref[3 + TILE :] = south_ref[...]
            for i in range(-3, 0):
                fill(i)

    else:
        for i in (-3, -2, -1, TILE, TILE + 1, TILE + 2):
            fill(i)

    def columns(i, b):
        return pad_ref[i, TILE * b : TILE * (b + 1), :]

    waves = []
    for b in range(count):
        cells = patch(
            [columns(i, b + 1) for i in range(SPAN)],
            [columns(i, b).astype(F32)[8:] for i in range(SPAN)],
            [columns(i, b + 2).astype(F32)[:8] for i in range(SPAN)],
        )
        waves.append(dot(place_ref[...], cells))
    field = jnp.concatenate([filtered(w, taps_ref, back_ref) for w in waves]) + bias_ref[...]

    def by_tile(ref):
        return jnp.concatenate(
            [
                ref[:, TILE * b : TILE * (b + 1), :].reshape(CELLS, ref.shape[2])
                for b in range(count)
            ]
        )

    masked_grad = by_tile(cot_ref) * both(by_tile(wet_ref))
    average = jnp.mean(field, axis=-1, keepdims=True)
    centred = field - average
    variance = jnp.mean(centred * centred, axis=-1, keepdims=True)
    inv_std = lax.rsqrt(variance + 1e-06)
    normed = centred * inv_std
    gain = gain_ref[...]
    normed_out = (normed * gain + shift_ref[...]).astype(BF16)
    hidden = dot(normed_out, up_ref[...]) + up_bias_ref[...]
    bell = jnp.exp(-0.5 * hidden * hidden)
    t = pl.reciprocal(1.0 + (0.3275911 * 0.7071067811865476) * jnp.abs(hidden), approx=True)
    poly = 0.5 * 1.061405429
    for c in (-1.453152027, 1.421413741, -0.284496736, 0.254829592):
        poly = poly * t + 0.5 * c
    tail = poly * t * bell
    cumulative = jnp.where(hidden >= 0, 1.0 - tail, tail)
    activated = (hidden * cumulative).astype(BF16)
    act_grad = dot_cols(masked_grad, down_ref[...])
    hidden_grad = (act_grad * (cumulative + hidden * (bell * 0.3989422804014327))).astype(BF16)
    up_part = dot_rows(normed_out, hidden_grad)
    down_part = dot_rows(activated, masked_grad)
    at = 0
    for part in (up_part, down_part):
        for n in range(0, part.shape[1], LANES):
            sum_ref[at : at + part.shape[0], :] += part[:, n : n + LANES]
            at += part.shape[0]
    bias_part = jnp.sum(hidden_grad.astype(F32), axis=0, keepdims=True)
    for n in range(units // channels):
        small_ref[52 + n : 53 + n, :] += bias_part[:, n * channels : (n + 1) * channels]
    normed_grad = dot_cols(hidden_grad, up_ref[...])
    product = normed_grad * normed
    small_ref[49:50, :] += jnp.sum(product, axis=0, keepdims=True)
    small_ref[50:51, :] += jnp.sum(normed_grad, axis=0, keepdims=True)
    scaled = normed_grad * gain
    scaled_mean = jnp.mean(scaled, axis=-1, keepdims=True)
    product_mean = jnp.mean(product * gain, axis=-1, keepdims=True)
    wide_grad = inv_std * (scaled - scaled_mean - normed * product_mean)
    field_grad = wide_grad.astype(BF16)
    for n in range(count):
        fg_ref[:, TILE * n : TILE * (n + 1), :] = field_grad[CELLS * n : CELLS * (n + 1)].reshape(
            TILE, TILE, channels
        )
    lows = [wide_grad[TILE * i : TILE * i + 8] for i in range(TILE)]
    start = CELLS * (count - 1)
    highs = [wide_grad[start + TILE * i + 8 : start + TILE * i + TILE] for i in range(TILE)]

    for out_ref, packed in ((to_west_ref, pack_low(lows)), (to_east_ref, pack_high(highs))):
        for n, tile in enumerate(packed_tiles(packed)):
            out_ref[n] = tile
    ripples = [
        dot(own_ref[...], field_grad[CELLS * n : CELLS * (n + 1)]) for n in range(count)
    ]
    for r in range(0, HALF, 8):
        p1, p2, p3 = 0.0, 0.0, 0.0
        for wave, ripple in zip(waves, ripples):
            g_real, g_imag = ripple[r : r + 8], ripple[HALF + r : HALF + r + 8]
            x_real, x_imag = wave[r : r + 8], wave[HALF + r : HALF + r + 8]
            p1 += g_real * x_real
            p2 += g_imag * x_imag
            p3 += g_real * x_imag - g_imag * x_real
        p_ref[0, r : r + 8, :] += p1
        p_ref[1, r : r + 8, :] += p2
        p_ref[2, r : r + 8, :] += p3
    small_ref[51:52, :] += sum(ripple[0:1] for ripple in ripples)

    if not ends:
        return

    @pl.when(step == 1)
    def _():
        total = 0.0
        for n in range(3):
            total += jnp.dot(
                collect_ref[:, n * HALF : (n + 1) * HALF],
                p_ref[n],
                precision=lax.Precision.HIGHEST,
                preferred_element_type=F32,
            )
        small_ref[:49, :] = total
        start = 4 * units * channels // LANES // 2
        for n in range(0, channels, LANES):
            sum_ref[start : start + 64, :] = small_ref[:, n : n + LANES]
            start += 64
        for n, ref in enumerate((keep_ref, send_ref)):
            for k in range(BLOCKS // 2):
                ref[k] = sum_ref[block_rows(who_ref[n], k, ref.shape[1]), :]


def join_kernel(*refs):
    for n, ref in enumerate(refs[:-1]):
        refs[-1][n] = ref[0]


def finish_kernel(
    scale, who_ref, own_ref, other_ref, taps_ref, conv_bias_ref, gain_ref, shift_ref, up_ref,
    up_bias_ref, down_ref, sum_ref,
):
    for n, ref in enumerate((own_ref, other_ref)):
        for k in range(BLOCKS // 2):
            sum_ref[block_rows(who_ref[n], k, ref.shape[1]), :] = ref[k].astype(F32) * scale
    at = 0
    for ref in (up_ref, down_ref):
        for n in range(0, ref.shape[1], LANES):
            ref[:, n : n + LANES] = sum_ref[at : at + ref.shape[0], :]
            at += ref.shape[0]
    small = jnp.concatenate([sum_ref[at : at + 64, :], sum_ref[at + 64 : at + 128, :]], axis=1)
    taps_ref[...] = small[:49]
    gain_ref[...] = small[49:50]
    shift_ref[...] = small[50:51]
    conv_bias_ref[...] = small[51:52]
    channels = small.shape[1]
    for n in range(up_bias_ref.shape[1] // channels):
        up_bias_ref[:, n * channels : (n + 1) * channels] = small[52 + n : 53 + n]


def spread_kernel(
    at, rows, before_ref, fg_ref, after_ref, north_ref, south_ref, west_ref, east_ref, cot_ref,
    wet_ref, place_ref, back_ref, taps_ref, *out_refs,
):
    lat, channels = fg_ref.shape[1:]
    count = lat // TILE

    def columns(i, b):
        if i < 0 and at == 0:
            return north_ref[i + 3, TILE * (b + 1) : TILE * (b + 2), :]
        if i >= TILE and at == rows - 1:
            return south_ref[i - TILE, TILE * (b + 1) : TILE * (b + 2), :]
        if b < 0:
            return outer(side_group(west_ref, 4 * at, i, False), False)
        if b == count:
            return outer(side_group(east_ref, 4 * at, i, True), True)
        ref, n = fg_ref, i
        if i < 0:
            ref, n = before_ref, i + 8
        elif i >= TILE:
            ref, n = after_ref, i - TILE
        return ref[n, TILE * b : TILE * (b + 1), :]

    slabs = range(-3, TILE + 3)
    for b in range(count):
        cells = patch(
            [columns(i, b) for i in slabs],
            [columns(i, b - 1).astype(F32)[8:] for i in slabs],
            [columns(i, b + 1).astype(F32)[:8] for i in slabs],
        )
        spread = filtered(dot(place_ref[...], cells), taps_ref, back_ref)
        here = slice(TILE * b, TILE * (b + 1))
        wet = both(wet_ref[:, here, :].reshape(CELLS, LANES).astype(F32))
        cot = cot_ref[:, here, :].reshape(CELLS, channels).astype(F32)
        out_refs[-1][:, here, :] = (cot + wet * spread).reshape(TILE, TILE, channels)


def whole(*shape):
    return pl.BlockSpec(shape, lambda *_: (0,) * len(shape))


def shape_of(shape, dtype=F32):
    return jax.ShapeDtypeStruct(shape, dtype)


ANY = pl.BlockSpec(memory_space=pl.ANY)
IN_SMEM = pl.BlockSpec(memory_space=pltpu.SMEM)
IN_VMEM = pl.BlockSpec(memory_space=pltpu.VMEM)


def sides(x, wet):
    lon, lat, channels = x.shape

    def specs(depth):
        return [
            pl.BlockSpec((lon, TILE, depth), lambda i: (0, 0, 0)),
            pl.BlockSpec((lon, TILE, depth), lambda i: (0, lat // TILE - 1, 0)),
        ]

    shapes = [shape_of((lon // 4, TILE, channels), BF16)] * 2
    return pl.pallas_call(
        side_kernel,
        grid=(1,),
        in_specs=specs(channels) + specs(LANES),
        out_specs=[whole(*s.shape) for s in shapes],
        out_shape=shapes,
        name="sides",
    )(x, x, wet, wet)


def ends(x, wet, halos):
    lon, lat, channels = x.shape

    def specs(depth):
        return [
            pl.BlockSpec((4, lat, depth), lambda i: (0, 0, 0)),
            pl.BlockSpec((4, lat, depth), lambda i: (lon // 4 - 1, 0, 0)),
        ]

    masks = [] if wet is None else [wet, wet]
    shapes = [shape_of((3, lat + 2 * TILE, channels), BF16)] * 2
    return pl.pallas_call(
        functools.partial(end_kernel, len(masks)),
        grid=(1,),
        in_specs=specs(channels) + specs(LANES)[: len(masks)] + [whole(*h.shape) for h in halos],
        out_specs=[whole(*s.shape) for s in shapes],
        out_shape=shapes,
        name="ends",
    )(x, x, *masks, *halos)


def cell_pass(who, x, halos, cotangent, wet, taps, params, end_halos=(), earlier=()):
    table = tables()
    lon, lat, channels = x.shape
    at_ends = len(end_halos) > 0
    rows = lon // TILE
    units = params[3].shape[1]
    sum_rows = (4 * units * channels // 2 + 64 * channels) // LANES
    sums = [shape_of((sum_rows, LANES)), shape_of((3, HALF, channels)), shape_of((64, channels))]
    half = shape_of((BLOCKS // 2, sum_rows // BLOCKS, LANES))

    def row(step):
        return row_of_step(at_ends, step, rows)

    def tiled(depth):
        return pl.BlockSpec((TILE, lat, depth), lambda i: (row(i), 0, 0))

    def around(depth):
        return [
            pl.BlockSpec((8, lat, depth), lambda i: (jnp.maximum(2 * row(i) - 1, 0), 0, 0)),
            tiled(depth),
            pl.BlockSpec(
                (8, lat, depth), lambda i: (jnp.minimum(2 * row(i) + 2, 2 * rows - 1), 0, 0)
            ),
        ]

    packed = pl.BlockSpec((4, TILE, channels), lambda i: (row(i), 0, 0))
    constants = [table["place"], table["own"], table["back"], taps, table["collect"], *params]
    operands = [who, x, x, x, wet, wet, wet, *halos, cotangent, *constants]
    in_specs = [IN_SMEM, *around(channels), *around(LANES), *[whole(*h.shape) for h in halos]]
    in_specs += [tiled(channels)] + [whole(*c.shape) for c in constants]
    out_shape = [shape_of(x.shape, BF16)] + [shape_of(h.shape, BF16) for h in halos]
    out_specs = [tiled(channels), packed, packed]
    scratch = [pltpu.VMEM((SPAN, lat + 2 * TILE, channels), BF16)]
    aliases = {}
    if at_ends:
        first = len(operands) + len(end_halos)
        aliases = {first + n: n for n in range(3)}
        operands += [*end_halos, *earlier]
        in_specs += [whole(*h.shape) for h in end_halos] + [ANY] * 3
        in_specs += [whole(*s.shape) for s in sums]
        out_shape += [half, half]
        scratch = [pltpu.VMEM(s.shape, F32) for s in sums] + scratch
    else:
        out_shape += sums
    out_specs += [whole(*s.shape) for s in out_shape[3:]]
    return pl.pallas_call(
        functools.partial(cell_kernel, at_ends, rows),
        grid=(2,),
        in_specs=in_specs,
        out_specs=out_specs,
        out_shape=out_shape,
        scratch_shapes=scratch,
        input_output_aliases=aliases,
        compiler_params=pltpu.CompilerParams(vmem_limit_bytes=56 * 2**20),
        cost_estimate=pl.CostEstimate(
            flops=10 * 10**9, bytes_accessed=8 * 2**20, transcendentals=0
        ),
        name="end_cells" if at_ends else "inner_cells",
    )(*operands)


def join(parts):
    return pl.pallas_call(
        join_kernel,
        in_specs=[IN_VMEM] * len(parts),
        out_specs=IN_VMEM,
        out_shape=shape_of((len(parts),) + parts[0].shape[1:], parts[0].dtype),
        name="join",
    )(*parts)


def finish(who, own, other, scale, channels, units):
    shapes = [(49, channels)] + [(1, channels)] * 3 + [(channels, units), (1, units), (units, channels)]
    return pl.pallas_call(
        functools.partial(finish_kernel, scale),
        in_specs=[IN_SMEM, IN_VMEM, IN_VMEM],
        out_specs=[IN_VMEM] * len(shapes),
        out_shape=[shape_of(s) for s in shapes],
        scratch_shapes=[pltpu.VMEM((BLOCKS * own.shape[1], LANES), F32)],
        name="finish",
    )(who, own, other)


def spread_pass(at, field_grad, halos, end_halos, cotangent, wet, taps, out):
    table = tables()
    lon, lat, channels = cotangent.shape
    rows = lon // TILE

    def row_of(depth):
        return pl.BlockSpec((TILE, lat, depth), lambda i: (at, 0, 0))

    def near(n):
        return pl.BlockSpec((8, lat, channels), lambda i: (n, 0, 0))

    return pl.pallas_call(
        functools.partial(spread_kernel, at, rows),
        grid=(1,),
        in_specs=[
            near(max(2 * at - 1, 0)), row_of(channels), near(min(2 * at + 2, 2 * rows - 1))
        ]
        + [whole(*h.shape) for h in (*end_halos, *halos)]
        + [
            row_of(channels), row_of(LANES),
            whole(2 * HALF, 2 * HALF), whole(HALF, 2 * HALF), whole(3 * HALF, channels),
        ]
        + [ANY] * (out is not None),
        out_specs=row_of(channels),
        out_shape=shape_of((lon, lat, channels)),
        input_output_aliases={} if out is None else {12: 0},
        compiler_params=pltpu.CompilerParams(vmem_limit_bytes=40 * 2**20),
        cost_estimate=pl.CostEstimate(
            flops=4 * 10**9, bytes_accessed=4 * 2**20, transcendentals=0
        ),
        name="spread_pass",
    )(
        field_grad, field_grad, field_grad, *end_halos, *halos, cotangent, wet, table["place"],
        table["back"], taps, *([] if out is None else [out]),
    )


def ring(axis, step):
    size = lax.axis_size(axis)
    return [(i, (i + step) % size) for i in range(size)]


def line(axis, step):
    size = lax.axis_size(axis)
    return [(i, i + step) for i in range(size) if 0 <= i + step < size]


def across_lat(west, east):
    return [lax.ppermute(east, "gy", line("gy", 1)), lax.ppermute(west, "gy", line("gy", -1))]


def across_lon(north, south):
    return [lax.ppermute(south, "gx", ring("gx", 1)), lax.ppermute(north, "gx", ring("gx", -1))]


def swapped(mesh_shape, stage, step):
    gx, gy = mesh_shape
    pairs = []
    for n in range(gx * gy):
        i, j = divmod(n, gy)
        core, x, y, z = i % 2, i // 2 % 4, j // 2, i // 8 * 2 + j % 2
        if stage == "core":
            core ^= step
        else:
            axis = "abc".index(stage) if core == 0 else ("abc".index(stage) + 1) % 3
            place = [x, y, z]
            place[axis] ^= step
            x, y, z = place
        pairs.append((n, (z // 2 * 8 + x * 2 + core) * gy + y * 2 + z % 2))
    return pairs


def places():
    i, j = lax.axis_index("gx"), lax.axis_index("gy")
    core, x, y = i % 2, i // 2 % 4, j // 2
    own, other = jnp.where(core == 0, x, 4 + y), jnp.where(core == 0, 4 + y, x)
    return jnp.stack([own, other]).astype(jnp.int32)


def summed_blocks(keep, send):
    mesh_shape = (lax.axis_size("gx"), lax.axis_size("gy"))

    def move(x, stage, step):
        return lax.ppermute(x, AXES, swapped(mesh_shape, stage, step))

    def added(parts):
        parts = [part.astype(F32) for part in parts]
        return (parts[0] + parts[1]) + (parts[2] + parts[3])

    held = keep + move(send, "core", 1)
    held = added(
        [held[:1]] + [move(held[n : n + 1].astype(BF16), "a", n) for n in range(1, 4)]
    )
    for stage in ("b", "c"):
        held = held.astype(BF16)
        held = added([held] + [move(held, stage, n) for n in range(1, 4)])
    held = held.astype(BF16)
    own = join([held] + [move(held, "a", n) for n in range(1, 4)])
    return own, move(own, "core", 1)


def local(
    inputs, cotangent, wet_mask, kernel, conv_bias, norm_gain, norm_shift, up_weight, up_bias,
    down_weight,
):
    lon, lat, channels = inputs.shape
    units = up_weight.shape[1]
    wet = jnp.broadcast_to(wet_mask.astype(BF16)[:, :, None], (lon, lat, LANES))
    halos = across_lat(*sides(inputs, wet))
    end_halos = across_lon(*ends(inputs, wet, halos))
    taps = jnp.dot(
        tables()["taps"], kernel.astype(F32), precision=lax.Precision.HIGHEST,
        preferred_element_type=F32,
    )
    who = places()

    def row(x):
        return x.astype(F32)[None, :]

    params = (
        row(conv_bias), row(norm_gain), row(norm_shift), up_weight, row(up_bias), down_weight
    )
    first = (who, inputs, halos, cotangent, wet, taps[: 3 * HALF], params)
    inner = cell_pass(*first)
    field_grad, west, east, keep, send = cell_pass(*first, end_halos, inner)
    halos = across_lat(west, east)
    end_halos = across_lon(*ends(field_grad, None, halos))
    own, other = summed_blocks(keep, send)
    input_grad = None
    middle = range(1, lon // TILE - 1)
    for at in (*middle, 0, lon // TILE - 1):
        far = halos if at in middle else end_halos
        input_grad = spread_pass(
            at, field_grad, halos, far, cotangent, wet, taps[3 * HALF :], input_grad
        )
    cells = lon * lat * lax.axis_size("gx") * lax.axis_size("gy")
    grads = finish(who, own, other, float(cells) ** -0.5, channels, units)
    taps_grad, bias_grad, gain_grad, shift_grad, up_grad, up_bias_grad, down_grad = grads
    return (
        input_grad, taps_grad, bias_grad[0], gain_grad[0], shift_grad[0], up_grad,
        up_bias_grad[0], down_grad,
    )


def solution(mesh):
    whole_in = (P(),) * 7
    in_specs = (P("gx", "gy", None), P("gx", "gy", None), P("gx", "gy")) + whole_in
    out_specs = (P("gx", "gy", None),) + whole_in
    return jax.shard_map(local, mesh=mesh, in_specs=in_specs, out_specs=out_specs, check_vma=False)
```

time: 135 us -> 127 us (0.941)
  waiting for transfers between devices: 18.8 us -> 2.34 us
  local copies, waits for them, and re-layouts: 6.41 us -> 20 us
  starting transfers between devices: 48.6 us -> 41.7 us
  Pallas kernels: 51.5 us -> 53.4 us
    unnamed x44 -> x66, local copies, waits for them, and re-layouts: 2.55 us -> 16.4 us
    ppermute x8, waiting for transfers between devices: 12.1 us -> 0.02 us  [the longest x2 0.01 us: across_lon(): lax.ppermute(north, 'gx', ring('gx', -1))]
    ppermute x17 -> x14, waiting for transfers between devices: 6.72 us -> 2.32 us  [move(): return lax.ppermute(x, AXES, swapped(mesh_shape, stage, step))]
    ppermute x17 -> x14, starting transfers between devices: 32.2 us -> 27.9 us  [move(): return lax.ppermute(x, AXES, swapped(mesh_shape, stage, step))]
    concatenate x3 -> x0, other arithmetic: 3.63 us -> none  [the longest x2 3.62 us: padded_2(): return jnp.concatenate([before, x, after, zeros], axis=1)]
    ppermute x8, starting transfers between devices: 16.4 us -> 13.8 us  [the longest x2 8.53 us: across_lat(): lax.ppermute(east, 'gy', line('gy', 1))]
    slice x7 -> x1, local copies, waits for them, and re-layouts: 3 us -> 0.71 us  [summed_blocks(): held[n:n + 1].astype(BF16)]
    broadcast_in_dim x4, other arithmetic: 0.01 us -> 2.27 us  [row(): return x.astype(F32)[None, :]]
  transfers between devices with their start and end apart: 25 -> 22, of which waited for: 13 -> 3; matrix products, arithmetic and copies ran while one was open for 2% -> 7% of each run, Pallas kernels for 10% -> 23%
where the time goes in v4:
time: 127 us; the launch traced here: 126 us
  Pallas kernels  53.4 us (42%)
  starting transfers between devices  41.7 us (33%)
  local copies, waits for them, and re-layouts  20 us (16%)
  other arithmetic  6.81 us (5%)
  waiting for transfers between devices  2.34 us (2%)
    pallas_call x2, Pallas kernels, cell_pass(): pl.pallas_call(functools.partial(cell_kernel, at_ends, rows), grid=(2,),...  30.4 us
    ppermute x14, starting transfers between devices, move(): return lax.ppermute(x, AXES, swapped(mesh_shape, stage, step))  27.9 us
    unnamed x66, local copies, waits for them, and re-layouts  16.4 us
    pallas_call x4, Pallas kernels, spread_pass(): pl.pallas_call(functools.partial(spread_kernel, at, rows), grid=(1,), in_...  13.1 us
    ppermute x2, starting transfers between devices, across_lat(): lax.ppermute(east, 'gy', line('gy', 1))  8.53 us
    pallas_call x2, Pallas kernels, ends(): pl.pallas_call(functools.partial(end_kernel, len(masks)), grid=(1,), in_s...  3.87 us
    ppermute x2, starting transfers between devices, across_lat(): lax.ppermute(west, 'gy', line('gy', -1))  2.58 us
  transfers between devices with their start and end apart: 22, of which 3 were waited for; matrix products, arithmetic and copies ran while one was open for 7% of the time, Pallas kernels for 23%

profile of v4, /device:TPU:1, one launch (start us, length us, event | category | flops | bytes accessed | tf_op | source)
XLA Modules:
  0.0 125.9 jit_solution(2672070449761652967)
XLA Ops:
  0.6 0.0 copy-start
  0.6 0.8 convert_element_type.53
  1.4 1.6 %broadcast_in_dim.26.wet_left_ref.wet_right_ref.refs_0_.refs_1_.refs_4_.refs_5_.refs_6_.wet_ref = bf16[64,64,128]{2,1,0:T(8,128)(2,1)} broadcast(bf16[64,64]{1,0:T(8,128)(2,1)S(1)} %convert_element_type.53), dimensions={0,1} | broadcast | bytes 1056768 | tf_op jit(solution)/shard_map/broadcast_in_dim | solution.py:662
  3.0 2.2 %sides.1 = (bf16[16,16,256]{2,1,0:T(8,128)(2,1)}, bf16[16,16,256]{2,1,0:T(8,128)(2,1)}) custom-call(bf16[64,64,256]{2,1,0:T(8,128)(2,1)} %refs_3_.3, bf16[64,64,256]{2,1,0:T(8,128)(2,1)} %refs_3_.3, bf16[64,64,128]{2,1,0:T(8,128)(2,1)} %broadcast_in_dim.26.wet_left_ref.wet_right_ref.refs_0_.refs_1_.refs_4_.refs_5_.refs_6_.wet_ref, ...), custom_call_target="tpu_custom_call" | custom-call | tf_op jit(solution)/shard_map/sides/pallas_call | solution.py:441
  5.2 4.4 %collective-permute-start = (bf16[16,16,256]{2,1,0:T(8,128)(2,1)}, bf16[16,16,256]{2,1,0:T(8,128)(2,1)S(1)}, u32[]{:S(2)}, u32[]{:S(2)}) collective-permute-start(bf16[16,16,256]{2,1,0:T(8,128)(2,1)} %get-tuple-element.32), channel_id=1, source_target_pairs={{0,1},{1,2},{2,3},{3,4},{4,5},{5,6},{6,7},{8,9},{9,10},{10,11},{11... | collective-permute-start | bytes 393224 | tf_op jit(solution)/shard_map/ppermute | solution.py:603
  9.6 1.3 %collective-permute-start.1 = (bf16[16,16,256]{2,1,0:T(8,128)(2,1)}, bf16[16,16,256]{2,1,0:T(8,128)(2,1)S(1)}, u32[]{:S(2)}, u32[]{:S(2)}) collective-permute-start(bf16[16,16,256]{2,1,0:T(8,128)(2,1)} %get-tuple-element.33), channel_id=1, source_target_pairs={{1,0},{2,1},{3,2},{4,3},{5,4},{6,5},{7,6},{9,8},{10,9},{11,10},{12... | collective-permute-start | bytes 393224 | tf_op jit(solution)/shard_map/ppermute | solution.py:603
  10.9 0.8 fusion.5
  11.7 1.3 fusion.3
  13.0 0.6 broadcast_in_dim.35
  13.6 0.6 broadcast_in_dim.36
  14.1 0.6 broadcast_in_dim.37
  14.7 0.6 broadcast_in_dim.38
  15.3 0.6 pad_add_fusion.refs_0_.who_ref
  15.9 0.6 copy-done.23
  16.6 0.6 copy-done.24
  17.2 1.9 %ends.2 = (bf16[3,96,256]{2,1,0:T(8,128)(2,1)}, bf16[3,96,256]{2,1,0:T(8,128)(2,1)}) custom-call(bf16[64,64,256]{2,1,0:T(8,128)(2,1)} %refs_3_.3, bf16[64,64,256]{2,1,0:T(8,128)(2,1)} %refs_3_.3, bf16[64,64,128]{2,1,0:T(8,128)(2,1)} %broadcast_in_dim.26.wet_left_ref.wet_right_ref.refs_0_.refs_1_.refs_4_.refs_5_.refs_6_.wet_ref, ...), custom_call_target="tpu_custom_call" | custom-call | tf_op jit(solution)/shard_map/ends/pallas_call | solution.py:462
  19.1 2.1 %collective-permute-start.2 = (bf16[3,96,256]{2,1,0:T(8,128)(2,1)}, bf16[3,96,256]{2,1,0:T(8,128)(2,1)S(1)}, u32[]{:S(2)}, u32[]{:S(2)}) collective-permute-start(bf16[3,96,256]{2,1,0:T(8,128)(2,1)} %get-tuple-element.34), channel_id=1, source_target_pairs={{0,8},{8,16},{16,24},{24,32},{32,40},{40,48},{48,56},{56,64},{64,7... | collective-permute-start | bytes 442376 | tf_op jit(solution)/shard_map/ppermute | solution.py:607
  21.3 14.4 %inner_cells.1 = (bf16[64,64,256]{2,1,0:T(8,128)(2,1)}, bf16[16,16,256]{2,1,0:T(8,128)(2,1)}, bf16[16,16,256]{2,1,0:T(8,128)(2,1)}, f32[2176,128]{1,0:T(8,128)},...) custom-call(s32[2]{0:T(128)} %pad_add_fusion.refs_0_.who_ref, bf16[64,64,256]{2,1,0:T(8,128)(2,1)} %refs_3_.3, ...), custom_call_target="tpu_custom_call" | custom-call | flops 10000000000 | bytes 8388608 | tf_op jit(solution)/shard_map/inner_cells/pallas_call | solution.py:517
  35.7 0.6 copy-done.28
  36.3 0.0 copy-done.29
  36.3 16.0 %end_cells.1 = (bf16[64,64,256]{2,1,0:T(8,128)(2,1)}, bf16[16,16,256]{2,1,0:T(8,128)(2,1)}, bf16[16,16,256]{2,1,0:T(8,128)(2,1)}, f32[4,272,128]{2,1,0:T(8,128)}, f32[4,272,128]{2,1,0:T(8,128)}) custom-call(s32[2]{0:T(128)} %pad_add_fusion.refs_0_.who_ref, ...), custom_call_target="tpu_custom_call", output_to_operand_aliasing={{0}: (23, {}), {1}: (24, {}), {2}: (25, {})} | custom-call | flops 10000000000 | bytes 8388608 | tf_op jit(solution)/shard_map/end_cells/pallas_call | solution.py:517
  52.4 4.3 %collective-permute-start.8 = (f32[4,272,128]{2,1,0:T(8,128)}, f32[4,272,128]{2,1,0:T(8,128)S(1)}, u32[]{:S(2)}, u32[]{:S(2)}) collective-permute-start(f32[4,272,128]{2,1,0:T(8,128)} %get-tuple-element.48), channel_id=1, source_target_pairs={{0,8},{1,9},{2,10},{3,11},{4,12},{5,13},{6,14},{7,15},{8,0},{9,1},... | collective-permute-start | bytes 1671176 | tf_op jit(solution)/shard_map/ppermute | solution.py:638
  56.7 4.2 %collective-permute-start.4 = (bf16[16,16,256]{2,1,0:T(8,128)(2,1)}, bf16[16,16,256]{2,1,0:T(8,128)(2,1)S(1)}, u32[]{:S(2)}, u32[]{:S(2)}) collective-permute-start(bf16[16,16,256]{2,1,0:T(8,128)(2,1)} %get-tuple-element.43), channel_id=1, source_target_pairs={{0,1},{1,2},{2,3},{3,4},{4,5},{5,6},{6,7},{8,9},{9,10},{10,11},{11... | collective-permute-start | bytes 393224 | tf_op jit(solution)/shard_map/ppermute | solution.py:603
  60.9 1.3 %collective-permute-start.5 = (bf16[16,16,256]{2,1,0:T(8,128)(2,1)}, bf16[16,16,256]{2,1,0:T(8,128)(2,1)S(1)}, u32[]{:S(2)}, u32[]{:S(2)}) collective-permute-start(bf16[16,16,256]{2,1,0:T(8,128)(2,1)} %get-tuple-element.44), channel_id=1, source_target_pairs={{1,0},{2,1},{3,2},{4,3},{5,4},{6,5},{7,6},{9,8},{10,9},{11,10},{12... | collective-permute-start | bytes 393224 | tf_op jit(solution)/shard_map/ppermute | solution.py:603
  62.2 2.0 %fusion.2 = (bf16[4,272,128]{2,1,0:T(8,128)(2,1)S(1)}, f32[4,272,128]{2,1,0:T(8,128)}) fusion(f32[4,272,128]{2,1,0:T(8,128)} %get-tuple-element.47, f32[4,272,128]{2,1,0:T(8,128)S(1)} %collective-permute-done.8), kind=kLoop, calls=%fused_computation.6 | loop fusion | flops 278528 | bytes 1949696 | tf_op jit(solution)/shard_map/convert.6
  64.2 0.7 fusion.4
  64.9 3.5 %collective-permute-start.9 = (bf16[1,272,128]{2,1,0:T(8,128)(2,1)}, bf16[1,272,128]{2,1,0:T(8,128)(2,1)S(1)}, u32[]{:S(2)}, u32[]{:S(2)}) collective-permute-start(bf16[1,272,128]{2,1,0:T(8,128)(2,1)} %get-tuple-element.60), channel_id=1, source_target_pairs={{0,16},{1,17},{2,18},{3,19},{4,20},{5,21},{6,22},{7,23},{8,10},{9,... | collective-permute-start | bytes 208904 | tf_op jit(solution)/shard_map/ppermute | solution.py:638
  68.4 1.9 %collective-permute-start.11 = (bf16[1,272,128]{2,1,0:T(8,128)(2,1)}, bf16[1,272,128]{2,1,0:T(8,128)(2,1)}, u32[]{:S(2)}, u32[]{:S(2)}) collective-permute-start(bf16[1,272,128]{2,1,0:T(8,128)(2,1)} %get-tuple-element.61), channel_id=1, source_target_pairs={{0,48},{1,49},{2,50},{3,51},{4,52},{5,53},{6,54},{7,55},{8,14},{9,... | collective-permute-start | bytes 208904 | tf_op jit(solution)/shard_map/ppermute | solution.py:638
  70.3 0.7 collective-permute-start.10
  71.1 0.6 copy-done.9
  71.7 0.0 copy-done.12
  71.8 2.0 %ends.3 = (bf16[3,96,256]{2,1,0:T(8,128)(2,1)}, bf16[3,96,256]{2,1,0:T(8,128)(2,1)}) custom-call(bf16[64,64,256]{2,1,0:T(8,128)(2,1)} %get-tuple-element.42.top_ref.bottom_ref.before_ref.fg_ref.after_ref, bf16[64,64,256]{2,1,0:T(8,128)(2,1)} %get-tuple-element.42.top_ref.bottom_ref.before_ref.fg_ref.after_ref, bf16[16,16,256]{2,1,0:T(8,128)(2,1)} %copy-done.9, ...), custom_call_target="tpu_custom_call" | custom-call | tf_op jit(solution)/shard_map/ends/pallas_call | solution.py:462
  73.8 0.5 collective-permute-start.7
  74.3 1.1 collective-permute-done.10
  75.3 1.0 fusion.1
  76.3 2.3 %collective-permute-start.14 = (bf16[1,272,128]{2,1,0:T(8,128)(2,1)S(1)}, bf16[1,272,128]{2,1,0:T(8,128)(2,1)S(1)}, u32[]{:S(2)}, u32[]{:S(2)}) collective-permute-start(bf16[1,272,128]{2,1,0:T(8,128)(2,1)S(1)} %fusion.1), channel_id=1, source_target_pairs={{0,6},{1,7},{2,4},{3,5},{4,2},{5,3},{6,0},{7,1},{8,73},{9,72},{10,... | collective-permute-start | bytes 208904 | tf_op jit(solution)/shard_map/ppermute | solution.py:638
  78.7 1.4 %collective-permute-start.13 = (bf16[1,272,128]{2,1,0:T(8,128)(2,1)S(1)}, bf16[1,272,128]{2,1,0:T(8,128)(2,1)S(1)}, u32[]{:S(2)}, u32[]{:S(2)}) collective-permute-start(bf16[1,272,128]{2,1,0:T(8,128)(2,1)S(1)} %fusion.1), channel_id=1, source_target_pairs={{0,4},{1,5},{2,6},{3,7},{4,0},{5,1},{6,2},{7,3},{8,72},{9,73},{10,... | collective-permute-start | bytes 208904 | tf_op jit(solution)/shard_map/ppermute | solution.py:638
  80.1 1.6 %copy-done.3 = bf16[64,64,256]{2,1,0:T(8,128)(2,1)S(1)} copy-done((bf16[64,64,256]{2,1,0:T(8,128)(2,1)S(1)}, bf16[64,64,256]{2,1,0:T(8,128)(2,1)}, u32[]{:S(2)}) %copy-start.3) | copy-done | bytes 2097176
  81.7 1.1 copy-done.5
  82.9 1.0 copy-done.7
  83.9 0.9 copy-done.10
  84.8 0.9 copy-done.13
  85.7 0.9 copy-done.15
  86.7 3.3 %spread_pass.4.out_refs_0_ = f32[64,64,256]{2,1,0:T(8,128)} custom-call(bf16[64,64,256]{2,1,0:T(8,128)(2,1)S(1)} %copy-done.1, bf16[64,64,256]{2,1,0:T(8,128)(2,1)S(1)} %copy-done.1, bf16[64,64,256]{2,1,0:T(8,128)(2,1)S(1)} %copy-done.1, bf16[16,16,256]{2,1,0:T(8,128)(2,1)S(1)} %copy-done.10, bf16[16,16,256]{2,1,0:T(8,128)(2,1)S(1)} %copy-done.13, ...), custom_call_target="tpu_custom_call" | custom-call | flops 4000000000 | bytes 4194304 | tf_op jit(solution)/shard_map/spread_pass/pallas_call | solution.py:566
  90.0 2.5 %collective-permute-start.17 = (bf16[1,272,128]{2,1,0:T(8,128)(2,1)S(1)}, bf16[1,272,128]{2,1,0:T(8,128)(2,1)S(1)}, u32[]{:S(2)}, u32[]{:S(2)}) collective-permute-start(bf16[1,272,128]{2,1,0:T(8,128)(2,1)S(1)} %add_convert_fusion.1), channel_id=1, source_target_pairs={{0,65},{1,64},{2,67},{3,66},{4,69},{5,68},{6,71},{7,70},{8,56},{9,... | collective-permute-start | bytes 208904 | tf_op jit(solution)/shard_map/ppermute | solution.py:638
  92.5 0.8 collective-permute-start.15
  93.3 3.3 %spread_pass.5.out_refs_0_ = f32[64,64,256]{2,1,0:T(8,128)} custom-call(bf16[64,64,256]{2,1,0:T(8,128)(2,1)S(1)} %copy-done.1, bf16[64,64,256]{2,1,0:T(8,128)(2,1)S(1)} %copy-done.1, bf16[64,64,256]{2,1,0:T(8,128)(2,1)S(1)} %copy-done.1, bf16[16,16,256]{2,1,0:T(8,128)(2,1)S(1)} %copy-done.10, ...), custom_call_target="tpu_custom_call", output_to_operand_aliasing={{}: (12, {})} | custom-call | flops 4000000000 | bytes 4194304 | tf_op jit(solution)/shard_map/spread_pass/pallas_call | solution.py:566
  96.6 0.6 collective-permute-done.16
  97.2 5.0 %collective-permute-start.20 = (bf16[1,272,128]{2,1,0:T(8,128)(2,1)S(1)}, bf16[1,272,128]{2,1,0:T(8,128)(2,1)S(1)}, u32[]{:S(2)}, u32[]{:S(2)}) collective-permute-start(bf16[1,272,128]{2,1,0:T(8,128)(2,1)S(1)} %add_convert_fusion.refs_0_), channel_id=1, source_target_pairs={{0,48},{1,49},{2,50},{3,51},{4,52},{5,53},{6,54},{7,55},{8,14},{9,... | collective-permute-start | bytes 208904 | tf_op jit(solution)/shard_map/ppermute | solution.py:638
  102.3 0.3 collective-permute-start.19
  102.6 0.3 collective-permute-start.18
  103.0 3.3 %spread_pass.6.out_refs_0_ = f32[64,64,256]{2,1,0:T(8,128)} custom-call(bf16[64,64,256]{2,1,0:T(8,128)(2,1)S(1)} %copy-done.1, bf16[64,64,256]{2,1,0:T(8,128)(2,1)S(1)} %copy-done.1, bf16[64,64,256]{2,1,0:T(8,128)(2,1)S(1)} %copy-done.1, bf16[3,96,256]{2,1,0:T(8,128)(2,1)S(1)} %collective-permute-done.6.north_ref, ...), custom_call_target="tpu_custom_call", output_to_operand_aliasing={{}: (12, {})} | custom-call | flops 4000000000 | bytes 4194304 | tf_op jit(solution)/shard_map/spread_pass/pallas_call | solution.py:566
  106.3 0.7 collective-permute-done.19.refs_2_
  106.9 0.6 copy-done.26
  107.6 1.7 %join.1.own_ref = bf16[4,272,128]{2,1,0:T(8,128)(2,1)} custom-call(bf16[1,272,128]{2,1,0:T(8,128)(2,1)} %copy-done.22, bf16[1,272,128]{2,1,0:T(8,128)(2,1)} %collective-permute-done.18.refs_1_, bf16[1,272,128]{2,1,0:T(8,128)(2,1)} %copy-done.26, bf16[1,272,128]{2,1,0:T(8,128)(2,1)} %copy-done.25), custom_call_target="tpu_custom_call" | custom-call | tf_op jit(solution)/shard_map/join/pallas_call | solution.py:534
  109.3 4.6 %collective-permute-start.21 = (bf16[4,272,128]{2,1,0:T(8,128)(2,1)}, bf16[4,272,128]{2,1,0:T(8,128)(2,1)}, u32[]{:S(2)}, u32[]{:S(2)}) collective-permute-start(bf16[4,272,128]{2,1,0:T(8,128)(2,1)} %join.1.own_ref), channel_id=1, source_target_pairs={{0,8},{1,9},{2,10},{3,11},{4,12},{5,13},{6,14},{7,15},{8,0},{9,1},... | collective-permute-start | bytes 835592 | tf_op jit(solution)/shard_map/ppermute | solution.py:638
  113.9 1.6 %copy-done.4 = bf16[64,64,256]{2,1,0:T(8,128)(2,1)S(1)} copy-done((bf16[64,64,256]{2,1,0:T(8,128)(2,1)S(1)}, bf16[64,64,256]{2,1,0:T(8,128)(2,1)}, u32[]{:S(2)}) %copy-start.4) | copy-done | bytes 2097176
  115.5 1.1 copy-done.6
  116.7 1.0 copy-done.8
  117.7 0.9 copy-done.16
  118.6 0.9 copy-done.18
  119.6 0.9 copy-done.20
  120.5 3.3 %spread_pass.7 = f32[64,64,256]{2,1,0:T(8,128)} custom-call(bf16[64,64,256]{2,1,0:T(8,128)(2,1)S(1)} %copy-done.1, bf16[64,64,256]{2,1,0:T(8,128)(2,1)S(1)} %copy-done.1, bf16[64,64,256]{2,1,0:T(8,128)(2,1)S(1)} %copy-done.1, bf16[3,96,256]{2,1,0:T(8,128)(2,1)S(1)} %copy-done.18, ...), custom_call_target="tpu_custom_call", output_to_operand_aliasing={{}: (12, {})} | custom-call | flops 4000000000 | bytes 4194304 | tf_op jit(solution)/shard_map/spread_pass/pallas_call | solution.py:566
  123.7 2.2 %finish.1 = (f32[49,256]{1,0:T(8,128)}, f32[1,256]{1,0:T(1,128)}, f32[1,256]{1,0:T(1,128)}, f32[1,256]{1,0:T(1,128)}, f32[256,512]{1,0:T(8,128)}, /*index=5*/f32[1,512]{1,0:T(1,128)}, f32[512,256]{1,0:T(8,128)}) custom-call(s32[2]{0:T(128)} %pad_add_fusion.refs_0_.who_ref, bf16[4,272,128]{2,1,0:T(8,128)(2,1)} %join.1.own_ref, ...), custom_call_target="tpu_custom_call" | custom-call | tf_op jit(solution)/shard_map/finish/pallas_call | solution.py:545
  (71 shorter events, 0.2 us)
Async XLA Ops:
  0.6 10.3 %copy-start = (bf16[49,256]{1,0:T(8,128)(2,1)S(1)}, bf16[49,256]{1,0:T(8,128)(2,1)}, u32[]{:S(2)}) copy-start(bf16[49,256]{1,0:T(8,128)(2,1)} %param.18) | copy-start | bytes 75268
  3.0 7.9 %copy-start.21 = (f32[1536,49]{1,0:T(8,128)S(1)}, f32[1536,49]{1,0:T(8,128)}, u32[]{:S(2)}) copy-start(f32[1536,49]{1,0:T(8,128)} %constant.61.clone) | copy-start | bytes 903172
  5.2 10.7 %collective-permute-start = (bf16[16,16,256]{2,1,0:T(8,128)(2,1)}, bf16[16,16,256]{2,1,0:T(8,128)(2,1)S(1)}, u32[]{:S(2)}, u32[]{:S(2)}) collective-permute-start(bf16[16,16,256]{2,1,0:T(8,128)(2,1)} %get-tuple-element.32), channel_id=1, source_target_pairs={{0,1},{1,2},{2,3},{3,4},{4,5},{5,6},{6,7},{8,9},{9,10},{10,11},{11... | collective-permute-start | bytes 393224 | tf_op jit(solution)/shard_map/ppermute | solution.py:603
  9.6 6.3 %collective-permute-start.1 = (bf16[16,16,256]{2,1,0:T(8,128)(2,1)}, bf16[16,16,256]{2,1,0:T(8,128)(2,1)S(1)}, u32[]{:S(2)}, u32[]{:S(2)}) collective-permute-start(bf16[16,16,256]{2,1,0:T(8,128)(2,1)} %get-tuple-element.33), channel_id=1, source_target_pairs={{1,0},{2,1},{3,2},{4,3},{5,4},{6,5},{7,6},{9,8},{10,9},{11,10},{12... | collective-permute-start | bytes 393224 | tf_op jit(solution)/shard_map/ppermute | solution.py:603
  11.7 1.3 %copy-start.30 = (bf16[256]{0:T(256)(128)(2,1)S(1)}, bf16[256]{0:T(256)(128)(2,1)}, u32[]{:S(2)}) copy-start(bf16[256]{0:T(256)(128)(2,1)} %param.19) | copy-start | bytes 1540
  11.7 1.9 %copy-start.31 = (bf16[256]{0:T(256)(128)(2,1)S(1)}, bf16[256]{0:T(256)(128)(2,1)}, u32[]{:S(2)}) copy-start(bf16[256]{0:T(256)(128)(2,1)} %param.20) | copy-start | bytes 1540
  11.7 2.4 %copy-start.32 = (bf16[256]{0:T(256)(128)(2,1)S(1)}, bf16[256]{0:T(256)(128)(2,1)}, u32[]{:S(2)}) copy-start(bf16[256]{0:T(256)(128)(2,1)} %param.21) | copy-start | bytes 1540
  11.7 3.0 %copy-start.27 = (bf16[512]{0:T(512)(128)(2,1)S(1)}, bf16[512]{0:T(512)(128)(2,1)}, u32[]{:S(2)}) copy-start(bf16[512]{0:T(512)(128)(2,1)} %param.23) | copy-start | bytes 3076
  15.9 0.7 copy-start.23
  16.6 0.6 copy-start.24
  19.1 16.5 %collective-permute-start.2 = (bf16[3,96,256]{2,1,0:T(8,128)(2,1)}, bf16[3,96,256]{2,1,0:T(8,128)(2,1)S(1)}, u32[]{:S(2)}, u32[]{:S(2)}) collective-permute-start(bf16[3,96,256]{2,1,0:T(8,128)(2,1)} %get-tuple-element.34), channel_id=1, source_target_pairs={{0,8},{8,16},{16,24},{24,32},{32,40},{40,48},{48,56},{56,64},{64,7... | collective-permute-start | bytes 442376 | tf_op jit(solution)/shard_map/ppermute | solution.py:607
  21.3 14.4 %collective-permute-start.3 = (bf16[3,96,256]{2,1,0:T(8,128)(2,1)}, bf16[3,96,256]{2,1,0:T(8,128)(2,1)S(1)}, u32[]{:S(2)}, u32[]{:S(2)}) collective-permute-start(bf16[3,96,256]{2,1,0:T(8,128)(2,1)} %get-tuple-element.35), channel_id=1, source_target_pairs={{0,120},{8,0},{16,8},{24,16},{32,24},{40,32},{48,40},{56,48},{64,5... | collective-permute-start | bytes 442376 | tf_op jit(solution)/shard_map/ppermute | solution.py:607
  35.6 0.7 copy-start.28
  35.7 0.7 copy-start.29
  52.4 9.8 %collective-permute-start.8 = (f32[4,272,128]{2,1,0:T(8,128)}, f32[4,272,128]{2,1,0:T(8,128)S(1)}, u32[]{:S(2)}, u32[]{:S(2)}) collective-permute-start(f32[4,272,128]{2,1,0:T(8,128)} %get-tuple-element.48), channel_id=1, source_target_pairs={{0,8},{1,9},{2,10},{3,11},{4,12},{5,13},{6,14},{7,15},{8,0},{9,1},... | collective-permute-start | bytes 1671176 | tf_op jit(solution)/shard_map/ppermute | solution.py:638
  56.7 14.4 %collective-permute-start.4 = (bf16[16,16,256]{2,1,0:T(8,128)(2,1)}, bf16[16,16,256]{2,1,0:T(8,128)(2,1)S(1)}, u32[]{:S(2)}, u32[]{:S(2)}) collective-permute-start(bf16[16,16,256]{2,1,0:T(8,128)(2,1)} %get-tuple-element.43), channel_id=1, source_target_pairs={{0,1},{1,2},{2,3},{3,4},{4,5},{5,6},{6,7},{8,9},{9,10},{10,11},{11... | collective-permute-start | bytes 393224 | tf_op jit(solution)/shard_map/ppermute | solution.py:603
  60.9 10.2 %collective-permute-start.5 = (bf16[16,16,256]{2,1,0:T(8,128)(2,1)}, bf16[16,16,256]{2,1,0:T(8,128)(2,1)S(1)}, u32[]{:S(2)}, u32[]{:S(2)}) collective-permute-start(bf16[16,16,256]{2,1,0:T(8,128)(2,1)} %get-tuple-element.44), channel_id=1, source_target_pairs={{1,0},{2,1},{3,2},{4,3},{5,4},{6,5},{7,6},{9,8},{10,9},{11,10},{12... | collective-permute-start | bytes 393224 | tf_op jit(solution)/shard_map/ppermute | solution.py:603
  64.9 9.4 %collective-permute-start.9 = (bf16[1,272,128]{2,1,0:T(8,128)(2,1)}, bf16[1,272,128]{2,1,0:T(8,128)(2,1)S(1)}, u32[]{:S(2)}, u32[]{:S(2)}) collective-permute-start(bf16[1,272,128]{2,1,0:T(8,128)(2,1)} %get-tuple-element.60), channel_id=1, source_target_pairs={{0,16},{1,17},{2,18},{3,19},{4,20},{5,21},{6,22},{7,23},{8,10},{9,... | collective-permute-start | bytes 208904 | tf_op jit(solution)/shard_map/ppermute | solution.py:638
  68.4 5.8 %collective-permute-start.11 = (bf16[1,272,128]{2,1,0:T(8,128)(2,1)}, bf16[1,272,128]{2,1,0:T(8,128)(2,1)}, u32[]{:S(2)}, u32[]{:S(2)}) collective-permute-start(bf16[1,272,128]{2,1,0:T(8,128)(2,1)} %get-tuple-element.61), channel_id=1, source_target_pairs={{0,48},{1,49},{2,50},{3,51},{4,52},{5,53},{6,54},{7,55},{8,14},{9,... | collective-permute-start | bytes 208904 | tf_op jit(solution)/shard_map/ppermute | solution.py:638
  70.3 5.0 %collective-permute-start.10 = (bf16[1,272,128]{2,1,0:T(8,128)(2,1)}, bf16[1,272,128]{2,1,0:T(8,128)(2,1)}, u32[]{:S(2)}, u32[]{:S(2)}) collective-permute-start(bf16[1,272,128]{2,1,0:T(8,128)(2,1)} %get-tuple-element.62), channel_id=1, source_target_pairs={{0,32},{1,33},{2,34},{3,35},{4,36},{5,37},{6,38},{7,39},{8,12},{9,... | collective-permute-start | bytes 208904 | tf_op jit(solution)/shard_map/ppermute | solution.py:638
  71.1 0.7 copy-start.9
  71.1 0.7 copy-start.12
  71.8 8.4 %copy-start.1 = (bf16[64,64,256]{2,1,0:T(8,128)(2,1)S(1)}, bf16[64,64,256]{2,1,0:T(8,128)(2,1)}, u32[]{:S(2)}) copy-start(bf16[64,64,256]{2,1,0:T(8,128)(2,1)} %get-tuple-element.42.top_ref.bottom_ref.before_ref.fg_ref.after_ref) | copy-start | bytes 6291460
  71.8 8.4 %copy-start.2 = (bf16[64,64,128]{2,1,0:T(8,128)(2,1)S(1)}, bf16[64,64,128]{2,1,0:T(8,128)(2,1)}, u32[]{:S(2)}) copy-start(bf16[64,64,128]{2,1,0:T(8,128)(2,1)} %broadcast_in_dim.26.wet_left_ref.wet_right_ref.refs_0_.refs_1_.refs_4_.refs_5_.refs_6_.wet_ref) | copy-start | bytes 3145732
  73.7 29.2 %collective-permute-start.6 = (bf16[3,96,256]{2,1,0:T(8,128)(2,1)}, bf16[3,96,256]{2,1,0:T(8,128)(2,1)S(1)}, u32[]{:S(2)}, u32[]{:S(2)}) collective-permute-start(bf16[3,96,256]{2,1,0:T(8,128)(2,1)} %get-tuple-element.45), channel_id=1, source_target_pairs={{0,8},{8,16},{16,24},{24,32},{32,40},{40,48},{48,56},{56,64},{64,7... | collective-permute-start | bytes 442376 | tf_op jit(solution)/shard_map/ppermute | solution.py:607
  73.8 29.2 %collective-permute-start.7 = (bf16[3,96,256]{2,1,0:T(8,128)(2,1)}, bf16[3,96,256]{2,1,0:T(8,128)(2,1)S(1)}, u32[]{:S(2)}, u32[]{:S(2)}) collective-permute-start(bf16[3,96,256]{2,1,0:T(8,128)(2,1)} %get-tuple-element.46), channel_id=1, source_target_pairs={{0,120},{8,0},{16,8},{24,16},{32,24},{40,32},{48,40},{56,48},{64,5... | collective-permute-start | bytes 442376 | tf_op jit(solution)/shard_map/ppermute | solution.py:607
  76.3 13.6 %collective-permute-start.14 = (bf16[1,272,128]{2,1,0:T(8,128)(2,1)S(1)}, bf16[1,272,128]{2,1,0:T(8,128)(2,1)S(1)}, u32[]{:S(2)}, u32[]{:S(2)}) collective-permute-start(bf16[1,272,128]{2,1,0:T(8,128)(2,1)S(1)} %fusion.1), channel_id=1, source_target_pairs={{0,6},{1,7},{2,4},{3,5},{4,2},{5,3},{6,0},{7,1},{8,73},{9,72},{10,... | collective-permute-start | bytes 208904 | tf_op jit(solution)/shard_map/ppermute | solution.py:638
  78.7 11.3 %collective-permute-start.13 = (bf16[1,272,128]{2,1,0:T(8,128)(2,1)S(1)}, bf16[1,272,128]{2,1,0:T(8,128)(2,1)S(1)}, u32[]{:S(2)}, u32[]{:S(2)}) collective-permute-start(bf16[1,272,128]{2,1,0:T(8,128)(2,1)S(1)} %fusion.1), channel_id=1, source_target_pairs={{0,4},{1,5},{2,6},{3,7},{4,0},{5,1},{6,2},{7,3},{8,72},{9,73},{10,... | collective-permute-start | bytes 208904 | tf_op jit(solution)/shard_map/ppermute | solution.py:638
  80.1 9.8 %collective-permute-start.12 = (bf16[1,272,128]{2,1,0:T(8,128)(2,1)S(1)}, bf16[1,272,128]{2,1,0:T(8,128)(2,1)S(1)}, u32[]{:S(2)}, u32[]{:S(2)}) collective-permute-start(bf16[1,272,128]{2,1,0:T(8,128)(2,1)S(1)} %fusion.1), channel_id=1, source_target_pairs={{0,2},{1,3},{2,0},{3,1},{4,6},{5,7},{6,4},{7,5},{8,9},{9,8},{10,11... | collective-permute-start | bytes 208904 | tf_op jit(solution)/shard_map/ppermute | solution.py:638
  80.1 1.6 %copy-start.3 = (bf16[64,64,256]{2,1,0:T(8,128)(2,1)S(1)}, bf16[64,64,256]{2,1,0:T(8,128)(2,1)}, u32[]{:S(2)}) copy-start(bf16[64,64,256]{2,1,0:T(8,128)(2,1)} %cot_ref.7) | copy-start | bytes 6291460
  81.7 1.1 copy-start.5
  82.9 1.0 copy-start.7
  83.9 0.9 copy-start.10
  84.8 0.9 copy-start.13
  85.7 0.9 copy-start.15
  90.0 6.6 %collective-permute-start.17 = (bf16[1,272,128]{2,1,0:T(8,128)(2,1)S(1)}, bf16[1,272,128]{2,1,0:T(8,128)(2,1)S(1)}, u32[]{:S(2)}, u32[]{:S(2)}) collective-permute-start(bf16[1,272,128]{2,1,0:T(8,128)(2,1)S(1)} %add_convert_fusion.1), channel_id=1, source_target_pairs={{0,65},{1,64},{2,67},{3,66},{4,69},{5,68},{6,71},{7,70},{8,56},{9,... | collective-permute-start | bytes 208904 | tf_op jit(solution)/shard_map/ppermute | solution.py:638
  92.5 4.7 %collective-permute-start.16 = (bf16[1,272,128]{2,1,0:T(8,128)(2,1)S(1)}, bf16[1,272,128]{2,1,0:T(8,128)(2,1)S(1)}, u32[]{:S(2)}, u32[]{:S(2)}) collective-permute-start(bf16[1,272,128]{2,1,0:T(8,128)(2,1)S(1)} %add_convert_fusion.1), channel_id=1, source_target_pairs={{0,64},{1,65},{2,66},{3,67},{4,68},{5,69},{6,70},{7,71},{8,40},{9,... | collective-permute-start | bytes 208904 | tf_op jit(solution)/shard_map/ppermute | solution.py:638
  92.5 4.7 %collective-permute-start.15 = (bf16[1,272,128]{2,1,0:T(8,128)(2,1)S(1)}, bf16[1,272,128]{2,1,0:T(8,128)(2,1)S(1)}, u32[]{:S(2)}, u32[]{:S(2)}) collective-permute-start(bf16[1,272,128]{2,1,0:T(8,128)(2,1)S(1)} %add_convert_fusion.1), channel_id=1, source_target_pairs={{0,1},{1,0},{2,3},{3,2},{4,5},{5,4},{6,7},{7,6},{8,24},{9,25},{10,... | collective-permute-start | bytes 208904 | tf_op jit(solution)/shard_map/ppermute | solution.py:638
  97.2 9.0 %copy-start.22 = (bf16[1,272,128]{2,1,0:T(8,128)(2,1)}, bf16[1,272,128]{2,1,0:T(8,128)(2,1)S(1)}, u32[]{:S(2)}) copy-start(bf16[1,272,128]{2,1,0:T(8,128)(2,1)S(1)} %add_convert_fusion.refs_0_) | copy-start | bytes 208900
  97.2 16.7 %copy-start.11 = (bf16[16,16,256]{2,1,0:T(8,128)(2,1)S(1)}, bf16[16,16,256]{2,1,0:T(8,128)(2,1)}, u32[]{:S(2)}) copy-start(bf16[16,16,256]{2,1,0:T(8,128)(2,1)} %copy-done.9) | copy-start | bytes 393220
  97.2 16.7 %copy-start.14 = (bf16[16,16,256]{2,1,0:T(8,128)(2,1)S(1)}, bf16[16,16,256]{2,1,0:T(8,128)(2,1)}, u32[]{:S(2)}) copy-start(bf16[16,16,256]{2,1,0:T(8,128)(2,1)} %copy-done.12) | copy-start | bytes 393220
  97.2 9.0 %collective-permute-start.20 = (bf16[1,272,128]{2,1,0:T(8,128)(2,1)S(1)}, bf16[1,272,128]{2,1,0:T(8,128)(2,1)S(1)}, u32[]{:S(2)}, u32[]{:S(2)}) collective-permute-start(bf16[1,272,128]{2,1,0:T(8,128)(2,1)S(1)} %add_convert_fusion.refs_0_), channel_id=1, source_target_pairs={{0,48},{1,49},{2,50},{3,51},{4,52},{5,53},{6,54},{7,55},{8,14},{9,... | collective-permute-start | bytes 208904 | tf_op jit(solution)/shard_map/ppermute | solution.py:638
  102.3 4.7 %collective-permute-start.19 = (bf16[1,272,128]{2,1,0:T(8,128)(2,1)S(1)}, bf16[1,272,128]{2,1,0:T(8,128)(2,1)S(1)}, u32[]{:S(2)}, u32[]{:S(2)}) collective-permute-start(bf16[1,272,128]{2,1,0:T(8,128)(2,1)S(1)} %add_convert_fusion.refs_0_), channel_id=1, source_target_pairs={{0,32},{1,33},{2,34},{3,35},{4,36},{5,37},{6,38},{7,39},{8,12},{9,... | collective-permute-start | bytes 208904 | tf_op jit(solution)/shard_map/ppermute | solution.py:638
  102.6 5.0 %collective-permute-start.18 = (bf16[1,272,128]{2,1,0:T(8,128)(2,1)S(1)}, bf16[1,272,128]{2,1,0:T(8,128)(2,1)}, u32[]{:S(2)}, u32[]{:S(2)}) collective-permute-start(bf16[1,272,128]{2,1,0:T(8,128)(2,1)S(1)} %add_convert_fusion.refs_0_), channel_id=1, source_target_pairs={{0,16},{1,17},{2,18},{3,19},{4,20},{5,21},{6,22},{7,23},{8,10},{9,... | collective-permute-start | bytes 208904 | tf_op jit(solution)/shard_map/ppermute | solution.py:638
  102.9 3.3 %copy-start.17 = (bf16[3,96,256]{2,1,0:T(8,128)(2,1)}, bf16[3,96,256]{2,1,0:T(8,128)(2,1)S(1)}, u32[]{:S(2)}) copy-start(bf16[3,96,256]{2,1,0:T(8,128)(2,1)S(1)} %collective-permute-done.6.north_ref) | copy-start | bytes 442372
  103.0 3.3 %copy-start.19 = (bf16[3,96,256]{2,1,0:T(8,128)(2,1)}, bf16[3,96,256]{2,1,0:T(8,128)(2,1)S(1)}, u32[]{:S(2)}) copy-start(bf16[3,96,256]{2,1,0:T(8,128)(2,1)S(1)} %collective-permute-done.7.south_ref) | copy-start | bytes 442372
  106.3 0.7 copy-start.25
  106.9 0.6 copy-start.26
  109.3 14.4 %collective-permute-start.21 = (bf16[4,272,128]{2,1,0:T(8,128)(2,1)}, bf16[4,272,128]{2,1,0:T(8,128)(2,1)}, u32[]{:S(2)}, u32[]{:S(2)}) collective-permute-start(bf16[4,272,128]{2,1,0:T(8,128)(2,1)} %join.1.own_ref), channel_id=1, source_target_pairs={{0,8},{1,9},{2,10},{3,11},{4,12},{5,13},{6,14},{7,15},{8,0},{9,1},... | collective-permute-start | bytes 835592 | tf_op jit(solution)/shard_map/ppermute | solution.py:638
  113.9 1.6 %copy-start.4 = (bf16[64,64,256]{2,1,0:T(8,128)(2,1)S(1)}, bf16[64,64,256]{2,1,0:T(8,128)(2,1)}, u32[]{:S(2)}) copy-start(bf16[64,64,256]{2,1,0:T(8,128)(2,1)} %cot_ref.7) | copy-start | bytes 6291460
  115.5 1.1 copy-start.6
  116.7 1.0 copy-start.8
  117.7 0.9 copy-start.16
  118.6 0.9 copy-start.18
  119.6 0.9 copy-start.20

commit v5 on v4

--- a/solution.py
+++ b/solution.py
@@ -18,6 +18,9 @@
 BLOCKS = 8
 LANES = 128
 CELLS = TILE * TILE
+VMEM_BYTES = 56 * 2**20
+SPREAD_BYTES = 24 * 2**20
+SMALL_BYTES = 12 * 2**20
 
 
 def basis():
@@ -138,27 +141,46 @@
     return jnp.concatenate([wet, wet], axis=-1)
 
 
-def side_kernel(left_ref, right_ref, wet_left_ref, wet_right_ref, west_ref, east_ref):
-    lon = left_ref.shape[0]
-    low = [(left_ref[i] * both(wet_left_ref[i])).astype(F32)[:8] for i in range(lon)]
-    high = [(right_ref[i] * both(wet_right_ref[i])).astype(F32)[8:] for i in range(lon)]
-    for ref, groups in ((west_ref, pack_low(low)), (east_ref, pack_high(high))):
-        for n, tile in enumerate(packed_tiles(groups)):
+def wet_at(ref, i, start, count, channels):
+    return jnp.broadcast_to(ref[start : start + count, i : i + 1], (count, channels))
+
+
+def side_kernel(who_ref, left_ref, right_ref, wet_ref, west_ref, east_ref):
+    lon, _, channels = left_ref.shape
+    lat = wet_ref.shape[1]
+    low, high = [], []
+    for i in range(lon):
+        wet = wet_ref.at[i // TILE]
+        low.append(
+            left_ref[i].astype(F32)[:8] * wet_at(wet, i % TILE, 0, 8, channels)
+        )
+        high.append(
+            right_ref[i].astype(F32)[8:] * wet_at(wet, i % TILE, lat - 8, 8, channels)
+        )
+    send_sides(who_ref, low, high, west_ref, east_ref)
+
+
+def send_sides(who_ref, low, high, west_ref, east_ref):
+    for ref, groups, flag in ((west_ref, pack_low(low), 2), (east_ref, pack_high(high), 3)):
+        inside = jnp.where(who_ref[flag] > 0, 1.0, 0.0)
+        for n, tile in enumerate(packed_tiles([group * inside for group in groups])):
             ref[n] = tile
 
 
 def end_kernel(masks, top_ref, bottom_ref, *refs):
     west_ref, east_ref, north_ref, south_ref = refs[masks:]
-    lat = top_ref.shape[1]
+    lat, channels = top_ref.shape[1:]
     tiles = west_ref.shape[0]
     for i in range(3):
-        for out_ref, ref, n, tile, at in (
-            (north_ref, top_ref, i, 0, i),
-            (south_ref, bottom_ref, i + 1, tiles - 1, i + 1),
+        for out_ref, ref, n, tile, at, row, column in (
+            (north_ref, top_ref, i, 0, i, 0, i),
+            (south_ref, bottom_ref, i + 1, tiles - 1, i + 1, -1, TILE - 3 + i),
         ):
             cells = ref[n]
             if masks:
-                cells = cells * both(refs[0 if ref is top_ref else 1][n])
+                wet_ref = refs[0]
+                wet = wet_at(wet_ref.at[row % wet_ref.shape[0]], column, 0, lat, channels)
+                cells = (cells.astype(F32) * wet).astype(BF16)
             out_ref[i, :TILE, :] = outer(side_group(west_ref, tile, at, False), False)
             out_ref[i, TILE : TILE + lat, :] = cells
             out_ref[i, TILE + lat :, :] = outer(side_group(east_ref, tile, at, True), True)
@@ -180,6 +202,12 @@
 
 def row_of_step(ends, step, rows):
     return (rows - 1) * step if ends else 1 + step
+
+
+def cdf_and_slope(hidden):
+    cumulative = 0.5 + 0.5 * lax.erf(hidden * 0.7071067811865476)
+    bell = jnp.exp2(hidden * (hidden * (-0.5 * 1.4426950408889634)))
+    return cumulative, cumulative + (hidden * 0.3989422804014327) * bell
 
 
 def cell_kernel(ends, rows, *refs):
@@ -245,6 +273,8 @@
     def columns(i, b):
         return pad_ref[i, TILE * b : TILE * (b + 1), :]
 
+    gain, shift = gain_ref[...].astype(F32), shift_ref[...].astype(F32)
+    conv_bias, up_bias = bias_ref[...].astype(F32), up_bias_ref[...].astype(F32)
     waves = []
     for b in range(count):
         cells = patch(
@@ -253,7 +283,7 @@
             [columns(i, b + 2).astype(F32)[:8] for i in range(SPAN)],
         )
         waves.append(dot(place_ref[...], cells))
-    field = jnp.concatenate([filtered(w, taps_ref, back_ref) for w in waves]) + bias_ref[...]
+    field = jnp.concatenate([filtered(w, taps_ref, back_ref) for w in waves]) + conv_bias
 
     def by_tile(ref):
         return jnp.concatenate(
@@ -269,19 +299,12 @@
     variance = jnp.mean(centred * centred, axis=-1, keepdims=True)
     inv_std = lax.rsqrt(variance + 1e-06)
     normed = centred * inv_std
-    gain = gain_ref[...]
-    normed_out = (normed * gain + shift_ref[...]).astype(BF16)
-    hidden = dot(normed_out, up_ref[...]) + up_bias_ref[...]
-    bell = jnp.exp(-0.5 * hidden * hidden)
-    t = pl.reciprocal(1.0 + (0.3275911 * 0.7071067811865476) * jnp.abs(hidden), approx=True)
-    poly = 0.5 * 1.061405429
-    for c in (-1.453152027, 1.421413741, -0.284496736, 0.254829592):
-        poly = poly * t + 0.5 * c
-    tail = poly * t * bell
-    cumulative = jnp.where(hidden >= 0, 1.0 - tail, tail)
+    normed_out = (normed * gain + shift).astype(BF16)
+    hidden = dot(normed_out, up_ref[...]) + up_bias
+    act_grad = dot_cols(masked_grad, down_ref[...])
+    cumulative, slope = cdf_and_slope(hidden)
     activated = (hidden * cumulative).astype(BF16)
-    act_grad = dot_cols(masked_grad, down_ref[...])
-    hidden_grad = (act_grad * (cumulative + hidden * (bell * 0.3989422804014327))).astype(BF16)
+    hidden_grad = (act_grad * slope).astype(BF16)
     up_part = dot_rows(normed_out, hidden_grad)
     down_part = dot_rows(activated, masked_grad)
     at = 0
@@ -301,20 +324,15 @@
     product_mean = jnp.mean(product * gain, axis=-1, keepdims=True)
     wide_grad = inv_std * (scaled - scaled_mean - normed * product_mean)
     field_grad = wide_grad.astype(BF16)
-    for n in range(count):
-        fg_ref[:, TILE * n : TILE * (n + 1), :] = field_grad[CELLS * n : CELLS * (n + 1)].reshape(
-            TILE, TILE, channels
-        )
+    ripples = []
+    for b in range(count):
+        own = field_grad[CELLS * b : CELLS * (b + 1)]
+        fg_ref[:, TILE * b : TILE * (b + 1), :] = own.reshape(TILE, TILE, channels)
+        ripples.append(dot(own_ref[...], own))
+    last = CELLS * (count - 1)
     lows = [wide_grad[TILE * i : TILE * i + 8] for i in range(TILE)]
-    start = CELLS * (count - 1)
-    highs = [wide_grad[start + TILE * i + 8 : start + TILE * i + TILE] for i in range(TILE)]
-
-    for out_ref, packed in ((to_west_ref, pack_low(lows)), (to_east_ref, pack_high(highs))):
-        for n, tile in enumerate(packed_tiles(packed)):
-            out_ref[n] = tile
-    ripples = [
-        dot(own_ref[...], field_grad[CELLS * n : CELLS * (n + 1)]) for n in range(count)
-    ]
+    highs = [wide_grad[last + TILE * i + 8 : last + TILE * (i + 1)] for i in range(TILE)]
+    send_sides(who_ref, lows, highs, to_west_ref, to_east_ref)
     for r in range(0, HALF, 8):
         p1, p2, p3 = 0.0, 0.0, 0.0
         for wave, ripple in zip(waves, ripples):
@@ -349,6 +367,12 @@
         for n, ref in enumerate((keep_ref, send_ref)):
             for k in range(BLOCKS // 2):
                 ref[k] = sum_ref[block_rows(who_ref[n], k, ref.shape[1]), :]
+
+
+def fold_kernel(held_ref, come_ref, own_ref, *refs):
+    own_ref[...] = held_ref[:1] + come_ref[:1]
+    for n, ref in enumerate(refs, start=1):
+        ref[...] = (held_ref[n : n + 1] + come_ref[n : n + 1]).astype(BF16)
 
 
 def join_kernel(*refs):
@@ -428,43 +452,40 @@
 IN_VMEM = pl.BlockSpec(memory_space=pltpu.VMEM)
 
 
-def sides(x, wet):
+def sides(who, x, wet):
     lon, lat, channels = x.shape
-
-    def specs(depth):
-        return [
-            pl.BlockSpec((lon, TILE, depth), lambda i: (0, 0, 0)),
-            pl.BlockSpec((lon, TILE, depth), lambda i: (0, lat // TILE - 1, 0)),
-        ]
-
     shapes = [shape_of((lon // 4, TILE, channels), BF16)] * 2
     return pl.pallas_call(
         side_kernel,
         grid=(1,),
-        in_specs=specs(channels) + specs(LANES),
+        in_specs=[
+            IN_SMEM,
+            pl.BlockSpec((lon, TILE, channels), lambda i: (0, 0, 0)),
+            pl.BlockSpec((lon, TILE, channels), lambda i: (0, lat // TILE - 1, 0)),
+            whole(*wet.shape),
+        ],
         out_specs=[whole(*s.shape) for s in shapes],
         out_shape=shapes,
+        compiler_params=pltpu.CompilerParams(vmem_limit_bytes=SMALL_BYTES),
         name="sides",
-    )(x, x, wet, wet)
+    )(who, x, x, wet)
 
 
 def ends(x, wet, halos):
     lon, lat, channels = x.shape
-
-    def specs(depth):
-        return [
-            pl.BlockSpec((4, lat, depth), lambda i: (0, 0, 0)),
-            pl.BlockSpec((4, lat, depth), lambda i: (lon // 4 - 1, 0, 0)),
-        ]
-
-    masks = [] if wet is None else [wet, wet]
+    masks = [] if wet is None else [wet]
     shapes = [shape_of((3, lat + 2 * TILE, channels), BF16)] * 2
     return pl.pallas_call(
         functools.partial(end_kernel, len(masks)),
         grid=(1,),
-        in_specs=specs(channels) + specs(LANES)[: len(masks)] + [whole(*h.shape) for h in halos],
+        in_specs=[
+            pl.BlockSpec((4, lat, channels), lambda i: (0, 0, 0)),
+            pl.BlockSpec((4, lat, channels), lambda i: (lon // 4 - 1, 0, 0)),
+        ]
+        + [whole(*m.shape) for m in (*masks, *halos)],
         out_specs=[whole(*s.shape) for s in shapes],
         out_shape=shapes,
+        compiler_params=pltpu.CompilerParams(vmem_limit_bytes=SMALL_BYTES),
         name="ends",
     )(x, x, *masks, *halos)
 
@@ -522,12 +543,24 @@
         out_shape=out_shape,
         scratch_shapes=scratch,
         input_output_aliases=aliases,
-        compiler_params=pltpu.CompilerParams(vmem_limit_bytes=56 * 2**20),
+        compiler_params=pltpu.CompilerParams(vmem_limit_bytes=VMEM_BYTES),
         cost_estimate=pl.CostEstimate(
             flops=10 * 10**9, bytes_accessed=8 * 2**20, transcendentals=0
         ),
         name="end_cells" if at_ends else "inner_cells",
     )(*operands)
+
+
+def fold(held, come):
+    block = (1,) + held.shape[1:]
+    return pl.pallas_call(
+        fold_kernel,
+        in_specs=[IN_VMEM] * 2,
+        out_specs=[IN_VMEM] * held.shape[0],
+        out_shape=[shape_of(block)] + [shape_of(block, BF16)] * (held.shape[0] - 1),
+        compiler_params=pltpu.CompilerParams(vmem_limit_bytes=SMALL_BYTES),
+        name="fold",
+    )(held, come)
 
 
 def join(parts):
@@ -536,6 +569,7 @@
         in_specs=[IN_VMEM] * len(parts),
         out_specs=IN_VMEM,
         out_shape=shape_of((len(parts),) + parts[0].shape[1:], parts[0].dtype),
+        compiler_params=pltpu.CompilerParams(vmem_limit_bytes=SMALL_BYTES),
         name="join",
     )(*parts)
 
@@ -548,6 +582,7 @@
         out_specs=[IN_VMEM] * len(shapes),
         out_shape=[shape_of(s) for s in shapes],
         scratch_shapes=[pltpu.VMEM((BLOCKS * own.shape[1], LANES), F32)],
+        compiler_params=pltpu.CompilerParams(vmem_limit_bytes=SMALL_BYTES),
         name="finish",
     )(who, own, other)
 
@@ -578,7 +613,7 @@
         out_specs=row_of(channels),
         out_shape=shape_of((lon, lat, channels)),
         input_output_aliases={} if out is None else {12: 0},
-        compiler_params=pltpu.CompilerParams(vmem_limit_bytes=40 * 2**20),
+        compiler_params=pltpu.CompilerParams(vmem_limit_bytes=SPREAD_BYTES),
         cost_estimate=pl.CostEstimate(
             flops=4 * 10**9, bytes_accessed=4 * 2**20, transcendentals=0
         ),
@@ -594,13 +629,8 @@
     return [(i, (i + step) % size) for i in range(size)]
 
 
-def line(axis, step):
-    size = lax.axis_size(axis)
-    return [(i, i + step) for i in range(size) if 0 <= i + step < size]
-
-
 def across_lat(west, east):
-    return [lax.ppermute(east, "gy", line("gy", 1)), lax.ppermute(west, "gy", line("gy", -1))]
+    return [lax.ppermute(east, "gy", ring("gy", 1)), lax.ppermute(west, "gy", ring("gy", -1))]
 
 
 def across_lon(north, south):
@@ -628,7 +658,8 @@
     i, j = lax.axis_index("gx"), lax.axis_index("gy")
     core, x, y = i % 2, i // 2 % 4, j // 2
     own, other = jnp.where(core == 0, x, 4 + y), jnp.where(core == 0, 4 + y, x)
-    return jnp.stack([own, other]).astype(jnp.int32)
+    west, east = j > 0, j < lax.axis_size("gy") - 1
+    return jnp.stack([own, other, west.astype(jnp.int32), east.astype(jnp.int32)]).astype(jnp.int32)
 
 
 def summed_blocks(keep, send):
@@ -641,10 +672,8 @@
         parts = [part.astype(F32) for part in parts]
         return (parts[0] + parts[1]) + (parts[2] + parts[3])
 
-    held = keep + move(send, "core", 1)
-    held = added(
-        [held[:1]] + [move(held[n : n + 1].astype(BF16), "a", n) for n in range(1, 4)]
-    )
+    held, *parts = fold(keep, move(send, "core", 1))
+    held = added([held] + [move(part, "a", n) for n, part in enumerate(parts, start=1)])
     for stage in ("b", "c"):
         held = held.astype(BF16)
         held = added([held] + [move(held, stage, n) for n in range(1, 4)])
@@ -659,20 +688,18 @@
 ):
     lon, lat, channels = inputs.shape
     units = up_weight.shape[1]
+    wet_rows = wet_mask.astype(F32).reshape(lon // TILE, TILE, lat).transpose(0, 2, 1)
     wet = jnp.broadcast_to(wet_mask.astype(BF16)[:, :, None], (lon, lat, LANES))
-    halos = across_lat(*sides(inputs, wet))
-    end_halos = across_lon(*ends(inputs, wet, halos))
+    who = places()
+    halos = across_lat(*sides(who, inputs, wet_rows))
+    end_halos = across_lon(*ends(inputs, wet_rows, halos))
     taps = jnp.dot(
         tables()["taps"], kernel.astype(F32), precision=lax.Precision.HIGHEST,
         preferred_element_type=F32,
     )
-    who = places()
-
-    def row(x):
-        return x.astype(F32)[None, :]
-
     params = (
-        row(conv_bias), row(norm_gain), row(norm_shift), up_weight, row(up_bias), down_weight
+        conv_bias[None, :], norm_gain[None, :], norm_shift[None, :], up_weight, up_bias[None, :],
+        down_weight,
     )
     first = (who, inputs, halos, cotangent, wet, taps[: 3 * HALF], params)
     inner = cell_pass(*first)

time: 127 us -> 97 us (0.76)
  Pallas kernels: 53.4 us -> 42.3 us
  local copies, waits for them, and re-layouts: 20 us -> 10.4 us
  other arithmetic: 6.81 us -> 1.05 us
  starting transfers between devices: 41.7 us -> 39 us
    unnamed x66 -> x42, local copies, waits for them, and re-layouts: 16.4 us -> 5.52 us
    pallas_call x2, Pallas kernels: 3.87 us -> 0.14 us  [ends(): pl.pallas_call(functools.partial(end_kernel, len(masks)), grid=(1,), in_s...]
    pallas_call x2, Pallas kernels: 30.4 us -> 26.7 us  [cell_pass(): pl.pallas_call(functools.partial(cell_kernel, at_ends, rows), grid=(2,),...]
    another operation x2 -> x1, other arithmetic: 2.66 us -> 0.08 us  [places(): jnp.stack([own, other, west.astype(jnp.int32), east.astype(jnp.int32)])]
    ppermute x4, starting transfers between devices: 11.1 us -> 8.66 us  [the longest x2 6.06 us: across_lat(): lax.ppermute(west, 'gy', ring('gy', -1))]
    broadcast_in_dim x0 -> x4, local copies, waits for them, and re-layouts: none -> 2.28 us  [the longest x1 0.58 us: local(): up_bias[None, :]]
    broadcast_in_dim x4 -> x0, other arithmetic: 2.27 us -> none  [row(): return x.astype(F32)[None, :]]
    ppermute x14, starting transfers between devices: 27.9 us -> 25.9 us  [move(): return lax.ppermute(x, AXES, swapped(mesh_shape, stage, step))]
  transfers between devices with their start and end apart: 22 -> 22, of which waited for: 3 -> 3; matrix products, arithmetic and copies ran while one was open for 7% -> 6% of each run, Pallas kernels for 23% -> 26%
where the time goes in v5:
time: 97 us; the launch traced here: 96.7 us
  Pallas kernels  42.3 us (44%)
  starting transfers between devices  39 us (40%)
  local copies, waits for them, and re-layouts  10.4 us (11%)
  waiting for transfers between devices  2.27 us (2%)
  other arithmetic  1.05 us (1%)
    pallas_call x2, Pallas kernels, cell_pass(): pl.pallas_call(functools.partial(cell_kernel, at_ends, rows), grid=(2,),...  26.7 us
    ppermute x14, starting transfers between devices, move(): return lax.ppermute(x, AXES, swapped(mesh_shape, stage, step))  25.9 us
    pallas_call x4, Pallas kernels, spread_pass(): pl.pallas_call(functools.partial(spread_kernel, at, rows), grid=(1,), in_...  12.9 us
    ppermute x2, starting transfers between devices, across_lat(): lax.ppermute(west, 'gy', ring('gy', -1))  6.06 us
    unnamed x42, local copies, waits for them, and re-layouts  5.52 us
    ppermute x2, starting transfers between devices, across_lon(): lax.ppermute(south, 'gx', ring('gx', 1))  2.71 us
    ppermute x2, starting transfers between devices, across_lat(): lax.ppermute(east, 'gy', ring('gy', 1))  2.6 us
  transfers between devices with their start and end apart: 22, of which 3 were waited for; matrix products, arithmetic and copies ran while one was open for 6% of the time, Pallas kernels for 26%

profile of v5, /device:TPU:1, one launch (start us, length us, event | category | flops | bytes accessed | tf_op | source)
XLA Modules:
  0.0 96.7 jit_solution(9475946616566606570)
XLA Ops:
  0.6 0.0 copy-start
  0.7 0.8 fusion.1
  1.5 0.1 copy.29
  1.6 0.1 pad_add_fusion.who_ref.refs_0_
  1.7 1.6 %copy-done.4 = bf16[64,64,256]{2,1,0:T(8,128)(2,1)S(1)} copy-done((bf16[64,64,256]{2,1,0:T(8,128)(2,1)S(1)}, bf16[64,64,256]{2,1,0:T(8,128)(2,1)}, u32[]{:S(2)}) %copy-start.4) | copy-done | bytes 2097176
  3.3 0.8 sides.1
  4.2 2.5 %collective-permute-start = (bf16[16,16,256]{2,1,0:T(8,128)(2,1)S(1)}, bf16[16,16,256]{2,1,0:T(8,128)(2,1)S(1)}, u32[]{:S(2)}, u32[]{:S(2)}) collective-permute-start(bf16[16,16,256]{2,1,0:T(8,128)(2,1)S(1)} %get-tuple-element.36), channel_id=1, source_target_pairs={{0,1},{1,2},{2,3},{3,4},{4,5},{5,6},{6,7},{7,0},{8,9},{9,10},{10,1... | collective-permute-start | bytes 393224 | tf_op jit(solution)/shard_map/ppermute | solution.py:633
  6.7 2.5 %collective-permute-start.1 = (bf16[16,16,256]{2,1,0:T(8,128)(2,1)S(1)}, bf16[16,16,256]{2,1,0:T(8,128)(2,1)S(1)}, u32[]{:S(2)}, u32[]{:S(2)}) collective-permute-start(bf16[16,16,256]{2,1,0:T(8,128)(2,1)S(1)} %get-tuple-element.37), channel_id=1, source_target_pairs={{0,7},{1,0},{2,1},{3,2},{4,3},{5,4},{6,5},{7,6},{8,15},{9,8},{10,9... | collective-permute-start | bytes 393224 | tf_op jit(solution)/shard_map/ppermute | solution.py:633
  9.2 0.8 fusion.2
  10.0 0.0 copy-start.18
  10.0 0.0 copy-start.19
  10.0 0.0 copy-start.20
  10.0 0.0 copy-start.15
  10.0 0.0 copy-start.5
  10.1 1.0 %fusion = (f32[768,256]{1,0:T(8,128)S(1)}, f32[768,256]{1,0:T(8,128)}) fusion(f32[1536,256]{1,0:T(8,128)S(1)} %fusion.2), kind=kLoop, calls=%fused_computation.4 | loop fusion | bytes 3145728 | tf_op jit(solution)/shard_map/slice | solution.py:715
  11.0 0.6 broadcast_in_dim.19.refs_15_
  11.6 0.6 broadcast_in_dim.20.refs_16_
  12.2 0.6 broadcast_in_dim.21.refs_17_
  12.8 0.6 broadcast_in_dim.22.refs_19_
  13.3 0.0 collective-permute-done.refs_1_.refs_7_
  13.3 0.5 collective-permute-done.1.refs_2_.refs_8_
  13.9 0.1 ends.2
  14.0 0.5 copy-done.11
  14.5 2.6 %collective-permute-start.2 = (bf16[3,96,256]{2,1,0:T(8,128)(2,1)S(1)}, bf16[3,96,256]{2,1,0:T(8,128)(2,1)S(1)}, u32[]{:S(2)}, u32[]{:S(2)}) collective-permute-start(bf16[3,96,256]{2,1,0:T(8,128)(2,1)S(1)} %get-tuple-element.38), channel_id=1, source_target_pairs={{0,8},{8,16},{16,24},{24,32},{32,40},{40,48},{48,56},{56,64},{64,7... | collective-permute-start | bytes 442376 | tf_op jit(solution)/shard_map/ppermute | solution.py:637
  17.2 0.0 collective-permute-start.3
  17.2 1.6 %broadcast_in_dim.18.refs_4_.refs_5_.refs_6_.wet_ref = bf16[64,64,128]{2,1,0:T(8,128)(2,1)} broadcast(bf16[64,64]{1,0:T(8,128)(2,1)S(1)} %get-tuple-element.67), dimensions={0,1} | broadcast | bytes 1056768 | tf_op jit(solution)/shard_map/broadcast_in_dim | solution.py:692
  18.7 12.5 %inner_cells.1 = (bf16[64,64,256]{2,1,0:T(8,128)(2,1)}, bf16[16,16,256]{2,1,0:T(8,128)(2,1)}, bf16[16,16,256]{2,1,0:T(8,128)(2,1)}, f32[2176,128]{1,0:T(8,128)},...) custom-call(s32[4]{0:T(128)} %copy-done.12, bf16[64,64,256]{2,1,0:T(8,128)(2,1)} %refs_3_.3, bf16[64,64,256]{2,1,0:T(8,128)(2,1)} %refs_3_.3, ...), custom_call_target="tpu_custom_call" | custom-call | flops 10000000000 | bytes 8388608 | tf_op jit(solution)/shard_map/inner_cells/pallas_call | solution.py:538
  31.3 0.0 collective-permute-done.2.refs_21_
  31.3 0.0 copy-start.16
  31.3 0.0 copy-start.17
  31.3 0.6 copy-done.16
  32.0 0.0 copy-done.17
  32.0 14.2 %end_cells.1 = (bf16[64,64,256]{2,1,0:T(8,128)(2,1)}, bf16[16,16,256]{2,1,0:T(8,128)(2,1)}, bf16[16,16,256]{2,1,0:T(8,128)(2,1)}, f32[4,272,128]{2,1,0:T(8,128)}, f32[4,272,128]{2,1,0:T(8,128)}) custom-call(s32[4]{0:T(128)} %copy-done.12, bf16[64,64,256]{2,1,0:T(8,128)(2,1)} %refs_3_.3, ...), custom_call_target="tpu_custom_call", output_to_operand_aliasing={{0}: (23, {}), {1}: (24, {}), {2}: (25, {})} | custom-call | flops 10000000000 | bytes 8388608 | tf_op jit(solution)/shard_map/end_cells/pallas_call | solution.py:538
  46.2 4.3 %collective-permute-start.8 = (f32[4,272,128]{2,1,0:T(8,128)}, f32[4,272,128]{2,1,0:T(8,128)S(1)}, u32[]{:S(2)}, u32[]{:S(2)}) collective-permute-start(f32[4,272,128]{2,1,0:T(8,128)} %get-tuple-element.52), channel_id=1, source_target_pairs={{0,8},{1,9},{2,10},{3,11},{4,12},{5,13},{6,14},{7,15},{8,0},{9,1},... | collective-permute-start | bytes 1671176 | tf_op jit(solution)/shard_map/ppermute | solution.py:669
  50.5 0.1 collective-permute-start.4
  50.6 3.5 %collective-permute-start.5 = (bf16[16,16,256]{2,1,0:T(8,128)(2,1)}, bf16[16,16,256]{2,1,0:T(8,128)(2,1)S(1)}, u32[]{:S(2)}, u32[]{:S(2)}) collective-permute-start(bf16[16,16,256]{2,1,0:T(8,128)(2,1)} %get-tuple-element.48), channel_id=1, source_target_pairs={{0,7},{1,0},{2,1},{3,2},{4,3},{5,4},{6,5},{7,6},{8,15},{9,8},{10,9... | collective-permute-start | bytes 393224 | tf_op jit(solution)/shard_map/ppermute | solution.py:633
  54.1 1.1 %copy-done.9 = f32[4,272,128]{2,1,0:T(8,128)S(1)} copy-done((f32[4,272,128]{2,1,0:T(8,128)S(1)}, f32[4,272,128]{2,1,0:T(8,128)}, u32[]{:S(2)}) %copy-start.9) | copy-done | bytes 557080
  55.2 0.1 fold.1
  55.2 0.1 collective-permute-start.9
  55.3 2.3 %collective-permute-start.10 = (bf16[1,272,128]{2,1,0:T(8,128)(2,1)S(1)}, bf16[1,272,128]{2,1,0:T(8,128)(2,1)S(1)}, u32[]{:S(2)}, u32[]{:S(2)}) collective-permute-start(bf16[1,272,128]{2,1,0:T(8,128)(2,1)S(1)} %get-tuple-element.55), channel_id=1, source_target_pairs={{0,32},{1,33},{2,34},{3,35},{4,36},{5,37},{6,38},{7,39},{8,12},{9,... | collective-permute-start | bytes 208904 | tf_op jit(solution)/shard_map/ppermute | solution.py:669
  57.6 1.6 %collective-permute-start.11 = (bf16[1,272,128]{2,1,0:T(8,128)(2,1)S(1)}, bf16[1,272,128]{2,1,0:T(8,128)(2,1)S(1)}, u32[]{:S(2)}, u32[]{:S(2)}) collective-permute-start(bf16[1,272,128]{2,1,0:T(8,128)(2,1)S(1)} %get-tuple-element.56), channel_id=1, source_target_pairs={{0,48},{1,49},{2,50},{3,51},{4,52},{5,53},{6,54},{7,55},{8,14},{9,... | collective-permute-start | bytes 208904 | tf_op jit(solution)/shard_map/ppermute | solution.py:669
  59.2 0.0 collective-permute-done.4.refs_0_.north_ref.west_ref
  59.2 0.0 collective-permute-done.5.refs_1_.south_ref.east_ref
  59.2 1.6 %copy-done.1 = bf16[64,64,256]{2,1,0:T(8,128)(2,1)S(1)} copy-done((bf16[64,64,256]{2,1,0:T(8,128)(2,1)S(1)}, bf16[64,64,256]{2,1,0:T(8,128)(2,1)}, u32[]{:S(2)}) %copy-start.1) | copy-done | bytes 2097176
  60.8 0.1 collective-permute-start.6
  60.9 1.7 %collective-permute-start.7 = (bf16[3,96,256]{2,1,0:T(8,128)(2,1)S(1)}, bf16[3,96,256]{2,1,0:T(8,128)(2,1)S(1)}, u32[]{:S(2)}, u32[]{:S(2)}) collective-permute-start(bf16[3,96,256]{2,1,0:T(8,128)(2,1)S(1)} %get-tuple-element.50), channel_id=1, source_target_pairs={{0,120},{8,0},{16,8},{24,16},{32,24},{40,32},{48,40},{56,48},{64,5... | collective-permute-start | bytes 442376 | tf_op jit(solution)/shard_map/ppermute | solution.py:637
  62.6 0.0 collective-permute-done.9
  62.6 0.0 collective-permute-done.10
  62.7 1.4 %collective-permute-start.14 = (bf16[1,272,128]{2,1,0:T(8,128)(2,1)S(1)}, bf16[1,272,128]{2,1,0:T(8,128)(2,1)S(1)}, u32[]{:S(2)}, u32[]{:S(2)}) collective-permute-start(bf16[1,272,128]{2,1,0:T(8,128)(2,1)S(1)} %add_convert_fusion.2), channel_id=1, source_target_pairs={{0,6},{1,7},{2,4},{3,5},{4,2},{5,3},{6,0},{7,1},{8,73},{9,72},{10,... | collective-permute-start | bytes 208904 | tf_op jit(solution)/shard_map/ppermute | solution.py:669
  64.1 2.1 %collective-permute-start.13 = (bf16[1,272,128]{2,1,0:T(8,128)(2,1)S(1)}, bf16[1,272,128]{2,1,0:T(8,128)(2,1)S(1)}, u32[]{:S(2)}, u32[]{:S(2)}) collective-permute-start(bf16[1,272,128]{2,1,0:T(8,128)(2,1)S(1)} %add_convert_fusion.2), channel_id=1, source_target_pairs={{0,4},{1,5},{2,6},{3,7},{4,0},{5,1},{6,2},{7,3},{8,72},{9,73},{10,... | collective-permute-start | bytes 208904 | tf_op jit(solution)/shard_map/ppermute | solution.py:669
  66.2 3.2 %spread_pass.4.out_refs_0_ = f32[64,64,256]{2,1,0:T(8,128)} custom-call(bf16[64,64,256]{2,1,0:T(8,128)(2,1)S(1)} %copy-done.2, bf16[64,64,256]{2,1,0:T(8,128)(2,1)S(1)} %copy-done.2, bf16[64,64,256]{2,1,0:T(8,128)(2,1)S(1)} %copy-done.2, bf16[16,16,256]{2,1,0:T(8,128)(2,1)S(1)} %collective-permute-done.4.refs_0_.north_ref.west_ref, ...), custom_call_target="tpu_custom_call" | custom-call | flops 4000000000 | bytes 4194304 | tf_op jit(solution)/shard_map/spread_pass/pallas_call | solution.py:601
  69.4 0.9 collective-permute-done.13
  70.4 4.3 %collective-permute-start.17 = (bf16[1,272,128]{2,1,0:T(8,128)(2,1)S(1)}, bf16[1,272,128]{2,1,0:T(8,128)(2,1)S(1)}, u32[]{:S(2)}, u32[]{:S(2)}) collective-permute-start(bf16[1,272,128]{2,1,0:T(8,128)(2,1)S(1)} %add_convert_fusion.1), channel_id=1, source_target_pairs={{0,65},{1,64},{2,67},{3,66},{4,69},{5,68},{6,71},{7,70},{8,56},{9,... | collective-permute-start | bytes 208904 | tf_op jit(solution)/shard_map/ppermute | solution.py:669
  74.7 0.7 collective-permute-start.15
  75.4 3.2 %spread_pass.5.out_refs_0_ = f32[64,64,256]{2,1,0:T(8,128)} custom-call(bf16[64,64,256]{2,1,0:T(8,128)(2,1)S(1)} %copy-done.2, bf16[64,64,256]{2,1,0:T(8,128)(2,1)S(1)} %copy-done.2, bf16[64,64,256]{2,1,0:T(8,128)(2,1)S(1)} %copy-done.2, bf16[16,16,256]{2,1,0:T(8,128)(2,1)S(1)} %collective-permute-done.4.refs_0_.north_ref.west_ref, ...), custom_call_target="tpu_custom_call", output_to_operand_aliasing={{}: (12, {})} | custom-call | flops 4000000000 | bytes 4194304 | tf_op jit(solution)/shard_map/spread_pass/pallas_call | solution.py:601
  78.6 0.8 collective-permute-done.16
  79.4 1.8 %collective-permute-start.20 = (bf16[1,272,128]{2,1,0:T(8,128)(2,1)S(1)}, bf16[1,272,128]{2,1,0:T(8,128)(2,1)S(1)}, u32[]{:S(2)}, u32[]{:S(2)}) collective-permute-start(bf16[1,272,128]{2,1,0:T(8,128)(2,1)S(1)} %add_convert_fusion.refs_0_), channel_id=1, source_target_pairs={{0,48},{1,49},{2,50},{3,51},{4,52},{5,53},{6,54},{7,55},{8,14},{9,... | collective-permute-start | bytes 208904 | tf_op jit(solution)/shard_map/ppermute | solution.py:669
  81.2 0.7 collective-permute-start.19
  81.9 0.9 collective-permute-start.18
  82.8 3.2 %spread_pass.6.out_refs_0_ = f32[64,64,256]{2,1,0:T(8,128)} custom-call(bf16[64,64,256]{2,1,0:T(8,128)(2,1)S(1)} %copy-done.2, bf16[64,64,256]{2,1,0:T(8,128)(2,1)S(1)} %copy-done.2, bf16[64,64,256]{2,1,0:T(8,128)(2,1)S(1)} %copy-done.2, bf16[3,96,256]{2,1,0:T(8,128)(2,1)S(1)} %collective-permute-done.6.north_ref, ...), custom_call_target="tpu_custom_call", output_to_operand_aliasing={{}: (12, {})} | custom-call | flops 4000000000 | bytes 4194304 | tf_op jit(solution)/shard_map/spread_pass/pallas_call | solution.py:601
  86.0 0.0 copy-start.13
  86.0 5.8 %collective-permute-start.21 = (bf16[4,272,128]{2,1,0:T(8,128)(2,1)S(1)}, bf16[4,272,128]{2,1,0:T(8,128)(2,1)S(1)}, u32[]{:S(2)}, u32[]{:S(2)}) collective-permute-start(bf16[4,272,128]{2,1,0:T(8,128)(2,1)S(1)} %join.1.own_ref), channel_id=1, source_target_pairs={{0,8},{1,9},{2,10},{3,11},{4,12},{5,13},{6,14},{7,15},{8,0},{9,1},... | collective-permute-start | bytes 835592 | tf_op jit(solution)/shard_map/ppermute | solution.py:669
  91.8 3.2 %spread_pass.7 = f32[64,64,256]{2,1,0:T(8,128)} custom-call(bf16[64,64,256]{2,1,0:T(8,128)(2,1)S(1)} %copy-done.2, bf16[64,64,256]{2,1,0:T(8,128)(2,1)S(1)} %copy-done.2, bf16[64,64,256]{2,1,0:T(8,128)(2,1)S(1)} %copy-done.2, bf16[3,96,256]{2,1,0:T(8,128)(2,1)S(1)} %collective-permute-done.6.north_ref, ...), custom_call_target="tpu_custom_call", output_to_operand_aliasing={{}: (12, {})} | custom-call | flops 4000000000 | bytes 4194304 | tf_op jit(solution)/shard_map/spread_pass/pallas_call | solution.py:601
  95.1 1.7 %finish.1 = (f32[49,256]{1,0:T(8,128)}, f32[1,256]{1,0:T(1,128)}, f32[1,256]{1,0:T(1,128)}, f32[1,256]{1,0:T(1,128)}, f32[256,512]{1,0:T(8,128)}, /*index=5*/f32[1,512]{1,0:T(1,128)}, f32[512,256]{1,0:T(8,128)}) custom-call(s32[4]{0:T(128)S(1)} %copy-done.13, bf16[4,272,128]{2,1,0:T(8,128)(2,1)S(1)} %join.1.own_ref, ...), custom_call_target="tpu_custom_call" | custom-call | tf_op jit(solution)/shard_map/finish/pallas_call | solution.py:579
  (47 shorter events, 0.3 us)
Async XLA Ops:
  0.6 8.6 %copy-start = (bf16[49,256]{1,0:T(8,128)(2,1)S(1)}, bf16[49,256]{1,0:T(8,128)(2,1)}, u32[]{:S(2)}) copy-start(bf16[49,256]{1,0:T(8,128)(2,1)} %param.18) | copy-start | bytes 75268
  1.7 2.4 %copy-start.12 = (s32[4]{0:T(128)}, s32[4]{0:T(128)S(1)}, u32[]{:S(2)}) copy-start(s32[4]{0:T(128)S(1)} %pad_add_fusion.who_ref.refs_0_) | copy-start | bytes 52
  1.7 1.6 %copy-start.4 = (bf16[64,64,256]{2,1,0:T(8,128)(2,1)S(1)}, bf16[64,64,256]{2,1,0:T(8,128)(2,1)}, u32[]{:S(2)}) copy-start(bf16[64,64,256]{2,1,0:T(8,128)(2,1)} %refs_3_.3) | copy-start | bytes 6291460
  3.3 5.9 %copy-start.14 = (f32[1536,49]{1,0:T(8,128)S(1)}, f32[1536,49]{1,0:T(8,128)}, u32[]{:S(2)}) copy-start(f32[1536,49]{1,0:T(8,128)} %constant.63.clone) | copy-start | bytes 903172
  4.2 9.2 %collective-permute-start = (bf16[16,16,256]{2,1,0:T(8,128)(2,1)S(1)}, bf16[16,16,256]{2,1,0:T(8,128)(2,1)S(1)}, u32[]{:S(2)}, u32[]{:S(2)}) collective-permute-start(bf16[16,16,256]{2,1,0:T(8,128)(2,1)S(1)} %get-tuple-element.36), channel_id=1, source_target_pairs={{0,1},{1,2},{2,3},{3,4},{4,5},{5,6},{6,7},{7,0},{8,9},{9,10},{10,1... | collective-permute-start | bytes 393224 | tf_op jit(solution)/shard_map/ppermute | solution.py:633
  6.7 7.2 %collective-permute-start.1 = (bf16[16,16,256]{2,1,0:T(8,128)(2,1)S(1)}, bf16[16,16,256]{2,1,0:T(8,128)(2,1)S(1)}, u32[]{:S(2)}, u32[]{:S(2)}) collective-permute-start(bf16[16,16,256]{2,1,0:T(8,128)(2,1)S(1)} %get-tuple-element.37), channel_id=1, source_target_pairs={{0,7},{1,0},{2,1},{3,2},{4,3},{5,4},{6,5},{7,6},{8,15},{9,8},{10,9... | collective-permute-start | bytes 393224 | tf_op jit(solution)/shard_map/ppermute | solution.py:633
  10.0 1.1 %copy-start.18 = (bf16[256]{0:T(256)(128)(2,1)S(1)}, bf16[256]{0:T(256)(128)(2,1)}, u32[]{:S(2)}) copy-start(bf16[256]{0:T(256)(128)(2,1)} %param.19) | copy-start | bytes 1540
  10.0 1.6 %copy-start.19 = (bf16[256]{0:T(256)(128)(2,1)S(1)}, bf16[256]{0:T(256)(128)(2,1)}, u32[]{:S(2)}) copy-start(bf16[256]{0:T(256)(128)(2,1)} %param.20) | copy-start | bytes 1540
  10.0 2.2 %copy-start.20 = (bf16[256]{0:T(256)(128)(2,1)S(1)}, bf16[256]{0:T(256)(128)(2,1)}, u32[]{:S(2)}) copy-start(bf16[256]{0:T(256)(128)(2,1)} %param.21) | copy-start | bytes 1540
  10.0 2.7 %copy-start.15 = (bf16[512]{0:T(512)(128)(2,1)S(1)}, bf16[512]{0:T(512)(128)(2,1)}, u32[]{:S(2)}) copy-start(bf16[512]{0:T(512)(128)(2,1)} %param.23) | copy-start | bytes 3076
  10.0 3.8 %copy-start.5 = (bf16[64,64,256]{2,1,0:T(8,128)(2,1)S(1)}, bf16[64,64,256]{2,1,0:T(8,128)(2,1)}, u32[]{:S(2)}) copy-start(bf16[64,64,256]{2,1,0:T(8,128)(2,1)} %refs_3_.3) | copy-start | bytes 6291460
  13.3 0.7 copy-start.10
  13.9 0.7 copy-start.11
  14.5 16.8 %collective-permute-start.2 = (bf16[3,96,256]{2,1,0:T(8,128)(2,1)S(1)}, bf16[3,96,256]{2,1,0:T(8,128)(2,1)S(1)}, u32[]{:S(2)}, u32[]{:S(2)}) collective-permute-start(bf16[3,96,256]{2,1,0:T(8,128)(2,1)S(1)} %get-tuple-element.38), channel_id=1, source_target_pairs={{0,8},{8,16},{16,24},{24,32},{32,40},{40,48},{48,56},{56,64},{64,7... | collective-permute-start | bytes 442376 | tf_op jit(solution)/shard_map/ppermute | solution.py:637
  17.2 14.1 %collective-permute-start.3 = (bf16[3,96,256]{2,1,0:T(8,128)(2,1)S(1)}, bf16[3,96,256]{2,1,0:T(8,128)(2,1)S(1)}, u32[]{:S(2)}, u32[]{:S(2)}) collective-permute-start(bf16[3,96,256]{2,1,0:T(8,128)(2,1)S(1)} %get-tuple-element.39), channel_id=1, source_target_pairs={{0,120},{8,0},{16,8},{24,16},{32,24},{40,32},{48,40},{56,48},{64,5... | collective-permute-start | bytes 442376 | tf_op jit(solution)/shard_map/ppermute | solution.py:637
  31.3 0.7 copy-start.16
  31.3 0.7 copy-start.17
  32.0 34.2 %copy-start.8 = (bf16[256,512]{1,0:T(8,128)(2,1)S(1)}, bf16[256,512]{1,0:T(8,128)(2,1)}, u32[]{:S(2)}) copy-start(bf16[256,512]{1,0:T(8,128)(2,1)} %constant.66.clone.refs_12_.back_ref) | copy-start | bytes 786436
  46.2 7.9 %collective-permute-start.8 = (f32[4,272,128]{2,1,0:T(8,128)}, f32[4,272,128]{2,1,0:T(8,128)S(1)}, u32[]{:S(2)}, u32[]{:S(2)}) collective-permute-start(f32[4,272,128]{2,1,0:T(8,128)} %get-tuple-element.52), channel_id=1, source_target_pairs={{0,8},{1,9},{2,10},{3,11},{4,12},{5,13},{6,14},{7,15},{8,0},{9,1},... | collective-permute-start | bytes 1671176 | tf_op jit(solution)/shard_map/ppermute | solution.py:669
  50.5 8.6 %collective-permute-start.4 = (bf16[16,16,256]{2,1,0:T(8,128)(2,1)}, bf16[16,16,256]{2,1,0:T(8,128)(2,1)S(1)}, u32[]{:S(2)}, u32[]{:S(2)}) collective-permute-start(bf16[16,16,256]{2,1,0:T(8,128)(2,1)} %get-tuple-element.47), channel_id=1, source_target_pairs={{0,1},{1,2},{2,3},{3,4},{4,5},{5,6},{6,7},{7,0},{8,9},{9,10},{10,1... | collective-permute-start | bytes 393224 | tf_op jit(solution)/shard_map/ppermute | solution.py:633
  50.6 8.6 %collective-permute-start.5 = (bf16[16,16,256]{2,1,0:T(8,128)(2,1)}, bf16[16,16,256]{2,1,0:T(8,128)(2,1)S(1)}, u32[]{:S(2)}, u32[]{:S(2)}) collective-permute-start(bf16[16,16,256]{2,1,0:T(8,128)(2,1)} %get-tuple-element.48), channel_id=1, source_target_pairs={{0,7},{1,0},{2,1},{3,2},{4,3},{5,4},{6,5},{7,6},{8,15},{9,8},{10,9... | collective-permute-start | bytes 393224 | tf_op jit(solution)/shard_map/ppermute | solution.py:633
  54.1 1.1 %copy-start.9 = (f32[4,272,128]{2,1,0:T(8,128)S(1)}, f32[4,272,128]{2,1,0:T(8,128)}, u32[]{:S(2)}) copy-start(f32[4,272,128]{2,1,0:T(8,128)} %get-tuple-element.51.held_ref) | copy-start | bytes 1671172
  55.2 11.0 %copy-start.6 = (bf16[64,64,128]{2,1,0:T(8,128)(2,1)S(1)}, bf16[64,64,128]{2,1,0:T(8,128)(2,1)}, u32[]{:S(2)}) copy-start(bf16[64,64,128]{2,1,0:T(8,128)(2,1)} %broadcast_in_dim.18.refs_4_.refs_5_.refs_6_.wet_ref) | copy-start | bytes 3145732
  55.2 7.4 %collective-permute-start.9 = (bf16[1,272,128]{2,1,0:T(8,128)(2,1)S(1)}, bf16[1,272,128]{2,1,0:T(8,128)(2,1)S(1)}, u32[]{:S(2)}, u32[]{:S(2)}) collective-permute-start(bf16[1,272,128]{2,1,0:T(8,128)(2,1)S(1)} %get-tuple-element.54), channel_id=1, source_target_pairs={{0,16},{1,17},{2,18},{3,19},{4,20},{5,21},{6,22},{7,23},{8,10},{9,... | collective-permute-start | bytes 208904 | tf_op jit(solution)/shard_map/ppermute | solution.py:669
  55.3 7.3 %collective-permute-start.10 = (bf16[1,272,128]{2,1,0:T(8,128)(2,1)S(1)}, bf16[1,272,128]{2,1,0:T(8,128)(2,1)S(1)}, u32[]{:S(2)}, u32[]{:S(2)}) collective-permute-start(bf16[1,272,128]{2,1,0:T(8,128)(2,1)S(1)} %get-tuple-element.55), channel_id=1, source_target_pairs={{0,32},{1,33},{2,34},{3,35},{4,36},{5,37},{6,38},{7,39},{8,12},{9,... | collective-permute-start | bytes 208904 | tf_op jit(solution)/shard_map/ppermute | solution.py:669
  57.6 5.0 %collective-permute-start.11 = (bf16[1,272,128]{2,1,0:T(8,128)(2,1)S(1)}, bf16[1,272,128]{2,1,0:T(8,128)(2,1)S(1)}, u32[]{:S(2)}, u32[]{:S(2)}) collective-permute-start(bf16[1,272,128]{2,1,0:T(8,128)(2,1)S(1)} %get-tuple-element.56), channel_id=1, source_target_pairs={{0,48},{1,49},{2,50},{3,51},{4,52},{5,53},{6,54},{7,55},{8,14},{9,... | collective-permute-start | bytes 208904 | tf_op jit(solution)/shard_map/ppermute | solution.py:669
  59.2 1.6 %copy-start.1 = (bf16[64,64,256]{2,1,0:T(8,128)(2,1)S(1)}, bf16[64,64,256]{2,1,0:T(8,128)(2,1)}, u32[]{:S(2)}) copy-start(bf16[64,64,256]{2,1,0:T(8,128)(2,1)} %get-tuple-element.46.top_ref.bottom_ref.before_ref.fg_ref.after_ref) | copy-start | bytes 6291460
  60.8 5.4 %copy-start.2 = (bf16[64,64,256]{2,1,0:T(8,128)(2,1)S(1)}, bf16[64,64,256]{2,1,0:T(8,128)(2,1)}, u32[]{:S(2)}) copy-start(bf16[64,64,256]{2,1,0:T(8,128)(2,1)} %get-tuple-element.46.top_ref.bottom_ref.before_ref.fg_ref.after_ref) | copy-start | bytes 6291460
  60.8 5.4 %copy-start.3 = (bf16[64,64,256]{2,1,0:T(8,128)(2,1)S(1)}, bf16[64,64,256]{2,1,0:T(8,128)(2,1)}, u32[]{:S(2)}) copy-start(bf16[64,64,256]{2,1,0:T(8,128)(2,1)} %cot_ref.7) | copy-start | bytes 6291460
  60.8 5.4 %copy-start.7 = (bf16[512,512]{1,0:T(8,128)(2,1)S(1)}, bf16[512,512]{1,0:T(8,128)(2,1)}, u32[]{:S(2)}) copy-start(bf16[512,512]{1,0:T(8,128)(2,1)} %constant.64.clone.refs_10_.place_ref) | copy-start | bytes 1572868
  60.8 21.9 %collective-permute-start.6 = (bf16[3,96,256]{2,1,0:T(8,128)(2,1)S(1)}, bf16[3,96,256]{2,1,0:T(8,128)(2,1)S(1)}, u32[]{:S(2)}, u32[]{:S(2)}) collective-permute-start(bf16[3,96,256]{2,1,0:T(8,128)(2,1)S(1)} %get-tuple-element.49), channel_id=1, source_target_pairs={{0,8},{8,16},{16,24},{24,32},{32,40},{40,48},{48,56},{56,64},{64,7... | collective-permute-start | bytes 442376 | tf_op jit(solution)/shard_map/ppermute | solution.py:637
  60.9 21.8 %collective-permute-start.7 = (bf16[3,96,256]{2,1,0:T(8,128)(2,1)S(1)}, bf16[3,96,256]{2,1,0:T(8,128)(2,1)S(1)}, u32[]{:S(2)}, u32[]{:S(2)}) collective-permute-start(bf16[3,96,256]{2,1,0:T(8,128)(2,1)S(1)} %get-tuple-element.50), channel_id=1, source_target_pairs={{0,120},{8,0},{16,8},{24,16},{32,24},{40,32},{48,40},{56,48},{64,5... | collective-permute-start | bytes 442376 | tf_op jit(solution)/shard_map/ppermute | solution.py:637
  62.7 6.7 %collective-permute-start.14 = (bf16[1,272,128]{2,1,0:T(8,128)(2,1)S(1)}, bf16[1,272,128]{2,1,0:T(8,128)(2,1)S(1)}, u32[]{:S(2)}, u32[]{:S(2)}) collective-permute-start(bf16[1,272,128]{2,1,0:T(8,128)(2,1)S(1)} %add_convert_fusion.2), channel_id=1, source_target_pairs={{0,6},{1,7},{2,4},{3,5},{4,2},{5,3},{6,0},{7,1},{8,73},{9,72},{10,... | collective-permute-start | bytes 208904 | tf_op jit(solution)/shard_map/ppermute | solution.py:669
  64.1 6.2 %collective-permute-start.13 = (bf16[1,272,128]{2,1,0:T(8,128)(2,1)S(1)}, bf16[1,272,128]{2,1,0:T(8,128)(2,1)S(1)}, u32[]{:S(2)}, u32[]{:S(2)}) collective-permute-start(bf16[1,272,128]{2,1,0:T(8,128)(2,1)S(1)} %add_convert_fusion.2), channel_id=1, source_target_pairs={{0,4},{1,5},{2,6},{3,7},{4,0},{5,1},{6,2},{7,3},{8,72},{9,73},{10,... | collective-permute-start | bytes 208904 | tf_op jit(solution)/shard_map/ppermute | solution.py:669
  66.2 4.2 %collective-permute-start.12 = (bf16[1,272,128]{2,1,0:T(8,128)(2,1)S(1)}, bf16[1,272,128]{2,1,0:T(8,128)(2,1)S(1)}, u32[]{:S(2)}, u32[]{:S(2)}) collective-permute-start(bf16[1,272,128]{2,1,0:T(8,128)(2,1)S(1)} %add_convert_fusion.2), channel_id=1, source_target_pairs={{0,2},{1,3},{2,0},{3,1},{4,6},{5,7},{6,4},{7,5},{8,9},{9,8},{10,11... | collective-permute-start | bytes 208904 | tf_op jit(solution)/shard_map/ppermute | solution.py:669
  70.4 8.2 %collective-permute-start.17 = (bf16[1,272,128]{2,1,0:T(8,128)(2,1)S(1)}, bf16[1,272,128]{2,1,0:T(8,128)(2,1)S(1)}, u32[]{:S(2)}, u32[]{:S(2)}) collective-permute-start(bf16[1,272,128]{2,1,0:T(8,128)(2,1)S(1)} %add_convert_fusion.1), channel_id=1, source_target_pairs={{0,65},{1,64},{2,67},{3,66},{4,69},{5,68},{6,71},{7,70},{8,56},{9,... | collective-permute-start | bytes 208904 | tf_op jit(solution)/shard_map/ppermute | solution.py:669
  74.7 4.7 %collective-permute-start.16 = (bf16[1,272,128]{2,1,0:T(8,128)(2,1)S(1)}, bf16[1,272,128]{2,1,0:T(8,128)(2,1)S(1)}, u32[]{:S(2)}, u32[]{:S(2)}) collective-permute-start(bf16[1,272,128]{2,1,0:T(8,128)(2,1)S(1)} %add_convert_fusion.1), channel_id=1, source_target_pairs={{0,64},{1,65},{2,66},{3,67},{4,68},{5,69},{6,70},{7,71},{8,40},{9,... | collective-permute-start | bytes 208904 | tf_op jit(solution)/shard_map/ppermute | solution.py:669
  74.7 4.7 %collective-permute-start.15 = (bf16[1,272,128]{2,1,0:T(8,128)(2,1)S(1)}, bf16[1,272,128]{2,1,0:T(8,128)(2,1)S(1)}, u32[]{:S(2)}, u32[]{:S(2)}) collective-permute-start(bf16[1,272,128]{2,1,0:T(8,128)(2,1)S(1)} %add_convert_fusion.1), channel_id=1, source_target_pairs={{0,1},{1,0},{2,3},{3,2},{4,5},{5,4},{6,7},{7,6},{8,24},{9,25},{10,... | collective-permute-start | bytes 208904 | tf_op jit(solution)/shard_map/ppermute | solution.py:669
  79.4 6.6 %collective-permute-start.20 = (bf16[1,272,128]{2,1,0:T(8,128)(2,1)S(1)}, bf16[1,272,128]{2,1,0:T(8,128)(2,1)S(1)}, u32[]{:S(2)}, u32[]{:S(2)}) collective-permute-start(bf16[1,272,128]{2,1,0:T(8,128)(2,1)S(1)} %add_convert_fusion.refs_0_), channel_id=1, source_target_pairs={{0,48},{1,49},{2,50},{3,51},{4,52},{5,53},{6,54},{7,55},{8,14},{9,... | collective-permute-start | bytes 208904 | tf_op jit(solution)/shard_map/ppermute | solution.py:669
  81.2 4.8 %collective-permute-start.19 = (bf16[1,272,128]{2,1,0:T(8,128)(2,1)S(1)}, bf16[1,272,128]{2,1,0:T(8,128)(2,1)S(1)}, u32[]{:S(2)}, u32[]{:S(2)}) collective-permute-start(bf16[1,272,128]{2,1,0:T(8,128)(2,1)S(1)} %add_convert_fusion.refs_0_), channel_id=1, source_target_pairs={{0,32},{1,33},{2,34},{3,35},{4,36},{5,37},{6,38},{7,39},{8,12},{9,... | collective-permute-start | bytes 208904 | tf_op jit(solution)/shard_map/ppermute | solution.py:669
  81.9 4.1 %collective-permute-start.18 = (bf16[1,272,128]{2,1,0:T(8,128)(2,1)S(1)}, bf16[1,272,128]{2,1,0:T(8,128)(2,1)S(1)}, u32[]{:S(2)}, u32[]{:S(2)}) collective-permute-start(bf16[1,272,128]{2,1,0:T(8,128)(2,1)S(1)} %add_convert_fusion.refs_0_), channel_id=1, source_target_pairs={{0,16},{1,17},{2,18},{3,19},{4,20},{5,21},{6,22},{7,23},{8,10},{9,... | collective-permute-start | bytes 208904 | tf_op jit(solution)/shard_map/ppermute | solution.py:669
  86.0 9.0 %copy-start.13 = (s32[4]{0:T(128)S(1)}, s32[4]{0:T(128)}, u32[]{:S(2)}) copy-start(s32[4]{0:T(128)} %copy-done.12) | copy-start | bytes 52
  86.0 9.0 %collective-permute-start.21 = (bf16[4,272,128]{2,1,0:T(8,128)(2,1)S(1)}, bf16[4,272,128]{2,1,0:T(8,128)(2,1)S(1)}, u32[]{:S(2)}, u32[]{:S(2)}) collective-permute-start(bf16[4,272,128]{2,1,0:T(8,128)(2,1)S(1)} %join.1.own_ref), channel_id=1, source_target_pairs={{0,8},{1,9},{2,10},{3,11},{4,12},{5,13},{6,14},{7,15},{8,0},{9,1},... | collective-permute-start | bytes 835592 | tf_op jit(solution)/shard_map/ppermute | solution.py:669

commit v6 on v5

--- a/solution.py
+++ b/solution.py
@@ -18,9 +18,10 @@
 BLOCKS = 8
 LANES = 128
 CELLS = TILE * TILE
-VMEM_BYTES = 56 * 2**20
+VMEM_BYTES = 32 * 2**20
 SPREAD_BYTES = 24 * 2**20
 SMALL_BYTES = 12 * 2**20
+LARGE_BYTES = 56 * 2**20
 
 
 def basis():
@@ -169,31 +170,38 @@
 
 def end_kernel(masks, top_ref, bottom_ref, *refs):
     west_ref, east_ref, north_ref, south_ref = refs[masks:]
-    lat, channels = top_ref.shape[1:]
+    lat = top_ref.shape[1]
     tiles = west_ref.shape[0]
     for i in range(3):
-        for out_ref, ref, n, tile, at, row, column in (
-            (north_ref, top_ref, i, 0, i, 0, i),
-            (south_ref, bottom_ref, i + 1, tiles - 1, i + 1, -1, TILE - 3 + i),
+        for n, (out_ref, ref, tile) in enumerate(
+            ((north_ref, top_ref, 0), (south_ref, bottom_ref, tiles - 1))
         ):
-            cells = ref[n]
+            at = i + n
+            cells = ref[at if masks else i]
             if masks:
-                wet_ref = refs[0]
-                wet = wet_at(wet_ref.at[row % wet_ref.shape[0]], column, 0, lat, channels)
-                cells = (cells.astype(F32) * wet).astype(BF16)
+                cells = cells * both(refs[n][at])
             out_ref[i, :TILE, :] = outer(side_group(west_ref, tile, at, False), False)
             out_ref[i, TILE : TILE + lat, :] = cells
             out_ref[i, TILE + lat :, :] = outer(side_group(east_ref, tile, at, True), True)
 
 
-def filtered(wave, taps_ref, back_ref):
-    real, imag = wave[:HALF], wave[HALF:]
+def transformed(patches, place_ref):
+    wide = dot(place_ref[...], jnp.concatenate(patches, axis=1))
+    depth = wide.shape[1] // len(patches)
+    return [wide[:, depth * n : depth * (n + 1)] for n in range(len(patches))]
+
+
+def filtered(waves, taps_ref, back_ref):
     k_real, k_imag, k_last = taps_ref[:HALF], taps_ref[HALF : 2 * HALF], taps_ref[2 * HALF :]
-    out_real = real * k_real + imag * k_imag
-    out_imag = imag * k_last - real * k_imag
-    return dot(back_ref[:, :HALF], out_real.astype(BF16)) + dot(
-        back_ref[:, HALF:], out_imag.astype(BF16)
-    )
+    products = []
+    for wave in waves:
+        real, imag = wave[:HALF], wave[HALF:]
+        out_real = real * k_real + imag * k_imag
+        out_imag = imag * k_last - real * k_imag
+        products.append(jnp.concatenate([out_real.astype(BF16), out_imag.astype(BF16)], axis=0))
+    wide = dot(back_ref[...], jnp.concatenate(products, axis=1))
+    depth = wide.shape[1] // len(waves)
+    return [wide[:, depth * n : depth * (n + 1)] for n in range(len(waves))]
 
 
 def block_rows(place, k, rows):
@@ -214,16 +222,16 @@
     (
         who_ref, before_ref, x_ref, after_ref, wet_before_ref, wet_ref, wet_after_ref,
         west_ref, east_ref, cot_ref, place_ref, own_ref, back_ref, taps_ref, collect_ref,
-        bias_ref, gain_ref, shift_ref, up_ref, up_bias_ref, down_ref,
-    ) = refs[:21]
+        vectors_ref, up_ref, down_ref,
+    ) = refs[:18]
     if ends:
         (
             north_ref, south_ref, _, _, _, sum_in_ref, p_in_ref, small_in_ref,
-            fg_ref, to_west_ref, to_east_ref, keep_ref, send_ref,
+            fg_ref, to_west_ref, to_east_ref, keep_ref, send_ref, top_ref, bottom_ref,
             sum_ref, p_ref, small_ref, pad_ref,
-        ) = refs[21:]
+        ) = refs[18:]
     else:
-        fg_ref, to_west_ref, to_east_ref, sum_ref, p_ref, small_ref, pad_ref = refs[21:]
+        fg_ref, to_west_ref, to_east_ref, sum_ref, p_ref, small_ref, pad_ref = refs[18:]
     step = pl.program_id(0)
     a = row_of_step(ends, step, rows)
     lat, channels = x_ref.shape[1:]
@@ -273,17 +281,19 @@
     def columns(i, b):
         return pad_ref[i, TILE * b : TILE * (b + 1), :]
 
-    gain, shift = gain_ref[...].astype(F32), shift_ref[...].astype(F32)
-    conv_bias, up_bias = bias_ref[...].astype(F32), up_bias_ref[...].astype(F32)
-    waves = []
-    for b in range(count):
-        cells = patch(
+    vectors = vectors_ref[...].astype(F32)
+    conv_bias, gain, shift = (vectors[:, channels * n : channels * (n + 1)] for n in range(3))
+    up_bias = vectors[:, 3 * channels :]
+    patches = [
+        patch(
             [columns(i, b + 1) for i in range(SPAN)],
             [columns(i, b).astype(F32)[8:] for i in range(SPAN)],
             [columns(i, b + 2).astype(F32)[:8] for i in range(SPAN)],
         )
-        waves.append(dot(place_ref[...], cells))
-    field = jnp.concatenate([filtered(w, taps_ref, back_ref) for w in waves]) + conv_bias
+        for b in range(count)
+    ]
+    waves = transformed(patches, place_ref)
+    field = jnp.concatenate(filtered(waves, taps_ref, back_ref)) + conv_bias
 
     def by_tile(ref):
         return jnp.concatenate(
@@ -349,8 +359,13 @@
     if not ends:
         return
 
+    @pl.when(step == 0)
+    def _():
+        top_ref[...] = fg_ref[:3]
+
     @pl.when(step == 1)
     def _():
+        bottom_ref[...] = fg_ref[-3:]
         total = 0.0
         for n in range(3):
             total += jnp.dot(
@@ -426,13 +441,15 @@
         return ref[n, TILE * b : TILE * (b + 1), :]
 
     slabs = range(-3, TILE + 3)
-    for b in range(count):
-        cells = patch(
+    patches = [
+        patch(
             [columns(i, b) for i in slabs],
             [columns(i, b - 1).astype(F32)[8:] for i in slabs],
             [columns(i, b + 1).astype(F32)[:8] for i in slabs],
         )
-        spread = filtered(dot(place_ref[...], cells), taps_ref, back_ref)
+        for b in range(count)
+    ]
+    for b, spread in enumerate(filtered(transformed(patches, place_ref), taps_ref, back_ref)):
         here = slice(TILE * b, TILE * (b + 1))
         wet = both(wet_ref[:, here, :].reshape(CELLS, LANES).astype(F32))
         cot = cot_ref[:, here, :].reshape(CELLS, channels).astype(F32)
@@ -466,28 +483,35 @@
         ],
         out_specs=[whole(*s.shape) for s in shapes],
         out_shape=shapes,
-        compiler_params=pltpu.CompilerParams(vmem_limit_bytes=SMALL_BYTES),
+        compiler_params=pltpu.CompilerParams(vmem_limit_bytes=LARGE_BYTES),
         name="sides",
     )(who, x, x, wet)
 
 
-def ends(x, wet, halos):
-    lon, lat, channels = x.shape
-    masks = [] if wet is None else [wet]
+def ends(rows, halos):
+    lon, lat, channels = rows[0].shape
+    if rows[1].shape == rows[0].shape:
+        masks = 0
+        operands = rows
+        in_specs = [whole(*r.shape) for r in rows]
+    else:
+        masks = 2
+        operands = [r for row in rows for r in (row, row)]
+        in_specs = [
+            pl.BlockSpec((4, lat, r.shape[2]), lambda i, n=n: (n, 0, 0))
+            for r in rows
+            for n in (0, lon // 4 - 1)
+        ]
     shapes = [shape_of((3, lat + 2 * TILE, channels), BF16)] * 2
     return pl.pallas_call(
-        functools.partial(end_kernel, len(masks)),
+        functools.partial(end_kernel, masks),
         grid=(1,),
-        in_specs=[
-            pl.BlockSpec((4, lat, channels), lambda i: (0, 0, 0)),
-            pl.BlockSpec((4, lat, channels), lambda i: (lon // 4 - 1, 0, 0)),
-        ]
-        + [whole(*m.shape) for m in (*masks, *halos)],
+        in_specs=in_specs + [whole(*h.shape) for h in halos],
         out_specs=[whole(*s.shape) for s in shapes],
         out_shape=shapes,
         compiler_params=pltpu.CompilerParams(vmem_limit_bytes=SMALL_BYTES),
         name="ends",
-    )(x, x, *masks, *halos)
+    )(*operands, *halos)
 
 
 def cell_pass(who, x, halos, cotangent, wet, taps, params, end_halos=(), earlier=()):
@@ -495,7 +519,7 @@
     lon, lat, channels = x.shape
     at_ends = len(end_halos) > 0
     rows = lon // TILE
-    units = params[3].shape[1]
+    units = params[1].shape[1]
     sum_rows = (4 * units * channels // 2 + 64 * channels) // LANES
     sums = [shape_of((sum_rows, LANES)), shape_of((3, HALF, channels)), shape_of((64, channels))]
     half = shape_of((BLOCKS // 2, sum_rows // BLOCKS, LANES))
@@ -530,7 +554,7 @@
         operands += [*end_halos, *earlier]
         in_specs += [whole(*h.shape) for h in end_halos] + [ANY] * 3
         in_specs += [whole(*s.shape) for s in sums]
-        out_shape += [half, half]
+        out_shape += [half, half] + [shape_of((3, lat, channels), BF16)] * 2
         scratch = [pltpu.VMEM(s.shape, F32) for s in sums] + scratch
     else:
         out_shape += sums
@@ -692,20 +716,18 @@
     wet = jnp.broadcast_to(wet_mask.astype(BF16)[:, :, None], (lon, lat, LANES))
     who = places()
     halos = across_lat(*sides(who, inputs, wet_rows))
-    end_halos = across_lon(*ends(inputs, wet_rows, halos))
+    end_halos = across_lon(*ends((inputs, wet), halos))
     taps = jnp.dot(
         tables()["taps"], kernel.astype(F32), precision=lax.Precision.HIGHEST,
         preferred_element_type=F32,
     )
-    params = (
-        conv_bias[None, :], norm_gain[None, :], norm_shift[None, :], up_weight, up_bias[None, :],
-        down_weight,
-    )
+    vectors = jnp.concatenate([conv_bias, norm_gain, norm_shift, up_bias])[None, :]
+    params = (vectors, up_weight, down_weight)
     first = (who, inputs, halos, cotangent, wet, taps[: 3 * HALF], params)
     inner = cell_pass(*first)
-    field_grad, west, east, keep, send = cell_pass(*first, end_halos, inner)
+    field_grad, west, east, keep, send, top, bottom = cell_pass(*first, end_halos, inner)
     halos = across_lat(west, east)
-    end_halos = across_lon(*ends(field_grad, None, halos))
+    end_halos = across_lon(*ends((top, bottom), halos))
     own, other = summed_blocks(keep, send)
     input_grad = None
     middle = range(1, lon // TILE - 1)

time: 97 us -> 86.7 us (0.89)
  Pallas kernels: 42.3 us -> 33.2 us
  local copies, waits for them, and re-layouts: 10.4 us -> 2.09 us
  waiting for transfers between devices: 2.27 us -> 9.96 us
  starting transfers between devices: 39 us -> 37.9 us
    pallas_call x2, Pallas kernels: 26.7 us -> 20.4 us  [cell_pass(): pl.pallas_call(functools.partial(cell_kernel, at_ends, rows), grid=(2,),...]
    unnamed x42 -> x30, local copies, waits for them, and re-layouts: 5.52 us -> 0.62 us
    pallas_call x4, Pallas kernels: 12.9 us -> 8.69 us  [spread_pass(): pl.pallas_call(functools.partial(spread_kernel, at, rows), grid=(1,), in_...]
    ppermute x14, waiting for transfers between devices: 1.69 us -> 5.36 us  [move(): return lax.ppermute(x, AXES, swapped(mesh_shape, stage, step))]
    broadcast_in_dim x4 -> x1, local copies, waits for them, and re-layouts: 2.28 us -> 0.01 us  [local(): jnp.concatenate([conv_bias, norm_gain, norm_shift, up_bias])[None, :]]
    ppermute x2, waiting for transfers between devices: 0.57 us -> 2.66 us  [across_lat(): lax.ppermute(west, 'gy', ring('gy', -1))]
    ppermute x2, waiting for transfers between devices: 0.01 us -> 1.93 us  [across_lat(): lax.ppermute(east, 'gy', ring('gy', 1))]
    pallas_call x1, Pallas kernels: 0.82 us -> 2.29 us  [sides(): pl.pallas_call(side_kernel, grid=(1,), in_specs=[IN_SMEM, pl.BlockSpec((l...]
  transfers between devices with their start and end apart: 22 -> 22, of which waited for: 3 -> 8; matrix products, arithmetic and copies ran while one was open for 6% -> 1% of each run, Pallas kernels for 26% -> 21%
where the time goes in v6:
time: 86.7 us; the launch traced here: 86.5 us
  starting transfers between devices  37.9 us (44%)
  Pallas kernels  33.2 us (38%)
  waiting for transfers between devices  9.96 us (11%)
  local copies, waits for them, and re-layouts  2.09 us (2%)
  other arithmetic  1.56 us (2%)
  between operations  0.99 us (1%)
    ppermute x14, starting transfers between devices, move(): return lax.ppermute(x, AXES, swapped(mesh_shape, stage, step))  25.7 us
    pallas_call x2, Pallas kernels, cell_pass(): pl.pallas_call(functools.partial(cell_kernel, at_ends, rows), grid=(2,),...  20.4 us
    pallas_call x4, Pallas kernels, spread_pass(): pl.pallas_call(functools.partial(spread_kernel, at, rows), grid=(1,), in_...  8.69 us
    ppermute x2, starting transfers between devices, across_lat(): lax.ppermute(west, 'gy', ring('gy', -1))  6.04 us
    ppermute x14, waiting for transfers between devices, move(): return lax.ppermute(x, AXES, swapped(mesh_shape, stage, step))  5.36 us
    ppermute x2, starting transfers between devices, across_lon(): lax.ppermute(south, 'gx', ring('gx', 1))  2.78 us
    ppermute x2, waiting for transfers between devices, across_lat(): lax.ppermute(west, 'gy', ring('gy', -1))  2.66 us
    ppermute x2, starting transfers between devices, across_lat(): lax.ppermute(east, 'gy', ring('gy', 1))  2.47 us
  transfers between devices with their start and end apart: 22, of which 8 were waited for; matrix products, arithmetic and copies ran while one was open for 1% of the time, Pallas kernels for 21%

profile of v6, /device:TPU:1, one launch (start us, length us, event | category | flops | bytes accessed | tf_op | source)
XLA Modules:
  0.0 86.5 jit_solution(8625675373106425587)
XLA Ops:
  0.6 0.0 copy-start
  0.7 0.8 fusion.1
  1.5 0.8 copy.29
  2.3 0.6 pad_add_fusion.who_ref.refs_0_
  2.9 2.3 %sides.1 = (bf16[16,16,256]{2,1,0:T(8,128)(2,1)}, bf16[16,16,256]{2,1,0:T(8,128)(2,1)}) custom-call(s32[4]{0:T(128)} %pad_add_fusion.who_ref.refs_0_, bf16[64,64,256]{2,1,0:T(8,128)(2,1)} %refs_3_.3, bf16[64,64,256]{2,1,0:T(8,128)(2,1)} %refs_3_.3, f32[4,64,16]{2,1,0:T(8,128)} %bitcast.12), custom_call_target="tpu_custom_call" | custom-call | tf_op jit(solution)/shard_map/sides/pallas_call | solution.py:475
  5.2 2.5 %collective-permute-start = (bf16[16,16,256]{2,1,0:T(8,128)(2,1)}, bf16[16,16,256]{2,1,0:T(8,128)(2,1)S(1)}, u32[]{:S(2)}, u32[]{:S(2)}) collective-permute-start(bf16[16,16,256]{2,1,0:T(8,128)(2,1)} %get-tuple-element.38), channel_id=1, source_target_pairs={{0,1},{1,2},{2,3},{3,4},{4,5},{5,6},{6,7},{7,0},{8,9},{9,10},{10,1... | collective-permute-start | bytes 393224 | tf_op jit(solution)/shard_map/ppermute | solution.py:657
  7.6 2.5 %collective-permute-start.1 = (bf16[16,16,256]{2,1,0:T(8,128)(2,1)}, bf16[16,16,256]{2,1,0:T(8,128)(2,1)S(1)}, u32[]{:S(2)}, u32[]{:S(2)}) collective-permute-start(bf16[16,16,256]{2,1,0:T(8,128)(2,1)} %get-tuple-element.39), channel_id=1, source_target_pairs={{0,7},{1,0},{2,1},{3,2},{4,3},{5,4},{6,5},{7,6},{8,15},{9,8},{10,9... | collective-permute-start | bytes 393224 | tf_op jit(solution)/shard_map/ppermute | solution.py:657
  10.1 0.8 fusion.2
  10.9 0.0 copy-start.11
  10.9 0.0 copy-start.12
  10.9 0.0 copy-start.13
  10.9 0.0 copy-start.14
  10.9 0.0 copy-start.2
  10.9 0.1 fusion
  11.0 0.5 copy-done.11
  11.6 0.0 copy-done.13
  11.6 0.0 copy-done.14
  11.6 1.9 %collective-permute-done.refs_2_.refs_7_ = bf16[16,16,256]{2,1,0:T(8,128)(2,1)S(1)} collective-permute-done((bf16[16,16,256]{2,1,0:T(8,128)(2,1)}, bf16[16,16,256]{2,1,0:T(8,128)(2,1)S(1)}, u32[]{:S(2)}, u32[]{:S(2)}) %collective-permute-start) | collective-permute-done | bytes 131104 | tf_op jit(solution)/shard_map/ppermute | solution.py:657
  13.5 1.5 %collective-permute-done.1.refs_3_.refs_8_ = bf16[16,16,256]{2,1,0:T(8,128)(2,1)S(1)} collective-permute-done((bf16[16,16,256]{2,1,0:T(8,128)(2,1)}, bf16[16,16,256]{2,1,0:T(8,128)(2,1)S(1)}, u32[]{:S(2)}, u32[]{:S(2)}) %collective-permute-start.1) | collective-permute-done | bytes 131104 | tf_op jit(solution)/shard_map/ppermute | solution.py:657
  15.0 0.6 broadcast_in_dim.4.refs_0_.refs_1_.refs_4_.refs_5_.refs_6_.wet_ref
  15.7 0.0 copy-start.1
  15.7 0.0 copy-start.3
  15.7 0.0 copy-start.4
  15.7 0.0 copy-start.5
  15.7 0.0 copy-start.6
  15.7 0.0 copy-start.7
  15.7 0.0 copy-start.8
  15.7 0.0 copy-start.9
  15.8 2.7 %collective-permute-start.2 = (bf16[3,96,256]{2,1,0:T(8,128)(2,1)S(1)}, bf16[3,96,256]{2,1,0:T(8,128)(2,1)S(1)}, u32[]{:S(2)}, u32[]{:S(2)}) collective-permute-start(bf16[3,96,256]{2,1,0:T(8,128)(2,1)S(1)} %get-tuple-element.40), channel_id=1, source_target_pairs={{0,8},{8,16},{16,24},{24,32},{32,40},{40,48},{48,56},{56,64},{64,7... | collective-permute-start | bytes 442376 | tf_op jit(solution)/shard_map/ppermute | solution.py:661
  18.5 0.0 collective-permute-start.3
  18.6 9.8 %inner_cells.1 = (bf16[64,64,256]{2,1,0:T(8,128)(2,1)S(1)}, bf16[16,16,256]{2,1,0:T(8,128)(2,1)S(1)}, bf16[16,16,256]{2,1,0:T(8,128)(2,1)S(1)}, f32[2176,128]{1,...) custom-call(s32[4]{0:T(128)S(1)} %copy-done.5, bf16[64,64,256]{2,1,0:T(8,128)(2,1)S(1)} %copy-done.2, ...), custom_call_target="tpu_custom_call" | custom-call | flops 10000000000 | bytes 8388608 | tf_op jit(solution)/shard_map/inner_cells/pallas_call | solution.py:562
  28.4 0.0 collective-permute-done.2.refs_18_
  28.4 0.0 collective-permute-done.3.refs_19_
  28.4 10.6 %end_cells.1 = (bf16[64,64,256]{2,1,0:T(8,128)(2,1)S(1)}, bf16[16,16,256]{2,1,0:T(8,128)(2,1)S(1)}, bf16[16,16,256]{2,1,0:T(8,128)(2,1)S(1)}, f32[4,272,128]{2,1...) custom-call(s32[4]{0:T(128)S(1)} %copy-done.5, ...), custom_call_target="tpu_custom_call", output_to_operand_aliasing={{0}: (20, {}), {1}: (21, {}), {2}: (22, {})} | custom-call | flops 10000000000 | bytes 8388608 | tf_op jit(solution)/shard_map/end_cells/pallas_call | solution.py:562
  39.0 4.3 %collective-permute-start.8 = (f32[4,272,128]{2,1,0:T(8,128)S(1)}, f32[4,272,128]{2,1,0:T(8,128)S(1)}, u32[]{:S(2)}, u32[]{:S(2)}) collective-permute-start(f32[4,272,128]{2,1,0:T(8,128)S(1)} %get-tuple-element.56), channel_id=1, source_target_pairs={{0,8},{1,9},{2,10},{3,11},{4,12},{5,13},{6,14},{7,15},{8,0},{9,1},... | collective-permute-start | bytes 1671176 | tf_op jit(solution)/shard_map/ppermute | solution.py:693
  43.3 0.0 collective-permute-start.4
  43.3 3.6 %collective-permute-start.5 = (bf16[16,16,256]{2,1,0:T(8,128)(2,1)S(1)}, bf16[16,16,256]{2,1,0:T(8,128)(2,1)S(1)}, u32[]{:S(2)}, u32[]{:S(2)}) collective-permute-start(bf16[16,16,256]{2,1,0:T(8,128)(2,1)S(1)} %get-tuple-element.52), channel_id=1, source_target_pairs={{0,7},{1,0},{2,1},{3,2},{4,3},{5,4},{6,5},{7,6},{8,15},{9,8},{10,9... | collective-permute-start | bytes 393224 | tf_op jit(solution)/shard_map/ppermute | solution.py:657
  46.9 0.0 collective-permute-done.8.come_ref
  46.9 0.1 fold.1
  47.0 0.1 collective-permute-start.9
  47.1 2.5 %collective-permute-start.10 = (bf16[1,272,128]{2,1,0:T(8,128)(2,1)S(1)}, bf16[1,272,128]{2,1,0:T(8,128)(2,1)S(1)}, u32[]{:S(2)}, u32[]{:S(2)}) collective-permute-start(bf16[1,272,128]{2,1,0:T(8,128)(2,1)S(1)} %get-tuple-element.59), channel_id=1, source_target_pairs={{0,32},{1,33},{2,34},{3,35},{4,36},{5,37},{6,38},{7,39},{8,12},{9,... | collective-permute-start | bytes 208904 | tf_op jit(solution)/shard_map/ppermute | solution.py:693
  49.6 1.3 %collective-permute-start.11 = (bf16[1,272,128]{2,1,0:T(8,128)(2,1)S(1)}, bf16[1,272,128]{2,1,0:T(8,128)(2,1)S(1)}, u32[]{:S(2)}, u32[]{:S(2)}) collective-permute-start(bf16[1,272,128]{2,1,0:T(8,128)(2,1)S(1)} %get-tuple-element.60), channel_id=1, source_target_pairs={{0,48},{1,49},{2,50},{3,51},{4,52},{5,53},{6,54},{7,55},{8,14},{9,... | collective-permute-start | bytes 208904 | tf_op jit(solution)/shard_map/ppermute | solution.py:693
  50.9 0.0 collective-permute-done.4.refs_0_.north_ref.west_ref
  50.9 1.1 %collective-permute-done.5.refs_1_.south_ref.east_ref = bf16[16,16,256]{2,1,0:T(8,128)(2,1)S(1)} collective-permute-done((bf16[16,16,256]{2,1,0:T(8,128)(2,1)S(1)}, bf16[16,16,256]{2,1,0:T(8,128)(2,1)S(1)}, u32[]{:S(2)}, u32[]{:S(2)}) %collective-permute-start.5) | collective-permute-done | bytes 131104 | tf_op jit(solution)/shard_map/ppermute | solution.py:657
  52.1 0.1 collective-permute-start.6
  52.2 0.9 %collective-permute-start.7 = (bf16[3,96,256]{2,1,0:T(8,128)(2,1)S(1)}, bf16[3,96,256]{2,1,0:T(8,128)(2,1)S(1)}, u32[]{:S(2)}, u32[]{:S(2)}) collective-permute-start(bf16[3,96,256]{2,1,0:T(8,128)(2,1)S(1)} %get-tuple-element.54), channel_id=1, source_target_pairs={{0,120},{8,0},{16,8},{24,16},{32,24},{40,32},{48,40},{56,48},{64,5... | collective-permute-start | bytes 442376 | tf_op jit(solution)/shard_map/ppermute | solution.py:661
  53.1 0.9 %collective-permute-done.11 = bf16[1,272,128]{2,1,0:T(8,128)(2,1)S(1)} collective-permute-done((bf16[1,272,128]{2,1,0:T(8,128)(2,1)S(1)}, bf16[1,272,128]{2,1,0:T(8,128)(2,1)S(1)}, u32[]{:S(2)}, u32[]{:S(2)}) %collective-permute-start.11) | collective-permute-done | bytes 69664 | tf_op jit(solution)/shard_map/ppermute | solution.py:693
  54.0 2.3 %collective-permute-start.14 = (bf16[1,272,128]{2,1,0:T(8,128)(2,1)S(1)}, bf16[1,272,128]{2,1,0:T(8,128)(2,1)S(1)}, u32[]{:S(2)}, u32[]{:S(2)}) collective-permute-start(bf16[1,272,128]{2,1,0:T(8,128)(2,1)S(1)} %add_convert_fusion.2), channel_id=1, source_target_pairs={{0,6},{1,7},{2,4},{3,5},{4,2},{5,3},{6,0},{7,1},{8,73},{9,72},{10,... | collective-permute-start | bytes 208904 | tf_op jit(solution)/shard_map/ppermute | solution.py:693
  56.3 1.4 %collective-permute-start.13 = (bf16[1,272,128]{2,1,0:T(8,128)(2,1)S(1)}, bf16[1,272,128]{2,1,0:T(8,128)(2,1)S(1)}, u32[]{:S(2)}, u32[]{:S(2)}) collective-permute-start(bf16[1,272,128]{2,1,0:T(8,128)(2,1)S(1)} %add_convert_fusion.2), channel_id=1, source_target_pairs={{0,4},{1,5},{2,6},{3,7},{4,0},{5,1},{6,2},{7,3},{8,72},{9,73},{10,... | collective-permute-start | bytes 208904 | tf_op jit(solution)/shard_map/ppermute | solution.py:693
  57.7 2.2 %spread_pass.4.out_refs_0_ = f32[64,64,256]{2,1,0:T(8,128)} custom-call(bf16[64,64,256]{2,1,0:T(8,128)(2,1)S(1)} %get-tuple-element.48.before_ref.fg_ref.after_ref, bf16[64,64,256]{2,1,0:T(8,128)(2,1)S(1)} %get-tuple-element.48.before_ref.fg_ref.after_ref, bf16[64,64,256]{2,1,0:T(8,128)(2,1)S(1)} %get-tuple-element.48.before_ref.fg_ref.after_ref, ...), custom_call_target="tpu_custom_call" | custom-call | flops 4000000000 | bytes 4194304 | tf_op jit(solution)/shard_map/spread_pass/pallas_call | solution.py:625
  59.9 1.4 %collective-permute-done.13 = bf16[1,272,128]{2,1,0:T(8,128)(2,1)S(1)} collective-permute-done((bf16[1,272,128]{2,1,0:T(8,128)(2,1)S(1)}, bf16[1,272,128]{2,1,0:T(8,128)(2,1)S(1)}, u32[]{:S(2)}, u32[]{:S(2)}) %collective-permute-start.13) | collective-permute-done | bytes 69664 | tf_op jit(solution)/shard_map/ppermute | solution.py:693
  61.3 0.1 collective-permute-done.12
  61.4 4.0 %collective-permute-start.17 = (bf16[1,272,128]{2,1,0:T(8,128)(2,1)S(1)}, bf16[1,272,128]{2,1,0:T(8,128)(2,1)S(1)}, u32[]{:S(2)}, u32[]{:S(2)}) collective-permute-start(bf16[1,272,128]{2,1,0:T(8,128)(2,1)S(1)} %add_convert_fusion.1), channel_id=1, source_target_pairs={{0,65},{1,64},{2,67},{3,66},{4,69},{5,68},{6,71},{7,70},{8,56},{9,... | collective-permute-start | bytes 208904 | tf_op jit(solution)/shard_map/ppermute | solution.py:693
  65.4 0.7 collective-permute-start.15
  66.1 2.2 %spread_pass.5.out_refs_0_ = f32[64,64,256]{2,1,0:T(8,128)} custom-call(bf16[64,64,256]{2,1,0:T(8,128)(2,1)S(1)} %get-tuple-element.48.before_ref.fg_ref.after_ref, bf16[64,64,256]{2,1,0:T(8,128)(2,1)S(1)} %get-tuple-element.48.before_ref.fg_ref.after_ref, ...), custom_call_target="tpu_custom_call", output_to_operand_aliasing={{}: (12, {})} | custom-call | flops 4000000000 | bytes 4194304 | tf_op jit(solution)/shard_map/spread_pass/pallas_call | solution.py:625
  68.3 1.8 %collective-permute-done.16 = bf16[1,272,128]{2,1,0:T(8,128)(2,1)S(1)} collective-permute-done((bf16[1,272,128]{2,1,0:T(8,128)(2,1)S(1)}, bf16[1,272,128]{2,1,0:T(8,128)(2,1)S(1)}, u32[]{:S(2)}, u32[]{:S(2)}) %collective-permute-start.16) | collective-permute-done | bytes 69664 | tf_op jit(solution)/shard_map/ppermute | solution.py:693
  70.1 2.0 %collective-permute-start.20 = (bf16[1,272,128]{2,1,0:T(8,128)(2,1)S(1)}, bf16[1,272,128]{2,1,0:T(8,128)(2,1)S(1)}, u32[]{:S(2)}, u32[]{:S(2)}) collective-permute-start(bf16[1,272,128]{2,1,0:T(8,128)(2,1)S(1)} %add_convert_fusion.refs_0_), channel_id=1, source_target_pairs={{0,48},{1,49},{2,50},{3,51},{4,52},{5,53},{6,54},{7,55},{8,14},{9,... | collective-permute-start | bytes 208904 | tf_op jit(solution)/shard_map/ppermute | solution.py:693
  72.2 0.7 collective-permute-start.19
  72.9 0.5 collective-permute-start.18
  73.5 2.2 %spread_pass.6.out_refs_0_ = f32[64,64,256]{2,1,0:T(8,128)} custom-call(bf16[64,64,256]{2,1,0:T(8,128)(2,1)S(1)} %get-tuple-element.48.before_ref.fg_ref.after_ref, bf16[64,64,256]{2,1,0:T(8,128)(2,1)S(1)} %get-tuple-element.48.before_ref.fg_ref.after_ref, ...), custom_call_target="tpu_custom_call", output_to_operand_aliasing={{}: (12, {})} | custom-call | flops 4000000000 | bytes 4194304 | tf_op jit(solution)/shard_map/spread_pass/pallas_call | solution.py:625
  75.7 1.2 %collective-permute-done.19.refs_2_ = bf16[1,272,128]{2,1,0:T(8,128)(2,1)S(1)} collective-permute-done((bf16[1,272,128]{2,1,0:T(8,128)(2,1)S(1)}, bf16[1,272,128]{2,1,0:T(8,128)(2,1)S(1)}, u32[]{:S(2)}, u32[]{:S(2)}) %collective-permute-start.19) | collective-permute-done | bytes 69664 | tf_op jit(solution)/shard_map/ppermute | solution.py:693
  76.9 5.7 %collective-permute-start.21 = (bf16[4,272,128]{2,1,0:T(8,128)(2,1)S(1)}, bf16[4,272,128]{2,1,0:T(8,128)(2,1)S(1)}, u32[]{:S(2)}, u32[]{:S(2)}) collective-permute-start(bf16[4,272,128]{2,1,0:T(8,128)(2,1)S(1)} %join.1.own_ref), channel_id=1, source_target_pairs={{0,8},{1,9},{2,10},{3,11},{4,12},{5,13},{6,14},{7,15},{8,0},{9,1},... | collective-permute-start | bytes 835592 | tf_op jit(solution)/shard_map/ppermute | solution.py:693
  82.6 2.2 %spread_pass.7 = f32[64,64,256]{2,1,0:T(8,128)} custom-call(bf16[64,64,256]{2,1,0:T(8,128)(2,1)S(1)} %get-tuple-element.48.before_ref.fg_ref.after_ref, bf16[64,64,256]{2,1,0:T(8,128)(2,1)S(1)} %get-tuple-element.48.before_ref.fg_ref.after_ref, ...), custom_call_target="tpu_custom_call", output_to_operand_aliasing={{}: (12, {})} | custom-call | flops 4000000000 | bytes 4194304 | tf_op jit(solution)/shard_map/spread_pass/pallas_call | solution.py:625
  84.8 1.7 %finish.1 = (f32[49,256]{1,0:T(8,128)}, f32[1,256]{1,0:T(1,128)}, f32[1,256]{1,0:T(1,128)}, f32[1,256]{1,0:T(1,128)}, f32[256,512]{1,0:T(8,128)}, /*index=5*/f32[1,512]{1,0:T(1,128)}, f32[512,256]{1,0:T(8,128)}) custom-call(s32[4]{0:T(128)S(1)} %copy-done.5, bf16[4,272,128]{2,1,0:T(8,128)(2,1)S(1)} %join.1.own_ref, ...), custom_call_target="tpu_custom_call" | custom-call | tf_op jit(solution)/shard_map/finish/pallas_call | solution.py:603
  (33 shorter events, 0.3 us)
Async XLA Ops:
  0.6 9.5 %copy-start = (bf16[49,256]{1,0:T(8,128)(2,1)S(1)}, bf16[49,256]{1,0:T(8,128)(2,1)}, u32[]{:S(2)}) copy-start(bf16[49,256]{1,0:T(8,128)(2,1)} %param.18) | copy-start | bytes 75268
  2.9 7.2 %copy-start.10 = (f32[1536,49]{1,0:T(8,128)S(1)}, f32[1536,49]{1,0:T(8,128)}, u32[]{:S(2)}) copy-start(f32[1536,49]{1,0:T(8,128)} %constant.63.clone) | copy-start | bytes 903172
  5.2 8.3 %collective-permute-start = (bf16[16,16,256]{2,1,0:T(8,128)(2,1)}, bf16[16,16,256]{2,1,0:T(8,128)(2,1)S(1)}, u32[]{:S(2)}, u32[]{:S(2)}) collective-permute-start(bf16[16,16,256]{2,1,0:T(8,128)(2,1)} %get-tuple-element.38), channel_id=1, source_target_pairs={{0,1},{1,2},{2,3},{3,4},{4,5},{5,6},{6,7},{7,0},{8,9},{9,10},{10,1... | collective-permute-start | bytes 393224 | tf_op jit(solution)/shard_map/ppermute | solution.py:657
  7.6 7.4 %collective-permute-start.1 = (bf16[16,16,256]{2,1,0:T(8,128)(2,1)}, bf16[16,16,256]{2,1,0:T(8,128)(2,1)S(1)}, u32[]{:S(2)}, u32[]{:S(2)}) collective-permute-start(bf16[16,16,256]{2,1,0:T(8,128)(2,1)} %get-tuple-element.39), channel_id=1, source_target_pairs={{0,7},{1,0},{2,1},{3,2},{4,3},{5,4},{6,5},{7,6},{8,15},{9,8},{10,9... | collective-permute-start | bytes 393224 | tf_op jit(solution)/shard_map/ppermute | solution.py:657
  10.9 0.7 copy-start.11
  10.9 0.7 copy-start.12
  10.9 0.7 copy-start.13
  10.9 0.7 copy-start.14
  10.9 4.7 %copy-start.2 = (bf16[64,64,256]{2,1,0:T(8,128)(2,1)S(1)}, bf16[64,64,256]{2,1,0:T(8,128)(2,1)}, u32[]{:S(2)}) copy-start(bf16[64,64,256]{2,1,0:T(8,128)(2,1)} %refs_3_.3) | copy-start | bytes 6291460
  15.7 2.8 %copy-start.1 = (bf16[64,64,256]{2,1,0:T(8,128)(2,1)S(1)}, bf16[64,64,256]{2,1,0:T(8,128)(2,1)}, u32[]{:S(2)}) copy-start(bf16[64,64,256]{2,1,0:T(8,128)(2,1)} %cot_ref.7) | copy-start | bytes 6291460
  15.7 2.8 %copy-start.3 = (bf16[512,512]{1,0:T(8,128)(2,1)S(1)}, bf16[512,512]{1,0:T(8,128)(2,1)}, u32[]{:S(2)}) copy-start(bf16[512,512]{1,0:T(8,128)(2,1)} %constant.64.clone.refs_10_.place_ref) | copy-start | bytes 1572868
  15.7 2.8 %copy-start.4 = (bf16[256,512]{1,0:T(8,128)(2,1)S(1)}, bf16[256,512]{1,0:T(8,128)(2,1)}, u32[]{:S(2)}) copy-start(bf16[256,512]{1,0:T(8,128)(2,1)} %constant.66.clone.refs_12_.back_ref) | copy-start | bytes 786436
  15.7 2.8 %copy-start.5 = (s32[4]{0:T(128)S(1)}, s32[4]{0:T(128)}, u32[]{:S(2)}) copy-start(s32[4]{0:T(128)} %pad_add_fusion.who_ref.refs_0_) | copy-start | bytes 52
  15.7 2.8 %copy-start.6 = (bf16[256,512]{1,0:T(8,128)(2,1)S(1)}, bf16[256,512]{1,0:T(8,128)(2,1)}, u32[]{:S(2)}) copy-start(bf16[256,512]{1,0:T(8,128)(2,1)} %refs_16_.3) | copy-start | bytes 786436
  15.7 2.8 %copy-start.7 = (bf16[512,256]{1,0:T(8,128)(2,1)S(1)}, bf16[512,256]{1,0:T(8,128)(2,1)}, u32[]{:S(2)}) copy-start(bf16[512,256]{1,0:T(8,128)(2,1)} %refs_17_.3) | copy-start | bytes 786436
  15.7 2.8 %copy-start.8 = (bf16[512,256]{1,0:T(8,128)(2,1)S(1)}, bf16[512,256]{1,0:T(8,128)(2,1)}, u32[]{:S(2)}) copy-start(bf16[512,256]{1,0:T(8,128)(2,1)} %constant.65.clone.refs_11_) | copy-start | bytes 786436
  15.7 2.8 %copy-start.9 = (f32[49,768]{1,0:T(8,128)S(1)}, f32[49,768]{1,0:T(8,128)}, u32[]{:S(2)}) copy-start(f32[49,768]{1,0:T(8,128)} %constant.67.clone.refs_14_) | copy-start | bytes 451588
  15.8 12.6 %collective-permute-start.2 = (bf16[3,96,256]{2,1,0:T(8,128)(2,1)S(1)}, bf16[3,96,256]{2,1,0:T(8,128)(2,1)S(1)}, u32[]{:S(2)}, u32[]{:S(2)}) collective-permute-start(bf16[3,96,256]{2,1,0:T(8,128)(2,1)S(1)} %get-tuple-element.40), channel_id=1, source_target_pairs={{0,8},{8,16},{16,24},{24,32},{32,40},{40,48},{48,56},{56,64},{64,7... | collective-permute-start | bytes 442376 | tf_op jit(solution)/shard_map/ppermute | solution.py:661
  18.5 9.9 %collective-permute-start.3 = (bf16[3,96,256]{2,1,0:T(8,128)(2,1)S(1)}, bf16[3,96,256]{2,1,0:T(8,128)(2,1)S(1)}, u32[]{:S(2)}, u32[]{:S(2)}) collective-permute-start(bf16[3,96,256]{2,1,0:T(8,128)(2,1)S(1)} %get-tuple-element.41), channel_id=1, source_target_pairs={{0,120},{8,0},{16,8},{24,16},{32,24},{40,32},{48,40},{56,48},{64,5... | collective-permute-start | bytes 442376 | tf_op jit(solution)/shard_map/ppermute | solution.py:661
  39.0 7.9 %collective-permute-start.8 = (f32[4,272,128]{2,1,0:T(8,128)S(1)}, f32[4,272,128]{2,1,0:T(8,128)S(1)}, u32[]{:S(2)}, u32[]{:S(2)}) collective-permute-start(f32[4,272,128]{2,1,0:T(8,128)S(1)} %get-tuple-element.56), channel_id=1, source_target_pairs={{0,8},{1,9},{2,10},{3,11},{4,12},{5,13},{6,14},{7,15},{8,0},{9,1},... | collective-permute-start | bytes 1671176 | tf_op jit(solution)/shard_map/ppermute | solution.py:693
  43.3 7.6 %collective-permute-start.4 = (bf16[16,16,256]{2,1,0:T(8,128)(2,1)S(1)}, bf16[16,16,256]{2,1,0:T(8,128)(2,1)S(1)}, u32[]{:S(2)}, u32[]{:S(2)}) collective-permute-start(bf16[16,16,256]{2,1,0:T(8,128)(2,1)S(1)} %get-tuple-element.51), channel_id=1, source_target_pairs={{0,1},{1,2},{2,3},{3,4},{4,5},{5,6},{6,7},{7,0},{8,9},{9,10},{10,1... | collective-permute-start | bytes 393224 | tf_op jit(solution)/shard_map/ppermute | solution.py:657
  43.3 8.7 %collective-permute-start.5 = (bf16[16,16,256]{2,1,0:T(8,128)(2,1)S(1)}, bf16[16,16,256]{2,1,0:T(8,128)(2,1)S(1)}, u32[]{:S(2)}, u32[]{:S(2)}) collective-permute-start(bf16[16,16,256]{2,1,0:T(8,128)(2,1)S(1)} %get-tuple-element.52), channel_id=1, source_target_pairs={{0,7},{1,0},{2,1},{3,2},{4,3},{5,4},{6,5},{7,6},{8,15},{9,8},{10,9... | collective-permute-start | bytes 393224 | tf_op jit(solution)/shard_map/ppermute | solution.py:657
  47.0 6.1 %collective-permute-start.9 = (bf16[1,272,128]{2,1,0:T(8,128)(2,1)S(1)}, bf16[1,272,128]{2,1,0:T(8,128)(2,1)S(1)}, u32[]{:S(2)}, u32[]{:S(2)}) collective-permute-start(bf16[1,272,128]{2,1,0:T(8,128)(2,1)S(1)} %get-tuple-element.58), channel_id=1, source_target_pairs={{0,16},{1,17},{2,18},{3,19},{4,20},{5,21},{6,22},{7,23},{8,10},{9,... | collective-permute-start | bytes 208904 | tf_op jit(solution)/shard_map/ppermute | solution.py:693
  47.1 6.0 %collective-permute-start.10 = (bf16[1,272,128]{2,1,0:T(8,128)(2,1)S(1)}, bf16[1,272,128]{2,1,0:T(8,128)(2,1)S(1)}, u32[]{:S(2)}, u32[]{:S(2)}) collective-permute-start(bf16[1,272,128]{2,1,0:T(8,128)(2,1)S(1)} %get-tuple-element.59), channel_id=1, source_target_pairs={{0,32},{1,33},{2,34},{3,35},{4,36},{5,37},{6,38},{7,39},{8,12},{9,... | collective-permute-start | bytes 208904 | tf_op jit(solution)/shard_map/ppermute | solution.py:693
  49.6 4.4 %collective-permute-start.11 = (bf16[1,272,128]{2,1,0:T(8,128)(2,1)S(1)}, bf16[1,272,128]{2,1,0:T(8,128)(2,1)S(1)}, u32[]{:S(2)}, u32[]{:S(2)}) collective-permute-start(bf16[1,272,128]{2,1,0:T(8,128)(2,1)S(1)} %get-tuple-element.60), channel_id=1, source_target_pairs={{0,48},{1,49},{2,50},{3,51},{4,52},{5,53},{6,54},{7,55},{8,14},{9,... | collective-permute-start | bytes 208904 | tf_op jit(solution)/shard_map/ppermute | solution.py:693
  52.1 21.4 %collective-permute-start.6 = (bf16[3,96,256]{2,1,0:T(8,128)(2,1)S(1)}, bf16[3,96,256]{2,1,0:T(8,128)(2,1)S(1)}, u32[]{:S(2)}, u32[]{:S(2)}) collective-permute-start(bf16[3,96,256]{2,1,0:T(8,128)(2,1)S(1)} %get-tuple-element.53), channel_id=1, source_target_pairs={{0,8},{8,16},{16,24},{24,32},{32,40},{40,48},{48,56},{56,64},{64,7... | collective-permute-start | bytes 442376 | tf_op jit(solution)/shard_map/ppermute | solution.py:661
  52.2 21.3 %collective-permute-start.7 = (bf16[3,96,256]{2,1,0:T(8,128)(2,1)S(1)}, bf16[3,96,256]{2,1,0:T(8,128)(2,1)S(1)}, u32[]{:S(2)}, u32[]{:S(2)}) collective-permute-start(bf16[3,96,256]{2,1,0:T(8,128)(2,1)S(1)} %get-tuple-element.54), channel_id=1, source_target_pairs={{0,120},{8,0},{16,8},{24,16},{32,24},{40,32},{48,40},{56,48},{64,5... | collective-permute-start | bytes 442376 | tf_op jit(solution)/shard_map/ppermute | solution.py:661
  54.0 5.9 %collective-permute-start.14 = (bf16[1,272,128]{2,1,0:T(8,128)(2,1)S(1)}, bf16[1,272,128]{2,1,0:T(8,128)(2,1)S(1)}, u32[]{:S(2)}, u32[]{:S(2)}) collective-permute-start(bf16[1,272,128]{2,1,0:T(8,128)(2,1)S(1)} %add_convert_fusion.2), channel_id=1, source_target_pairs={{0,6},{1,7},{2,4},{3,5},{4,2},{5,3},{6,0},{7,1},{8,73},{9,72},{10,... | collective-permute-start | bytes 208904 | tf_op jit(solution)/shard_map/ppermute | solution.py:693
  56.3 5.0 %collective-permute-start.13 = (bf16[1,272,128]{2,1,0:T(8,128)(2,1)S(1)}, bf16[1,272,128]{2,1,0:T(8,128)(2,1)S(1)}, u32[]{:S(2)}, u32[]{:S(2)}) collective-permute-start(bf16[1,272,128]{2,1,0:T(8,128)(2,1)S(1)} %add_convert_fusion.2), channel_id=1, source_target_pairs={{0,4},{1,5},{2,6},{3,7},{4,0},{5,1},{6,2},{7,3},{8,72},{9,73},{10,... | collective-permute-start | bytes 208904 | tf_op jit(solution)/shard_map/ppermute | solution.py:693
  57.7 3.6 %collective-permute-start.12 = (bf16[1,272,128]{2,1,0:T(8,128)(2,1)S(1)}, bf16[1,272,128]{2,1,0:T(8,128)(2,1)S(1)}, u32[]{:S(2)}, u32[]{:S(2)}) collective-permute-start(bf16[1,272,128]{2,1,0:T(8,128)(2,1)S(1)} %add_convert_fusion.2), channel_id=1, source_target_pairs={{0,2},{1,3},{2,0},{3,1},{4,6},{5,7},{6,4},{7,5},{8,9},{9,8},{10,11... | collective-permute-start | bytes 208904 | tf_op jit(solution)/shard_map/ppermute | solution.py:693
  61.4 6.9 %collective-permute-start.17 = (bf16[1,272,128]{2,1,0:T(8,128)(2,1)S(1)}, bf16[1,272,128]{2,1,0:T(8,128)(2,1)S(1)}, u32[]{:S(2)}, u32[]{:S(2)}) collective-permute-start(bf16[1,272,128]{2,1,0:T(8,128)(2,1)S(1)} %add_convert_fusion.1), channel_id=1, source_target_pairs={{0,65},{1,64},{2,67},{3,66},{4,69},{5,68},{6,71},{7,70},{8,56},{9,... | collective-permute-start | bytes 208904 | tf_op jit(solution)/shard_map/ppermute | solution.py:693
  65.4 4.7 %collective-permute-start.16 = (bf16[1,272,128]{2,1,0:T(8,128)(2,1)S(1)}, bf16[1,272,128]{2,1,0:T(8,128)(2,1)S(1)}, u32[]{:S(2)}, u32[]{:S(2)}) collective-permute-start(bf16[1,272,128]{2,1,0:T(8,128)(2,1)S(1)} %add_convert_fusion.1), channel_id=1, source_target_pairs={{0,64},{1,65},{2,66},{3,67},{4,68},{5,69},{6,70},{7,71},{8,40},{9,... | collective-permute-start | bytes 208904 | tf_op jit(solution)/shard_map/ppermute | solution.py:693
  65.4 4.7 %collective-permute-start.15 = (bf16[1,272,128]{2,1,0:T(8,128)(2,1)S(1)}, bf16[1,272,128]{2,1,0:T(8,128)(2,1)S(1)}, u32[]{:S(2)}, u32[]{:S(2)}) collective-permute-start(bf16[1,272,128]{2,1,0:T(8,128)(2,1)S(1)} %add_convert_fusion.1), channel_id=1, source_target_pairs={{0,1},{1,0},{2,3},{3,2},{4,5},{5,4},{6,7},{7,6},{8,24},{9,25},{10,... | collective-permute-start | bytes 208904 | tf_op jit(solution)/shard_map/ppermute | solution.py:693
  70.1 5.5 %collective-permute-start.20 = (bf16[1,272,128]{2,1,0:T(8,128)(2,1)S(1)}, bf16[1,272,128]{2,1,0:T(8,128)(2,1)S(1)}, u32[]{:S(2)}, u32[]{:S(2)}) collective-permute-start(bf16[1,272,128]{2,1,0:T(8,128)(2,1)S(1)} %add_convert_fusion.refs_0_), channel_id=1, source_target_pairs={{0,48},{1,49},{2,50},{3,51},{4,52},{5,53},{6,54},{7,55},{8,14},{9,... | collective-permute-start | bytes 208904 | tf_op jit(solution)/shard_map/ppermute | solution.py:693
  72.2 4.7 %collective-permute-start.19 = (bf16[1,272,128]{2,1,0:T(8,128)(2,1)S(1)}, bf16[1,272,128]{2,1,0:T(8,128)(2,1)S(1)}, u32[]{:S(2)}, u32[]{:S(2)}) collective-permute-start(bf16[1,272,128]{2,1,0:T(8,128)(2,1)S(1)} %add_convert_fusion.refs_0_), channel_id=1, source_target_pairs={{0,32},{1,33},{2,34},{3,35},{4,36},{5,37},{6,38},{7,39},{8,12},{9,... | collective-permute-start | bytes 208904 | tf_op jit(solution)/shard_map/ppermute | solution.py:693
  72.9 3.9 %collective-permute-start.18 = (bf16[1,272,128]{2,1,0:T(8,128)(2,1)S(1)}, bf16[1,272,128]{2,1,0:T(8,128)(2,1)S(1)}, u32[]{:S(2)}, u32[]{:S(2)}) collective-permute-start(bf16[1,272,128]{2,1,0:T(8,128)(2,1)S(1)} %add_convert_fusion.refs_0_), channel_id=1, source_target_pairs={{0,16},{1,17},{2,18},{3,19},{4,20},{5,21},{6,22},{7,23},{8,10},{9,... | collective-permute-start | bytes 208904 | tf_op jit(solution)/shard_map/ppermute | solution.py:693
  76.9 7.9 %collective-permute-start.21 = (bf16[4,272,128]{2,1,0:T(8,128)(2,1)S(1)}, bf16[4,272,128]{2,1,0:T(8,128)(2,1)S(1)}, u32[]{:S(2)}, u32[]{:S(2)}) collective-permute-start(bf16[4,272,128]{2,1,0:T(8,128)(2,1)S(1)} %join.1.own_ref), channel_id=1, source_target_pairs={{0,8},{1,9},{2,10},{3,11},{4,12},{5,13},{6,14},{7,15},{8,0},{9,1},... | collective-permute-start | bytes 835592 | tf_op jit(solution)/shard_map/ppermute | solution.py:693

commit v7 on v6

--- a/solution.py
+++ b/solution.py
@@ -142,28 +142,22 @@
     return jnp.concatenate([wet, wet], axis=-1)
 
 
-def wet_at(ref, i, start, count, channels):
-    return jnp.broadcast_to(ref[start : start + count, i : i + 1], (count, channels))
-
-
-def side_kernel(who_ref, left_ref, right_ref, wet_ref, west_ref, east_ref):
+def side_kernel(left_ref, right_ref, wet_ref, west_ref, east_ref):
     lon, _, channels = left_ref.shape
-    lat = wet_ref.shape[1]
+    wet = jnp.transpose(wet_ref[...].astype(F32))
     low, high = [], []
     for i in range(lon):
-        wet = wet_ref.at[i // TILE]
-        low.append(
-            left_ref[i].astype(F32)[:8] * wet_at(wet, i % TILE, 0, 8, channels)
-        )
-        high.append(
-            right_ref[i].astype(F32)[8:] * wet_at(wet, i % TILE, lat - 8, 8, channels)
-        )
-    send_sides(who_ref, low, high, west_ref, east_ref)
-
-
-def send_sides(who_ref, low, high, west_ref, east_ref):
-    for ref, groups, flag in ((west_ref, pack_low(low), 2), (east_ref, pack_high(high), 3)):
-        inside = jnp.where(who_ref[flag] > 0, 1.0, 0.0)
+        here = wet[:, i : i + 1]
+        low.append(left_ref[i].astype(F32)[:8] * jnp.broadcast_to(here[:8], (8, channels)))
+        high.append(right_ref[i].astype(F32)[8:] * jnp.broadcast_to(here[-8:], (8, channels)))
+    send_sides(low, high, west_ref, east_ref)
+
+
+def send_sides(low, high, west_ref, east_ref):
+    j = lax.axis_index("gy")
+    last = lax.axis_size("gy") - 1
+    for ref, groups, on in ((west_ref, pack_low(low), j > 0), (east_ref, pack_high(high), j < last)):
+        inside = jnp.where(on, 1.0, 0.0)
         for n, tile in enumerate(packed_tiles([group * inside for group in groups])):
             ref[n] = tile
 
@@ -342,7 +336,7 @@
     last = CELLS * (count - 1)
     lows = [wide_grad[TILE * i : TILE * i + 8] for i in range(TILE)]
     highs = [wide_grad[last + TILE * i + 8 : last + TILE * (i + 1)] for i in range(TILE)]
-    send_sides(who_ref, lows, highs, to_west_ref, to_east_ref)
+    send_sides(lows, highs, to_west_ref, to_east_ref)
     for r in range(0, HALF, 8):
         p1, p2, p3 = 0.0, 0.0, 0.0
         for wave, ripple in zip(waves, ripples):
@@ -469,14 +463,13 @@
 IN_VMEM = pl.BlockSpec(memory_space=pltpu.VMEM)
 
 
-def sides(who, x, wet):
+def sides(x, wet):
     lon, lat, channels = x.shape
     shapes = [shape_of((lon // 4, TILE, channels), BF16)] * 2
     return pl.pallas_call(
         side_kernel,
         grid=(1,),
         in_specs=[
-            IN_SMEM,
             pl.BlockSpec((lon, TILE, channels), lambda i: (0, 0, 0)),
             pl.BlockSpec((lon, TILE, channels), lambda i: (0, lat // TILE - 1, 0)),
             whole(*wet.shape),
@@ -485,7 +478,7 @@
         out_shape=shapes,
         compiler_params=pltpu.CompilerParams(vmem_limit_bytes=LARGE_BYTES),
         name="sides",
-    )(who, x, x, wet)
+    )(x, x, wet)
 
 
 def ends(rows, halos):
@@ -682,8 +675,7 @@
     i, j = lax.axis_index("gx"), lax.axis_index("gy")
     core, x, y = i % 2, i // 2 % 4, j // 2
     own, other = jnp.where(core == 0, x, 4 + y), jnp.where(core == 0, 4 + y, x)
-    west, east = j > 0, j < lax.axis_size("gy") - 1
-    return jnp.stack([own, other, west.astype(jnp.int32), east.astype(jnp.int32)]).astype(jnp.int32)
+    return jnp.stack([own, other]).astype(jnp.int32)
 
 
 def summed_blocks(keep, send):
@@ -712,10 +704,9 @@
 ):
     lon, lat, channels = inputs.shape
     units = up_weight.shape[1]
-    wet_rows = wet_mask.astype(F32).reshape(lon // TILE, TILE, lat).transpose(0, 2, 1)
     wet = jnp.broadcast_to(wet_mask.astype(BF16)[:, :, None], (lon, lat, LANES))
     who = places()
-    halos = across_lat(*sides(who, inputs, wet_rows))
+    halos = across_lat(*sides(inputs, wet_mask))
     end_halos = across_lon(*ends((inputs, wet), halos))
     taps = jnp.dot(
         tables()["taps"], kernel.astype(F32), precision=lax.Precision.HIGHEST,

time: 86.7 us -> 84.5 us (0.975)
  other arithmetic: 1.56 us -> 0.22 us
    slice x1, local copies, waits for them, and re-layouts: 0.1 us -> 0.98 us  [local(): taps[3 * HALF:]]
  transfers between devices with their start and end apart: 22 -> 22, of which waited for: 8 -> 8; matrix products, arithmetic and copies ran while one was open for 1% -> 2% of each run, Pallas kernels for 21% -> 22%
where the time goes in v7:
time: 84.5 us; the launch traced here: 84.4 us
  starting transfers between devices  37.9 us (45%)
  Pallas kernels  33.4 us (40%)
  waiting for transfers between devices  9.44 us (11%)
  local copies, waits for them, and re-layouts  1.7 us (2%)
  between operations  1.01 us (1%)
    ppermute x14, starting transfers between devices, move(): return lax.ppermute(x, AXES, swapped(mesh_shape, stage, step))  25.7 us
    pallas_call x2, Pallas kernels, cell_pass(): pl.pallas_call(functools.partial(cell_kernel, at_ends, rows), grid=(2,),...  20.5 us
    pallas_call x4, Pallas kernels, spread_pass(): pl.pallas_call(functools.partial(spread_kernel, at, rows), grid=(1,), in_...  8.73 us
    ppermute x2, starting transfers between devices, across_lat(): lax.ppermute(west, 'gy', ring('gy', -1))  6.02 us
    ppermute x14, waiting for transfers between devices, move(): return lax.ppermute(x, AXES, swapped(mesh_shape, stage, step))  5.35 us
    ppermute x2, starting transfers between devices, across_lon(): lax.ppermute(south, 'gx', ring('gx', 1))  2.77 us
    ppermute x2, waiting for transfers between devices, across_lat(): lax.ppermute(west, 'gy', ring('gy', -1))  2.67 us
    ppermute x2, starting transfers between devices, across_lat(): lax.ppermute(east, 'gy', ring('gy', 1))  2.49 us
  transfers between devices with their start and end apart: 22, of which 8 were waited for; matrix products, arithmetic and copies ran while one was open for 2% of the time, Pallas kernels for 22%

profile of v7, /device:TPU:1, one launch (start us, length us, event | category | flops | bytes accessed | tf_op | source)
XLA Modules:
  0.0 84.4 jit_solution(11143618524552229901)
XLA Ops:
  0.6 0.0 copy-start
  0.6 0.0 copy-start.10
  0.7 2.4 %sides.1 = (bf16[16,16,256]{2,1,0:T(8,128)(2,1)}, bf16[16,16,256]{2,1,0:T(8,128)(2,1)}) custom-call(bf16[64,64,256]{2,1,0:T(8,128)(2,1)} %refs_3_.3, bf16[64,64,256]{2,1,0:T(8,128)(2,1)} %refs_3_.3, s32[64,64]{1,0:T(8,128)} %wet_ref.1), custom_call_target="tpu_custom_call" | custom-call | tf_op jit(solution)/shard_map/sides/pallas_call | solution.py:469
  3.0 2.5 %collective-permute-start = (bf16[16,16,256]{2,1,0:T(8,128)(2,1)}, bf16[16,16,256]{2,1,0:T(8,128)(2,1)S(1)}, u32[]{:S(2)}, u32[]{:S(2)}) collective-permute-start(bf16[16,16,256]{2,1,0:T(8,128)(2,1)} %get-tuple-element.38), channel_id=1, source_target_pairs={{0,1},{1,2},{2,3},{3,4},{4,5},{5,6},{6,7},{7,0},{8,9},{9,10},{10,1... | collective-permute-start | bytes 393224 | tf_op jit(solution)/shard_map/ppermute | solution.py:650
  5.5 2.5 %collective-permute-start.1 = (bf16[16,16,256]{2,1,0:T(8,128)(2,1)}, bf16[16,16,256]{2,1,0:T(8,128)(2,1)S(1)}, u32[]{:S(2)}, u32[]{:S(2)}) collective-permute-start(bf16[16,16,256]{2,1,0:T(8,128)(2,1)} %get-tuple-element.39), channel_id=1, source_target_pairs={{0,7},{1,0},{2,1},{3,2},{4,3},{5,4},{6,5},{7,6},{8,15},{9,8},{10,9... | collective-permute-start | bytes 393224 | tf_op jit(solution)/shard_map/ppermute | solution.py:650
  7.9 0.8 fusion.1
  8.7 0.0 copy-start.12
  8.7 0.0 copy-start.13
  8.7 0.0 copy-start.14
  8.8 0.0 copy-start.15
  8.8 0.0 copy-start.11
  8.8 0.0 copy-start.2
  8.8 1.0 %fusion = (f32[768,256]{1,0:T(8,128)S(1)}, f32[768,256]{1,0:T(8,128)}) fusion(f32[1536,256]{1,0:T(8,128)S(1)} %fusion.1), kind=kLoop, calls=%fused_computation.5 | loop fusion | bytes 3145728 | tf_op jit(solution)/shard_map/slice | solution.py:728
  9.9 0.1 pad_add_fusion.refs_0_.who_ref
  10.0 1.4 %collective-permute-done.refs_2_.refs_7_ = bf16[16,16,256]{2,1,0:T(8,128)(2,1)S(1)} collective-permute-done((bf16[16,16,256]{2,1,0:T(8,128)(2,1)}, bf16[16,16,256]{2,1,0:T(8,128)(2,1)S(1)}, u32[]{:S(2)}, u32[]{:S(2)}) %collective-permute-start) | collective-permute-done | bytes 131104 | tf_op jit(solution)/shard_map/ppermute | solution.py:650
  11.4 1.5 %collective-permute-done.1.refs_3_.refs_8_ = bf16[16,16,256]{2,1,0:T(8,128)(2,1)S(1)} collective-permute-done((bf16[16,16,256]{2,1,0:T(8,128)(2,1)}, bf16[16,16,256]{2,1,0:T(8,128)(2,1)S(1)}, u32[]{:S(2)}, u32[]{:S(2)}) %collective-permute-start.1) | collective-permute-done | bytes 131104 | tf_op jit(solution)/shard_map/ppermute | solution.py:650
  12.9 0.6 broadcast_in_dim.4.refs_0_.refs_1_.refs_4_.refs_5_.refs_6_.wet_ref
  13.5 0.0 copy-start.1
  13.5 0.0 copy-start.3
  13.5 0.0 copy-start.4
  13.5 0.0 copy-start.5
  13.6 0.0 copy-start.6
  13.6 0.0 copy-start.7
  13.6 0.0 copy-start.8
  13.6 0.0 copy-start.9
  13.6 2.7 %collective-permute-start.2 = (bf16[3,96,256]{2,1,0:T(8,128)(2,1)S(1)}, bf16[3,96,256]{2,1,0:T(8,128)(2,1)S(1)}, u32[]{:S(2)}, u32[]{:S(2)}) collective-permute-start(bf16[3,96,256]{2,1,0:T(8,128)(2,1)S(1)} %get-tuple-element.40), channel_id=1, source_target_pairs={{0,8},{8,16},{16,24},{24,32},{32,40},{40,48},{48,56},{56,64},{64,7... | collective-permute-start | bytes 442376 | tf_op jit(solution)/shard_map/ppermute | solution.py:654
  16.3 0.0 collective-permute-start.3
  16.4 9.9 %inner_cells.1 = (bf16[64,64,256]{2,1,0:T(8,128)(2,1)S(1)}, bf16[16,16,256]{2,1,0:T(8,128)(2,1)S(1)}, bf16[16,16,256]{2,1,0:T(8,128)(2,1)S(1)}, f32[2176,128]{1,...) custom-call(s32[2]{0:T(128)S(1)} %pad_add_fusion.refs_0_.who_ref, bf16[64,64,256]{2,1,0:T(8,128)(2,1)S(1)} %copy-done.2, ...), custom_call_target="tpu_custom_call" | custom-call | flops 10000000000 | bytes 8388608 | tf_op jit(solution)/shard_map/inner_cells/pallas_call | solution.py:555
  26.3 0.0 collective-permute-done.2.refs_18_
  26.3 10.6 %end_cells.1 = (bf16[64,64,256]{2,1,0:T(8,128)(2,1)S(1)}, bf16[16,16,256]{2,1,0:T(8,128)(2,1)S(1)}, bf16[16,16,256]{2,1,0:T(8,128)(2,1)S(1)}, f32[4,272,128]{2,1...) custom-call(s32[2]{0:T(128)S(1)} %pad_add_fusion.refs_0_.who_ref, ...), custom_call_target="tpu_custom_call", output_to_operand_aliasing={{0}: (20, {}), {1}: (21, {}), {2}: (22, {})} | custom-call | flops 10000000000 | bytes 8388608 | tf_op jit(solution)/shard_map/end_cells/pallas_call | solution.py:555
  36.9 4.3 %collective-permute-start.8 = (f32[4,272,128]{2,1,0:T(8,128)S(1)}, f32[4,272,128]{2,1,0:T(8,128)S(1)}, u32[]{:S(2)}, u32[]{:S(2)}) collective-permute-start(f32[4,272,128]{2,1,0:T(8,128)S(1)} %get-tuple-element.56), channel_id=1, source_target_pairs={{0,8},{1,9},{2,10},{3,11},{4,12},{5,13},{6,14},{7,15},{8,0},{9,1},... | collective-permute-start | bytes 1671176 | tf_op jit(solution)/shard_map/ppermute | solution.py:685
  41.2 0.0 collective-permute-start.4
  41.3 3.6 %collective-permute-start.5 = (bf16[16,16,256]{2,1,0:T(8,128)(2,1)S(1)}, bf16[16,16,256]{2,1,0:T(8,128)(2,1)S(1)}, u32[]{:S(2)}, u32[]{:S(2)}) collective-permute-start(bf16[16,16,256]{2,1,0:T(8,128)(2,1)S(1)} %get-tuple-element.52), channel_id=1, source_target_pairs={{0,7},{1,0},{2,1},{3,2},{4,3},{5,4},{6,5},{7,6},{8,15},{9,8},{10,9... | collective-permute-start | bytes 393224 | tf_op jit(solution)/shard_map/ppermute | solution.py:650
  44.8 0.1 fold.1
  44.9 0.1 collective-permute-start.9
  45.0 2.6 %collective-permute-start.10 = (bf16[1,272,128]{2,1,0:T(8,128)(2,1)S(1)}, bf16[1,272,128]{2,1,0:T(8,128)(2,1)S(1)}, u32[]{:S(2)}, u32[]{:S(2)}) collective-permute-start(bf16[1,272,128]{2,1,0:T(8,128)(2,1)S(1)} %get-tuple-element.59), channel_id=1, source_target_pairs={{0,32},{1,33},{2,34},{3,35},{4,36},{5,37},{6,38},{7,39},{8,12},{9,... | collective-permute-start | bytes 208904 | tf_op jit(solution)/shard_map/ppermute | solution.py:685
  47.5 1.3 %collective-permute-start.11 = (bf16[1,272,128]{2,1,0:T(8,128)(2,1)S(1)}, bf16[1,272,128]{2,1,0:T(8,128)(2,1)S(1)}, u32[]{:S(2)}, u32[]{:S(2)}) collective-permute-start(bf16[1,272,128]{2,1,0:T(8,128)(2,1)S(1)} %get-tuple-element.60), channel_id=1, source_target_pairs={{0,48},{1,49},{2,50},{3,51},{4,52},{5,53},{6,54},{7,55},{8,14},{9,... | collective-permute-start | bytes 208904 | tf_op jit(solution)/shard_map/ppermute | solution.py:685
  48.8 1.2 %collective-permute-done.5.refs_1_.south_ref.east_ref = bf16[16,16,256]{2,1,0:T(8,128)(2,1)S(1)} collective-permute-done((bf16[16,16,256]{2,1,0:T(8,128)(2,1)S(1)}, bf16[16,16,256]{2,1,0:T(8,128)(2,1)S(1)}, u32[]{:S(2)}, u32[]{:S(2)}) %collective-permute-start.5) | collective-permute-done | bytes 131104 | tf_op jit(solution)/shard_map/ppermute | solution.py:650
  50.0 0.1 collective-permute-start.6
  50.1 0.9 %collective-permute-start.7 = (bf16[3,96,256]{2,1,0:T(8,128)(2,1)S(1)}, bf16[3,96,256]{2,1,0:T(8,128)(2,1)S(1)}, u32[]{:S(2)}, u32[]{:S(2)}) collective-permute-start(bf16[3,96,256]{2,1,0:T(8,128)(2,1)S(1)} %get-tuple-element.54), channel_id=1, source_target_pairs={{0,120},{8,0},{16,8},{24,16},{32,24},{40,32},{48,40},{56,48},{64,5... | collective-permute-start | bytes 442376 | tf_op jit(solution)/shard_map/ppermute | solution.py:654
  51.0 0.9 %collective-permute-done.11 = bf16[1,272,128]{2,1,0:T(8,128)(2,1)S(1)} collective-permute-done((bf16[1,272,128]{2,1,0:T(8,128)(2,1)S(1)}, bf16[1,272,128]{2,1,0:T(8,128)(2,1)S(1)}, u32[]{:S(2)}, u32[]{:S(2)}) %collective-permute-start.11) | collective-permute-done | bytes 69664 | tf_op jit(solution)/shard_map/ppermute | solution.py:685
  52.0 2.2 %collective-permute-start.14 = (bf16[1,272,128]{2,1,0:T(8,128)(2,1)S(1)}, bf16[1,272,128]{2,1,0:T(8,128)(2,1)S(1)}, u32[]{:S(2)}, u32[]{:S(2)}) collective-permute-start(bf16[1,272,128]{2,1,0:T(8,128)(2,1)S(1)} %add_convert_fusion.2), channel_id=1, source_target_pairs={{0,6},{1,7},{2,4},{3,5},{4,2},{5,3},{6,0},{7,1},{8,73},{9,72},{10,... | collective-permute-start | bytes 208904 | tf_op jit(solution)/shard_map/ppermute | solution.py:685
  54.2 1.4 %collective-permute-start.13 = (bf16[1,272,128]{2,1,0:T(8,128)(2,1)S(1)}, bf16[1,272,128]{2,1,0:T(8,128)(2,1)S(1)}, u32[]{:S(2)}, u32[]{:S(2)}) collective-permute-start(bf16[1,272,128]{2,1,0:T(8,128)(2,1)S(1)} %add_convert_fusion.2), channel_id=1, source_target_pairs={{0,4},{1,5},{2,6},{3,7},{4,0},{5,1},{6,2},{7,3},{8,72},{9,73},{10,... | collective-permute-start | bytes 208904 | tf_op jit(solution)/shard_map/ppermute | solution.py:685
  55.6 2.2 %spread_pass.4.out_refs_0_ = f32[64,64,256]{2,1,0:T(8,128)} custom-call(bf16[64,64,256]{2,1,0:T(8,128)(2,1)S(1)} %get-tuple-element.48.before_ref.fg_ref.after_ref, bf16[64,64,256]{2,1,0:T(8,128)(2,1)S(1)} %get-tuple-element.48.before_ref.fg_ref.after_ref, bf16[64,64,256]{2,1,0:T(8,128)(2,1)S(1)} %get-tuple-element.48.before_ref.fg_ref.after_ref, ...), custom_call_target="tpu_custom_call" | custom-call | flops 4000000000 | bytes 4194304 | tf_op jit(solution)/shard_map/spread_pass/pallas_call | solution.py:618
  57.8 0.0 collective-permute-done.14
  57.8 1.3 %collective-permute-done.13 = bf16[1,272,128]{2,1,0:T(8,128)(2,1)S(1)} collective-permute-done((bf16[1,272,128]{2,1,0:T(8,128)(2,1)S(1)}, bf16[1,272,128]{2,1,0:T(8,128)(2,1)S(1)}, u32[]{:S(2)}, u32[]{:S(2)}) %collective-permute-start.13) | collective-permute-done | bytes 69664 | tf_op jit(solution)/shard_map/ppermute | solution.py:685
  59.2 0.1 collective-permute-done.12
  59.4 4.0 %collective-permute-start.17 = (bf16[1,272,128]{2,1,0:T(8,128)(2,1)S(1)}, bf16[1,272,128]{2,1,0:T(8,128)(2,1)S(1)}, u32[]{:S(2)}, u32[]{:S(2)}) collective-permute-start(bf16[1,272,128]{2,1,0:T(8,128)(2,1)S(1)} %add_convert_fusion.1), channel_id=1, source_target_pairs={{0,65},{1,64},{2,67},{3,66},{4,69},{5,68},{6,71},{7,70},{8,56},{9,... | collective-permute-start | bytes 208904 | tf_op jit(solution)/shard_map/ppermute | solution.py:685
  63.4 0.7 collective-permute-start.15
  64.0 2.2 %spread_pass.5.out_refs_0_ = f32[64,64,256]{2,1,0:T(8,128)} custom-call(bf16[64,64,256]{2,1,0:T(8,128)(2,1)S(1)} %get-tuple-element.48.before_ref.fg_ref.after_ref, bf16[64,64,256]{2,1,0:T(8,128)(2,1)S(1)} %get-tuple-element.48.before_ref.fg_ref.after_ref, ...), custom_call_target="tpu_custom_call", output_to_operand_aliasing={{}: (12, {})} | custom-call | flops 4000000000 | bytes 4194304 | tf_op jit(solution)/shard_map/spread_pass/pallas_call | solution.py:618
  66.2 0.0 collective-permute-done.17
  66.2 1.8 %collective-permute-done.16 = bf16[1,272,128]{2,1,0:T(8,128)(2,1)S(1)} collective-permute-done((bf16[1,272,128]{2,1,0:T(8,128)(2,1)S(1)}, bf16[1,272,128]{2,1,0:T(8,128)(2,1)S(1)}, u32[]{:S(2)}, u32[]{:S(2)}) %collective-permute-start.16) | collective-permute-done | bytes 69664 | tf_op jit(solution)/shard_map/ppermute | solution.py:685
  68.0 0.0 collective-permute-done.15
  68.1 2.0 %collective-permute-start.20 = (bf16[1,272,128]{2,1,0:T(8,128)(2,1)S(1)}, bf16[1,272,128]{2,1,0:T(8,128)(2,1)S(1)}, u32[]{:S(2)}, u32[]{:S(2)}) collective-permute-start(bf16[1,272,128]{2,1,0:T(8,128)(2,1)S(1)} %add_convert_fusion.refs_0_), channel_id=1, source_target_pairs={{0,48},{1,49},{2,50},{3,51},{4,52},{5,53},{6,54},{7,55},{8,14},{9,... | collective-permute-start | bytes 208904 | tf_op jit(solution)/shard_map/ppermute | solution.py:685
  70.1 0.8 collective-permute-start.19
  70.9 0.5 collective-permute-start.18
  71.4 2.2 %spread_pass.6.out_refs_0_ = f32[64,64,256]{2,1,0:T(8,128)} custom-call(bf16[64,64,256]{2,1,0:T(8,128)(2,1)S(1)} %get-tuple-element.48.before_ref.fg_ref.after_ref, bf16[64,64,256]{2,1,0:T(8,128)(2,1)S(1)} %get-tuple-element.48.before_ref.fg_ref.after_ref, ...), custom_call_target="tpu_custom_call", output_to_operand_aliasing={{}: (12, {})} | custom-call | flops 4000000000 | bytes 4194304 | tf_op jit(solution)/shard_map/spread_pass/pallas_call | solution.py:618
  73.6 0.0 collective-permute-done.20.refs_3_
  73.6 1.2 %collective-permute-done.19.refs_2_ = bf16[1,272,128]{2,1,0:T(8,128)(2,1)S(1)} collective-permute-done((bf16[1,272,128]{2,1,0:T(8,128)(2,1)S(1)}, bf16[1,272,128]{2,1,0:T(8,128)(2,1)S(1)}, u32[]{:S(2)}, u32[]{:S(2)}) %collective-permute-start.19) | collective-permute-done | bytes 69664 | tf_op jit(solution)/shard_map/ppermute | solution.py:685
  74.8 0.0 collective-permute-done.18.refs_1_
  74.8 5.7 %collective-permute-start.21 = (bf16[4,272,128]{2,1,0:T(8,128)(2,1)S(1)}, bf16[4,272,128]{2,1,0:T(8,128)(2,1)S(1)}, u32[]{:S(2)}, u32[]{:S(2)}) collective-permute-start(bf16[4,272,128]{2,1,0:T(8,128)(2,1)S(1)} %join.1.own_ref), channel_id=1, source_target_pairs={{0,8},{1,9},{2,10},{3,11},{4,12},{5,13},{6,14},{7,15},{8,0},{9,1},... | collective-permute-start | bytes 835592 | tf_op jit(solution)/shard_map/ppermute | solution.py:685
  80.5 2.2 %spread_pass.7 = f32[64,64,256]{2,1,0:T(8,128)} custom-call(bf16[64,64,256]{2,1,0:T(8,128)(2,1)S(1)} %get-tuple-element.48.before_ref.fg_ref.after_ref, bf16[64,64,256]{2,1,0:T(8,128)(2,1)S(1)} %get-tuple-element.48.before_ref.fg_ref.after_ref, ...), custom_call_target="tpu_custom_call", output_to_operand_aliasing={{}: (12, {})} | custom-call | flops 4000000000 | bytes 4194304 | tf_op jit(solution)/shard_map/spread_pass/pallas_call | solution.py:618
  82.7 0.0 collective-permute-done.21.other_ref
  82.7 1.7 %finish.1 = (f32[49,256]{1,0:T(8,128)}, f32[1,256]{1,0:T(1,128)}, f32[1,256]{1,0:T(1,128)}, f32[1,256]{1,0:T(1,128)}, f32[256,512]{1,0:T(8,128)}, /*index=5*/f32[1,512]{1,0:T(1,128)}, f32[512,256]{1,0:T(8,128)}) custom-call(s32[2]{0:T(128)S(1)} %pad_add_fusion.refs_0_.who_ref, bf16[4,272,128]{2,1,0:T(8,128)(2,1)S(1)} %join.1.own_ref, ...), custom_call_target="tpu_custom_call" | custom-call | tf_op jit(solution)/shard_map/finish/pallas_call | solution.py:596
  (34 shorter events, 0.3 us)
Async XLA Ops:
  0.6 7.3 %copy-start = (bf16[49,256]{1,0:T(8,128)(2,1)S(1)}, bf16[49,256]{1,0:T(8,128)(2,1)}, u32[]{:S(2)}) copy-start(bf16[49,256]{1,0:T(8,128)(2,1)} %param.18) | copy-start | bytes 75268
  0.6 7.3 %copy-start.10 = (f32[1536,49]{1,0:T(8,128)S(1)}, f32[1536,49]{1,0:T(8,128)}, u32[]{:S(2)}) copy-start(f32[1536,49]{1,0:T(8,128)} %constant.61.clone) | copy-start | bytes 903172
  3.0 8.3 %collective-permute-start = (bf16[16,16,256]{2,1,0:T(8,128)(2,1)}, bf16[16,16,256]{2,1,0:T(8,128)(2,1)S(1)}, u32[]{:S(2)}, u32[]{:S(2)}) collective-permute-start(bf16[16,16,256]{2,1,0:T(8,128)(2,1)} %get-tuple-element.38), channel_id=1, source_target_pairs={{0,1},{1,2},{2,3},{3,4},{4,5},{5,6},{6,7},{7,0},{8,9},{9,10},{10,1... | collective-permute-start | bytes 393224 | tf_op jit(solution)/shard_map/ppermute | solution.py:650
  5.5 7.4 %collective-permute-start.1 = (bf16[16,16,256]{2,1,0:T(8,128)(2,1)}, bf16[16,16,256]{2,1,0:T(8,128)(2,1)S(1)}, u32[]{:S(2)}, u32[]{:S(2)}) collective-permute-start(bf16[16,16,256]{2,1,0:T(8,128)(2,1)} %get-tuple-element.39), channel_id=1, source_target_pairs={{0,7},{1,0},{2,1},{3,2},{4,3},{5,4},{6,5},{7,6},{8,15},{9,8},{10,9... | collective-permute-start | bytes 393224 | tf_op jit(solution)/shard_map/ppermute | solution.py:650
  8.7 1.1 %copy-start.12 = (bf16[512]{0:T(512)(128)(2,1)S(1)}, bf16[512]{0:T(512)(128)(2,1)}, u32[]{:S(2)}) copy-start(bf16[512]{0:T(512)(128)(2,1)} %param.23) | copy-start | bytes 3076
  8.7 1.0 %copy-start.13 = (bf16[256]{0:T(256)(128)(2,1)S(1)}, bf16[256]{0:T(256)(128)(2,1)}, u32[]{:S(2)}) copy-start(bf16[256]{0:T(256)(128)(2,1)} %param.21) | copy-start | bytes 1540
  8.7 1.0 %copy-start.14 = (bf16[256]{0:T(256)(128)(2,1)S(1)}, bf16[256]{0:T(256)(128)(2,1)}, u32[]{:S(2)}) copy-start(bf16[256]{0:T(256)(128)(2,1)} %param.20) | copy-start | bytes 1540
  8.8 1.0 %copy-start.15 = (bf16[256]{0:T(256)(128)(2,1)S(1)}, bf16[256]{0:T(256)(128)(2,1)}, u32[]{:S(2)}) copy-start(bf16[256]{0:T(256)(128)(2,1)} %param.19) | copy-start | bytes 1540
  8.8 1.1 %copy-start.11 = (s32[64,64]{1,0:T(8,128)S(1)}, s32[64,64]{1,0:T(8,128)}, u32[]{:S(2)}) copy-start(s32[64,64]{1,0:T(8,128)} %wet_ref.1) | copy-start | bytes 49156
  8.8 4.7 %copy-start.2 = (bf16[64,64,256]{2,1,0:T(8,128)(2,1)S(1)}, bf16[64,64,256]{2,1,0:T(8,128)(2,1)}, u32[]{:S(2)}) copy-start(bf16[64,64,256]{2,1,0:T(8,128)(2,1)} %refs_3_.3) | copy-start | bytes 6291460
  13.5 2.8 %copy-start.1 = (bf16[64,64,256]{2,1,0:T(8,128)(2,1)S(1)}, bf16[64,64,256]{2,1,0:T(8,128)(2,1)}, u32[]{:S(2)}) copy-start(bf16[64,64,256]{2,1,0:T(8,128)(2,1)} %cot_ref.7) | copy-start | bytes 6291460
  13.5 2.8 %copy-start.3 = (bf16[512,512]{1,0:T(8,128)(2,1)S(1)}, bf16[512,512]{1,0:T(8,128)(2,1)}, u32[]{:S(2)}) copy-start(bf16[512,512]{1,0:T(8,128)(2,1)} %constant.62.clone.refs_10_.place_ref) | copy-start | bytes 1572868
  13.5 2.8 %copy-start.4 = (bf16[256,512]{1,0:T(8,128)(2,1)S(1)}, bf16[256,512]{1,0:T(8,128)(2,1)}, u32[]{:S(2)}) copy-start(bf16[256,512]{1,0:T(8,128)(2,1)} %constant.64.clone.refs_12_.back_ref) | copy-start | bytes 786436
  13.5 2.8 %copy-start.5 = (f32[768,256]{1,0:T(8,128)S(1)}, f32[768,256]{1,0:T(8,128)}, u32[]{:S(2)}) copy-start(f32[768,256]{1,0:T(8,128)} %get-tuple-element.69.refs_13_) | copy-start | bytes 2359300
  13.6 2.8 %copy-start.6 = (bf16[256,512]{1,0:T(8,128)(2,1)S(1)}, bf16[256,512]{1,0:T(8,128)(2,1)}, u32[]{:S(2)}) copy-start(bf16[256,512]{1,0:T(8,128)(2,1)} %refs_16_.3) | copy-start | bytes 786436
  13.6 2.8 %copy-start.7 = (bf16[512,256]{1,0:T(8,128)(2,1)S(1)}, bf16[512,256]{1,0:T(8,128)(2,1)}, u32[]{:S(2)}) copy-start(bf16[512,256]{1,0:T(8,128)(2,1)} %refs_17_.3) | copy-start | bytes 786436
  13.6 2.8 %copy-start.8 = (bf16[512,256]{1,0:T(8,128)(2,1)S(1)}, bf16[512,256]{1,0:T(8,128)(2,1)}, u32[]{:S(2)}) copy-start(bf16[512,256]{1,0:T(8,128)(2,1)} %constant.63.clone.refs_11_) | copy-start | bytes 786436
  13.6 2.8 %copy-start.9 = (f32[49,768]{1,0:T(8,128)S(1)}, f32[49,768]{1,0:T(8,128)}, u32[]{:S(2)}) copy-start(f32[49,768]{1,0:T(8,128)} %constant.65.clone.refs_14_) | copy-start | bytes 451588
  13.6 12.6 %collective-permute-start.2 = (bf16[3,96,256]{2,1,0:T(8,128)(2,1)S(1)}, bf16[3,96,256]{2,1,0:T(8,128)(2,1)S(1)}, u32[]{:S(2)}, u32[]{:S(2)}) collective-permute-start(bf16[3,96,256]{2,1,0:T(8,128)(2,1)S(1)} %get-tuple-element.40), channel_id=1, source_target_pairs={{0,8},{8,16},{16,24},{24,32},{32,40},{40,48},{48,56},{56,64},{64,7... | collective-permute-start | bytes 442376 | tf_op jit(solution)/shard_map/ppermute | solution.py:654
  16.3 9.9 %collective-permute-start.3 = (bf16[3,96,256]{2,1,0:T(8,128)(2,1)S(1)}, bf16[3,96,256]{2,1,0:T(8,128)(2,1)S(1)}, u32[]{:S(2)}, u32[]{:S(2)}) collective-permute-start(bf16[3,96,256]{2,1,0:T(8,128)(2,1)S(1)} %get-tuple-element.41), channel_id=1, source_target_pairs={{0,120},{8,0},{16,8},{24,16},{32,24},{40,32},{48,40},{56,48},{64,5... | collective-permute-start | bytes 442376 | tf_op jit(solution)/shard_map/ppermute | solution.py:654
  36.9 7.9 %collective-permute-start.8 = (f32[4,272,128]{2,1,0:T(8,128)S(1)}, f32[4,272,128]{2,1,0:T(8,128)S(1)}, u32[]{:S(2)}, u32[]{:S(2)}) collective-permute-start(f32[4,272,128]{2,1,0:T(8,128)S(1)} %get-tuple-element.56), channel_id=1, source_target_pairs={{0,8},{1,9},{2,10},{3,11},{4,12},{5,13},{6,14},{7,15},{8,0},{9,1},... | collective-permute-start | bytes 1671176 | tf_op jit(solution)/shard_map/ppermute | solution.py:685
  41.2 7.6 %collective-permute-start.4 = (bf16[16,16,256]{2,1,0:T(8,128)(2,1)S(1)}, bf16[16,16,256]{2,1,0:T(8,128)(2,1)S(1)}, u32[]{:S(2)}, u32[]{:S(2)}) collective-permute-start(bf16[16,16,256]{2,1,0:T(8,128)(2,1)S(1)} %get-tuple-element.51), channel_id=1, source_target_pairs={{0,1},{1,2},{2,3},{3,4},{4,5},{5,6},{6,7},{7,0},{8,9},{9,10},{10,1... | collective-permute-start | bytes 393224 | tf_op jit(solution)/shard_map/ppermute | solution.py:650
  41.3 8.7 %collective-permute-start.5 = (bf16[16,16,256]{2,1,0:T(8,128)(2,1)S(1)}, bf16[16,16,256]{2,1,0:T(8,128)(2,1)S(1)}, u32[]{:S(2)}, u32[]{:S(2)}) collective-permute-start(bf16[16,16,256]{2,1,0:T(8,128)(2,1)S(1)} %get-tuple-element.52), channel_id=1, source_target_pairs={{0,7},{1,0},{2,1},{3,2},{4,3},{5,4},{6,5},{7,6},{8,15},{9,8},{10,9... | collective-permute-start | bytes 393224 | tf_op jit(solution)/shard_map/ppermute | solution.py:650
  44.9 6.1 %collective-permute-start.9 = (bf16[1,272,128]{2,1,0:T(8,128)(2,1)S(1)}, bf16[1,272,128]{2,1,0:T(8,128)(2,1)S(1)}, u32[]{:S(2)}, u32[]{:S(2)}) collective-permute-start(bf16[1,272,128]{2,1,0:T(8,128)(2,1)S(1)} %get-tuple-element.58), channel_id=1, source_target_pairs={{0,16},{1,17},{2,18},{3,19},{4,20},{5,21},{6,22},{7,23},{8,10},{9,... | collective-permute-start | bytes 208904 | tf_op jit(solution)/shard_map/ppermute | solution.py:685
  45.0 6.0 %collective-permute-start.10 = (bf16[1,272,128]{2,1,0:T(8,128)(2,1)S(1)}, bf16[1,272,128]{2,1,0:T(8,128)(2,1)S(1)}, u32[]{:S(2)}, u32[]{:S(2)}) collective-permute-start(bf16[1,272,128]{2,1,0:T(8,128)(2,1)S(1)} %get-tuple-element.59), channel_id=1, source_target_pairs={{0,32},{1,33},{2,34},{3,35},{4,36},{5,37},{6,38},{7,39},{8,12},{9,... | collective-permute-start | bytes 208904 | tf_op jit(solution)/shard_map/ppermute | solution.py:685
  47.5 4.4 %collective-permute-start.11 = (bf16[1,272,128]{2,1,0:T(8,128)(2,1)S(1)}, bf16[1,272,128]{2,1,0:T(8,128)(2,1)S(1)}, u32[]{:S(2)}, u32[]{:S(2)}) collective-permute-start(bf16[1,272,128]{2,1,0:T(8,128)(2,1)S(1)} %get-tuple-element.60), channel_id=1, source_target_pairs={{0,48},{1,49},{2,50},{3,51},{4,52},{5,53},{6,54},{7,55},{8,14},{9,... | collective-permute-start | bytes 208904 | tf_op jit(solution)/shard_map/ppermute | solution.py:685
  50.0 21.4 %collective-permute-start.6 = (bf16[3,96,256]{2,1,0:T(8,128)(2,1)S(1)}, bf16[3,96,256]{2,1,0:T(8,128)(2,1)S(1)}, u32[]{:S(2)}, u32[]{:S(2)}) collective-permute-start(bf16[3,96,256]{2,1,0:T(8,128)(2,1)S(1)} %get-tuple-element.53), channel_id=1, source_target_pairs={{0,8},{8,16},{16,24},{24,32},{32,40},{40,48},{48,56},{56,64},{64,7... | collective-permute-start | bytes 442376 | tf_op jit(solution)/shard_map/ppermute | solution.py:654
  50.1 21.3 %collective-permute-start.7 = (bf16[3,96,256]{2,1,0:T(8,128)(2,1)S(1)}, bf16[3,96,256]{2,1,0:T(8,128)(2,1)S(1)}, u32[]{:S(2)}, u32[]{:S(2)}) collective-permute-start(bf16[3,96,256]{2,1,0:T(8,128)(2,1)S(1)} %get-tuple-element.54), channel_id=1, source_target_pairs={{0,120},{8,0},{16,8},{24,16},{32,24},{40,32},{48,40},{56,48},{64,5... | collective-permute-start | bytes 442376 | tf_op jit(solution)/shard_map/ppermute | solution.py:654
  52.0 5.9 %collective-permute-start.14 = (bf16[1,272,128]{2,1,0:T(8,128)(2,1)S(1)}, bf16[1,272,128]{2,1,0:T(8,128)(2,1)S(1)}, u32[]{:S(2)}, u32[]{:S(2)}) collective-permute-start(bf16[1,272,128]{2,1,0:T(8,128)(2,1)S(1)} %add_convert_fusion.2), channel_id=1, source_target_pairs={{0,6},{1,7},{2,4},{3,5},{4,2},{5,3},{6,0},{7,1},{8,73},{9,72},{10,... | collective-permute-start | bytes 208904 | tf_op jit(solution)/shard_map/ppermute | solution.py:685
  54.2 5.0 %collective-permute-start.13 = (bf16[1,272,128]{2,1,0:T(8,128)(2,1)S(1)}, bf16[1,272,128]{2,1,0:T(8,128)(2,1)S(1)}, u32[]{:S(2)}, u32[]{:S(2)}) collective-permute-start(bf16[1,272,128]{2,1,0:T(8,128)(2,1)S(1)} %add_convert_fusion.2), channel_id=1, source_target_pairs={{0,4},{1,5},{2,6},{3,7},{4,0},{5,1},{6,2},{7,3},{8,72},{9,73},{10,... | collective-permute-start | bytes 208904 | tf_op jit(solution)/shard_map/ppermute | solution.py:685
  55.6 3.7 %collective-permute-start.12 = (bf16[1,272,128]{2,1,0:T(8,128)(2,1)S(1)}, bf16[1,272,128]{2,1,0:T(8,128)(2,1)S(1)}, u32[]{:S(2)}, u32[]{:S(2)}) collective-permute-start(bf16[1,272,128]{2,1,0:T(8,128)(2,1)S(1)} %add_convert_fusion.2), channel_id=1, source_target_pairs={{0,2},{1,3},{2,0},{3,1},{4,6},{5,7},{6,4},{7,5},{8,9},{9,8},{10,11... | collective-permute-start | bytes 208904 | tf_op jit(solution)/shard_map/ppermute | solution.py:685
  59.4 6.9 %collective-permute-start.17 = (bf16[1,272,128]{2,1,0:T(8,128)(2,1)S(1)}, bf16[1,272,128]{2,1,0:T(8,128)(2,1)S(1)}, u32[]{:S(2)}, u32[]{:S(2)}) collective-permute-start(bf16[1,272,128]{2,1,0:T(8,128)(2,1)S(1)} %add_convert_fusion.1), channel_id=1, source_target_pairs={{0,65},{1,64},{2,67},{3,66},{4,69},{5,68},{6,71},{7,70},{8,56},{9,... | collective-permute-start | bytes 208904 | tf_op jit(solution)/shard_map/ppermute | solution.py:685
  63.4 4.7 %collective-permute-start.16 = (bf16[1,272,128]{2,1,0:T(8,128)(2,1)S(1)}, bf16[1,272,128]{2,1,0:T(8,128)(2,1)S(1)}, u32[]{:S(2)}, u32[]{:S(2)}) collective-permute-start(bf16[1,272,128]{2,1,0:T(8,128)(2,1)S(1)} %add_convert_fusion.1), channel_id=1, source_target_pairs={{0,64},{1,65},{2,66},{3,67},{4,68},{5,69},{6,70},{7,71},{8,40},{9,... | collective-permute-start | bytes 208904 | tf_op jit(solution)/shard_map/ppermute | solution.py:685
  63.4 4.7 %collective-permute-start.15 = (bf16[1,272,128]{2,1,0:T(8,128)(2,1)S(1)}, bf16[1,272,128]{2,1,0:T(8,128)(2,1)S(1)}, u32[]{:S(2)}, u32[]{:S(2)}) collective-permute-start(bf16[1,272,128]{2,1,0:T(8,128)(2,1)S(1)} %add_convert_fusion.1), channel_id=1, source_target_pairs={{0,1},{1,0},{2,3},{3,2},{4,5},{5,4},{6,7},{7,6},{8,24},{9,25},{10,... | collective-permute-start | bytes 208904 | tf_op jit(solution)/shard_map/ppermute | solution.py:685
  68.1 5.5 %collective-permute-start.20 = (bf16[1,272,128]{2,1,0:T(8,128)(2,1)S(1)}, bf16[1,272,128]{2,1,0:T(8,128)(2,1)S(1)}, u32[]{:S(2)}, u32[]{:S(2)}) collective-permute-start(bf16[1,272,128]{2,1,0:T(8,128)(2,1)S(1)} %add_convert_fusion.refs_0_), channel_id=1, source_target_pairs={{0,48},{1,49},{2,50},{3,51},{4,52},{5,53},{6,54},{7,55},{8,14},{9,... | collective-permute-start | bytes 208904 | tf_op jit(solution)/shard_map/ppermute | solution.py:685
  70.1 4.7 %collective-permute-start.19 = (bf16[1,272,128]{2,1,0:T(8,128)(2,1)S(1)}, bf16[1,272,128]{2,1,0:T(8,128)(2,1)S(1)}, u32[]{:S(2)}, u32[]{:S(2)}) collective-permute-start(bf16[1,272,128]{2,1,0:T(8,128)(2,1)S(1)} %add_convert_fusion.refs_0_), channel_id=1, source_target_pairs={{0,32},{1,33},{2,34},{3,35},{4,36},{5,37},{6,38},{7,39},{8,12},{9,... | collective-permute-start | bytes 208904 | tf_op jit(solution)/shard_map/ppermute | solution.py:685
  70.9 3.9 %collective-permute-start.18 = (bf16[1,272,128]{2,1,0:T(8,128)(2,1)S(1)}, bf16[1,272,128]{2,1,0:T(8,128)(2,1)S(1)}, u32[]{:S(2)}, u32[]{:S(2)}) collective-permute-start(bf16[1,272,128]{2,1,0:T(8,128)(2,1)S(1)} %add_convert_fusion.refs_0_), channel_id=1, source_target_pairs={{0,16},{1,17},{2,18},{3,19},{4,20},{5,21},{6,22},{7,23},{8,10},{9,... | collective-permute-start | bytes 208904 | tf_op jit(solution)/shard_map/ppermute | solution.py:685
  74.8 7.9 %collective-permute-start.21 = (bf16[4,272,128]{2,1,0:T(8,128)(2,1)S(1)}, bf16[4,272,128]{2,1,0:T(8,128)(2,1)S(1)}, u32[]{:S(2)}, u32[]{:S(2)}) collective-permute-start(bf16[4,272,128]{2,1,0:T(8,128)(2,1)S(1)} %join.1.own_ref), channel_id=1, source_target_pairs={{0,8},{1,9},{2,10},{3,11},{4,12},{5,13},{6,14},{7,15},{8,0},{9,1},... | collective-permute-start | bytes 835592 | tf_op jit(solution)/shard_map/ppermute | solution.py:685

commit v8 on v7

--- a/solution.py
+++ b/solution.py
@@ -48,6 +48,14 @@
     for n, f in enumerate(pairs, start=2):
         cos[n], sin[n], weight[n], paired[n] = np.cos(angle(f)), -np.sin(angle(f)), 2, 1
     return cos, sin, weight / SPAN**2, paired
+
+
+def in_parts(values):
+    parts = []
+    for _ in range(3):
+        parts.append(values.astype(jnp.bfloat16))
+        values = values - parts[-1].astype(np.float64)
+    return np.concatenate(parts, axis=1)
 
 
 @functools.cache
@@ -76,7 +84,7 @@
         place=place.astype(jnp.bfloat16),
         own=own.astype(jnp.bfloat16),
         back=back.astype(jnp.bfloat16),
-        taps=np.concatenate([taps, flipped]).astype(np.float32),
+        taps=in_parts(np.concatenate([taps, flipped])),
         collect=collect.astype(np.float32),
     )
 
@@ -202,102 +210,20 @@
     return pl.ds(pl.multiple_of((place ^ k) * rows, 16), rows)
 
 
-def row_of_step(ends, step, rows):
-    return (rows - 1) * step if ends else 1 + step
-
-
 def cdf_and_slope(hidden):
     cumulative = 0.5 + 0.5 * lax.erf(hidden * 0.7071067811865476)
     bell = jnp.exp2(hidden * (hidden * (-0.5 * 1.4426950408889634)))
     return cumulative, cumulative + (hidden * 0.3989422804014327) * bell
 
 
-def cell_kernel(ends, rows, *refs):
-    (
-        who_ref, before_ref, x_ref, after_ref, wet_before_ref, wet_ref, wet_after_ref,
-        west_ref, east_ref, cot_ref, place_ref, own_ref, back_ref, taps_ref, collect_ref,
-        vectors_ref, up_ref, down_ref,
-    ) = refs[:18]
-    if ends:
-        (
-            north_ref, south_ref, _, _, _, sum_in_ref, p_in_ref, small_in_ref,
-            fg_ref, to_west_ref, to_east_ref, keep_ref, send_ref, top_ref, bottom_ref,
-            sum_ref, p_ref, small_ref, pad_ref,
-        ) = refs[18:]
-    else:
-        fg_ref, to_west_ref, to_east_ref, sum_ref, p_ref, small_ref, pad_ref = refs[18:]
-    step = pl.program_id(0)
-    a = row_of_step(ends, step, rows)
-    lat, channels = x_ref.shape[1:]
-    units = up_ref.shape[1]
-    count = lat // TILE
-
-    @pl.when(step == 0)
-    def _():
-        if ends:
-            sum_ref[...] = sum_in_ref[...]
-            p_ref[...] = p_in_ref[...]
-            small_ref[...] = small_in_ref[...]
-        else:
-            for ref in (sum_ref, p_ref, small_ref):
-                ref[...] = jnp.zeros_like(ref)
-
-    def fill(i):
-        ref, wets, n = x_ref, wet_ref, i
-        if i < 0:
-            ref, wets, n = before_ref, wet_before_ref, i + 8
-        elif i >= TILE:
-            ref, wets, n = after_ref, wet_after_ref, i - TILE
-        pad_ref[3 + i, :TILE, :] = outer(side_group(west_ref, 4 * a, i, False), False)
-        pad_ref[3 + i, TILE : TILE + lat, :] = ref[n] * both(wets[n])
-        pad_ref[3 + i, TILE + lat :, :] = outer(side_group(east_ref, 4 * a, i, True), True)
-
-    for i in range(TILE):
-        fill(i)
-    if ends:
-
-        @pl.when(step == 0)
-        def _():
-            pad_ref[:3] = north_ref[...]
-            for i in range(TILE, TILE + 3):
-                fill(i)
-
-        @pl.when(step == 1)
-        def _():
-            pad_ref[3 + TILE :] = south_ref[...]
-            for i in range(-3, 0):
-                fill(i)
-
-    else:
-        for i in (-3, -2, -1, TILE, TILE + 1, TILE + 2):
-            fill(i)
-
-    def columns(i, b):
-        return pad_ref[i, TILE * b : TILE * (b + 1), :]
-
+def cell_body(patches, masked_grad, constants, sum_ref, p_ref, small_ref):
+    place_ref, own_ref, back_ref, taps_ref, vectors_ref, up_ref, down_ref = constants
+    channels, units = up_ref.shape
     vectors = vectors_ref[...].astype(F32)
     conv_bias, gain, shift = (vectors[:, channels * n : channels * (n + 1)] for n in range(3))
     up_bias = vectors[:, 3 * channels :]
-    patches = [
-        patch(
-            [columns(i, b + 1) for i in range(SPAN)],
-            [columns(i, b).astype(F32)[8:] for i in range(SPAN)],
-            [columns(i, b + 2).astype(F32)[:8] for i in range(SPAN)],
-        )
-        for b in range(count)
-    ]
     waves = transformed(patches, place_ref)
     field = jnp.concatenate(filtered(waves, taps_ref, back_ref)) + conv_bias
-
-    def by_tile(ref):
-        return jnp.concatenate(
-            [
-                ref[:, TILE * b : TILE * (b + 1), :].reshape(CELLS, ref.shape[2])
-                for b in range(count)
-            ]
-        )
-
-    masked_grad = by_tile(cot_ref) * both(by_tile(wet_ref))
     average = jnp.mean(field, axis=-1, keepdims=True)
     centred = field - average
     variance = jnp.mean(centred * centred, axis=-1, keepdims=True)
@@ -328,15 +254,9 @@
     product_mean = jnp.mean(product * gain, axis=-1, keepdims=True)
     wide_grad = inv_std * (scaled - scaled_mean - normed * product_mean)
     field_grad = wide_grad.astype(BF16)
-    ripples = []
-    for b in range(count):
-        own = field_grad[CELLS * b : CELLS * (b + 1)]
-        fg_ref[:, TILE * b : TILE * (b + 1), :] = own.reshape(TILE, TILE, channels)
-        ripples.append(dot(own_ref[...], own))
-    last = CELLS * (count - 1)
-    lows = [wide_grad[TILE * i : TILE * i + 8] for i in range(TILE)]
-    highs = [wide_grad[last + TILE * i + 8 : last + TILE * (i + 1)] for i in range(TILE)]
-    send_sides(lows, highs, to_west_ref, to_east_ref)
+    ripples = [
+        dot(own_ref[...], field_grad[CELLS * n : CELLS * (n + 1)]) for n in range(len(waves))
+    ]
     for r in range(0, HALF, 8):
         p1, p2, p3 = 0.0, 0.0, 0.0
         for wave, ripple in zip(waves, ripples):
@@ -349,9 +269,158 @@
         p_ref[1, r : r + 8, :] += p2
         p_ref[2, r : r + 8, :] += p3
     small_ref[51:52, :] += sum(ripple[0:1] for ripple in ripples)
-
-    if not ends:
-        return
+    return wide_grad, field_grad
+
+
+def groups_of(wide_grad, tiles, start):
+    return [
+        wide_grad[CELLS * n + TILE * i + start :][:8] for n in tiles for i in range(TILE)
+    ]
+
+
+def tile_cells(ref, b):
+    return ref[:, TILE * b : TILE * (b + 1), :].reshape(CELLS, ref.shape[2])
+
+
+def middle_kernel(sides, *refs):
+    x_refs, wet_refs, cot_refs = refs[:4], refs[4:8], refs[8:10]
+    place_ref, own_ref, back_ref, taps_ref, vectors_ref, up_ref, down_ref = refs[10:17]
+    lat, channels = x_refs[0].shape[1:]
+    count = lat // TILE
+    if sides:
+        west_ref, east_ref, _, sum_in_ref, p_in_ref, small_in_ref = refs[17:23]
+        fg_ref, sum_ref, p_ref, small_ref, to_west_ref, to_east_ref = refs[23:29]
+        pad_ref, tile_ref, low_ref, high_ref, sems = refs[29:]
+        sum_ref[...] = sum_in_ref[...]
+        p_ref[...] = p_in_ref[...]
+        small_ref[...] = small_in_ref[...]
+    else:
+        kernel_ref = refs[17]
+        fg_ref, sum_ref, p_ref, small_ref, wave_taps_ref, flipped_ref = refs[18:24]
+        pad_ref, tile_ref, sems = refs[24:]
+        for ref in (sum_ref, p_ref, small_ref):
+            ref[...] = jnp.zeros_like(ref)
+        kernel = jnp.concatenate([kernel_ref[...]] * 3, axis=0)
+        for n, ref in enumerate((wave_taps_ref, flipped_ref)):
+            ref[...] = dot(taps_ref[3 * HALF * n : 3 * HALF * (n + 1), :], kernel)
+        taps_ref = wave_taps_ref
+    for i in range(2 * TILE + 6):
+        n = i - 3
+        if n < 0:
+            k, n = 0, n + 8
+        else:
+            k, n = 1 + n // TILE, n % TILE
+        pad_ref[i, TILE : TILE + lat, :] = x_refs[k][n] * both(wet_refs[k][n])
+        if sides:
+            pad_ref[i, :TILE, :] = outer(side_group(west_ref, 4, i - 3, False), False)
+            pad_ref[i, TILE + lat :, :] = outer(side_group(east_ref, 4, i - 3, True), True)
+
+    def columns(i, b):
+        return pad_ref[i, TILE * b : TILE * (b + 1), :]
+
+    edge = [0, count - 1]
+    order = [(a, b) for b in (edge if sides else range(1, count - 1)) for a in range(2)]
+    patches = []
+    for a, b in order:
+        slabs = range(TILE * a, TILE * a + SPAN)
+        patches.append(
+            patch(
+                [columns(i, b + 1) for i in slabs],
+                [columns(i, b).astype(F32)[8:] for i in slabs],
+                [columns(i, b + 2).astype(F32)[:8] for i in slabs],
+            )
+        )
+    masked_grad = jnp.concatenate(
+        [tile_cells(cot_refs[a], b) * both(tile_cells(wet_refs[1 + a], b)) for a, b in order]
+    )
+    constants = place_ref, own_ref, back_ref, taps_ref, vectors_ref, up_ref, down_ref
+    wide_grad, field_grad = cell_body(patches, masked_grad, constants, sum_ref, p_ref, small_ref)
+    rows = slice(TILE, 3 * TILE)
+    copies = []
+    for n, (a, b) in enumerate(order):
+        own = field_grad[CELLS * n : CELLS * (n + 1)].reshape(TILE, TILE, channels)
+        tile_ref[n // 2, TILE * a : TILE * (a + 1)] = own
+    for n, b in enumerate(sorted({b for _, b in order})):
+        here = slice(TILE * b, TILE * (b + 1))
+        copies.append(pltpu.make_async_copy(tile_ref.at[n], fg_ref.at[rows, here], sems.at[n]))
+    if sides:
+        send_sides(
+            groups_of(wide_grad, (0, 1), 0), groups_of(wide_grad, (2, 3), 8), low_ref, high_ref
+        )
+        for n, (ref, out_ref) in enumerate(((low_ref, to_west_ref), (high_ref, to_east_ref))):
+            copies.append(pltpu.make_async_copy(ref, out_ref.at[4:12], sems.at[2 + n]))
+    for copy in copies:
+        copy.start()
+    for copy in copies:
+        copy.wait()
+
+
+def end_rows_kernel(rows, *refs):
+    (
+        who_ref, before_ref, x_ref, after_ref, wet_before_ref, wet_ref, wet_after_ref,
+        west_ref, east_ref, cot_ref, collect_ref,
+    ) = refs[:11]
+    constants = refs[11:18]
+    north_ref, south_ref, _, _, _, sum_in_ref, p_in_ref, small_in_ref = refs[18:26]
+    fg_ref, to_west_ref, to_east_ref, keep_ref, send_ref, top_ref, bottom_ref = refs[26:33]
+    sum_ref, p_ref, small_ref, pad_ref = refs[33:]
+    step = pl.program_id(0)
+    a = (rows - 1) * step
+    lat, channels = x_ref.shape[1:]
+    units = constants[5].shape[1]
+    count = lat // TILE
+
+    @pl.when(step == 0)
+    def _():
+        sum_ref[...] = sum_in_ref[...]
+        p_ref[...] = p_in_ref[...]
+        small_ref[...] = small_in_ref[...]
+
+    def fill(i):
+        ref, wets, n = x_ref, wet_ref, i
+        if i < 0:
+            ref, wets, n = before_ref, wet_before_ref, i + 8
+        elif i >= TILE:
+            ref, wets, n = after_ref, wet_after_ref, i - TILE
+        pad_ref[3 + i, :TILE, :] = outer(side_group(west_ref, 4 * a, i, False), False)
+        pad_ref[3 + i, TILE : TILE + lat, :] = ref[n] * both(wets[n])
+        pad_ref[3 + i, TILE + lat :, :] = outer(side_group(east_ref, 4 * a, i, True), True)
+
+    for i in range(TILE):
+        fill(i)
+
+    @pl.when(step == 0)
+    def _():
+        pad_ref[:3] = north_ref[...]
+        for i in range(TILE, TILE + 3):
+            fill(i)
+
+    @pl.when(step == 1)
+    def _():
+        pad_ref[3 + TILE :] = south_ref[...]
+        for i in range(-3, 0):
+            fill(i)
+
+    def columns(i, b):
+        return pad_ref[i, TILE * b : TILE * (b + 1), :]
+
+    patches = [
+        patch(
+            [columns(i, b + 1) for i in range(SPAN)],
+            [columns(i, b).astype(F32)[8:] for i in range(SPAN)],
+            [columns(i, b + 2).astype(F32)[:8] for i in range(SPAN)],
+        )
+        for b in range(count)
+    ]
+    masked_grad = jnp.concatenate(
+        [tile_cells(cot_ref, b) * both(tile_cells(wet_ref, b)) for b in range(count)]
+    )
+    wide_grad, field_grad = cell_body(patches, masked_grad, constants, sum_ref, p_ref, small_ref)
+    for b in range(count):
+        own = field_grad[CELLS * b : CELLS * (b + 1)]
+        fg_ref[:, TILE * b : TILE * (b + 1), :] = own.reshape(TILE, TILE, channels)
+    lows, highs = groups_of(wide_grad, (0,), 0), groups_of(wide_grad, (count - 1,), 8)
+    send_sides(lows, highs, to_west_ref, to_east_ref)
 
     @pl.when(step == 0)
     def _():
@@ -507,18 +576,69 @@
     )(*operands, *halos)
 
 
-def cell_pass(who, x, halos, cotangent, wet, taps, params, end_halos=(), earlier=()):
+def sum_shapes(channels, units):
+    rows = (4 * units * channels // 2 + 64 * channels) // LANES
+    return [shape_of((rows, LANES)), shape_of((3, HALF, channels)), shape_of((64, channels))]
+
+
+def middle_cells(x, cotangent, wet, taps, params, kernel=None, halos=(), earlier=()):
     table = tables()
     lon, lat, channels = x.shape
-    at_ends = len(end_halos) > 0
+    sides_too = len(halos) > 0
+    sums = sum_shapes(channels, params[1].shape[1])
+
+    def rows(depth, *blocks):
+        return [pl.BlockSpec((size, lat, depth), lambda i, n=n: (n, 0, 0)) for size, n in blocks]
+
+    around = (8, 1), (TILE, 1), (TILE, 2), (8, 6)
+    constants = [table["place"], table["own"], table["back"], taps, *params]
+    operands = [x] * 4 + [wet] * 4 + [cotangent] * 2 + constants
+    in_specs = rows(channels, *around) + rows(LANES, *around) + rows(channels, *around[1:3])
+    in_specs += [whole(*c.shape) for c in constants]
+    out_shape = [shape_of(x.shape, BF16)] + sums
+    out_specs = [ANY] + [whole(*s.shape) for s in sums]
+    scratch = [
+        pltpu.VMEM((2 * TILE + 6, lat + 2 * TILE, channels), BF16),
+        pltpu.VMEM((2, 2 * TILE, TILE, channels), BF16),
+    ]
+    aliases = {}
+    if sides_too:
+        aliases = {len(operands) + 2: 0}
+        operands += [*halos, *earlier]
+        in_specs += [whole(*h.shape) for h in halos] + [ANY] + [whole(*s.shape) for s in sums]
+        out_shape += [shape_of(h.shape, BF16) for h in halos]
+        out_specs += [ANY] * 2
+        scratch += [pltpu.VMEM((8, TILE, channels), BF16)] * 2
+    else:
+        operands.append(kernel)
+        in_specs.append(whole(*kernel.shape))
+        out_shape += [shape_of((3 * HALF, channels))] * 2
+        out_specs += [whole(3 * HALF, channels)] * 2
+    return pl.pallas_call(
+        functools.partial(middle_kernel, sides_too),
+        grid=(1,),
+        in_specs=in_specs,
+        out_specs=out_specs,
+        out_shape=out_shape,
+        scratch_shapes=scratch + [pltpu.SemaphoreType.DMA((4 if sides_too else 2,))],
+        input_output_aliases=aliases,
+        compiler_params=pltpu.CompilerParams(vmem_limit_bytes=VMEM_BYTES),
+        cost_estimate=pl.CostEstimate(
+            flops=5 * 10**9, bytes_accessed=8 * 2**20, transcendentals=0
+        ),
+        name="flank_cells" if sides_too else "core_cells",
+    )(*operands)
+
+
+def end_cells(who, x, halos, cotangent, wet, taps, params, end_halos, earlier):
+    table = tables()
+    lon, lat, channels = x.shape
     rows = lon // TILE
-    units = params[1].shape[1]
-    sum_rows = (4 * units * channels // 2 + 64 * channels) // LANES
-    sums = [shape_of((sum_rows, LANES)), shape_of((3, HALF, channels)), shape_of((64, channels))]
-    half = shape_of((BLOCKS // 2, sum_rows // BLOCKS, LANES))
+    sums = sum_shapes(channels, params[1].shape[1])
+    half = shape_of((BLOCKS // 2, sums[0].shape[0] // BLOCKS, LANES))
 
     def row(step):
-        return row_of_step(at_ends, step, rows)
+        return (rows - 1) * step
 
     def tiled(depth):
         return pl.BlockSpec((TILE, lat, depth), lambda i: (row(i), 0, 0))
@@ -533,38 +653,30 @@
         ]
 
     packed = pl.BlockSpec((4, TILE, channels), lambda i: (row(i), 0, 0))
-    constants = [table["place"], table["own"], table["back"], taps, table["collect"], *params]
-    operands = [who, x, x, x, wet, wet, wet, *halos, cotangent, *constants]
+    constants = [table["collect"], table["place"], table["own"], table["back"], taps, *params]
+    operands = [who, x, x, x, wet, wet, wet, *halos, cotangent, *constants, *end_halos]
     in_specs = [IN_SMEM, *around(channels), *around(LANES), *[whole(*h.shape) for h in halos]]
-    in_specs += [tiled(channels)] + [whole(*c.shape) for c in constants]
+    in_specs += [tiled(channels)] + [whole(*c.shape) for c in (*constants, *end_halos)]
+    aliases = {len(operands) + n: n for n in range(3)}
+    operands += earlier
+    in_specs += [ANY] * 3 + [whole(*s.shape) for s in sums]
     out_shape = [shape_of(x.shape, BF16)] + [shape_of(h.shape, BF16) for h in halos]
-    out_specs = [tiled(channels), packed, packed]
-    scratch = [pltpu.VMEM((SPAN, lat + 2 * TILE, channels), BF16)]
-    aliases = {}
-    if at_ends:
-        first = len(operands) + len(end_halos)
-        aliases = {first + n: n for n in range(3)}
-        operands += [*end_halos, *earlier]
-        in_specs += [whole(*h.shape) for h in end_halos] + [ANY] * 3
-        in_specs += [whole(*s.shape) for s in sums]
-        out_shape += [half, half] + [shape_of((3, lat, channels), BF16)] * 2
-        scratch = [pltpu.VMEM(s.shape, F32) for s in sums] + scratch
-    else:
-        out_shape += sums
-    out_specs += [whole(*s.shape) for s in out_shape[3:]]
+    out_shape += [half, half] + [shape_of((3, lat, channels), BF16)] * 2
+    out_specs = [tiled(channels), packed, packed] + [whole(*s.shape) for s in out_shape[3:]]
+    scratch = [pltpu.VMEM(s.shape, F32) for s in sums]
     return pl.pallas_call(
-        functools.partial(cell_kernel, at_ends, rows),
+        functools.partial(end_rows_kernel, rows),
         grid=(2,),
         in_specs=in_specs,
         out_specs=out_specs,
         out_shape=out_shape,
-        scratch_shapes=scratch,
+        scratch_shapes=scratch + [pltpu.VMEM((SPAN, lat + 2 * TILE, channels), BF16)],
         input_output_aliases=aliases,
         compiler_params=pltpu.CompilerParams(vmem_limit_bytes=VMEM_BYTES),
         cost_estimate=pl.CostEstimate(
             flops=10 * 10**9, bytes_accessed=8 * 2**20, transcendentals=0
         ),
-        name="end_cells" if at_ends else "inner_cells",
+        name="end_cells",
     )(*operands)
 
 
@@ -704,19 +816,19 @@
 ):
     lon, lat, channels = inputs.shape
     units = up_weight.shape[1]
+    halos = across_lat(*sides(inputs, wet_mask))
     wet = jnp.broadcast_to(wet_mask.astype(BF16)[:, :, None], (lon, lat, LANES))
-    who = places()
-    halos = across_lat(*sides(inputs, wet_mask))
-    end_halos = across_lon(*ends((inputs, wet), halos))
-    taps = jnp.dot(
-        tables()["taps"], kernel.astype(F32), precision=lax.Precision.HIGHEST,
-        preferred_element_type=F32,
-    )
     vectors = jnp.concatenate([conv_bias, norm_gain, norm_shift, up_bias])[None, :]
     params = (vectors, up_weight, down_weight)
-    first = (who, inputs, halos, cotangent, wet, taps[: 3 * HALF], params)
-    inner = cell_pass(*first)
-    field_grad, west, east, keep, send, top, bottom = cell_pass(*first, end_halos, inner)
+    *core, taps, flipped = middle_cells(inputs, cotangent, wet, tables()["taps"], params, kernel)
+    end_halos = across_lon(*ends((inputs, wet), halos))
+    field_grad, *sums, west, east = middle_cells(
+        inputs, cotangent, wet, taps, params, None, halos, core
+    )
+    earlier = (field_grad, west, east, *sums)
+    field_grad, west, east, keep, send, top, bottom = end_cells(
+        places(), inputs, halos, cotangent, wet, taps, params, end_halos, earlier
+    )
     halos = across_lat(west, east)
     end_halos = across_lon(*ends((top, bottom), halos))
     own, other = summed_blocks(keep, send)
@@ -725,10 +837,10 @@
     for at in (*middle, 0, lon // TILE - 1):
         far = halos if at in middle else end_halos
         input_grad = spread_pass(
-            at, field_grad, halos, far, cotangent, wet, taps[3 * HALF :], input_grad
+            at, field_grad, halos, far, cotangent, wet, flipped, input_grad
         )
     cells = lon * lat * lax.axis_size("gx") * lax.axis_size("gy")
-    grads = finish(who, own, other, float(cells) ** -0.5, channels, units)
+    grads = finish(places(), own, other, float(cells) ** -0.5, channels, units)
     taps_grad, bias_grad, gain_grad, shift_grad, up_grad, up_bias_grad, down_grad = grads
     return (
         input_grad, taps_grad, bias_grad[0], gain_grad[0], shift_grad[0], up_grad,

time: 84.5 us -> 95.3 us (1.13)
  local copies, waits for them, and re-layouts: 1.7 us -> 13.8 us
  waiting for transfers between devices: 9.44 us -> 6.03 us
  Pallas kernels: 33.4 us -> 34.9 us
  starting transfers between devices: 37.9 us -> 38.9 us
    unnamed x32 -> x66, local copies, waits for them, and re-layouts: 0.11 us -> 13.2 us
    ppermute x2, waiting for transfers between devices: 2.67 us -> 0.17 us  [across_lat(): lax.ppermute(west, 'gy', ring('gy', -1))]
    ppermute x2, waiting for transfers between devices: 1.41 us -> 0.01 us  [across_lat(): lax.ppermute(east, 'gy', ring('gy', 1))]
    ppermute x14, starting transfers between devices: 25.7 us -> 26.8 us  [move(): return lax.ppermute(x, AXES, swapped(mesh_shape, stage, step))]
    pallas_call x2, Pallas kernels: 0.06 us -> 1.1 us  [ends(): pl.pallas_call(functools.partial(end_kernel, masks), grid=(1,), in_specs=...]
    slice x1 -> x0, local copies, waits for them, and re-layouts: 0.98 us -> none  [local(): taps[3 * HALF:]]
    pallas_call x2 -> x3, Pallas kernels: 20.5 us -> 21.2 us  [the longest x1 10.8 us: end_cells(): pl.pallas_call(functools.partial(end_rows_kernel, rows), grid=(2,), in_sp...]
  transfers between devices with their start and end apart: 22 -> 22, of which waited for: 8 -> 5; matrix products, arithmetic and copies ran while one was open for 2% -> 1% of each run, Pallas kernels for 22% -> 20%
where the time goes in v8:
time: 95.3 us; the launch traced here: 94.8 us
  starting transfers between devices  38.9 us (41%)
  Pallas kernels  34.9 us (37%)
  local copies, waits for them, and re-layouts  13.8 us (14%)
  waiting for transfers between devices  6.03 us (6%)
  between operations  1.04 us (1%)
    ppermute x14, starting transfers between devices, move(): return lax.ppermute(x, AXES, swapped(mesh_shape, stage, step))  26.8 us
    unnamed x66, local copies, waits for them, and re-layouts  13.2 us
    pallas_call x1, Pallas kernels, end_cells(): pl.pallas_call(functools.partial(end_rows_kernel, rows), grid=(2,), in_sp...  10.8 us
    pallas_call x2, Pallas kernels, middle_cells(): pl.pallas_call(functools.partial(middle_kernel, sides_too), grid=(1,), in...  10.5 us
    pallas_call x4, Pallas kernels, spread_pass(): pl.pallas_call(functools.partial(spread_kernel, at, rows), grid=(1,), in_...  8.37 us
    ppermute x2, starting transfers between devices, across_lat(): lax.ppermute(west, 'gy', ring('gy', -1))  6.04 us
    ppermute x14, waiting for transfers between devices, move(): return lax.ppermute(x, AXES, swapped(mesh_shape, stage, step))  5.85 us
    ppermute x2, starting transfers between devices, across_lat(): lax.ppermute(east, 'gy', ring('gy', 1))  2.47 us
  transfers between devices with their start and end apart: 22, of which 5 were waited for; matrix products, arithmetic and copies ran while one was open for 1% of the time, Pallas kernels for 20%

profile of v8, /device:TPU:1, one launch (start us, length us, event | category | flops | bytes accessed | tf_op | source)
XLA Modules:
  0.0 94.8 jit_solution(7774366895383980565)
XLA Ops:
  0.6 0.0 copy-start.5
  0.6 0.0 copy-start.9
  0.7 0.0 copy-start
  0.7 0.0 copy-start.3
  0.7 2.4 %sides.1 = (bf16[16,16,256]{2,1,0:T(8,128)(2,1)}, bf16[16,16,256]{2,1,0:T(8,128)(2,1)}) custom-call(bf16[64,64,256]{2,1,0:T(8,128)(2,1)} %refs_3_.5, bf16[64,64,256]{2,1,0:T(8,128)(2,1)} %refs_3_.5, s32[64,64]{1,0:T(8,128)} %wet_ref.1), custom_call_target="tpu_custom_call" | custom-call | tf_op jit(solution)/shard_map/sides/pallas_call | solution.py:538
  3.2 2.5 %collective-permute-start = (bf16[16,16,256]{2,1,0:T(8,128)(2,1)}, bf16[16,16,256]{2,1,0:T(8,128)(2,1)S(1)}, u32[]{:S(2)}, u32[]{:S(2)}) collective-permute-start(bf16[16,16,256]{2,1,0:T(8,128)(2,1)} %get-tuple-element.44), channel_id=1, source_target_pairs={{0,1},{1,2},{2,3},{3,4},{4,5},{5,6},{6,7},{7,0},{8,9},{9,10},{10,1... | collective-permute-start | bytes 393224 | tf_op jit(solution)/shard_map/ppermute | solution.py:762
  5.6 2.5 %collective-permute-start.1 = (bf16[16,16,256]{2,1,0:T(8,128)(2,1)}, bf16[16,16,256]{2,1,0:T(8,128)(2,1)}, u32[]{:S(2)}, u32[]{:S(2)}) collective-permute-start(bf16[16,16,256]{2,1,0:T(8,128)(2,1)} %get-tuple-element.45), channel_id=1, source_target_pairs={{0,7},{1,0},{2,1},{3,2},{4,3},{5,4},{6,5},{7,6},{8,15},{9,8},{10,9... | collective-permute-start | bytes 393224 | tf_op jit(solution)/shard_map/ppermute | solution.py:762
  8.2 0.6 broadcast_in_dim.4.refs_4_.refs_5_.refs_6_.refs_7_.refs_0_.refs_1_.wet_ref
  8.8 0.0 copy-start.12
  8.8 0.9 copy-done.12
  9.8 0.9 copy-done.14
  10.7 0.9 copy-done.16
  11.7 1.1 %copy-done.23 = bf16[1536,147]{1,0:T(8,128)(2,1)S(1)} copy-done((bf16[1536,147]{1,0:T(8,128)(2,1)S(1)}, bf16[1536,147]{1,0:T(8,128)(2,1)}, u32[]{:S(2)}) %copy-start.23) | copy-done | bytes 451608
  12.8 4.7 %core_cells.1 = (bf16[64,64,256]{2,1,0:T(8,128)(2,1)S(1)}, f32[2176,128]{1,0:T(8,128)S(1)}, f32[3,256,256]{2,1,0:T(8,128)S(1)}, f32[64,256]{1,0:T(8,128)S(1)}, f...) custom-call(bf16[64,64,256]{2,1,0:T(8,128)(2,1)S(1)} %copy-done, bf16[64,64,256]{2,1,0:T(8,128)(2,1)S(1)} %copy-done, ...), custom_call_target="tpu_custom_call" | custom-call | flops 5000000000 | bytes 8388608 | tf_op jit(solution)/shard_map/core_cells/pallas_call | solution.py:617
  17.5 0.9 copy-done.7
  18.4 1.0 %copy-done.10 = f32[2176,128]{1,0:T(8,128)} copy-done((f32[2176,128]{1,0:T(8,128)}, f32[2176,128]{1,0:T(8,128)S(1)}, u32[]{:S(2)}) %copy-start.10) | copy-done | bytes 1114136
  19.4 0.9 copy-done.18
  20.3 0.9 copy-done.21
  21.2 0.6 copy-done.24
  21.8 0.1 pad_add_fusion.refs_0_.who_ref
  21.9 0.0 collective-permute-done.refs_2_.refs_17_.refs_7_
  21.9 0.0 collective-permute-done.1.refs_3_.refs_18_.refs_8_
  21.9 1.6 %copy-done.1 = bf16[64,64,256]{2,1,0:T(8,128)(2,1)S(1)} copy-done((bf16[64,64,256]{2,1,0:T(8,128)(2,1)S(1)}, bf16[64,64,256]{2,1,0:T(8,128)(2,1)}, u32[]{:S(2)}) %copy-start.1) | copy-done | bytes 2097176
  23.5 0.0 copy-start.13
  23.5 0.0 copy-start.15
  23.5 1.1 %ends.2 = (bf16[3,96,256]{2,1,0:T(8,128)(2,1)S(1)}, bf16[3,96,256]{2,1,0:T(8,128)(2,1)S(1)}) custom-call(bf16[64,64,256]{2,1,0:T(8,128)(2,1)S(1)} %copy-done.1, bf16[64,64,256]{2,1,0:T(8,128)(2,1)S(1)} %copy-done.1, bf16[64,64,128]{2,1,0:T(8,128)(2,1)S(1)} %broadcast_in_dim.4.refs_4_.refs_5_.refs_6_.refs_7_.refs_0_.refs_1_.wet_ref, ...), custom_call_target="tpu_custom_call" | custom-call | tf_op jit(solution)/shard_map/ends/pallas_call | solution.py:568
  24.6 2.1 %collective-permute-start.2 = (bf16[3,96,256]{2,1,0:T(8,128)(2,1)S(1)}, bf16[3,96,256]{2,1,0:T(8,128)(2,1)S(1)}, u32[]{:S(2)}, u32[]{:S(2)}) collective-permute-start(bf16[3,96,256]{2,1,0:T(8,128)(2,1)S(1)} %get-tuple-element.47), channel_id=1, source_target_pairs={{0,8},{8,16},{16,24},{24,32},{32,40},{40,48},{48,56},{56,64},{64,7... | collective-permute-start | bytes 442376 | tf_op jit(solution)/shard_map/ppermute | solution.py:766
  26.7 0.0 collective-permute-start.3
  26.8 0.0 copy-start.17
  26.8 0.9 copy-done.17
  27.7 1.1 %copy-done.19 = f32[768,256]{1,0:T(8,128)S(1)} copy-done((f32[768,256]{1,0:T(8,128)S(1)}, f32[768,256]{1,0:T(8,128)}, u32[]{:S(2)}) %copy-start.19) | copy-done | bytes 786456
  28.9 1.1 %copy-done.22 = f32[3,256,256]{2,1,0:T(8,128)S(1)} copy-done((f32[3,256,256]{2,1,0:T(8,128)S(1)}, f32[3,256,256]{2,1,0:T(8,128)}, u32[]{:S(2)}) %copy-start.22) | copy-done | bytes 786456
  30.0 5.8 %flank_cells.1 = (bf16[64,64,256]{2,1,0:T(8,128)(2,1)S(1)}, f32[2176,128]{1,0:T(8,128)S(1)}, f32[3,256,256]{2,1,0:T(8,128)S(1)}, f32[64,256]{1,0:T(8,128)S(1)}, ...) custom-call(bf16[64,64,256]{2,1,0:T(8,128)(2,1)S(1)} %copy-done.2, ...), custom_call_target="tpu_custom_call", output_to_operand_aliasing={{0}: (19, {})} | custom-call | flops 5000000000 | bytes 8388608 | tf_op jit(solution)/shard_map/flank_cells/pallas_call | solution.py:617
  35.8 0.0 collective-permute-done.2.refs_18_
  35.8 0.0 collective-permute-done.3.refs_19_
  35.9 10.8 %end_cells.1 = (bf16[64,64,256]{2,1,0:T(8,128)(2,1)S(1)}, bf16[16,16,256]{2,1,0:T(8,128)(2,1)S(1)}, bf16[16,16,256]{2,1,0:T(8,128)(2,1)S(1)}, f32[4,272,128]{2,1...) custom-call(s32[2]{0:T(128)S(1)} %pad_add_fusion.refs_0_.who_ref, ...), custom_call_target="tpu_custom_call", output_to_operand_aliasing={{0}: (20, {}), {1}: (21, {}), {2}: (22, {})} | custom-call | flops 10000000000 | bytes 8388608 | tf_op jit(solution)/shard_map/end_cells/pallas_call | solution.py:667
  46.7 4.3 %collective-permute-start.8 = (f32[4,272,128]{2,1,0:T(8,128)S(1)}, f32[4,272,128]{2,1,0:T(8,128)S(1)}, u32[]{:S(2)}, u32[]{:S(2)}) collective-permute-start(f32[4,272,128]{2,1,0:T(8,128)S(1)} %get-tuple-element.68), channel_id=1, source_target_pairs={{0,8},{1,9},{2,10},{3,11},{4,12},{5,13},{6,14},{7,15},{8,0},{9,1},... | collective-permute-start | bytes 1671176 | tf_op jit(solution)/shard_map/ppermute | solution.py:797
  51.0 3.6 %collective-permute-start.5 = (bf16[16,16,256]{2,1,0:T(8,128)(2,1)S(1)}, bf16[16,16,256]{2,1,0:T(8,128)(2,1)S(1)}, u32[]{:S(2)}, u32[]{:S(2)}) collective-permute-start(bf16[16,16,256]{2,1,0:T(8,128)(2,1)S(1)} %get-tuple-element.63), channel_id=1, source_target_pairs={{0,7},{1,0},{2,1},{3,2},{4,3},{5,4},{6,5},{7,6},{8,15},{9,8},{10,9... | collective-permute-start | bytes 393224 | tf_op jit(solution)/shard_map/ppermute | solution.py:762
  54.6 0.0 collective-permute-done.8.come_ref
  54.6 0.1 fold.1
  54.6 0.1 collective-permute-start.9
  54.7 1.2 %collective-permute-start.10 = (bf16[1,272,128]{2,1,0:T(8,128)(2,1)S(1)}, bf16[1,272,128]{2,1,0:T(8,128)(2,1)S(1)}, u32[]{:S(2)}, u32[]{:S(2)}) collective-permute-start(bf16[1,272,128]{2,1,0:T(8,128)(2,1)S(1)} %get-tuple-element.71), channel_id=1, source_target_pairs={{0,32},{1,33},{2,34},{3,35},{4,36},{5,37},{6,38},{7,39},{8,12},{9,... | collective-permute-start | bytes 208904 | tf_op jit(solution)/shard_map/ppermute | solution.py:797
  56.0 2.6 %collective-permute-start.11 = (bf16[1,272,128]{2,1,0:T(8,128)(2,1)S(1)}, bf16[1,272,128]{2,1,0:T(8,128)(2,1)S(1)}, u32[]{:S(2)}, u32[]{:S(2)}) collective-permute-start(bf16[1,272,128]{2,1,0:T(8,128)(2,1)S(1)} %get-tuple-element.72), channel_id=1, source_target_pairs={{0,48},{1,49},{2,50},{3,51},{4,52},{5,53},{6,54},{7,55},{8,14},{9,... | collective-permute-start | bytes 208904 | tf_op jit(solution)/shard_map/ppermute | solution.py:797
  58.6 0.0 collective-permute-done.4.refs_0_.north_ref.west_ref
  58.6 0.2 collective-permute-done.5.refs_1_.south_ref.east_ref
  58.8 0.1 collective-permute-start.6
  58.9 1.4 %collective-permute-start.7 = (bf16[3,96,256]{2,1,0:T(8,128)(2,1)S(1)}, bf16[3,96,256]{2,1,0:T(8,128)(2,1)S(1)}, u32[]{:S(2)}, u32[]{:S(2)}) collective-permute-start(bf16[3,96,256]{2,1,0:T(8,128)(2,1)S(1)} %get-tuple-element.65), channel_id=1, source_target_pairs={{0,120},{8,0},{16,8},{24,16},{32,24},{40,32},{48,40},{56,48},{64,5... | collective-permute-start | bytes 442376 | tf_op jit(solution)/shard_map/ppermute | solution.py:766
  60.2 0.4 collective-permute-done.11
  60.7 2.5 %collective-permute-start.14 = (bf16[1,272,128]{2,1,0:T(8,128)(2,1)S(1)}, bf16[1,272,128]{2,1,0:T(8,128)(2,1)S(1)}, u32[]{:S(2)}, u32[]{:S(2)}) collective-permute-start(bf16[1,272,128]{2,1,0:T(8,128)(2,1)S(1)} %add_convert_fusion.2), channel_id=1, source_target_pairs={{0,6},{1,7},{2,4},{3,5},{4,2},{5,3},{6,0},{7,1},{8,73},{9,72},{10,... | collective-permute-start | bytes 208904 | tf_op jit(solution)/shard_map/ppermute | solution.py:797
  63.2 1.4 %collective-permute-start.13 = (bf16[1,272,128]{2,1,0:T(8,128)(2,1)S(1)}, bf16[1,272,128]{2,1,0:T(8,128)(2,1)S(1)}, u32[]{:S(2)}, u32[]{:S(2)}) collective-permute-start(bf16[1,272,128]{2,1,0:T(8,128)(2,1)S(1)} %add_convert_fusion.2), channel_id=1, source_target_pairs={{0,4},{1,5},{2,6},{3,7},{4,0},{5,1},{6,2},{7,3},{8,72},{9,73},{10,... | collective-permute-start | bytes 208904 | tf_op jit(solution)/shard_map/ppermute | solution.py:797
  64.7 2.1 %spread_pass.4.out_refs_0_ = f32[64,64,256]{2,1,0:T(8,128)} custom-call(bf16[64,64,256]{2,1,0:T(8,128)(2,1)S(1)} %get-tuple-element.59.before_ref.fg_ref.after_ref, bf16[64,64,256]{2,1,0:T(8,128)(2,1)S(1)} %get-tuple-element.59.before_ref.fg_ref.after_ref, bf16[64,64,256]{2,1,0:T(8,128)(2,1)S(1)} %get-tuple-element.59.before_ref.fg_ref.after_ref, ...), custom_call_target="tpu_custom_call" | custom-call | flops 4000000000 | bytes 4194304 | tf_op jit(solution)/shard_map/spread_pass/pallas_call | solution.py:730
  66.8 1.6 %collective-permute-done.13 = bf16[1,272,128]{2,1,0:T(8,128)(2,1)S(1)} collective-permute-done((bf16[1,272,128]{2,1,0:T(8,128)(2,1)S(1)}, bf16[1,272,128]{2,1,0:T(8,128)(2,1)S(1)}, u32[]{:S(2)}, u32[]{:S(2)}) %collective-permute-start.13) | collective-permute-done | bytes 69664 | tf_op jit(solution)/shard_map/ppermute | solution.py:797
  68.4 3.7 %collective-permute-start.17 = (bf16[1,272,128]{2,1,0:T(8,128)(2,1)S(1)}, bf16[1,272,128]{2,1,0:T(8,128)(2,1)S(1)}, u32[]{:S(2)}, u32[]{:S(2)}) collective-permute-start(bf16[1,272,128]{2,1,0:T(8,128)(2,1)S(1)} %add_convert_fusion.1), channel_id=1, source_target_pairs={{0,65},{1,64},{2,67},{3,66},{4,69},{5,68},{6,71},{7,70},{8,56},{9,... | collective-permute-start | bytes 208904 | tf_op jit(solution)/shard_map/ppermute | solution.py:797
  72.2 0.7 collective-permute-start.15
  72.9 2.1 %spread_pass.5.out_refs_0_ = f32[64,64,256]{2,1,0:T(8,128)} custom-call(bf16[64,64,256]{2,1,0:T(8,128)(2,1)S(1)} %get-tuple-element.59.before_ref.fg_ref.after_ref, bf16[64,64,256]{2,1,0:T(8,128)(2,1)S(1)} %get-tuple-element.59.before_ref.fg_ref.after_ref, ...), custom_call_target="tpu_custom_call", output_to_operand_aliasing={{}: (12, {})} | custom-call | flops 4000000000 | bytes 4194304 | tf_op jit(solution)/shard_map/spread_pass/pallas_call | solution.py:730
  74.9 0.0 collective-permute-done.17
  74.9 1.9 %collective-permute-done.16 = bf16[1,272,128]{2,1,0:T(8,128)(2,1)S(1)} collective-permute-done((bf16[1,272,128]{2,1,0:T(8,128)(2,1)S(1)}, bf16[1,272,128]{2,1,0:T(8,128)(2,1)S(1)}, u32[]{:S(2)}, u32[]{:S(2)}) %collective-permute-start.16) | collective-permute-done | bytes 69664 | tf_op jit(solution)/shard_map/ppermute | solution.py:797
  76.9 3.3 %collective-permute-start.20 = (bf16[1,272,128]{2,1,0:T(8,128)(2,1)S(1)}, bf16[1,272,128]{2,1,0:T(8,128)(2,1)S(1)}, u32[]{:S(2)}, u32[]{:S(2)}) collective-permute-start(bf16[1,272,128]{2,1,0:T(8,128)(2,1)S(1)} %add_convert_fusion.refs_0_), channel_id=1, source_target_pairs={{0,48},{1,49},{2,50},{3,51},{4,52},{5,53},{6,54},{7,55},{8,14},{9,... | collective-permute-start | bytes 208904 | tf_op jit(solution)/shard_map/ppermute | solution.py:797
  80.2 0.7 collective-permute-start.18
  80.9 2.1 %spread_pass.6.out_refs_0_ = f32[64,64,256]{2,1,0:T(8,128)} custom-call(bf16[64,64,256]{2,1,0:T(8,128)(2,1)S(1)} %get-tuple-element.59.before_ref.fg_ref.after_ref, bf16[64,64,256]{2,1,0:T(8,128)(2,1)S(1)} %get-tuple-element.59.before_ref.fg_ref.after_ref, ...), custom_call_target="tpu_custom_call", output_to_operand_aliasing={{}: (12, {})} | custom-call | flops 4000000000 | bytes 4194304 | tf_op jit(solution)/shard_map/spread_pass/pallas_call | solution.py:730
  83.0 1.9 %collective-permute-done.19.refs_2_ = bf16[1,272,128]{2,1,0:T(8,128)(2,1)S(1)} collective-permute-done((bf16[1,272,128]{2,1,0:T(8,128)(2,1)S(1)}, bf16[1,272,128]{2,1,0:T(8,128)(2,1)S(1)}, u32[]{:S(2)}, u32[]{:S(2)}) %collective-permute-start.19) | collective-permute-done | bytes 69664 | tf_op jit(solution)/shard_map/ppermute | solution.py:797
  84.9 6.2 %collective-permute-start.21 = (bf16[4,272,128]{2,1,0:T(8,128)(2,1)S(1)}, bf16[4,272,128]{2,1,0:T(8,128)(2,1)S(1)}, u32[]{:S(2)}, u32[]{:S(2)}) collective-permute-start(bf16[4,272,128]{2,1,0:T(8,128)(2,1)S(1)} %join.1.own_ref), channel_id=1, source_target_pairs={{0,8},{1,9},{2,10},{3,11},{4,12},{5,13},{6,14},{7,15},{8,0},{9,1},... | collective-permute-start | bytes 835592 | tf_op jit(solution)/shard_map/ppermute | solution.py:797
  91.1 2.1 %spread_pass.7 = f32[64,64,256]{2,1,0:T(8,128)} custom-call(bf16[64,64,256]{2,1,0:T(8,128)(2,1)S(1)} %get-tuple-element.59.before_ref.fg_ref.after_ref, bf16[64,64,256]{2,1,0:T(8,128)(2,1)S(1)} %get-tuple-element.59.before_ref.fg_ref.after_ref, ...), custom_call_target="tpu_custom_call", output_to_operand_aliasing={{}: (12, {})} | custom-call | flops 4000000000 | bytes 4194304 | tf_op jit(solution)/shard_map/spread_pass/pallas_call | solution.py:730
  93.2 1.7 %finish.1 = (f32[49,256]{1,0:T(8,128)}, f32[1,256]{1,0:T(1,128)}, f32[1,256]{1,0:T(1,128)}, f32[1,256]{1,0:T(1,128)}, f32[256,512]{1,0:T(8,128)}, /*index=5*/f32[1,512]{1,0:T(1,128)}, f32[512,256]{1,0:T(8,128)}) custom-call(s32[2]{0:T(128)S(1)} %pad_add_fusion.refs_0_.who_ref, bf16[4,272,128]{2,1,0:T(8,128)(2,1)S(1)} %join.1.own_ref, ...), custom_call_target="tpu_custom_call" | custom-call | tf_op jit(solution)/shard_map/finish/pallas_call | solution.py:708
  (67 shorter events, 0.3 us)
Async XLA Ops:
  0.6 8.2 %copy-start.5 = (bf16[512,512]{1,0:T(8,128)(2,1)S(1)}, bf16[512,512]{1,0:T(8,128)(2,1)}, u32[]{:S(2)}) copy-start(bf16[512,512]{1,0:T(8,128)(2,1)} %constant.69.clone.refs_10_.refs_11_.place_ref) | copy-start | bytes 1572868
  0.6 8.1 %copy-start.9 = (bf16[256,512]{1,0:T(8,128)(2,1)S(1)}, bf16[256,512]{1,0:T(8,128)(2,1)}, u32[]{:S(2)}) copy-start(bf16[256,512]{1,0:T(8,128)(2,1)} %constant.71.clone.refs_12_.refs_13_.back_ref) | copy-start | bytes 786436
  0.7 8.1 %copy-start = (bf16[64,64,256]{2,1,0:T(8,128)(2,1)S(1)}, bf16[64,64,256]{2,1,0:T(8,128)(2,1)}, u32[]{:S(2)}) copy-start(bf16[64,64,256]{2,1,0:T(8,128)(2,1)} %refs_3_.5) | copy-start | bytes 6291460
  0.7 7.4 %copy-start.28 = (s32[64,64]{1,0:T(8,128)S(1)}, s32[64,64]{1,0:T(8,128)}, u32[]{:S(2)}) copy-start(s32[64,64]{1,0:T(8,128)} %wet_ref.1) | copy-start | bytes 49156
  0.7 7.4 %copy-start.29 = (bf16[512]{0:T(512)(128)(2,1)S(1)}, bf16[512]{0:T(512)(128)(2,1)}, u32[]{:S(2)}) copy-start(bf16[512]{0:T(512)(128)(2,1)} %param.23) | copy-start | bytes 3076
  0.7 7.4 %copy-start.30 = (bf16[256]{0:T(256)(128)(2,1)S(1)}, bf16[256]{0:T(256)(128)(2,1)}, u32[]{:S(2)}) copy-start(bf16[256]{0:T(256)(128)(2,1)} %param.21) | copy-start | bytes 1540
  0.7 7.4 %copy-start.31 = (bf16[256]{0:T(256)(128)(2,1)S(1)}, bf16[256]{0:T(256)(128)(2,1)}, u32[]{:S(2)}) copy-start(bf16[256]{0:T(256)(128)(2,1)} %param.20) | copy-start | bytes 1540
  0.7 7.4 %copy-start.32 = (bf16[256]{0:T(256)(128)(2,1)S(1)}, bf16[256]{0:T(256)(128)(2,1)}, u32[]{:S(2)}) copy-start(bf16[256]{0:T(256)(128)(2,1)} %param.19) | copy-start | bytes 1540
  0.7 8.1 %copy-start.3 = (bf16[64,64,256]{2,1,0:T(8,128)(2,1)S(1)}, bf16[64,64,256]{2,1,0:T(8,128)(2,1)}, u32[]{:S(2)}) copy-start(bf16[64,64,256]{2,1,0:T(8,128)(2,1)} %cot_ref.7) | copy-start | bytes 6291460
  0.7 8.1 %copy-start.26 = (bf16[49,256]{1,0:T(8,128)(2,1)S(1)}, bf16[49,256]{1,0:T(8,128)(2,1)}, u32[]{:S(2)}) copy-start(bf16[49,256]{1,0:T(8,128)(2,1)} %refs_17_.2) | copy-start | bytes 75268
  3.2 18.7 %collective-permute-start = (bf16[16,16,256]{2,1,0:T(8,128)(2,1)}, bf16[16,16,256]{2,1,0:T(8,128)(2,1)S(1)}, u32[]{:S(2)}, u32[]{:S(2)}) collective-permute-start(bf16[16,16,256]{2,1,0:T(8,128)(2,1)} %get-tuple-element.44), channel_id=1, source_target_pairs={{0,1},{1,2},{2,3},{3,4},{4,5},{5,6},{6,7},{7,0},{8,9},{9,10},{10,1... | collective-permute-start | bytes 393224 | tf_op jit(solution)/shard_map/ppermute | solution.py:762
  5.6 16.2 %collective-permute-start.1 = (bf16[16,16,256]{2,1,0:T(8,128)(2,1)}, bf16[16,16,256]{2,1,0:T(8,128)(2,1)}, u32[]{:S(2)}, u32[]{:S(2)}) collective-permute-start(bf16[16,16,256]{2,1,0:T(8,128)(2,1)} %get-tuple-element.45), channel_id=1, source_target_pairs={{0,7},{1,0},{2,1},{3,2},{4,3},{5,4},{6,5},{7,6},{8,15},{9,8},{10,9... | collective-permute-start | bytes 393224 | tf_op jit(solution)/shard_map/ppermute | solution.py:762
  8.8 1.0 %copy-start.12 = (bf16[256,512]{1,0:T(8,128)(2,1)S(1)}, bf16[256,512]{1,0:T(8,128)(2,1)}, u32[]{:S(2)}) copy-start(bf16[256,512]{1,0:T(8,128)(2,1)} %refs_16_.5) | copy-start | bytes 786436
  9.8 0.9 %copy-start.14 = (bf16[512,256]{1,0:T(8,128)(2,1)S(1)}, bf16[512,256]{1,0:T(8,128)(2,1)}, u32[]{:S(2)}) copy-start(bf16[512,256]{1,0:T(8,128)(2,1)} %refs_17_.3) | copy-start | bytes 786436
  10.7 0.9 %copy-start.16 = (bf16[512,256]{1,0:T(8,128)(2,1)S(1)}, bf16[512,256]{1,0:T(8,128)(2,1)}, u32[]{:S(2)}) copy-start(bf16[512,256]{1,0:T(8,128)(2,1)} %constant.70.clone.refs_11_.refs_12_) | copy-start | bytes 786436
  11.7 1.1 %copy-start.23 = (bf16[1536,147]{1,0:T(8,128)(2,1)S(1)}, bf16[1536,147]{1,0:T(8,128)(2,1)}, u32[]{:S(2)}) copy-start(bf16[1536,147]{1,0:T(8,128)(2,1)} %constant.72.clone.refs_13_) | copy-start | bytes 1354756
  17.5 0.9 copy-start.7
  18.4 1.0 %copy-start.10 = (f32[2176,128]{1,0:T(8,128)}, f32[2176,128]{1,0:T(8,128)S(1)}, u32[]{:S(2)}) copy-start(f32[2176,128]{1,0:T(8,128)S(1)} %get-tuple-element.50.refs_20_) | copy-start | bytes 3342340
  19.4 0.9 copy-start.18
  20.3 0.9 copy-start.21
  21.2 0.6 copy-start.24
  21.9 1.6 %copy-start.1 = (bf16[64,64,256]{2,1,0:T(8,128)(2,1)S(1)}, bf16[64,64,256]{2,1,0:T(8,128)(2,1)}, u32[]{:S(2)}) copy-start(bf16[64,64,256]{2,1,0:T(8,128)(2,1)} %refs_3_.5) | copy-start | bytes 6291460
  23.5 3.3 %copy-start.2 = (bf16[64,64,256]{2,1,0:T(8,128)(2,1)S(1)}, bf16[64,64,256]{2,1,0:T(8,128)(2,1)}, u32[]{:S(2)}) copy-start(bf16[64,64,256]{2,1,0:T(8,128)(2,1)} %refs_3_.5) | copy-start | bytes 6291460
  23.5 3.3 %copy-start.4 = (bf16[64,64,256]{2,1,0:T(8,128)(2,1)S(1)}, bf16[64,64,256]{2,1,0:T(8,128)(2,1)}, u32[]{:S(2)}) copy-start(bf16[64,64,256]{2,1,0:T(8,128)(2,1)} %cot_ref.7) | copy-start | bytes 6291460
  23.5 3.3 %copy-start.6 = (bf16[512,512]{1,0:T(8,128)(2,1)S(1)}, bf16[512,512]{1,0:T(8,128)(2,1)}, u32[]{:S(2)}) copy-start(bf16[512,512]{1,0:T(8,128)(2,1)} %constant.69.clone.refs_10_.refs_11_.place_ref) | copy-start | bytes 1572868
  23.5 3.3 %copy-start.11 = (f32[2176,128]{1,0:T(8,128)S(1)}, f32[2176,128]{1,0:T(8,128)}, u32[]{:S(2)}) copy-start(f32[2176,128]{1,0:T(8,128)} %copy-done.10) | copy-start | bytes 3342340
  23.5 3.3 %copy-start.13 = (bf16[256,512]{1,0:T(8,128)(2,1)S(1)}, bf16[256,512]{1,0:T(8,128)(2,1)}, u32[]{:S(2)}) copy-start(bf16[256,512]{1,0:T(8,128)(2,1)} %refs_16_.5) | copy-start | bytes 786436
  23.5 3.3 %copy-start.15 = (bf16[512,256]{1,0:T(8,128)(2,1)S(1)}, bf16[512,256]{1,0:T(8,128)(2,1)}, u32[]{:S(2)}) copy-start(bf16[512,256]{1,0:T(8,128)(2,1)} %refs_17_.3) | copy-start | bytes 786436
  23.5 3.3 %copy-start.25 = (f32[64,256]{1,0:T(8,128)S(1)}, f32[64,256]{1,0:T(8,128)}, u32[]{:S(2)}) copy-start(f32[64,256]{1,0:T(8,128)} %copy-done.24) | copy-start | bytes 196612
  24.6 11.2 %collective-permute-start.2 = (bf16[3,96,256]{2,1,0:T(8,128)(2,1)S(1)}, bf16[3,96,256]{2,1,0:T(8,128)(2,1)S(1)}, u32[]{:S(2)}, u32[]{:S(2)}) collective-permute-start(bf16[3,96,256]{2,1,0:T(8,128)(2,1)S(1)} %get-tuple-element.47), channel_id=1, source_target_pairs={{0,8},{8,16},{16,24},{24,32},{32,40},{40,48},{48,56},{56,64},{64,7... | collective-permute-start | bytes 442376 | tf_op jit(solution)/shard_map/ppermute | solution.py:766
  26.7 9.1 %collective-permute-start.3 = (bf16[3,96,256]{2,1,0:T(8,128)(2,1)S(1)}, bf16[3,96,256]{2,1,0:T(8,128)(2,1)S(1)}, u32[]{:S(2)}, u32[]{:S(2)}) collective-permute-start(bf16[3,96,256]{2,1,0:T(8,128)(2,1)S(1)} %get-tuple-element.48), channel_id=1, source_target_pairs={{0,120},{8,0},{16,8},{24,16},{32,24},{40,32},{48,40},{56,48},{64,5... | collective-permute-start | bytes 442376 | tf_op jit(solution)/shard_map/ppermute | solution.py:766
  26.8 1.0 %copy-start.17 = (bf16[512,256]{1,0:T(8,128)(2,1)S(1)}, bf16[512,256]{1,0:T(8,128)(2,1)}, u32[]{:S(2)}) copy-start(bf16[512,256]{1,0:T(8,128)(2,1)} %constant.70.clone.refs_11_.refs_12_) | copy-start | bytes 786436
  27.7 1.1 %copy-start.19 = (f32[768,256]{1,0:T(8,128)S(1)}, f32[768,256]{1,0:T(8,128)}, u32[]{:S(2)}) copy-start(f32[768,256]{1,0:T(8,128)} %copy-done.18) | copy-start | bytes 2359300
  28.9 1.1 %copy-start.22 = (f32[3,256,256]{2,1,0:T(8,128)S(1)}, f32[3,256,256]{2,1,0:T(8,128)}, u32[]{:S(2)}) copy-start(f32[3,256,256]{2,1,0:T(8,128)} %copy-done.21) | copy-start | bytes 2359300
  30.0 5.8 %copy-start.20 = (f32[768,256]{1,0:T(8,128)S(1)}, f32[768,256]{1,0:T(8,128)}, u32[]{:S(2)}) copy-start(f32[768,256]{1,0:T(8,128)} %copy-done.18) | copy-start | bytes 2359300
  30.0 5.9 %copy-start.27 = (f32[49,768]{1,0:T(8,128)S(1)}, f32[49,768]{1,0:T(8,128)}, u32[]{:S(2)}) copy-start(f32[49,768]{1,0:T(8,128)} %constant.73.clone.refs_10_) | copy-start | bytes 451588
  46.7 18.0 %copy-start.8 = (f32[768,256]{1,0:T(8,128)S(1)}, f32[768,256]{1,0:T(8,128)}, u32[]{:S(2)}) copy-start(f32[768,256]{1,0:T(8,128)} %copy-done.7) | copy-start | bytes 2359300
  46.7 7.9 %collective-permute-start.8 = (f32[4,272,128]{2,1,0:T(8,128)S(1)}, f32[4,272,128]{2,1,0:T(8,128)S(1)}, u32[]{:S(2)}, u32[]{:S(2)}) collective-permute-start(f32[4,272,128]{2,1,0:T(8,128)S(1)} %get-tuple-element.68), channel_id=1, source_target_pairs={{0,8},{1,9},{2,10},{3,11},{4,12},{5,13},{6,14},{7,15},{8,0},{9,1},... | collective-permute-start | bytes 1671176 | tf_op jit(solution)/shard_map/ppermute | solution.py:797
  51.0 7.6 %collective-permute-start.4 = (bf16[16,16,256]{2,1,0:T(8,128)(2,1)S(1)}, bf16[16,16,256]{2,1,0:T(8,128)(2,1)S(1)}, u32[]{:S(2)}, u32[]{:S(2)}) collective-permute-start(bf16[16,16,256]{2,1,0:T(8,128)(2,1)S(1)} %get-tuple-element.62), channel_id=1, source_target_pairs={{0,1},{1,2},{2,3},{3,4},{4,5},{5,6},{6,7},{7,0},{8,9},{9,10},{10,1... | collective-permute-start | bytes 393224 | tf_op jit(solution)/shard_map/ppermute | solution.py:762
  51.0 7.8 %collective-permute-start.5 = (bf16[16,16,256]{2,1,0:T(8,128)(2,1)S(1)}, bf16[16,16,256]{2,1,0:T(8,128)(2,1)S(1)}, u32[]{:S(2)}, u32[]{:S(2)}) collective-permute-start(bf16[16,16,256]{2,1,0:T(8,128)(2,1)S(1)} %get-tuple-element.63), channel_id=1, source_target_pairs={{0,7},{1,0},{2,1},{3,2},{4,3},{5,4},{6,5},{7,6},{8,15},{9,8},{10,9... | collective-permute-start | bytes 393224 | tf_op jit(solution)/shard_map/ppermute | solution.py:762
  54.6 5.6 %collective-permute-start.9 = (bf16[1,272,128]{2,1,0:T(8,128)(2,1)S(1)}, bf16[1,272,128]{2,1,0:T(8,128)(2,1)S(1)}, u32[]{:S(2)}, u32[]{:S(2)}) collective-permute-start(bf16[1,272,128]{2,1,0:T(8,128)(2,1)S(1)} %get-tuple-element.70), channel_id=1, source_target_pairs={{0,16},{1,17},{2,18},{3,19},{4,20},{5,21},{6,22},{7,23},{8,10},{9,... | collective-permute-start | bytes 208904 | tf_op jit(solution)/shard_map/ppermute | solution.py:797
  54.7 5.5 %collective-permute-start.10 = (bf16[1,272,128]{2,1,0:T(8,128)(2,1)S(1)}, bf16[1,272,128]{2,1,0:T(8,128)(2,1)S(1)}, u32[]{:S(2)}, u32[]{:S(2)}) collective-permute-start(bf16[1,272,128]{2,1,0:T(8,128)(2,1)S(1)} %get-tuple-element.71), channel_id=1, source_target_pairs={{0,32},{1,33},{2,34},{3,35},{4,36},{5,37},{6,38},{7,39},{8,12},{9,... | collective-permute-start | bytes 208904 | tf_op jit(solution)/shard_map/ppermute | solution.py:797
  56.0 4.7 %collective-permute-start.11 = (bf16[1,272,128]{2,1,0:T(8,128)(2,1)S(1)}, bf16[1,272,128]{2,1,0:T(8,128)(2,1)S(1)}, u32[]{:S(2)}, u32[]{:S(2)}) collective-permute-start(bf16[1,272,128]{2,1,0:T(8,128)(2,1)S(1)} %get-tuple-element.72), channel_id=1, source_target_pairs={{0,48},{1,49},{2,50},{3,51},{4,52},{5,53},{6,54},{7,55},{8,14},{9,... | collective-permute-start | bytes 208904 | tf_op jit(solution)/shard_map/ppermute | solution.py:797
  58.8 22.1 %collective-permute-start.6 = (bf16[3,96,256]{2,1,0:T(8,128)(2,1)S(1)}, bf16[3,96,256]{2,1,0:T(8,128)(2,1)S(1)}, u32[]{:S(2)}, u32[]{:S(2)}) collective-permute-start(bf16[3,96,256]{2,1,0:T(8,128)(2,1)S(1)} %get-tuple-element.64), channel_id=1, source_target_pairs={{0,8},{8,16},{16,24},{24,32},{32,40},{40,48},{48,56},{56,64},{64,7... | collective-permute-start | bytes 442376 | tf_op jit(solution)/shard_map/ppermute | solution.py:766
  58.9 22.0 %collective-permute-start.7 = (bf16[3,96,256]{2,1,0:T(8,128)(2,1)S(1)}, bf16[3,96,256]{2,1,0:T(8,128)(2,1)S(1)}, u32[]{:S(2)}, u32[]{:S(2)}) collective-permute-start(bf16[3,96,256]{2,1,0:T(8,128)(2,1)S(1)} %get-tuple-element.65), channel_id=1, source_target_pairs={{0,120},{8,0},{16,8},{24,16},{32,24},{40,32},{48,40},{56,48},{64,5... | collective-permute-start | bytes 442376 | tf_op jit(solution)/shard_map/ppermute | solution.py:766
  60.7 6.1 %collective-permute-start.14 = (bf16[1,272,128]{2,1,0:T(8,128)(2,1)S(1)}, bf16[1,272,128]{2,1,0:T(8,128)(2,1)S(1)}, u32[]{:S(2)}, u32[]{:S(2)}) collective-permute-start(bf16[1,272,128]{2,1,0:T(8,128)(2,1)S(1)} %add_convert_fusion.2), channel_id=1, source_target_pairs={{0,6},{1,7},{2,4},{3,5},{4,2},{5,3},{6,0},{7,1},{8,73},{9,72},{10,... | collective-permute-start | bytes 208904 | tf_op jit(solution)/shard_map/ppermute | solution.py:797
  63.2 5.1 %collective-permute-start.13 = (bf16[1,272,128]{2,1,0:T(8,128)(2,1)S(1)}, bf16[1,272,128]{2,1,0:T(8,128)(2,1)S(1)}, u32[]{:S(2)}, u32[]{:S(2)}) collective-permute-start(bf16[1,272,128]{2,1,0:T(8,128)(2,1)S(1)} %add_convert_fusion.2), channel_id=1, source_target_pairs={{0,4},{1,5},{2,6},{3,7},{4,0},{5,1},{6,2},{7,3},{8,72},{9,73},{10,... | collective-permute-start | bytes 208904 | tf_op jit(solution)/shard_map/ppermute | solution.py:797
  64.7 3.7 %collective-permute-start.12 = (bf16[1,272,128]{2,1,0:T(8,128)(2,1)S(1)}, bf16[1,272,128]{2,1,0:T(8,128)(2,1)S(1)}, u32[]{:S(2)}, u32[]{:S(2)}) collective-permute-start(bf16[1,272,128]{2,1,0:T(8,128)(2,1)S(1)} %add_convert_fusion.2), channel_id=1, source_target_pairs={{0,2},{1,3},{2,0},{3,1},{4,6},{5,7},{6,4},{7,5},{8,9},{9,8},{10,11... | collective-permute-start | bytes 208904 | tf_op jit(solution)/shard_map/ppermute | solution.py:797
  68.4 6.5 %collective-permute-start.17 = (bf16[1,272,128]{2,1,0:T(8,128)(2,1)S(1)}, bf16[1,272,128]{2,1,0:T(8,128)(2,1)S(1)}, u32[]{:S(2)}, u32[]{:S(2)}) collective-permute-start(bf16[1,272,128]{2,1,0:T(8,128)(2,1)S(1)} %add_convert_fusion.1), channel_id=1, source_target_pairs={{0,65},{1,64},{2,67},{3,66},{4,69},{5,68},{6,71},{7,70},{8,56},{9,... | collective-permute-start | bytes 208904 | tf_op jit(solution)/shard_map/ppermute | solution.py:797
  72.2 4.7 %collective-permute-start.16 = (bf16[1,272,128]{2,1,0:T(8,128)(2,1)S(1)}, bf16[1,272,128]{2,1,0:T(8,128)(2,1)S(1)}, u32[]{:S(2)}, u32[]{:S(2)}) collective-permute-start(bf16[1,272,128]{2,1,0:T(8,128)(2,1)S(1)} %add_convert_fusion.1), channel_id=1, source_target_pairs={{0,64},{1,65},{2,66},{3,67},{4,68},{5,69},{6,70},{7,71},{8,40},{9,... | collective-permute-start | bytes 208904 | tf_op jit(solution)/shard_map/ppermute | solution.py:797
  72.2 4.7 %collective-permute-start.15 = (bf16[1,272,128]{2,1,0:T(8,128)(2,1)S(1)}, bf16[1,272,128]{2,1,0:T(8,128)(2,1)S(1)}, u32[]{:S(2)}, u32[]{:S(2)}) collective-permute-start(bf16[1,272,128]{2,1,0:T(8,128)(2,1)S(1)} %add_convert_fusion.1), channel_id=1, source_target_pairs={{0,1},{1,0},{2,3},{3,2},{4,5},{5,4},{6,7},{7,6},{8,24},{9,25},{10,... | collective-permute-start | bytes 208904 | tf_op jit(solution)/shard_map/ppermute | solution.py:797
  76.9 6.1 %collective-permute-start.20 = (bf16[1,272,128]{2,1,0:T(8,128)(2,1)S(1)}, bf16[1,272,128]{2,1,0:T(8,128)(2,1)S(1)}, u32[]{:S(2)}, u32[]{:S(2)}) collective-permute-start(bf16[1,272,128]{2,1,0:T(8,128)(2,1)S(1)} %add_convert_fusion.refs_0_), channel_id=1, source_target_pairs={{0,48},{1,49},{2,50},{3,51},{4,52},{5,53},{6,54},{7,55},{8,14},{9,... | collective-permute-start | bytes 208904 | tf_op jit(solution)/shard_map/ppermute | solution.py:797
  80.2 4.7 %collective-permute-start.19 = (bf16[1,272,128]{2,1,0:T(8,128)(2,1)S(1)}, bf16[1,272,128]{2,1,0:T(8,128)(2,1)S(1)}, u32[]{:S(2)}, u32[]{:S(2)}) collective-permute-start(bf16[1,272,128]{2,1,0:T(8,128)(2,1)S(1)} %add_convert_fusion.refs_0_), channel_id=1, source_target_pairs={{0,32},{1,33},{2,34},{3,35},{4,36},{5,37},{6,38},{7,39},{8,12},{9,... | collective-permute-start | bytes 208904 | tf_op jit(solution)/shard_map/ppermute | solution.py:797
  80.2 4.7 %collective-permute-start.18 = (bf16[1,272,128]{2,1,0:T(8,128)(2,1)S(1)}, bf16[1,272,128]{2,1,0:T(8,128)(2,1)S(1)}, u32[]{:S(2)}, u32[]{:S(2)}) collective-permute-start(bf16[1,272,128]{2,1,0:T(8,128)(2,1)S(1)} %add_convert_fusion.refs_0_), channel_id=1, source_target_pairs={{0,16},{1,17},{2,18},{3,19},{4,20},{5,21},{6,22},{7,23},{8,10},{9,... | collective-permute-start | bytes 208904 | tf_op jit(solution)/shard_map/ppermute | solution.py:797
  84.9 8.3 %collective-permute-start.21 = (bf16[4,272,128]{2,1,0:T(8,128)(2,1)S(1)}, bf16[4,272,128]{2,1,0:T(8,128)(2,1)S(1)}, u32[]{:S(2)}, u32[]{:S(2)}) collective-permute-start(bf16[4,272,128]{2,1,0:T(8,128)(2,1)S(1)} %join.1.own_ref), channel_id=1, source_target_pairs={{0,8},{1,9},{2,10},{3,11},{4,12},{5,13},{6,14},{7,15},{8,0},{9,1},... | collective-permute-start | bytes 835592 | tf_op jit(solution)/shard_map/ppermute | solution.py:797

commit v9 on v7

--- a/solution.py
+++ b/solution.py
@@ -106,31 +106,46 @@
     return jnp.concatenate(mains + [jnp.concatenate(tails[:20], axis=0).astype(BF16)], axis=0)
 
 
-def pack_low(groups):
+def packed(groups, low):
     row = rows_of(groups[0].shape[1])
-    return [
-        jnp.where(row < 4, groups[n], pltpu.roll(groups[n + 1], 5, 0))
-        for n in range(0, len(groups), 2)
-    ]
-
-
-def pack_high(groups):
-    row = rows_of(groups[0].shape[1])
-    return [
-        jnp.where(row < 4, pltpu.roll(groups[n], 3, 0), groups[n + 1])
-        for n in range(0, len(groups), 2)
-    ]
+
+    def turned(group, by):
+        return pltpu.roll(group, by % 8, 0) if by % 8 else group
+
+    out = []
+    for n in range(0, len(groups), 8):
+        slabs = groups[n : n + 8]
+        if low:
+            spare = [turned(slabs[6], 3), turned(slabs[7], 3)]
+            spare.append(jnp.where(row == 3, turned(slabs[6], 1), turned(slabs[7], 2)))
+        else:
+            spare = [turned(slabs[6], -2), turned(slabs[7], -2)]
+            spare.append(jnp.where(row == 3, turned(slabs[6], -4), turned(slabs[7], -3)))
+        for k in range(3):
+            first = turned(slabs[2 * k], 0 if low else 3)
+            second = turned(slabs[2 * k + 1], 5 if low else 0)
+            out.append(jnp.where(row < 3, first, jnp.where(row > 4, second, spare[k])))
+    return out
 
 
 def packed_tiles(groups):
     return [jnp.concatenate(groups[n : n + 2], axis=0).astype(BF16) for n in range(0, len(groups), 2)]
 
 
-def side_group(ref, tile, i, low):
-    group = ref[tile + i // 4].astype(F32)[i % 4 // 2 * 8 :][:8]
+def side_group(ref, a, i, low):
+    def group(k, by):
+        n = 3 * (i // 8) + k
+        cells = ref[3 * a + n // 2].astype(F32)[n % 2 * 8 :][:8]
+        return pltpu.roll(cells, by % 8, 0) if by % 8 else cells
+
+    n = i % 8
+    if n < 6:
+        shift = (0, 3) if low else (5, 0)
+        return group(n // 2, shift[n % 2])
+    row = rows_of(ref.shape[2])
     if low:
-        return group if i % 2 == 0 else pltpu.roll(group, 3, 0)
-    return group if i % 2 == 1 else pltpu.roll(group, 5, 0)
+        return jnp.where(row < 2, group(n - 6, -3), group(2, -1 if n == 6 else -2))
+    return jnp.where(row < 7, group(n - 6, 2), group(2, 4 if n == 6 else 3))
 
 
 def outer(group, low):
@@ -156,27 +171,28 @@
 def send_sides(low, high, west_ref, east_ref):
     j = lax.axis_index("gy")
     last = lax.axis_size("gy") - 1
-    for ref, groups, on in ((west_ref, pack_low(low), j > 0), (east_ref, pack_high(high), j < last)):
+    for ref, groups, on in ((west_ref, low, j > 0), (east_ref, high, j < last)):
         inside = jnp.where(on, 1.0, 0.0)
-        for n, tile in enumerate(packed_tiles([group * inside for group in groups])):
+        cells = [group * inside for group in packed(groups, ref is west_ref)]
+        for n, tile in enumerate(packed_tiles(cells)):
             ref[n] = tile
 
 
 def end_kernel(masks, top_ref, bottom_ref, *refs):
     west_ref, east_ref, north_ref, south_ref = refs[masks:]
     lat = top_ref.shape[1]
-    tiles = west_ref.shape[0]
+    last = west_ref.shape[0] // 3 - 1
     for i in range(3):
-        for n, (out_ref, ref, tile) in enumerate(
-            ((north_ref, top_ref, 0), (south_ref, bottom_ref, tiles - 1))
+        for n, (out_ref, ref, row) in enumerate(
+            ((north_ref, top_ref, 0), (south_ref, bottom_ref, last))
         ):
-            at = i + n
-            cells = ref[at if masks else i]
+            at = i + (TILE - 3) * n
+            cells = ref[i + n if masks else i]
             if masks:
-                cells = cells * both(refs[n][at])
-            out_ref[i, :TILE, :] = outer(side_group(west_ref, tile, at, False), False)
+                cells = cells * both(refs[n][i + n])
+            out_ref[i, :TILE, :] = outer(side_group(west_ref, row, at, False), False)
             out_ref[i, TILE : TILE + lat, :] = cells
-            out_ref[i, TILE + lat :, :] = outer(side_group(east_ref, tile, at, True), True)
+            out_ref[i, TILE + lat :, :] = outer(side_group(east_ref, row, at, True), True)
 
 
 def transformed(patches, place_ref):
@@ -248,9 +264,9 @@
             ref, wets, n = before_ref, wet_before_ref, i + 8
         elif i >= TILE:
             ref, wets, n = after_ref, wet_after_ref, i - TILE
-        pad_ref[3 + i, :TILE, :] = outer(side_group(west_ref, 4 * a, i, False), False)
+        pad_ref[3 + i, :TILE, :] = outer(side_group(west_ref, a, i, False), False)
         pad_ref[3 + i, TILE : TILE + lat, :] = ref[n] * both(wets[n])
-        pad_ref[3 + i, TILE + lat :, :] = outer(side_group(east_ref, 4 * a, i, True), True)
+        pad_ref[3 + i, TILE + lat :, :] = outer(side_group(east_ref, a, i, True), True)
 
     for i in range(TILE):
         fill(i)
@@ -424,9 +440,9 @@
         if i >= TILE and at == rows - 1:
             return south_ref[i - TILE, TILE * (b + 1) : TILE * (b + 2), :]
         if b < 0:
-            return outer(side_group(west_ref, 4 * at, i, False), False)
+            return outer(side_group(west_ref, at, i, False), False)
         if b == count:
-            return outer(side_group(east_ref, 4 * at, i, True), True)
+            return outer(side_group(east_ref, at, i, True), True)
         ref, n = fg_ref, i
         if i < 0:
             ref, n = before_ref, i + 8
@@ -465,7 +481,7 @@
 
 def sides(x, wet):
     lon, lat, channels = x.shape
-    shapes = [shape_of((lon // 4, TILE, channels), BF16)] * 2
+    shapes = [shape_of((3 * lon // TILE, TILE, channels), BF16)] * 2
     return pl.pallas_call(
         side_kernel,
         grid=(1,),
@@ -532,7 +548,7 @@
             ),
         ]
 
-    packed = pl.BlockSpec((4, TILE, channels), lambda i: (row(i), 0, 0))
+    packed = pl.BlockSpec((3, TILE, channels), lambda i: (row(i), 0, 0))
     constants = [table["place"], table["own"], table["back"], taps, table["collect"], *params]
     operands = [who, x, x, x, wet, wet, wet, *halos, cotangent, *constants]
     in_specs = [IN_SMEM, *around(channels), *around(LANES), *[whole(*h.shape) for h in halos]]

time: 84.5 us -> 82.4 us (0.975)
  waiting for transfers between devices: 9.44 us -> 7.66 us
  local copies, waits for them, and re-layouts: 1.7 us -> 0.8 us
    ppermute x2, waiting for transfers between devices: 2.67 us -> 0.01 us  [across_lat(): lax.ppermute(west, 'gy', ring('gy', -1))]
    slice x1, local copies, waits for them, and re-layouts: 0.98 us -> 0.1 us  [local(): taps[3 * HALF:]]
  transfers between devices with their start and end apart: 22 -> 22, of which waited for: 8 -> 6; matrix products, arithmetic and copies ran while one was open for 2% -> 1% of each run, Pallas kernels for 22% -> 23%
where the time goes in v9:
time: 82.4 us; the launch traced here: 82.2 us
  starting transfers between devices  38.6 us (47%)
  Pallas kernels  33.2 us (40%)
  waiting for transfers between devices  7.66 us (9%)
  between operations  0.99 us (1%)
    ppermute x14, starting transfers between devices, move(): return lax.ppermute(x, AXES, swapped(mesh_shape, stage, step))  25 us
    pallas_call x2, Pallas kernels, cell_pass(): pl.pallas_call(functools.partial(cell_kernel, at_ends, rows), grid=(2,),...  20.5 us
    pallas_call x4, Pallas kernels, spread_pass(): pl.pallas_call(functools.partial(spread_kernel, at, rows), grid=(1,), in_...  8.6 us
    ppermute x14, waiting for transfers between devices, move(): return lax.ppermute(x, AXES, swapped(mesh_shape, stage, step))  5.98 us
    ppermute x2, starting transfers between devices, across_lat(): lax.ppermute(west, 'gy', ring('gy', -1))  5.93 us
    ppermute x2, starting transfers between devices, across_lon(): lax.ppermute(south, 'gx', ring('gx', 1))  3.58 us
    ppermute x2, starting transfers between devices, across_lat(): lax.ppermute(east, 'gy', ring('gy', 1))  2.58 us
    pallas_call x1, Pallas kernels, sides(): pl.pallas_call(side_kernel, grid=(1,), in_specs=[pl.BlockSpec((lon, TILE,...  2.32 us
  transfers between devices with their start and end apart: 22, of which 6 were waited for; matrix products, arithmetic and copies ran while one was open for 1% of the time, Pallas kernels for 23%

profile of v9, /device:TPU:1, one launch (start us, length us, event | category | flops | bytes accessed | tf_op | source)
XLA Modules:
  0.0 82.2 jit_solution(18091811728877196753)
XLA Ops:
  0.6 0.0 copy-start
  0.7 0.0 copy-start.9
  0.7 2.3 %sides.1 = (bf16[12,16,256]{2,1,0:T(8,128)(2,1)}, bf16[12,16,256]{2,1,0:T(8,128)(2,1)}) custom-call(bf16[64,64,256]{2,1,0:T(8,128)(2,1)} %refs_3_.3, bf16[64,64,256]{2,1,0:T(8,128)(2,1)} %refs_3_.3, s32[64,64]{1,0:T(8,128)} %wet_ref.1), custom_call_target="tpu_custom_call" | custom-call | tf_op jit(solution)/shard_map/sides/pallas_call | solution.py:485
  3.0 2.5 %collective-permute-start = (bf16[12,16,256]{2,1,0:T(8,128)(2,1)}, bf16[12,16,256]{2,1,0:T(8,128)(2,1)S(1)}, u32[]{:S(2)}, u32[]{:S(2)}) collective-permute-start(bf16[12,16,256]{2,1,0:T(8,128)(2,1)} %get-tuple-element.38), channel_id=1, source_target_pairs={{0,1},{1,2},{2,3},{3,4},{4,5},{5,6},{6,7},{7,0},{8,9},{9,10},{10,1... | collective-permute-start | bytes 294920 | tf_op jit(solution)/shard_map/ppermute | solution.py:666
  5.5 2.5 %collective-permute-start.1 = (bf16[12,16,256]{2,1,0:T(8,128)(2,1)}, bf16[12,16,256]{2,1,0:T(8,128)(2,1)S(1)}, u32[]{:S(2)}, u32[]{:S(2)}) collective-permute-start(bf16[12,16,256]{2,1,0:T(8,128)(2,1)} %get-tuple-element.39), channel_id=1, source_target_pairs={{0,7},{1,0},{2,1},{3,2},{4,3},{5,4},{6,5},{7,6},{8,15},{9,8},{10,9... | collective-permute-start | bytes 294920 | tf_op jit(solution)/shard_map/ppermute | solution.py:666
  8.1 0.8 fusion.1
  8.8 0.0 copy-start.1
  8.8 0.1 fusion
  8.9 0.1 pad_add_fusion.refs_0_.who_ref
  9.0 1.7 %collective-permute-done.refs_2_.refs_7_ = bf16[12,16,256]{2,1,0:T(8,128)(2,1)S(1)} collective-permute-done((bf16[12,16,256]{2,1,0:T(8,128)(2,1)}, bf16[12,16,256]{2,1,0:T(8,128)(2,1)S(1)}, u32[]{:S(2)}, u32[]{:S(2)}) %collective-permute-start) | collective-permute-done | bytes 98336 | tf_op jit(solution)/shard_map/ppermute | solution.py:666
  10.7 0.0 collective-permute-done.1.refs_3_.refs_8_
  10.7 0.6 broadcast_in_dim.4.refs_0_.refs_1_.refs_4_.refs_5_.refs_6_.wet_ref
  11.3 0.0 copy-start.2
  11.3 0.0 copy-start.3
  11.3 0.0 copy-start.4
  11.3 0.0 copy-start.5
  11.4 0.0 copy-start.6
  11.4 0.0 copy-start.7
  11.4 0.0 copy-start.8
  11.4 3.5 %collective-permute-start.2 = (bf16[3,96,256]{2,1,0:T(8,128)(2,1)S(1)}, bf16[3,96,256]{2,1,0:T(8,128)(2,1)S(1)}, u32[]{:S(2)}, u32[]{:S(2)}) collective-permute-start(bf16[3,96,256]{2,1,0:T(8,128)(2,1)S(1)} %get-tuple-element.40), channel_id=1, source_target_pairs={{0,8},{8,16},{16,24},{24,32},{32,40},{40,48},{48,56},{56,64},{64,7... | collective-permute-start | bytes 442376 | tf_op jit(solution)/shard_map/ppermute | solution.py:670
  14.9 0.0 collective-permute-start.3
  15.0 9.9 %inner_cells.1 = (bf16[64,64,256]{2,1,0:T(8,128)(2,1)S(1)}, bf16[12,16,256]{2,1,0:T(8,128)(2,1)S(1)}, bf16[12,16,256]{2,1,0:T(8,128)(2,1)S(1)}, f32[2176,128]{1,...) custom-call(s32[2]{0:T(128)S(1)} %pad_add_fusion.refs_0_.who_ref, bf16[64,64,256]{2,1,0:T(8,128)(2,1)S(1)} %copy-done.1, ...), custom_call_target="tpu_custom_call" | custom-call | flops 10000000000 | bytes 8388608 | tf_op jit(solution)/shard_map/inner_cells/pallas_call | solution.py:571
  24.9 0.0 collective-permute-done.2.refs_18_
  24.9 0.0 collective-permute-done.3.refs_19_
  24.9 10.6 %end_cells.1 = (bf16[64,64,256]{2,1,0:T(8,128)(2,1)S(1)}, bf16[12,16,256]{2,1,0:T(8,128)(2,1)S(1)}, bf16[12,16,256]{2,1,0:T(8,128)(2,1)S(1)}, f32[4,272,128]{2,1...) custom-call(s32[2]{0:T(128)S(1)} %pad_add_fusion.refs_0_.who_ref, ...), custom_call_target="tpu_custom_call", output_to_operand_aliasing={{0}: (20, {}), {1}: (21, {}), {2}: (22, {})} | custom-call | flops 10000000000 | bytes 8388608 | tf_op jit(solution)/shard_map/end_cells/pallas_call | solution.py:571
  35.5 4.3 %collective-permute-start.8 = (f32[4,272,128]{2,1,0:T(8,128)S(1)}, f32[4,272,128]{2,1,0:T(8,128)S(1)}, u32[]{:S(2)}, u32[]{:S(2)}) collective-permute-start(f32[4,272,128]{2,1,0:T(8,128)S(1)} %get-tuple-element.56), channel_id=1, source_target_pairs={{0,8},{1,9},{2,10},{3,11},{4,12},{5,13},{6,14},{7,15},{8,0},{9,1},... | collective-permute-start | bytes 1671176 | tf_op jit(solution)/shard_map/ppermute | solution.py:701
  39.8 0.1 collective-permute-start.4
  39.9 3.5 %collective-permute-start.5 = (bf16[12,16,256]{2,1,0:T(8,128)(2,1)S(1)}, bf16[12,16,256]{2,1,0:T(8,128)(2,1)S(1)}, u32[]{:S(2)}, u32[]{:S(2)}) collective-permute-start(bf16[12,16,256]{2,1,0:T(8,128)(2,1)S(1)} %get-tuple-element.52), channel_id=1, source_target_pairs={{0,7},{1,0},{2,1},{3,2},{4,3},{5,4},{6,5},{7,6},{8,15},{9,8},{10,9... | collective-permute-start | bytes 294920 | tf_op jit(solution)/shard_map/ppermute | solution.py:666
  43.4 0.0 collective-permute-done.8.come_ref
  43.4 0.1 fold.1
  43.5 0.1 collective-permute-start.9
  43.6 2.5 %collective-permute-start.10 = (bf16[1,272,128]{2,1,0:T(8,128)(2,1)S(1)}, bf16[1,272,128]{2,1,0:T(8,128)(2,1)S(1)}, u32[]{:S(2)}, u32[]{:S(2)}) collective-permute-start(bf16[1,272,128]{2,1,0:T(8,128)(2,1)S(1)} %get-tuple-element.59), channel_id=1, source_target_pairs={{0,32},{1,33},{2,34},{3,35},{4,36},{5,37},{6,38},{7,39},{8,12},{9,... | collective-permute-start | bytes 208904 | tf_op jit(solution)/shard_map/ppermute | solution.py:701
  46.1 1.3 %collective-permute-start.11 = (bf16[1,272,128]{2,1,0:T(8,128)(2,1)S(1)}, bf16[1,272,128]{2,1,0:T(8,128)(2,1)S(1)}, u32[]{:S(2)}, u32[]{:S(2)}) collective-permute-start(bf16[1,272,128]{2,1,0:T(8,128)(2,1)S(1)} %get-tuple-element.60), channel_id=1, source_target_pairs={{0,48},{1,49},{2,50},{3,51},{4,52},{5,53},{6,54},{7,55},{8,14},{9,... | collective-permute-start | bytes 208904 | tf_op jit(solution)/shard_map/ppermute | solution.py:701
  47.4 0.0 collective-permute-done.4.refs_0_.north_ref.west_ref
  47.4 0.0 collective-permute-done.5.refs_1_.south_ref.east_ref
  47.4 0.1 collective-permute-start.6
  47.5 1.5 %collective-permute-start.7 = (bf16[3,96,256]{2,1,0:T(8,128)(2,1)S(1)}, bf16[3,96,256]{2,1,0:T(8,128)(2,1)S(1)}, u32[]{:S(2)}, u32[]{:S(2)}) collective-permute-start(bf16[3,96,256]{2,1,0:T(8,128)(2,1)S(1)} %get-tuple-element.54), channel_id=1, source_target_pairs={{0,120},{8,0},{16,8},{24,16},{32,24},{40,32},{48,40},{56,48},{64,5... | collective-permute-start | bytes 442376 | tf_op jit(solution)/shard_map/ppermute | solution.py:670
  49.1 0.0 collective-permute-done.9
  49.1 0.0 collective-permute-done.10
  49.1 1.4 %collective-permute-done.11 = bf16[1,272,128]{2,1,0:T(8,128)(2,1)S(1)} collective-permute-done((bf16[1,272,128]{2,1,0:T(8,128)(2,1)S(1)}, bf16[1,272,128]{2,1,0:T(8,128)(2,1)S(1)}, u32[]{:S(2)}, u32[]{:S(2)}) %collective-permute-start.11) | collective-permute-done | bytes 69664 | tf_op jit(solution)/shard_map/ppermute | solution.py:701
  50.5 1.7 %collective-permute-start.14 = (bf16[1,272,128]{2,1,0:T(8,128)(2,1)S(1)}, bf16[1,272,128]{2,1,0:T(8,128)(2,1)S(1)}, u32[]{:S(2)}, u32[]{:S(2)}) collective-permute-start(bf16[1,272,128]{2,1,0:T(8,128)(2,1)S(1)} %add_convert_fusion.2), channel_id=1, source_target_pairs={{0,6},{1,7},{2,4},{3,5},{4,2},{5,3},{6,0},{7,1},{8,73},{9,72},{10,... | collective-permute-start | bytes 208904 | tf_op jit(solution)/shard_map/ppermute | solution.py:701
  52.2 2.0 %collective-permute-start.13 = (bf16[1,272,128]{2,1,0:T(8,128)(2,1)S(1)}, bf16[1,272,128]{2,1,0:T(8,128)(2,1)S(1)}, u32[]{:S(2)}, u32[]{:S(2)}) collective-permute-start(bf16[1,272,128]{2,1,0:T(8,128)(2,1)S(1)} %add_convert_fusion.2), channel_id=1, source_target_pairs={{0,4},{1,5},{2,6},{3,7},{4,0},{5,1},{6,2},{7,3},{8,72},{9,73},{10,... | collective-permute-start | bytes 208904 | tf_op jit(solution)/shard_map/ppermute | solution.py:701
  54.2 0.0 collective-permute-start.12
  54.2 2.2 %spread_pass.4.out_refs_0_ = f32[64,64,256]{2,1,0:T(8,128)} custom-call(bf16[64,64,256]{2,1,0:T(8,128)(2,1)S(1)} %get-tuple-element.48.before_ref.fg_ref.after_ref, bf16[64,64,256]{2,1,0:T(8,128)(2,1)S(1)} %get-tuple-element.48.before_ref.fg_ref.after_ref, bf16[64,64,256]{2,1,0:T(8,128)(2,1)S(1)} %get-tuple-element.48.before_ref.fg_ref.after_ref, ...), custom_call_target="tpu_custom_call" | custom-call | flops 4000000000 | bytes 4194304 | tf_op jit(solution)/shard_map/spread_pass/pallas_call | solution.py:634
  56.4 0.0 collective-permute-done.14
  56.4 0.9 %collective-permute-done.13 = bf16[1,272,128]{2,1,0:T(8,128)(2,1)S(1)} collective-permute-done((bf16[1,272,128]{2,1,0:T(8,128)(2,1)S(1)}, bf16[1,272,128]{2,1,0:T(8,128)(2,1)S(1)}, u32[]{:S(2)}, u32[]{:S(2)}) %collective-permute-start.13) | collective-permute-done | bytes 69664 | tf_op jit(solution)/shard_map/ppermute | solution.py:701
  57.3 0.5 collective-permute-done.12
  57.9 3.3 %collective-permute-start.17 = (bf16[1,272,128]{2,1,0:T(8,128)(2,1)S(1)}, bf16[1,272,128]{2,1,0:T(8,128)(2,1)S(1)}, u32[]{:S(2)}, u32[]{:S(2)}) collective-permute-start(bf16[1,272,128]{2,1,0:T(8,128)(2,1)S(1)} %add_convert_fusion.1), channel_id=1, source_target_pairs={{0,65},{1,64},{2,67},{3,66},{4,69},{5,68},{6,71},{7,70},{8,56},{9,... | collective-permute-start | bytes 208904 | tf_op jit(solution)/shard_map/ppermute | solution.py:701
  61.1 0.0 collective-permute-start.16
  61.1 0.7 collective-permute-start.15
  61.8 2.2 %spread_pass.5.out_refs_0_ = f32[64,64,256]{2,1,0:T(8,128)} custom-call(bf16[64,64,256]{2,1,0:T(8,128)(2,1)S(1)} %get-tuple-element.48.before_ref.fg_ref.after_ref, bf16[64,64,256]{2,1,0:T(8,128)(2,1)S(1)} %get-tuple-element.48.before_ref.fg_ref.after_ref, ...), custom_call_target="tpu_custom_call", output_to_operand_aliasing={{}: (12, {})} | custom-call | flops 4000000000 | bytes 4194304 | tf_op jit(solution)/shard_map/spread_pass/pallas_call | solution.py:634
  64.0 1.8 %collective-permute-done.16 = bf16[1,272,128]{2,1,0:T(8,128)(2,1)S(1)} collective-permute-done((bf16[1,272,128]{2,1,0:T(8,128)(2,1)S(1)}, bf16[1,272,128]{2,1,0:T(8,128)(2,1)S(1)}, u32[]{:S(2)}, u32[]{:S(2)}) %collective-permute-start.16) | collective-permute-done | bytes 69664 | tf_op jit(solution)/shard_map/ppermute | solution.py:701
  65.8 0.0 collective-permute-done.15
  65.9 2.1 %collective-permute-start.20 = (bf16[1,272,128]{2,1,0:T(8,128)(2,1)S(1)}, bf16[1,272,128]{2,1,0:T(8,128)(2,1)S(1)}, u32[]{:S(2)}, u32[]{:S(2)}) collective-permute-start(bf16[1,272,128]{2,1,0:T(8,128)(2,1)S(1)} %add_convert_fusion.refs_0_), channel_id=1, source_target_pairs={{0,48},{1,49},{2,50},{3,51},{4,52},{5,53},{6,54},{7,55},{8,14},{9,... | collective-permute-start | bytes 208904 | tf_op jit(solution)/shard_map/ppermute | solution.py:701
  68.0 0.6 collective-permute-start.19
  68.6 0.6 collective-permute-start.18
  69.2 0.0 collective-permute-done.7.south_ref
  69.2 2.1 %spread_pass.6.out_refs_0_ = f32[64,64,256]{2,1,0:T(8,128)} custom-call(bf16[64,64,256]{2,1,0:T(8,128)(2,1)S(1)} %get-tuple-element.48.before_ref.fg_ref.after_ref, bf16[64,64,256]{2,1,0:T(8,128)(2,1)S(1)} %get-tuple-element.48.before_ref.fg_ref.after_ref, ...), custom_call_target="tpu_custom_call", output_to_operand_aliasing={{}: (12, {})} | custom-call | flops 4000000000 | bytes 4194304 | tf_op jit(solution)/shard_map/spread_pass/pallas_call | solution.py:634
  71.3 0.0 collective-permute-done.20.refs_3_
  71.3 1.3 %collective-permute-done.19.refs_2_ = bf16[1,272,128]{2,1,0:T(8,128)(2,1)S(1)} collective-permute-done((bf16[1,272,128]{2,1,0:T(8,128)(2,1)S(1)}, bf16[1,272,128]{2,1,0:T(8,128)(2,1)S(1)}, u32[]{:S(2)}, u32[]{:S(2)}) %collective-permute-start.19) | collective-permute-done | bytes 69664 | tf_op jit(solution)/shard_map/ppermute | solution.py:701
  72.6 0.0 collective-permute-done.18.refs_1_
  72.7 5.7 %collective-permute-start.21 = (bf16[4,272,128]{2,1,0:T(8,128)(2,1)S(1)}, bf16[4,272,128]{2,1,0:T(8,128)(2,1)S(1)}, u32[]{:S(2)}, u32[]{:S(2)}) collective-permute-start(bf16[4,272,128]{2,1,0:T(8,128)(2,1)S(1)} %join.1.own_ref), channel_id=1, source_target_pairs={{0,8},{1,9},{2,10},{3,11},{4,12},{5,13},{6,14},{7,15},{8,0},{9,1},... | collective-permute-start | bytes 835592 | tf_op jit(solution)/shard_map/ppermute | solution.py:701
  78.4 2.2 %spread_pass.7 = f32[64,64,256]{2,1,0:T(8,128)} custom-call(bf16[64,64,256]{2,1,0:T(8,128)(2,1)S(1)} %get-tuple-element.48.before_ref.fg_ref.after_ref, bf16[64,64,256]{2,1,0:T(8,128)(2,1)S(1)} %get-tuple-element.48.before_ref.fg_ref.after_ref, ...), custom_call_target="tpu_custom_call", output_to_operand_aliasing={{}: (12, {})} | custom-call | flops 4000000000 | bytes 4194304 | tf_op jit(solution)/shard_map/spread_pass/pallas_call | solution.py:634
  80.6 1.7 %finish.1 = (f32[49,256]{1,0:T(8,128)}, f32[1,256]{1,0:T(1,128)}, f32[1,256]{1,0:T(1,128)}, f32[1,256]{1,0:T(1,128)}, f32[256,512]{1,0:T(8,128)}, /*index=5*/f32[1,512]{1,0:T(1,128)}, f32[512,256]{1,0:T(8,128)}) custom-call(s32[2]{0:T(128)S(1)} %pad_add_fusion.refs_0_.who_ref, bf16[4,272,128]{2,1,0:T(8,128)(2,1)S(1)} %join.1.own_ref, ...), custom_call_target="tpu_custom_call" | custom-call | tf_op jit(solution)/shard_map/finish/pallas_call | solution.py:612
  (32 shorter events, 0.3 us)
Async XLA Ops:
  0.6 7.4 %copy-start = (bf16[49,256]{1,0:T(8,128)(2,1)S(1)}, bf16[49,256]{1,0:T(8,128)(2,1)}, u32[]{:S(2)}) copy-start(bf16[49,256]{1,0:T(8,128)(2,1)} %param.18) | copy-start | bytes 75268
  0.7 7.4 %copy-start.9 = (f32[1536,49]{1,0:T(8,128)S(1)}, f32[1536,49]{1,0:T(8,128)}, u32[]{:S(2)}) copy-start(f32[1536,49]{1,0:T(8,128)} %constant.61.clone) | copy-start | bytes 903172
  0.7 7.3 %copy-start.10 = (s32[64,64]{1,0:T(8,128)S(1)}, s32[64,64]{1,0:T(8,128)}, u32[]{:S(2)}) copy-start(s32[64,64]{1,0:T(8,128)} %wet_ref.1) | copy-start | bytes 49156
  0.7 7.3 %copy-start.11 = (bf16[512]{0:T(512)(128)(2,1)S(1)}, bf16[512]{0:T(512)(128)(2,1)}, u32[]{:S(2)}) copy-start(bf16[512]{0:T(512)(128)(2,1)} %param.23) | copy-start | bytes 3076
  0.7 7.3 %copy-start.12 = (bf16[256]{0:T(256)(128)(2,1)S(1)}, bf16[256]{0:T(256)(128)(2,1)}, u32[]{:S(2)}) copy-start(bf16[256]{0:T(256)(128)(2,1)} %param.21) | copy-start | bytes 1540
  0.7 7.3 %copy-start.13 = (bf16[256]{0:T(256)(128)(2,1)S(1)}, bf16[256]{0:T(256)(128)(2,1)}, u32[]{:S(2)}) copy-start(bf16[256]{0:T(256)(128)(2,1)} %param.20) | copy-start | bytes 1540
  0.7 7.3 %copy-start.14 = (bf16[256]{0:T(256)(128)(2,1)S(1)}, bf16[256]{0:T(256)(128)(2,1)}, u32[]{:S(2)}) copy-start(bf16[256]{0:T(256)(128)(2,1)} %param.19) | copy-start | bytes 1540
  3.0 7.6 %collective-permute-start = (bf16[12,16,256]{2,1,0:T(8,128)(2,1)}, bf16[12,16,256]{2,1,0:T(8,128)(2,1)S(1)}, u32[]{:S(2)}, u32[]{:S(2)}) collective-permute-start(bf16[12,16,256]{2,1,0:T(8,128)(2,1)} %get-tuple-element.38), channel_id=1, source_target_pairs={{0,1},{1,2},{2,3},{3,4},{4,5},{5,6},{6,7},{7,0},{8,9},{9,10},{10,1... | collective-permute-start | bytes 294920 | tf_op jit(solution)/shard_map/ppermute | solution.py:666
  5.5 5.2 %collective-permute-start.1 = (bf16[12,16,256]{2,1,0:T(8,128)(2,1)}, bf16[12,16,256]{2,1,0:T(8,128)(2,1)S(1)}, u32[]{:S(2)}, u32[]{:S(2)}) collective-permute-start(bf16[12,16,256]{2,1,0:T(8,128)(2,1)} %get-tuple-element.39), channel_id=1, source_target_pairs={{0,7},{1,0},{2,1},{3,2},{4,3},{5,4},{6,5},{7,6},{8,15},{9,8},{10,9... | collective-permute-start | bytes 294920 | tf_op jit(solution)/shard_map/ppermute | solution.py:666
  8.8 2.5 %copy-start.1 = (bf16[64,64,256]{2,1,0:T(8,128)(2,1)S(1)}, bf16[64,64,256]{2,1,0:T(8,128)(2,1)}, u32[]{:S(2)}) copy-start(bf16[64,64,256]{2,1,0:T(8,128)(2,1)} %refs_3_.3) | copy-start | bytes 6291460
  11.3 3.6 %copy-start.2 = (bf16[64,64,256]{2,1,0:T(8,128)(2,1)S(1)}, bf16[64,64,256]{2,1,0:T(8,128)(2,1)}, u32[]{:S(2)}) copy-start(bf16[64,64,256]{2,1,0:T(8,128)(2,1)} %cot_ref.7) | copy-start | bytes 6291460
  11.3 3.6 %copy-start.3 = (bf16[512,512]{1,0:T(8,128)(2,1)S(1)}, bf16[512,512]{1,0:T(8,128)(2,1)}, u32[]{:S(2)}) copy-start(bf16[512,512]{1,0:T(8,128)(2,1)} %constant.62.clone.refs_10_.place_ref) | copy-start | bytes 1572868
  11.3 3.6 %copy-start.4 = (bf16[256,512]{1,0:T(8,128)(2,1)S(1)}, bf16[256,512]{1,0:T(8,128)(2,1)}, u32[]{:S(2)}) copy-start(bf16[256,512]{1,0:T(8,128)(2,1)} %constant.64.clone.refs_12_.back_ref) | copy-start | bytes 786436
  11.3 3.6 %copy-start.5 = (bf16[256,512]{1,0:T(8,128)(2,1)S(1)}, bf16[256,512]{1,0:T(8,128)(2,1)}, u32[]{:S(2)}) copy-start(bf16[256,512]{1,0:T(8,128)(2,1)} %refs_16_.3) | copy-start | bytes 786436
  11.4 3.6 %copy-start.6 = (bf16[512,256]{1,0:T(8,128)(2,1)S(1)}, bf16[512,256]{1,0:T(8,128)(2,1)}, u32[]{:S(2)}) copy-start(bf16[512,256]{1,0:T(8,128)(2,1)} %refs_17_.3) | copy-start | bytes 786436
  11.4 3.6 %copy-start.7 = (bf16[512,256]{1,0:T(8,128)(2,1)S(1)}, bf16[512,256]{1,0:T(8,128)(2,1)}, u32[]{:S(2)}) copy-start(bf16[512,256]{1,0:T(8,128)(2,1)} %constant.63.clone.refs_11_) | copy-start | bytes 786436
  11.4 3.6 %copy-start.8 = (f32[49,768]{1,0:T(8,128)S(1)}, f32[49,768]{1,0:T(8,128)}, u32[]{:S(2)}) copy-start(f32[49,768]{1,0:T(8,128)} %constant.65.clone.refs_14_) | copy-start | bytes 451588
  11.4 13.4 %collective-permute-start.2 = (bf16[3,96,256]{2,1,0:T(8,128)(2,1)S(1)}, bf16[3,96,256]{2,1,0:T(8,128)(2,1)S(1)}, u32[]{:S(2)}, u32[]{:S(2)}) collective-permute-start(bf16[3,96,256]{2,1,0:T(8,128)(2,1)S(1)} %get-tuple-element.40), channel_id=1, source_target_pairs={{0,8},{8,16},{16,24},{24,32},{32,40},{40,48},{48,56},{56,64},{64,7... | collective-permute-start | bytes 442376 | tf_op jit(solution)/shard_map/ppermute | solution.py:670
  14.9 9.9 %collective-permute-start.3 = (bf16[3,96,256]{2,1,0:T(8,128)(2,1)S(1)}, bf16[3,96,256]{2,1,0:T(8,128)(2,1)S(1)}, u32[]{:S(2)}, u32[]{:S(2)}) collective-permute-start(bf16[3,96,256]{2,1,0:T(8,128)(2,1)S(1)} %get-tuple-element.41), channel_id=1, source_target_pairs={{0,120},{8,0},{16,8},{24,16},{32,24},{40,32},{48,40},{56,48},{64,5... | collective-permute-start | bytes 442376 | tf_op jit(solution)/shard_map/ppermute | solution.py:670
  35.5 7.9 %collective-permute-start.8 = (f32[4,272,128]{2,1,0:T(8,128)S(1)}, f32[4,272,128]{2,1,0:T(8,128)S(1)}, u32[]{:S(2)}, u32[]{:S(2)}) collective-permute-start(f32[4,272,128]{2,1,0:T(8,128)S(1)} %get-tuple-element.56), channel_id=1, source_target_pairs={{0,8},{1,9},{2,10},{3,11},{4,12},{5,13},{6,14},{7,15},{8,0},{9,1},... | collective-permute-start | bytes 1671176 | tf_op jit(solution)/shard_map/ppermute | solution.py:701
  39.8 7.6 %collective-permute-start.4 = (bf16[12,16,256]{2,1,0:T(8,128)(2,1)S(1)}, bf16[12,16,256]{2,1,0:T(8,128)(2,1)S(1)}, u32[]{:S(2)}, u32[]{:S(2)}) collective-permute-start(bf16[12,16,256]{2,1,0:T(8,128)(2,1)S(1)} %get-tuple-element.51), channel_id=1, source_target_pairs={{0,1},{1,2},{2,3},{3,4},{4,5},{5,6},{6,7},{7,0},{8,9},{9,10},{10,1... | collective-permute-start | bytes 294920 | tf_op jit(solution)/shard_map/ppermute | solution.py:666
  39.9 7.5 %collective-permute-start.5 = (bf16[12,16,256]{2,1,0:T(8,128)(2,1)S(1)}, bf16[12,16,256]{2,1,0:T(8,128)(2,1)S(1)}, u32[]{:S(2)}, u32[]{:S(2)}) collective-permute-start(bf16[12,16,256]{2,1,0:T(8,128)(2,1)S(1)} %get-tuple-element.52), channel_id=1, source_target_pairs={{0,7},{1,0},{2,1},{3,2},{4,3},{5,4},{6,5},{7,6},{8,15},{9,8},{10,9... | collective-permute-start | bytes 294920 | tf_op jit(solution)/shard_map/ppermute | solution.py:666
  43.5 5.6 %collective-permute-start.9 = (bf16[1,272,128]{2,1,0:T(8,128)(2,1)S(1)}, bf16[1,272,128]{2,1,0:T(8,128)(2,1)S(1)}, u32[]{:S(2)}, u32[]{:S(2)}) collective-permute-start(bf16[1,272,128]{2,1,0:T(8,128)(2,1)S(1)} %get-tuple-element.58), channel_id=1, source_target_pairs={{0,16},{1,17},{2,18},{3,19},{4,20},{5,21},{6,22},{7,23},{8,10},{9,... | collective-permute-start | bytes 208904 | tf_op jit(solution)/shard_map/ppermute | solution.py:701
  43.6 5.5 %collective-permute-start.10 = (bf16[1,272,128]{2,1,0:T(8,128)(2,1)S(1)}, bf16[1,272,128]{2,1,0:T(8,128)(2,1)S(1)}, u32[]{:S(2)}, u32[]{:S(2)}) collective-permute-start(bf16[1,272,128]{2,1,0:T(8,128)(2,1)S(1)} %get-tuple-element.59), channel_id=1, source_target_pairs={{0,32},{1,33},{2,34},{3,35},{4,36},{5,37},{6,38},{7,39},{8,12},{9,... | collective-permute-start | bytes 208904 | tf_op jit(solution)/shard_map/ppermute | solution.py:701
  46.1 4.4 %collective-permute-start.11 = (bf16[1,272,128]{2,1,0:T(8,128)(2,1)S(1)}, bf16[1,272,128]{2,1,0:T(8,128)(2,1)S(1)}, u32[]{:S(2)}, u32[]{:S(2)}) collective-permute-start(bf16[1,272,128]{2,1,0:T(8,128)(2,1)S(1)} %get-tuple-element.60), channel_id=1, source_target_pairs={{0,48},{1,49},{2,50},{3,51},{4,52},{5,53},{6,54},{7,55},{8,14},{9,... | collective-permute-start | bytes 208904 | tf_op jit(solution)/shard_map/ppermute | solution.py:701
  47.4 21.7 %collective-permute-start.6 = (bf16[3,96,256]{2,1,0:T(8,128)(2,1)S(1)}, bf16[3,96,256]{2,1,0:T(8,128)(2,1)S(1)}, u32[]{:S(2)}, u32[]{:S(2)}) collective-permute-start(bf16[3,96,256]{2,1,0:T(8,128)(2,1)S(1)} %get-tuple-element.53), channel_id=1, source_target_pairs={{0,8},{8,16},{16,24},{24,32},{32,40},{40,48},{48,56},{56,64},{64,7... | collective-permute-start | bytes 442376 | tf_op jit(solution)/shard_map/ppermute | solution.py:670
  47.5 21.7 %collective-permute-start.7 = (bf16[3,96,256]{2,1,0:T(8,128)(2,1)S(1)}, bf16[3,96,256]{2,1,0:T(8,128)(2,1)S(1)}, u32[]{:S(2)}, u32[]{:S(2)}) collective-permute-start(bf16[3,96,256]{2,1,0:T(8,128)(2,1)S(1)} %get-tuple-element.54), channel_id=1, source_target_pairs={{0,120},{8,0},{16,8},{24,16},{32,24},{40,32},{48,40},{56,48},{64,5... | collective-permute-start | bytes 442376 | tf_op jit(solution)/shard_map/ppermute | solution.py:670
  50.5 5.9 %collective-permute-start.14 = (bf16[1,272,128]{2,1,0:T(8,128)(2,1)S(1)}, bf16[1,272,128]{2,1,0:T(8,128)(2,1)S(1)}, u32[]{:S(2)}, u32[]{:S(2)}) collective-permute-start(bf16[1,272,128]{2,1,0:T(8,128)(2,1)S(1)} %add_convert_fusion.2), channel_id=1, source_target_pairs={{0,6},{1,7},{2,4},{3,5},{4,2},{5,3},{6,0},{7,1},{8,73},{9,72},{10,... | collective-permute-start | bytes 208904 | tf_op jit(solution)/shard_map/ppermute | solution.py:701
  52.2 5.1 %collective-permute-start.13 = (bf16[1,272,128]{2,1,0:T(8,128)(2,1)S(1)}, bf16[1,272,128]{2,1,0:T(8,128)(2,1)S(1)}, u32[]{:S(2)}, u32[]{:S(2)}) collective-permute-start(bf16[1,272,128]{2,1,0:T(8,128)(2,1)S(1)} %add_convert_fusion.2), channel_id=1, source_target_pairs={{0,4},{1,5},{2,6},{3,7},{4,0},{5,1},{6,2},{7,3},{8,72},{9,73},{10,... | collective-permute-start | bytes 208904 | tf_op jit(solution)/shard_map/ppermute | solution.py:701
  54.2 3.6 %collective-permute-start.12 = (bf16[1,272,128]{2,1,0:T(8,128)(2,1)S(1)}, bf16[1,272,128]{2,1,0:T(8,128)(2,1)S(1)}, u32[]{:S(2)}, u32[]{:S(2)}) collective-permute-start(bf16[1,272,128]{2,1,0:T(8,128)(2,1)S(1)} %add_convert_fusion.2), channel_id=1, source_target_pairs={{0,2},{1,3},{2,0},{3,1},{4,6},{5,7},{6,4},{7,5},{8,9},{9,8},{10,11... | collective-permute-start | bytes 208904 | tf_op jit(solution)/shard_map/ppermute | solution.py:701
  57.9 6.1 %collective-permute-start.17 = (bf16[1,272,128]{2,1,0:T(8,128)(2,1)S(1)}, bf16[1,272,128]{2,1,0:T(8,128)(2,1)S(1)}, u32[]{:S(2)}, u32[]{:S(2)}) collective-permute-start(bf16[1,272,128]{2,1,0:T(8,128)(2,1)S(1)} %add_convert_fusion.1), channel_id=1, source_target_pairs={{0,65},{1,64},{2,67},{3,66},{4,69},{5,68},{6,71},{7,70},{8,56},{9,... | collective-permute-start | bytes 208904 | tf_op jit(solution)/shard_map/ppermute | solution.py:701
  61.1 4.7 %collective-permute-start.16 = (bf16[1,272,128]{2,1,0:T(8,128)(2,1)S(1)}, bf16[1,272,128]{2,1,0:T(8,128)(2,1)S(1)}, u32[]{:S(2)}, u32[]{:S(2)}) collective-permute-start(bf16[1,272,128]{2,1,0:T(8,128)(2,1)S(1)} %add_convert_fusion.1), channel_id=1, source_target_pairs={{0,64},{1,65},{2,66},{3,67},{4,68},{5,69},{6,70},{7,71},{8,40},{9,... | collective-permute-start | bytes 208904 | tf_op jit(solution)/shard_map/ppermute | solution.py:701
  61.1 4.7 %collective-permute-start.15 = (bf16[1,272,128]{2,1,0:T(8,128)(2,1)S(1)}, bf16[1,272,128]{2,1,0:T(8,128)(2,1)S(1)}, u32[]{:S(2)}, u32[]{:S(2)}) collective-permute-start(bf16[1,272,128]{2,1,0:T(8,128)(2,1)S(1)} %add_convert_fusion.1), channel_id=1, source_target_pairs={{0,1},{1,0},{2,3},{3,2},{4,5},{5,4},{6,7},{7,6},{8,24},{9,25},{10,... | collective-permute-start | bytes 208904 | tf_op jit(solution)/shard_map/ppermute | solution.py:701
  65.9 5.5 %collective-permute-start.20 = (bf16[1,272,128]{2,1,0:T(8,128)(2,1)S(1)}, bf16[1,272,128]{2,1,0:T(8,128)(2,1)S(1)}, u32[]{:S(2)}, u32[]{:S(2)}) collective-permute-start(bf16[1,272,128]{2,1,0:T(8,128)(2,1)S(1)} %add_convert_fusion.refs_0_), channel_id=1, source_target_pairs={{0,48},{1,49},{2,50},{3,51},{4,52},{5,53},{6,54},{7,55},{8,14},{9,... | collective-permute-start | bytes 208904 | tf_op jit(solution)/shard_map/ppermute | solution.py:701
  68.0 4.7 %collective-permute-start.19 = (bf16[1,272,128]{2,1,0:T(8,128)(2,1)S(1)}, bf16[1,272,128]{2,1,0:T(8,128)(2,1)S(1)}, u32[]{:S(2)}, u32[]{:S(2)}) collective-permute-start(bf16[1,272,128]{2,1,0:T(8,128)(2,1)S(1)} %add_convert_fusion.refs_0_), channel_id=1, source_target_pairs={{0,32},{1,33},{2,34},{3,35},{4,36},{5,37},{6,38},{7,39},{8,12},{9,... | collective-permute-start | bytes 208904 | tf_op jit(solution)/shard_map/ppermute | solution.py:701
  68.6 4.0 %collective-permute-start.18 = (bf16[1,272,128]{2,1,0:T(8,128)(2,1)S(1)}, bf16[1,272,128]{2,1,0:T(8,128)(2,1)S(1)}, u32[]{:S(2)}, u32[]{:S(2)}) collective-permute-start(bf16[1,272,128]{2,1,0:T(8,128)(2,1)S(1)} %add_convert_fusion.refs_0_), channel_id=1, source_target_pairs={{0,16},{1,17},{2,18},{3,19},{4,20},{5,21},{6,22},{7,23},{8,10},{9,... | collective-permute-start | bytes 208904 | tf_op jit(solution)/shard_map/ppermute | solution.py:701
  72.7 7.9 %collective-permute-start.21 = (bf16[4,272,128]{2,1,0:T(8,128)(2,1)S(1)}, bf16[4,272,128]{2,1,0:T(8,128)(2,1)S(1)}, u32[]{:S(2)}, u32[]{:S(2)}) collective-permute-start(bf16[4,272,128]{2,1,0:T(8,128)(2,1)S(1)} %join.1.own_ref), channel_id=1, source_target_pairs={{0,8},{1,9},{2,10},{3,11},{4,12},{5,13},{6,14},{7,15},{8,0},{9,1},... | collective-permute-start | bytes 835592 | tf_op jit(solution)/shard_map/ppermute | solution.py:701

commit v10 on v9

--- a/solution.py
+++ b/solution.py
@@ -48,6 +48,14 @@
     for n, f in enumerate(pairs, start=2):
         cos[n], sin[n], weight[n], paired[n] = np.cos(angle(f)), -np.sin(angle(f)), 2, 1
     return cos, sin, weight / SPAN**2, paired
+
+
+def in_parts(values):
+    parts = []
+    for _ in range(3):
+        parts.append(values.astype(jnp.bfloat16))
+        values = values - parts[-1].astype(np.float64)
+    return np.concatenate(parts, axis=1)
 
 
 @functools.cache
@@ -76,7 +84,7 @@
         place=place.astype(jnp.bfloat16),
         own=own.astype(jnp.bfloat16),
         back=back.astype(jnp.bfloat16),
-        taps=np.concatenate([taps, flipped]).astype(np.float32),
+        taps=in_parts(np.concatenate([taps, flipped])),
         collect=collect.astype(np.float32),
     )
 
@@ -376,15 +384,12 @@
     @pl.when(step == 1)
     def _():
         bottom_ref[...] = fg_ref[-3:]
-        total = 0.0
-        for n in range(3):
-            total += jnp.dot(
-                collect_ref[:, n * HALF : (n + 1) * HALF],
-                p_ref[n],
-                precision=lax.Precision.HIGHEST,
-                preferred_element_type=F32,
-            )
-        small_ref[:49, :] = total
+        small_ref[:49, :] = jnp.dot(
+            collect_ref[...],
+            p_ref[...].reshape(3 * HALF, channels),
+            precision=lax.Precision.HIGHEST,
+            preferred_element_type=F32,
+        )
         start = 4 * units * channels // LANES // 2
         for n in range(0, channels, LANES):
             sum_ref[start : start + 64, :] = small_ref[:, n : n + LANES]
@@ -477,6 +482,28 @@
 ANY = pl.BlockSpec(memory_space=pl.ANY)
 IN_SMEM = pl.BlockSpec(memory_space=pltpu.SMEM)
 IN_VMEM = pl.BlockSpec(memory_space=pltpu.VMEM)
+
+
+def prepare_kernel(basis_ref, kernel_ref, wet_ref, taps_ref, flipped_ref, wide_ref):
+    kernel = jnp.concatenate([kernel_ref[...]] * 3, axis=0)
+    for n, ref in enumerate((taps_ref, flipped_ref)):
+        ref[...] = dot(basis_ref[3 * HALF * n : 3 * HALF * (n + 1), :], kernel)
+    wet = jnp.transpose(wet_ref[...].astype(F32))
+    lat = wet.shape[0]
+    for i in range(wet.shape[1]):
+        wide_ref[i] = jnp.broadcast_to(wet[:, i : i + 1], (lat, LANES)).astype(BF16)
+
+
+def prepare(kernel, wet_mask):
+    taps = shape_of((3 * HALF, kernel.shape[1]))
+    return pl.pallas_call(
+        prepare_kernel,
+        in_specs=[IN_VMEM] * 3,
+        out_specs=[IN_VMEM] * 3,
+        out_shape=[taps, taps, shape_of(wet_mask.shape + (LANES,), BF16)],
+        compiler_params=pltpu.CompilerParams(vmem_limit_bytes=SMALL_BYTES),
+        name="prepare",
+    )(tables()["taps"], kernel, wet_mask)
 
 
 def sides(x, wet):
@@ -720,17 +747,13 @@
 ):
     lon, lat, channels = inputs.shape
     units = up_weight.shape[1]
-    wet = jnp.broadcast_to(wet_mask.astype(BF16)[:, :, None], (lon, lat, LANES))
+    halos = across_lat(*sides(inputs, wet_mask))
+    taps, flipped, wet = prepare(kernel, wet_mask)
+    end_halos = across_lon(*ends((inputs, wet), halos))
     who = places()
-    halos = across_lat(*sides(inputs, wet_mask))
-    end_halos = across_lon(*ends((inputs, wet), halos))
-    taps = jnp.dot(
-        tables()["taps"], kernel.astype(F32), precision=lax.Precision.HIGHEST,
-        preferred_element_type=F32,
-    )
     vectors = jnp.concatenate([conv_bias, norm_gain, norm_shift, up_bias])[None, :]
     params = (vectors, up_weight, down_weight)
-    first = (who, inputs, halos, cotangent, wet, taps[: 3 * HALF], params)
+    first = (who, inputs, halos, cotangent, wet, taps, params)
     inner = cell_pass(*first)
     field_grad, west, east, keep, send, top, bottom = cell_pass(*first, end_halos, inner)
     halos = across_lat(west, east)
@@ -741,7 +764,7 @@
     for at in (*middle, 0, lon // TILE - 1):
         far = halos if at in middle else end_halos
         input_grad = spread_pass(
-            at, field_grad, halos, far, cotangent, wet, taps[3 * HALF :], input_grad
+            at, field_grad, halos, far, cotangent, wet, flipped, input_grad
         )
     cells = lon * lat * lax.axis_size("gx") * lax.axis_size("gy")
     grads = finish(who, own, other, float(cells) ** -0.5, channels, units)

time: 82.4 us -> 81.6 us (level)
  transfers between devices with their start and end apart: 22 -> 22, of which waited for: 6 -> 6; matrix products, arithmetic and copies ran while one was open for 1% -> 0% of each run, Pallas kernels for 23% -> 23%
where the time goes in v10:
time: 81.6 us; the launch traced here: 81.4 us
  starting transfers between devices  38.9 us (48%)
  Pallas kernels  33.6 us (41%)
  waiting for transfers between devices  7.72 us (9%)
  between operations  0.93 us (1%)
    ppermute x14, starting transfers between devices, move(): return lax.ppermute(x, AXES, swapped(mesh_shape, stage, step))  25.1 us
    pallas_call x2, Pallas kernels, cell_pass(): pl.pallas_call(functools.partial(cell_kernel, at_ends, rows), grid=(2,),...  20.2 us
    pallas_call x4, Pallas kernels, spread_pass(): pl.pallas_call(functools.partial(spread_kernel, at, rows), grid=(1,), in_...  8.6 us
    ppermute x2, starting transfers between devices, across_lat(): lax.ppermute(west, 'gy', ring('gy', -1))  5.92 us
    ppermute x14, waiting for transfers between devices, move(): return lax.ppermute(x, AXES, swapped(mesh_shape, stage, step))  5.7 us
    ppermute x2, starting transfers between devices, across_lon(): lax.ppermute(south, 'gx', ring('gx', 1))  3.71 us
    ppermute x2, starting transfers between devices, across_lat(): lax.ppermute(east, 'gy', ring('gy', 1))  2.58 us
    pallas_call x1, Pallas kernels, sides(): pl.pallas_call(side_kernel, grid=(1,), in_specs=[pl.BlockSpec((lon, TILE,...  2.41 us
  transfers between devices with their start and end apart: 22, of which 6 were waited for; matrix products, arithmetic and copies ran while one was open for 0% of the time, Pallas kernels for 23%

profile of v10, /device:TPU:1, one launch (start us, length us, event | category | flops | bytes accessed | tf_op | source)
XLA Modules:
  0.0 81.4 jit_solution(7888307145785073673)
XLA Ops:
  0.6 0.0 copy-start.4
  0.7 2.4 %sides.1 = (bf16[12,16,256]{2,1,0:T(8,128)(2,1)}, bf16[12,16,256]{2,1,0:T(8,128)(2,1)}) custom-call(bf16[64,64,256]{2,1,0:T(8,128)(2,1)} %refs_3_.3, bf16[64,64,256]{2,1,0:T(8,128)(2,1)} %refs_3_.3, s32[64,64]{1,0:T(8,128)} %wet_ref.3), custom_call_target="tpu_custom_call" | custom-call | tf_op jit(solution)/shard_map/sides/pallas_call | solution.py:512
  3.1 2.5 %collective-permute-start = (bf16[12,16,256]{2,1,0:T(8,128)(2,1)}, bf16[12,16,256]{2,1,0:T(8,128)(2,1)S(1)}, u32[]{:S(2)}, u32[]{:S(2)}) collective-permute-start(bf16[12,16,256]{2,1,0:T(8,128)(2,1)} %get-tuple-element.42), channel_id=1, source_target_pairs={{0,1},{1,2},{2,3},{3,4},{4,5},{5,6},{6,7},{7,0},{8,9},{9,10},{10,1... | collective-permute-start | bytes 294920 | tf_op jit(solution)/shard_map/ppermute | solution.py:693
  5.6 2.5 %collective-permute-start.1 = (bf16[12,16,256]{2,1,0:T(8,128)(2,1)}, bf16[12,16,256]{2,1,0:T(8,128)(2,1)S(1)}, u32[]{:S(2)}, u32[]{:S(2)}) collective-permute-start(bf16[12,16,256]{2,1,0:T(8,128)(2,1)} %get-tuple-element.43), channel_id=1, source_target_pairs={{0,7},{1,0},{2,1},{3,2},{4,3},{5,4},{6,5},{7,6},{8,15},{9,8},{10,9... | collective-permute-start | bytes 294920 | tf_op jit(solution)/shard_map/ppermute | solution.py:693
  8.1 0.0 copy-done.13
  8.1 0.6 prepare.1
  8.7 0.1 pad_add_fusion.refs_0_.who_ref
  8.8 2.0 %collective-permute-done.refs_2_.refs_7_ = bf16[12,16,256]{2,1,0:T(8,128)(2,1)S(1)} collective-permute-done((bf16[12,16,256]{2,1,0:T(8,128)(2,1)}, bf16[12,16,256]{2,1,0:T(8,128)(2,1)S(1)}, u32[]{:S(2)}, u32[]{:S(2)}) %collective-permute-start) | collective-permute-done | bytes 98336 | tf_op jit(solution)/shard_map/ppermute | solution.py:693
  10.8 0.0 collective-permute-done.1.refs_3_.refs_8_
  10.8 0.0 copy-done
  10.8 0.0 copy-start.2
  10.8 0.0 copy-start.3
  10.8 0.0 copy-start.7
  10.8 0.0 copy-start.8
  10.8 0.0 copy-start.9
  10.8 0.0 copy-start.10
  10.9 3.5 %collective-permute-start.2 = (bf16[3,96,256]{2,1,0:T(8,128)(2,1)S(1)}, bf16[3,96,256]{2,1,0:T(8,128)(2,1)S(1)}, u32[]{:S(2)}, u32[]{:S(2)}) collective-permute-start(bf16[3,96,256]{2,1,0:T(8,128)(2,1)S(1)} %get-tuple-element.45), channel_id=1, source_target_pairs={{0,8},{8,16},{16,24},{24,32},{32,40},{40,48},{48,56},{56,64},{64,7... | collective-permute-start | bytes 442376 | tf_op jit(solution)/shard_map/ppermute | solution.py:697
  14.4 0.0 collective-permute-start.3
  14.5 9.8 %inner_cells.1 = (bf16[64,64,256]{2,1,0:T(8,128)(2,1)S(1)}, bf16[12,16,256]{2,1,0:T(8,128)(2,1)S(1)}, bf16[12,16,256]{2,1,0:T(8,128)(2,1)S(1)}, f32[2176,128]{1,...) custom-call(s32[2]{0:T(128)S(1)} %pad_add_fusion.refs_0_.who_ref, bf16[64,64,256]{2,1,0:T(8,128)(2,1)S(1)} %copy-done, ...), custom_call_target="tpu_custom_call" | custom-call | flops 10000000000 | bytes 8388608 | tf_op jit(solution)/shard_map/inner_cells/pallas_call | solution.py:598
  24.2 0.0 collective-permute-done.2.refs_18_
  24.3 0.0 collective-permute-done.3.refs_19_
  24.3 10.5 %end_cells.1 = (bf16[64,64,256]{2,1,0:T(8,128)(2,1)S(1)}, bf16[12,16,256]{2,1,0:T(8,128)(2,1)S(1)}, bf16[12,16,256]{2,1,0:T(8,128)(2,1)S(1)}, f32[4,272,128]{2,1...) custom-call(s32[2]{0:T(128)S(1)} %pad_add_fusion.refs_0_.who_ref, ...), custom_call_target="tpu_custom_call", output_to_operand_aliasing={{0}: (20, {}), {1}: (21, {}), {2}: (22, {})} | custom-call | flops 10000000000 | bytes 8388608 | tf_op jit(solution)/shard_map/end_cells/pallas_call | solution.py:598
  34.7 4.3 %collective-permute-start.8 = (f32[4,272,128]{2,1,0:T(8,128)S(1)}, f32[4,272,128]{2,1,0:T(8,128)S(1)}, u32[]{:S(2)}, u32[]{:S(2)}) collective-permute-start(f32[4,272,128]{2,1,0:T(8,128)S(1)} %get-tuple-element.62), channel_id=1, source_target_pairs={{0,8},{1,9},{2,10},{3,11},{4,12},{5,13},{6,14},{7,15},{8,0},{9,1},... | collective-permute-start | bytes 1671176 | tf_op jit(solution)/shard_map/ppermute | solution.py:728
  39.1 0.1 collective-permute-start.4
  39.2 3.5 %collective-permute-start.5 = (bf16[12,16,256]{2,1,0:T(8,128)(2,1)S(1)}, bf16[12,16,256]{2,1,0:T(8,128)(2,1)S(1)}, u32[]{:S(2)}, u32[]{:S(2)}) collective-permute-start(bf16[12,16,256]{2,1,0:T(8,128)(2,1)S(1)} %get-tuple-element.57), channel_id=1, source_target_pairs={{0,7},{1,0},{2,1},{3,2},{4,3},{5,4},{6,5},{7,6},{8,15},{9,8},{10,9... | collective-permute-start | bytes 294920 | tf_op jit(solution)/shard_map/ppermute | solution.py:693
  42.6 0.0 collective-permute-done.8.come_ref
  42.6 0.1 fold.1
  42.7 0.1 collective-permute-start.9
  42.8 2.3 %collective-permute-start.10 = (bf16[1,272,128]{2,1,0:T(8,128)(2,1)S(1)}, bf16[1,272,128]{2,1,0:T(8,128)(2,1)S(1)}, u32[]{:S(2)}, u32[]{:S(2)}) collective-permute-start(bf16[1,272,128]{2,1,0:T(8,128)(2,1)S(1)} %get-tuple-element.65), channel_id=1, source_target_pairs={{0,32},{1,33},{2,34},{3,35},{4,36},{5,37},{6,38},{7,39},{8,12},{9,... | collective-permute-start | bytes 208904 | tf_op jit(solution)/shard_map/ppermute | solution.py:728
  45.1 1.5 %collective-permute-start.11 = (bf16[1,272,128]{2,1,0:T(8,128)(2,1)S(1)}, bf16[1,272,128]{2,1,0:T(8,128)(2,1)S(1)}, u32[]{:S(2)}, u32[]{:S(2)}) collective-permute-start(bf16[1,272,128]{2,1,0:T(8,128)(2,1)S(1)} %get-tuple-element.66), channel_id=1, source_target_pairs={{0,48},{1,49},{2,50},{3,51},{4,52},{5,53},{6,54},{7,55},{8,14},{9,... | collective-permute-start | bytes 208904 | tf_op jit(solution)/shard_map/ppermute | solution.py:728
  46.6 0.0 collective-permute-done.4.refs_0_.north_ref.west_ref
  46.6 0.0 collective-permute-done.5.refs_1_.south_ref.east_ref
  46.7 0.2 collective-permute-start.6
  46.9 1.6 %collective-permute-start.7 = (bf16[3,96,256]{2,1,0:T(8,128)(2,1)S(1)}, bf16[3,96,256]{2,1,0:T(8,128)(2,1)S(1)}, u32[]{:S(2)}, u32[]{:S(2)}) collective-permute-start(bf16[3,96,256]{2,1,0:T(8,128)(2,1)S(1)} %get-tuple-element.59), channel_id=1, source_target_pairs={{0,120},{8,0},{16,8},{24,16},{32,24},{40,32},{48,40},{56,48},{64,5... | collective-permute-start | bytes 442376 | tf_op jit(solution)/shard_map/ppermute | solution.py:697
  48.5 0.0 collective-permute-done.9
  48.5 0.0 collective-permute-done.10
  48.5 1.0 %collective-permute-done.11 = bf16[1,272,128]{2,1,0:T(8,128)(2,1)S(1)} collective-permute-done((bf16[1,272,128]{2,1,0:T(8,128)(2,1)S(1)}, bf16[1,272,128]{2,1,0:T(8,128)(2,1)S(1)}, u32[]{:S(2)}, u32[]{:S(2)}) %collective-permute-start.11) | collective-permute-done | bytes 69664 | tf_op jit(solution)/shard_map/ppermute | solution.py:728
  49.5 1.9 %collective-permute-start.14 = (bf16[1,272,128]{2,1,0:T(8,128)(2,1)S(1)}, bf16[1,272,128]{2,1,0:T(8,128)(2,1)S(1)}, u32[]{:S(2)}, u32[]{:S(2)}) collective-permute-start(bf16[1,272,128]{2,1,0:T(8,128)(2,1)S(1)} %add_convert_fusion.2), channel_id=1, source_target_pairs={{0,6},{1,7},{2,4},{3,5},{4,2},{5,3},{6,0},{7,1},{8,73},{9,72},{10,... | collective-permute-start | bytes 208904 | tf_op jit(solution)/shard_map/ppermute | solution.py:728
  51.5 1.8 %collective-permute-start.13 = (bf16[1,272,128]{2,1,0:T(8,128)(2,1)S(1)}, bf16[1,272,128]{2,1,0:T(8,128)(2,1)S(1)}, u32[]{:S(2)}, u32[]{:S(2)}) collective-permute-start(bf16[1,272,128]{2,1,0:T(8,128)(2,1)S(1)} %add_convert_fusion.2), channel_id=1, source_target_pairs={{0,4},{1,5},{2,6},{3,7},{4,0},{5,1},{6,2},{7,3},{8,72},{9,73},{10,... | collective-permute-start | bytes 208904 | tf_op jit(solution)/shard_map/ppermute | solution.py:728
  53.2 0.0 collective-permute-start.12
  53.2 2.2 %spread_pass.4.out_refs_0_ = f32[64,64,256]{2,1,0:T(8,128)} custom-call(bf16[64,64,256]{2,1,0:T(8,128)(2,1)S(1)} %get-tuple-element.53.before_ref.fg_ref.after_ref, bf16[64,64,256]{2,1,0:T(8,128)(2,1)S(1)} %get-tuple-element.53.before_ref.fg_ref.after_ref, bf16[64,64,256]{2,1,0:T(8,128)(2,1)S(1)} %get-tuple-element.53.before_ref.fg_ref.after_ref, ...), custom_call_target="tpu_custom_call" | custom-call | flops 4000000000 | bytes 4194304 | tf_op jit(solution)/shard_map/spread_pass/pallas_call | solution.py:661
  55.4 0.0 collective-permute-done.14
  55.4 1.2 %collective-permute-done.13 = bf16[1,272,128]{2,1,0:T(8,128)(2,1)S(1)} collective-permute-done((bf16[1,272,128]{2,1,0:T(8,128)(2,1)S(1)}, bf16[1,272,128]{2,1,0:T(8,128)(2,1)S(1)}, u32[]{:S(2)}, u32[]{:S(2)}) %collective-permute-start.13) | collective-permute-done | bytes 69664 | tf_op jit(solution)/shard_map/ppermute | solution.py:728
  56.6 0.2 collective-permute-done.12
  56.9 3.4 %collective-permute-start.17 = (bf16[1,272,128]{2,1,0:T(8,128)(2,1)S(1)}, bf16[1,272,128]{2,1,0:T(8,128)(2,1)S(1)}, u32[]{:S(2)}, u32[]{:S(2)}) collective-permute-start(bf16[1,272,128]{2,1,0:T(8,128)(2,1)S(1)} %add_convert_fusion.1), channel_id=1, source_target_pairs={{0,65},{1,64},{2,67},{3,66},{4,69},{5,68},{6,71},{7,70},{8,56},{9,... | collective-permute-start | bytes 208904 | tf_op jit(solution)/shard_map/ppermute | solution.py:728
  60.2 0.0 collective-permute-start.16
  60.2 0.7 collective-permute-start.15
  60.9 2.2 %spread_pass.5.out_refs_0_ = f32[64,64,256]{2,1,0:T(8,128)} custom-call(bf16[64,64,256]{2,1,0:T(8,128)(2,1)S(1)} %get-tuple-element.53.before_ref.fg_ref.after_ref, bf16[64,64,256]{2,1,0:T(8,128)(2,1)S(1)} %get-tuple-element.53.before_ref.fg_ref.after_ref, ...), custom_call_target="tpu_custom_call", output_to_operand_aliasing={{}: (12, {})} | custom-call | flops 4000000000 | bytes 4194304 | tf_op jit(solution)/shard_map/spread_pass/pallas_call | solution.py:661
  63.1 0.0 collective-permute-done.17
  63.1 1.8 %collective-permute-done.16 = bf16[1,272,128]{2,1,0:T(8,128)(2,1)S(1)} collective-permute-done((bf16[1,272,128]{2,1,0:T(8,128)(2,1)S(1)}, bf16[1,272,128]{2,1,0:T(8,128)(2,1)S(1)}, u32[]{:S(2)}, u32[]{:S(2)}) %collective-permute-start.16) | collective-permute-done | bytes 69664 | tf_op jit(solution)/shard_map/ppermute | solution.py:728
  64.9 0.0 collective-permute-done.15
  65.0 2.2 %collective-permute-start.20 = (bf16[1,272,128]{2,1,0:T(8,128)(2,1)S(1)}, bf16[1,272,128]{2,1,0:T(8,128)(2,1)S(1)}, u32[]{:S(2)}, u32[]{:S(2)}) collective-permute-start(bf16[1,272,128]{2,1,0:T(8,128)(2,1)S(1)} %add_convert_fusion.refs_0_), channel_id=1, source_target_pairs={{0,48},{1,49},{2,50},{3,51},{4,52},{5,53},{6,54},{7,55},{8,14},{9,... | collective-permute-start | bytes 208904 | tf_op jit(solution)/shard_map/ppermute | solution.py:728
  67.2 0.5 collective-permute-start.19
  67.7 0.6 collective-permute-start.18
  68.3 0.0 collective-permute-done.6.north_ref
  68.3 0.0 collective-permute-done.7.south_ref
  68.3 2.1 %spread_pass.6.out_refs_0_ = f32[64,64,256]{2,1,0:T(8,128)} custom-call(bf16[64,64,256]{2,1,0:T(8,128)(2,1)S(1)} %get-tuple-element.53.before_ref.fg_ref.after_ref, bf16[64,64,256]{2,1,0:T(8,128)(2,1)S(1)} %get-tuple-element.53.before_ref.fg_ref.after_ref, ...), custom_call_target="tpu_custom_call", output_to_operand_aliasing={{}: (12, {})} | custom-call | flops 4000000000 | bytes 4194304 | tf_op jit(solution)/shard_map/spread_pass/pallas_call | solution.py:661
  70.4 0.0 collective-permute-done.20.refs_3_
  70.4 1.4 %collective-permute-done.19.refs_2_ = bf16[1,272,128]{2,1,0:T(8,128)(2,1)S(1)} collective-permute-done((bf16[1,272,128]{2,1,0:T(8,128)(2,1)S(1)}, bf16[1,272,128]{2,1,0:T(8,128)(2,1)S(1)}, u32[]{:S(2)}, u32[]{:S(2)}) %collective-permute-start.19) | collective-permute-done | bytes 69664 | tf_op jit(solution)/shard_map/ppermute | solution.py:728
  71.9 0.0 collective-permute-done.18.refs_1_
  71.9 5.7 %collective-permute-start.21 = (bf16[4,272,128]{2,1,0:T(8,128)(2,1)S(1)}, bf16[4,272,128]{2,1,0:T(8,128)(2,1)S(1)}, u32[]{:S(2)}, u32[]{:S(2)}) collective-permute-start(bf16[4,272,128]{2,1,0:T(8,128)(2,1)S(1)} %join.1.own_ref), channel_id=1, source_target_pairs={{0,8},{1,9},{2,10},{3,11},{4,12},{5,13},{6,14},{7,15},{8,0},{9,1},... | collective-permute-start | bytes 835592 | tf_op jit(solution)/shard_map/ppermute | solution.py:728
  77.6 2.1 %spread_pass.7 = f32[64,64,256]{2,1,0:T(8,128)} custom-call(bf16[64,64,256]{2,1,0:T(8,128)(2,1)S(1)} %get-tuple-element.53.before_ref.fg_ref.after_ref, bf16[64,64,256]{2,1,0:T(8,128)(2,1)S(1)} %get-tuple-element.53.before_ref.fg_ref.after_ref, ...), custom_call_target="tpu_custom_call", output_to_operand_aliasing={{}: (12, {})} | custom-call | flops 4000000000 | bytes 4194304 | tf_op jit(solution)/shard_map/spread_pass/pallas_call | solution.py:661
  79.8 0.0 collective-permute-done.21.other_ref
  79.8 1.7 %finish.1 = (f32[49,256]{1,0:T(8,128)}, f32[1,256]{1,0:T(1,128)}, f32[1,256]{1,0:T(1,128)}, f32[1,256]{1,0:T(1,128)}, f32[256,512]{1,0:T(8,128)}, /*index=5*/f32[1,512]{1,0:T(1,128)}, f32[512,256]{1,0:T(8,128)}) custom-call(s32[2]{0:T(128)S(1)} %pad_add_fusion.refs_0_.who_ref, bf16[4,272,128]{2,1,0:T(8,128)(2,1)S(1)} %join.1.own_ref, ...), custom_call_target="tpu_custom_call" | custom-call | tf_op jit(solution)/shard_map/finish/pallas_call | solution.py:639
  (29 shorter events, 0.3 us)
Async XLA Ops:
  0.6 7.5 %copy-start.4 = (bf16[1536,147]{1,0:T(8,128)(2,1)S(1)}, bf16[1536,147]{1,0:T(8,128)(2,1)}, u32[]{:S(2)}) copy-start(bf16[1536,147]{1,0:T(8,128)(2,1)} %constant.61.clone.basis_ref) | copy-start | bytes 1354756
  0.6 10.1 %copy-start = (bf16[64,64,256]{2,1,0:T(8,128)(2,1)S(1)}, bf16[64,64,256]{2,1,0:T(8,128)(2,1)}, u32[]{:S(2)}) copy-start(bf16[64,64,256]{2,1,0:T(8,128)(2,1)} %refs_3_.3) | copy-start | bytes 6291460
  0.7 7.4 %copy-start.5 = (s32[64,64]{1,0:T(8,128)S(1)}, s32[64,64]{1,0:T(8,128)}, u32[]{:S(2)}) copy-start(s32[64,64]{1,0:T(8,128)} %wet_ref.3) | copy-start | bytes 49156
  0.7 7.4 %copy-start.11 = (bf16[512]{0:T(512)(128)(2,1)S(1)}, bf16[512]{0:T(512)(128)(2,1)}, u32[]{:S(2)}) copy-start(bf16[512]{0:T(512)(128)(2,1)} %param.23) | copy-start | bytes 3076
  0.7 7.4 %copy-start.12 = (bf16[256]{0:T(256)(128)(2,1)S(1)}, bf16[256]{0:T(256)(128)(2,1)}, u32[]{:S(2)}) copy-start(bf16[256]{0:T(256)(128)(2,1)} %param.21) | copy-start | bytes 1540
  0.7 7.4 %copy-start.13 = (bf16[256]{0:T(256)(128)(2,1)S(1)}, bf16[256]{0:T(256)(128)(2,1)}, u32[]{:S(2)}) copy-start(bf16[256]{0:T(256)(128)(2,1)} %param.20) | copy-start | bytes 1540
  0.7 7.4 %copy-start.14 = (bf16[256]{0:T(256)(128)(2,1)S(1)}, bf16[256]{0:T(256)(128)(2,1)}, u32[]{:S(2)}) copy-start(bf16[256]{0:T(256)(128)(2,1)} %param.19) | copy-start | bytes 1540
  0.7 7.4 %copy-start.6 = (bf16[49,256]{1,0:T(8,128)(2,1)S(1)}, bf16[49,256]{1,0:T(8,128)(2,1)}, u32[]{:S(2)}) copy-start(bf16[49,256]{1,0:T(8,128)(2,1)} %kernel_ref.1) | copy-start | bytes 75268
  3.1 7.6 %collective-permute-start = (bf16[12,16,256]{2,1,0:T(8,128)(2,1)}, bf16[12,16,256]{2,1,0:T(8,128)(2,1)S(1)}, u32[]{:S(2)}, u32[]{:S(2)}) collective-permute-start(bf16[12,16,256]{2,1,0:T(8,128)(2,1)} %get-tuple-element.42), channel_id=1, source_target_pairs={{0,1},{1,2},{2,3},{3,4},{4,5},{5,6},{6,7},{7,0},{8,9},{9,10},{10,1... | collective-permute-start | bytes 294920 | tf_op jit(solution)/shard_map/ppermute | solution.py:693
  5.6 5.2 %collective-permute-start.1 = (bf16[12,16,256]{2,1,0:T(8,128)(2,1)}, bf16[12,16,256]{2,1,0:T(8,128)(2,1)S(1)}, u32[]{:S(2)}, u32[]{:S(2)}) collective-permute-start(bf16[12,16,256]{2,1,0:T(8,128)(2,1)} %get-tuple-element.43), channel_id=1, source_target_pairs={{0,7},{1,0},{2,1},{3,2},{4,3},{5,4},{6,5},{7,6},{8,15},{9,8},{10,9... | collective-permute-start | bytes 294920 | tf_op jit(solution)/shard_map/ppermute | solution.py:693
  10.8 3.6 %copy-start.1 = (bf16[64,64,256]{2,1,0:T(8,128)(2,1)S(1)}, bf16[64,64,256]{2,1,0:T(8,128)(2,1)}, u32[]{:S(2)}) copy-start(bf16[64,64,256]{2,1,0:T(8,128)(2,1)} %cot_ref.7) | copy-start | bytes 6291460
  10.8 3.6 %copy-start.2 = (bf16[512,512]{1,0:T(8,128)(2,1)S(1)}, bf16[512,512]{1,0:T(8,128)(2,1)}, u32[]{:S(2)}) copy-start(bf16[512,512]{1,0:T(8,128)(2,1)} %constant.62.clone.refs_10_.place_ref) | copy-start | bytes 1572868
  10.8 3.6 %copy-start.3 = (bf16[256,512]{1,0:T(8,128)(2,1)S(1)}, bf16[256,512]{1,0:T(8,128)(2,1)}, u32[]{:S(2)}) copy-start(bf16[256,512]{1,0:T(8,128)(2,1)} %constant.64.clone.refs_12_.back_ref) | copy-start | bytes 786436
  10.8 3.6 %copy-start.7 = (bf16[256,512]{1,0:T(8,128)(2,1)S(1)}, bf16[256,512]{1,0:T(8,128)(2,1)}, u32[]{:S(2)}) copy-start(bf16[256,512]{1,0:T(8,128)(2,1)} %refs_16_.3) | copy-start | bytes 786436
  10.8 3.6 %copy-start.8 = (bf16[512,256]{1,0:T(8,128)(2,1)S(1)}, bf16[512,256]{1,0:T(8,128)(2,1)}, u32[]{:S(2)}) copy-start(bf16[512,256]{1,0:T(8,128)(2,1)} %refs_17_.3) | copy-start | bytes 786436
  10.8 3.6 %copy-start.9 = (bf16[512,256]{1,0:T(8,128)(2,1)S(1)}, bf16[512,256]{1,0:T(8,128)(2,1)}, u32[]{:S(2)}) copy-start(bf16[512,256]{1,0:T(8,128)(2,1)} %constant.63.clone.refs_11_) | copy-start | bytes 786436
  10.8 3.6 %copy-start.10 = (f32[49,768]{1,0:T(8,128)S(1)}, f32[49,768]{1,0:T(8,128)}, u32[]{:S(2)}) copy-start(f32[49,768]{1,0:T(8,128)} %constant.65.clone.refs_14_) | copy-start | bytes 451588
  10.9 13.4 %collective-permute-start.2 = (bf16[3,96,256]{2,1,0:T(8,128)(2,1)S(1)}, bf16[3,96,256]{2,1,0:T(8,128)(2,1)S(1)}, u32[]{:S(2)}, u32[]{:S(2)}) collective-permute-start(bf16[3,96,256]{2,1,0:T(8,128)(2,1)S(1)} %get-tuple-element.45), channel_id=1, source_target_pairs={{0,8},{8,16},{16,24},{24,32},{32,40},{40,48},{48,56},{56,64},{64,7... | collective-permute-start | bytes 442376 | tf_op jit(solution)/shard_map/ppermute | solution.py:697
  14.4 9.9 %collective-permute-start.3 = (bf16[3,96,256]{2,1,0:T(8,128)(2,1)S(1)}, bf16[3,96,256]{2,1,0:T(8,128)(2,1)S(1)}, u32[]{:S(2)}, u32[]{:S(2)}) collective-permute-start(bf16[3,96,256]{2,1,0:T(8,128)(2,1)S(1)} %get-tuple-element.46), channel_id=1, source_target_pairs={{0,120},{8,0},{16,8},{24,16},{32,24},{40,32},{48,40},{56,48},{64,5... | collective-permute-start | bytes 442376 | tf_op jit(solution)/shard_map/ppermute | solution.py:697
  34.7 7.9 %collective-permute-start.8 = (f32[4,272,128]{2,1,0:T(8,128)S(1)}, f32[4,272,128]{2,1,0:T(8,128)S(1)}, u32[]{:S(2)}, u32[]{:S(2)}) collective-permute-start(f32[4,272,128]{2,1,0:T(8,128)S(1)} %get-tuple-element.62), channel_id=1, source_target_pairs={{0,8},{1,9},{2,10},{3,11},{4,12},{5,13},{6,14},{7,15},{8,0},{9,1},... | collective-permute-start | bytes 1671176 | tf_op jit(solution)/shard_map/ppermute | solution.py:728
  39.1 7.6 %collective-permute-start.4 = (bf16[12,16,256]{2,1,0:T(8,128)(2,1)S(1)}, bf16[12,16,256]{2,1,0:T(8,128)(2,1)S(1)}, u32[]{:S(2)}, u32[]{:S(2)}) collective-permute-start(bf16[12,16,256]{2,1,0:T(8,128)(2,1)S(1)} %get-tuple-element.56), channel_id=1, source_target_pairs={{0,1},{1,2},{2,3},{3,4},{4,5},{5,6},{6,7},{7,0},{8,9},{9,10},{10,1... | collective-permute-start | bytes 294920 | tf_op jit(solution)/shard_map/ppermute | solution.py:693
  39.2 7.5 %collective-permute-start.5 = (bf16[12,16,256]{2,1,0:T(8,128)(2,1)S(1)}, bf16[12,16,256]{2,1,0:T(8,128)(2,1)S(1)}, u32[]{:S(2)}, u32[]{:S(2)}) collective-permute-start(bf16[12,16,256]{2,1,0:T(8,128)(2,1)S(1)} %get-tuple-element.57), channel_id=1, source_target_pairs={{0,7},{1,0},{2,1},{3,2},{4,3},{5,4},{6,5},{7,6},{8,15},{9,8},{10,9... | collective-permute-start | bytes 294920 | tf_op jit(solution)/shard_map/ppermute | solution.py:693
  42.7 5.8 %collective-permute-start.9 = (bf16[1,272,128]{2,1,0:T(8,128)(2,1)S(1)}, bf16[1,272,128]{2,1,0:T(8,128)(2,1)S(1)}, u32[]{:S(2)}, u32[]{:S(2)}) collective-permute-start(bf16[1,272,128]{2,1,0:T(8,128)(2,1)S(1)} %get-tuple-element.64), channel_id=1, source_target_pairs={{0,16},{1,17},{2,18},{3,19},{4,20},{5,21},{6,22},{7,23},{8,10},{9,... | collective-permute-start | bytes 208904 | tf_op jit(solution)/shard_map/ppermute | solution.py:728
  42.8 5.7 %collective-permute-start.10 = (bf16[1,272,128]{2,1,0:T(8,128)(2,1)S(1)}, bf16[1,272,128]{2,1,0:T(8,128)(2,1)S(1)}, u32[]{:S(2)}, u32[]{:S(2)}) collective-permute-start(bf16[1,272,128]{2,1,0:T(8,128)(2,1)S(1)} %get-tuple-element.65), channel_id=1, source_target_pairs={{0,32},{1,33},{2,34},{3,35},{4,36},{5,37},{6,38},{7,39},{8,12},{9,... | collective-permute-start | bytes 208904 | tf_op jit(solution)/shard_map/ppermute | solution.py:728
  45.1 4.4 %collective-permute-start.11 = (bf16[1,272,128]{2,1,0:T(8,128)(2,1)S(1)}, bf16[1,272,128]{2,1,0:T(8,128)(2,1)S(1)}, u32[]{:S(2)}, u32[]{:S(2)}) collective-permute-start(bf16[1,272,128]{2,1,0:T(8,128)(2,1)S(1)} %get-tuple-element.66), channel_id=1, source_target_pairs={{0,48},{1,49},{2,50},{3,51},{4,52},{5,53},{6,54},{7,55},{8,14},{9,... | collective-permute-start | bytes 208904 | tf_op jit(solution)/shard_map/ppermute | solution.py:728
  46.7 21.6 %collective-permute-start.6 = (bf16[3,96,256]{2,1,0:T(8,128)(2,1)S(1)}, bf16[3,96,256]{2,1,0:T(8,128)(2,1)S(1)}, u32[]{:S(2)}, u32[]{:S(2)}) collective-permute-start(bf16[3,96,256]{2,1,0:T(8,128)(2,1)S(1)} %get-tuple-element.58), channel_id=1, source_target_pairs={{0,8},{8,16},{16,24},{24,32},{32,40},{40,48},{48,56},{56,64},{64,7... | collective-permute-start | bytes 442376 | tf_op jit(solution)/shard_map/ppermute | solution.py:697
  46.9 21.4 %collective-permute-start.7 = (bf16[3,96,256]{2,1,0:T(8,128)(2,1)S(1)}, bf16[3,96,256]{2,1,0:T(8,128)(2,1)S(1)}, u32[]{:S(2)}, u32[]{:S(2)}) collective-permute-start(bf16[3,96,256]{2,1,0:T(8,128)(2,1)S(1)} %get-tuple-element.59), channel_id=1, source_target_pairs={{0,120},{8,0},{16,8},{24,16},{32,24},{40,32},{48,40},{56,48},{64,5... | collective-permute-start | bytes 442376 | tf_op jit(solution)/shard_map/ppermute | solution.py:697
  49.5 5.8 %collective-permute-start.14 = (bf16[1,272,128]{2,1,0:T(8,128)(2,1)S(1)}, bf16[1,272,128]{2,1,0:T(8,128)(2,1)S(1)}, u32[]{:S(2)}, u32[]{:S(2)}) collective-permute-start(bf16[1,272,128]{2,1,0:T(8,128)(2,1)S(1)} %add_convert_fusion.2), channel_id=1, source_target_pairs={{0,6},{1,7},{2,4},{3,5},{4,2},{5,3},{6,0},{7,1},{8,73},{9,72},{10,... | collective-permute-start | bytes 208904 | tf_op jit(solution)/shard_map/ppermute | solution.py:728
  51.5 5.2 %collective-permute-start.13 = (bf16[1,272,128]{2,1,0:T(8,128)(2,1)S(1)}, bf16[1,272,128]{2,1,0:T(8,128)(2,1)S(1)}, u32[]{:S(2)}, u32[]{:S(2)}) collective-permute-start(bf16[1,272,128]{2,1,0:T(8,128)(2,1)S(1)} %add_convert_fusion.2), channel_id=1, source_target_pairs={{0,4},{1,5},{2,6},{3,7},{4,0},{5,1},{6,2},{7,3},{8,72},{9,73},{10,... | collective-permute-start | bytes 208904 | tf_op jit(solution)/shard_map/ppermute | solution.py:728
  53.2 3.6 %collective-permute-start.12 = (bf16[1,272,128]{2,1,0:T(8,128)(2,1)S(1)}, bf16[1,272,128]{2,1,0:T(8,128)(2,1)S(1)}, u32[]{:S(2)}, u32[]{:S(2)}) collective-permute-start(bf16[1,272,128]{2,1,0:T(8,128)(2,1)S(1)} %add_convert_fusion.2), channel_id=1, source_target_pairs={{0,2},{1,3},{2,0},{3,1},{4,6},{5,7},{6,4},{7,5},{8,9},{9,8},{10,11... | collective-permute-start | bytes 208904 | tf_op jit(solution)/shard_map/ppermute | solution.py:728
  56.9 6.2 %collective-permute-start.17 = (bf16[1,272,128]{2,1,0:T(8,128)(2,1)S(1)}, bf16[1,272,128]{2,1,0:T(8,128)(2,1)S(1)}, u32[]{:S(2)}, u32[]{:S(2)}) collective-permute-start(bf16[1,272,128]{2,1,0:T(8,128)(2,1)S(1)} %add_convert_fusion.1), channel_id=1, source_target_pairs={{0,65},{1,64},{2,67},{3,66},{4,69},{5,68},{6,71},{7,70},{8,56},{9,... | collective-permute-start | bytes 208904 | tf_op jit(solution)/shard_map/ppermute | solution.py:728
  60.2 4.7 %collective-permute-start.16 = (bf16[1,272,128]{2,1,0:T(8,128)(2,1)S(1)}, bf16[1,272,128]{2,1,0:T(8,128)(2,1)S(1)}, u32[]{:S(2)}, u32[]{:S(2)}) collective-permute-start(bf16[1,272,128]{2,1,0:T(8,128)(2,1)S(1)} %add_convert_fusion.1), channel_id=1, source_target_pairs={{0,64},{1,65},{2,66},{3,67},{4,68},{5,69},{6,70},{7,71},{8,40},{9,... | collective-permute-start | bytes 208904 | tf_op jit(solution)/shard_map/ppermute | solution.py:728
  60.2 4.7 %collective-permute-start.15 = (bf16[1,272,128]{2,1,0:T(8,128)(2,1)S(1)}, bf16[1,272,128]{2,1,0:T(8,128)(2,1)S(1)}, u32[]{:S(2)}, u32[]{:S(2)}) collective-permute-start(bf16[1,272,128]{2,1,0:T(8,128)(2,1)S(1)} %add_convert_fusion.1), channel_id=1, source_target_pairs={{0,1},{1,0},{2,3},{3,2},{4,5},{5,4},{6,7},{7,6},{8,24},{9,25},{10,... | collective-permute-start | bytes 208904 | tf_op jit(solution)/shard_map/ppermute | solution.py:728
  65.0 5.5 %collective-permute-start.20 = (bf16[1,272,128]{2,1,0:T(8,128)(2,1)S(1)}, bf16[1,272,128]{2,1,0:T(8,128)(2,1)S(1)}, u32[]{:S(2)}, u32[]{:S(2)}) collective-permute-start(bf16[1,272,128]{2,1,0:T(8,128)(2,1)S(1)} %add_convert_fusion.refs_0_), channel_id=1, source_target_pairs={{0,48},{1,49},{2,50},{3,51},{4,52},{5,53},{6,54},{7,55},{8,14},{9,... | collective-permute-start | bytes 208904 | tf_op jit(solution)/shard_map/ppermute | solution.py:728
  67.2 4.7 %collective-permute-start.19 = (bf16[1,272,128]{2,1,0:T(8,128)(2,1)S(1)}, bf16[1,272,128]{2,1,0:T(8,128)(2,1)S(1)}, u32[]{:S(2)}, u32[]{:S(2)}) collective-permute-start(bf16[1,272,128]{2,1,0:T(8,128)(2,1)S(1)} %add_convert_fusion.refs_0_), channel_id=1, source_target_pairs={{0,32},{1,33},{2,34},{3,35},{4,36},{5,37},{6,38},{7,39},{8,12},{9,... | collective-permute-start | bytes 208904 | tf_op jit(solution)/shard_map/ppermute | solution.py:728
  67.7 4.2 %collective-permute-start.18 = (bf16[1,272,128]{2,1,0:T(8,128)(2,1)S(1)}, bf16[1,272,128]{2,1,0:T(8,128)(2,1)S(1)}, u32[]{:S(2)}, u32[]{:S(2)}) collective-permute-start(bf16[1,272,128]{2,1,0:T(8,128)(2,1)S(1)} %add_convert_fusion.refs_0_), channel_id=1, source_target_pairs={{0,16},{1,17},{2,18},{3,19},{4,20},{5,21},{6,22},{7,23},{8,10},{9,... | collective-permute-start | bytes 208904 | tf_op jit(solution)/shard_map/ppermute | solution.py:728
  71.9 7.9 %collective-permute-start.21 = (bf16[4,272,128]{2,1,0:T(8,128)(2,1)S(1)}, bf16[4,272,128]{2,1,0:T(8,128)(2,1)S(1)}, u32[]{:S(2)}, u32[]{:S(2)}) collective-permute-start(bf16[4,272,128]{2,1,0:T(8,128)(2,1)S(1)} %join.1.own_ref), channel_id=1, source_target_pairs={{0,8},{1,9},{2,10},{3,11},{4,12},{5,13},{6,14},{7,15},{8,0},{9,1},... | collective-permute-start | bytes 835592 | tf_op jit(solution)/shard_map/ppermute | solution.py:728

commit v11 on v10

--- a/solution.py
+++ b/solution.py
@@ -18,8 +18,8 @@
 BLOCKS = 8
 LANES = 128
 CELLS = TILE * TILE
-VMEM_BYTES = 32 * 2**20
-SPREAD_BYTES = 24 * 2**20
+VMEM_BYTES = 24 * 2**20
+SPREAD_BYTES = 16 * 2**20
 SMALL_BYTES = 12 * 2**20
 LARGE_BYTES = 56 * 2**20
 

time: 81.6 us -> 81.6 us (level)
  no operation moved by 1% of the time
where the time goes in v11:
time: 81.6 us; the launch traced here: 81.4 us
  starting transfers between devices  38.9 us (48%)
  Pallas kernels  33.6 us (41%)
  waiting for transfers between devices  7.72 us (9%)
  between operations  0.93 us (1%)
    ppermute x14, starting transfers between devices, move(): return lax.ppermute(x, AXES, swapped(mesh_shape, stage, step))  25.1 us
    pallas_call x2, Pallas kernels, cell_pass(): pl.pallas_call(functools.partial(cell_kernel, at_ends, rows), grid=(2,),...  20.2 us
    pallas_call x4, Pallas kernels, spread_pass(): pl.pallas_call(functools.partial(spread_kernel, at, rows), grid=(1,), in_...  8.6 us
    ppermute x2, starting transfers between devices, across_lat(): lax.ppermute(west, 'gy', ring('gy', -1))  5.92 us
    ppermute x14, waiting for transfers between devices, move(): return lax.ppermute(x, AXES, swapped(mesh_shape, stage, step))  5.7 us
    ppermute x2, starting transfers between devices, across_lon(): lax.ppermute(south, 'gx', ring('gx', 1))  3.71 us
    ppermute x2, starting transfers between devices, across_lat(): lax.ppermute(east, 'gy', ring('gy', 1))  2.58 us
    pallas_call x1, Pallas kernels, sides(): pl.pallas_call(side_kernel, grid=(1,), in_specs=[pl.BlockSpec((lon, TILE,...  2.41 us
  transfers between devices with their start and end apart: 22, of which 6 were waited for; matrix products, arithmetic and copies ran while one was open for 0% of the time, Pallas kernels for 23%

profile of v11, /device:TPU:1, one launch (start us, length us, event | category | flops | bytes accessed | tf_op | source)
XLA Modules:
  0.0 81.4 jit_solution(12044312519457672506)
XLA Ops:
  0.6 0.0 copy-start.4
  0.7 2.4 %sides.1 = (bf16[12,16,256]{2,1,0:T(8,128)(2,1)}, bf16[12,16,256]{2,1,0:T(8,128)(2,1)}) custom-call(bf16[64,64,256]{2,1,0:T(8,128)(2,1)} %refs_3_.3, bf16[64,64,256]{2,1,0:T(8,128)(2,1)} %refs_3_.3, s32[64,64]{1,0:T(8,128)} %wet_ref.3), custom_call_target="tpu_custom_call" | custom-call | tf_op jit(solution)/shard_map/sides/pallas_call | solution.py:512
  3.1 2.5 %collective-permute-start = (bf16[12,16,256]{2,1,0:T(8,128)(2,1)}, bf16[12,16,256]{2,1,0:T(8,128)(2,1)S(1)}, u32[]{:S(2)}, u32[]{:S(2)}) collective-permute-start(bf16[12,16,256]{2,1,0:T(8,128)(2,1)} %get-tuple-element.42), channel_id=1, source_target_pairs={{0,1},{1,2},{2,3},{3,4},{4,5},{5,6},{6,7},{7,0},{8,9},{9,10},{10,1... | collective-permute-start | bytes 294920 | tf_op jit(solution)/shard_map/ppermute | solution.py:693
  5.6 2.5 %collective-permute-start.1 = (bf16[12,16,256]{2,1,0:T(8,128)(2,1)}, bf16[12,16,256]{2,1,0:T(8,128)(2,1)S(1)}, u32[]{:S(2)}, u32[]{:S(2)}) collective-permute-start(bf16[12,16,256]{2,1,0:T(8,128)(2,1)} %get-tuple-element.43), channel_id=1, source_target_pairs={{0,7},{1,0},{2,1},{3,2},{4,3},{5,4},{6,5},{7,6},{8,15},{9,8},{10,9... | collective-permute-start | bytes 294920 | tf_op jit(solution)/shard_map/ppermute | solution.py:693
  8.1 0.0 copy-done.13
  8.1 0.6 prepare.1
  8.7 0.1 pad_add_fusion.refs_0_.who_ref
  8.8 2.0 %collective-permute-done.refs_2_.refs_7_ = bf16[12,16,256]{2,1,0:T(8,128)(2,1)S(1)} collective-permute-done((bf16[12,16,256]{2,1,0:T(8,128)(2,1)}, bf16[12,16,256]{2,1,0:T(8,128)(2,1)S(1)}, u32[]{:S(2)}, u32[]{:S(2)}) %collective-permute-start) | collective-permute-done | bytes 98336 | tf_op jit(solution)/shard_map/ppermute | solution.py:693
  10.8 0.0 collective-permute-done.1.refs_3_.refs_8_
  10.8 0.0 copy-done
  10.8 0.0 copy-start.2
  10.8 0.0 copy-start.3
  10.8 0.0 copy-start.7
  10.8 0.0 copy-start.8
  10.8 0.0 copy-start.9
  10.8 0.0 copy-start.10
  10.9 3.5 %collective-permute-start.2 = (bf16[3,96,256]{2,1,0:T(8,128)(2,1)S(1)}, bf16[3,96,256]{2,1,0:T(8,128)(2,1)S(1)}, u32[]{:S(2)}, u32[]{:S(2)}) collective-permute-start(bf16[3,96,256]{2,1,0:T(8,128)(2,1)S(1)} %get-tuple-element.45), channel_id=1, source_target_pairs={{0,8},{8,16},{16,24},{24,32},{32,40},{40,48},{48,56},{56,64},{64,7... | collective-permute-start | bytes 442376 | tf_op jit(solution)/shard_map/ppermute | solution.py:697
  14.4 0.0 collective-permute-start.3
  14.5 9.8 %inner_cells.1 = (bf16[64,64,256]{2,1,0:T(8,128)(2,1)S(1)}, bf16[12,16,256]{2,1,0:T(8,128)(2,1)S(1)}, bf16[12,16,256]{2,1,0:T(8,128)(2,1)S(1)}, f32[2176,128]{1,...) custom-call(s32[2]{0:T(128)S(1)} %pad_add_fusion.refs_0_.who_ref, bf16[64,64,256]{2,1,0:T(8,128)(2,1)S(1)} %copy-done, ...), custom_call_target="tpu_custom_call" | custom-call | flops 10000000000 | bytes 8388608 | tf_op jit(solution)/shard_map/inner_cells/pallas_call | solution.py:598
  24.2 0.0 collective-permute-done.2.refs_18_
  24.3 0.0 collective-permute-done.3.refs_19_
  24.3 10.5 %end_cells.1 = (bf16[64,64,256]{2,1,0:T(8,128)(2,1)S(1)}, bf16[12,16,256]{2,1,0:T(8,128)(2,1)S(1)}, bf16[12,16,256]{2,1,0:T(8,128)(2,1)S(1)}, f32[4,272,128]{2,1...) custom-call(s32[2]{0:T(128)S(1)} %pad_add_fusion.refs_0_.who_ref, ...), custom_call_target="tpu_custom_call", output_to_operand_aliasing={{0}: (20, {}), {1}: (21, {}), {2}: (22, {})} | custom-call | flops 10000000000 | bytes 8388608 | tf_op jit(solution)/shard_map/end_cells/pallas_call | solution.py:598
  34.7 4.3 %collective-permute-start.8 = (f32[4,272,128]{2,1,0:T(8,128)S(1)}, f32[4,272,128]{2,1,0:T(8,128)S(1)}, u32[]{:S(2)}, u32[]{:S(2)}) collective-permute-start(f32[4,272,128]{2,1,0:T(8,128)S(1)} %get-tuple-element.62), channel_id=1, source_target_pairs={{0,8},{1,9},{2,10},{3,11},{4,12},{5,13},{6,14},{7,15},{8,0},{9,1},... | collective-permute-start | bytes 1671176 | tf_op jit(solution)/shard_map/ppermute | solution.py:728
  39.1 0.1 collective-permute-start.4
  39.2 3.5 %collective-permute-start.5 = (bf16[12,16,256]{2,1,0:T(8,128)(2,1)S(1)}, bf16[12,16,256]{2,1,0:T(8,128)(2,1)S(1)}, u32[]{:S(2)}, u32[]{:S(2)}) collective-permute-start(bf16[12,16,256]{2,1,0:T(8,128)(2,1)S(1)} %get-tuple-element.57), channel_id=1, source_target_pairs={{0,7},{1,0},{2,1},{3,2},{4,3},{5,4},{6,5},{7,6},{8,15},{9,8},{10,9... | collective-permute-start | bytes 294920 | tf_op jit(solution)/shard_map/ppermute | solution.py:693
  42.6 0.0 collective-permute-done.8.come_ref
  42.6 0.1 fold.1
  42.7 0.1 collective-permute-start.9
  42.8 2.3 %collective-permute-start.10 = (bf16[1,272,128]{2,1,0:T(8,128)(2,1)S(1)}, bf16[1,272,128]{2,1,0:T(8,128)(2,1)S(1)}, u32[]{:S(2)}, u32[]{:S(2)}) collective-permute-start(bf16[1,272,128]{2,1,0:T(8,128)(2,1)S(1)} %get-tuple-element.65), channel_id=1, source_target_pairs={{0,32},{1,33},{2,34},{3,35},{4,36},{5,37},{6,38},{7,39},{8,12},{9,... | collective-permute-start | bytes 208904 | tf_op jit(solution)/shard_map/ppermute | solution.py:728
  45.1 1.5 %collective-permute-start.11 = (bf16[1,272,128]{2,1,0:T(8,128)(2,1)S(1)}, bf16[1,272,128]{2,1,0:T(8,128)(2,1)S(1)}, u32[]{:S(2)}, u32[]{:S(2)}) collective-permute-start(bf16[1,272,128]{2,1,0:T(8,128)(2,1)S(1)} %get-tuple-element.66), channel_id=1, source_target_pairs={{0,48},{1,49},{2,50},{3,51},{4,52},{5,53},{6,54},{7,55},{8,14},{9,... | collective-permute-start | bytes 208904 | tf_op jit(solution)/shard_map/ppermute | solution.py:728
  46.6 0.0 collective-permute-done.4.refs_0_.north_ref.west_ref
  46.6 0.0 collective-permute-done.5.refs_1_.south_ref.east_ref
  46.7 0.2 collective-permute-start.6
  46.9 1.6 %collective-permute-start.7 = (bf16[3,96,256]{2,1,0:T(8,128)(2,1)S(1)}, bf16[3,96,256]{2,1,0:T(8,128)(2,1)S(1)}, u32[]{:S(2)}, u32[]{:S(2)}) collective-permute-start(bf16[3,96,256]{2,1,0:T(8,128)(2,1)S(1)} %get-tuple-element.59), channel_id=1, source_target_pairs={{0,120},{8,0},{16,8},{24,16},{32,24},{40,32},{48,40},{56,48},{64,5... | collective-permute-start | bytes 442376 | tf_op jit(solution)/shard_map/ppermute | solution.py:697
  48.5 0.0 collective-permute-done.9
  48.5 0.0 collective-permute-done.10
  48.5 1.0 %collective-permute-done.11 = bf16[1,272,128]{2,1,0:T(8,128)(2,1)S(1)} collective-permute-done((bf16[1,272,128]{2,1,0:T(8,128)(2,1)S(1)}, bf16[1,272,128]{2,1,0:T(8,128)(2,1)S(1)}, u32[]{:S(2)}, u32[]{:S(2)}) %collective-permute-start.11) | collective-permute-done | bytes 69664 | tf_op jit(solution)/shard_map/ppermute | solution.py:728
  49.5 1.9 %collective-permute-start.14 = (bf16[1,272,128]{2,1,0:T(8,128)(2,1)S(1)}, bf16[1,272,128]{2,1,0:T(8,128)(2,1)S(1)}, u32[]{:S(2)}, u32[]{:S(2)}) collective-permute-start(bf16[1,272,128]{2,1,0:T(8,128)(2,1)S(1)} %add_convert_fusion.2), channel_id=1, source_target_pairs={{0,6},{1,7},{2,4},{3,5},{4,2},{5,3},{6,0},{7,1},{8,73},{9,72},{10,... | collective-permute-start | bytes 208904 | tf_op jit(solution)/shard_map/ppermute | solution.py:728
  51.5 1.8 %collective-permute-start.13 = (bf16[1,272,128]{2,1,0:T(8,128)(2,1)S(1)}, bf16[1,272,128]{2,1,0:T(8,128)(2,1)S(1)}, u32[]{:S(2)}, u32[]{:S(2)}) collective-permute-start(bf16[1,272,128]{2,1,0:T(8,128)(2,1)S(1)} %add_convert_fusion.2), channel_id=1, source_target_pairs={{0,4},{1,5},{2,6},{3,7},{4,0},{5,1},{6,2},{7,3},{8,72},{9,73},{10,... | collective-permute-start | bytes 208904 | tf_op jit(solution)/shard_map/ppermute | solution.py:728
  53.2 0.0 collective-permute-start.12
  53.2 2.2 %spread_pass.4.out_refs_0_ = f32[64,64,256]{2,1,0:T(8,128)} custom-call(bf16[64,64,256]{2,1,0:T(8,128)(2,1)S(1)} %get-tuple-element.53.before_ref.fg_ref.after_ref, bf16[64,64,256]{2,1,0:T(8,128)(2,1)S(1)} %get-tuple-element.53.before_ref.fg_ref.after_ref, bf16[64,64,256]{2,1,0:T(8,128)(2,1)S(1)} %get-tuple-element.53.before_ref.fg_ref.after_ref, ...), custom_call_target="tpu_custom_call" | custom-call | flops 4000000000 | bytes 4194304 | tf_op jit(solution)/shard_map/spread_pass/pallas_call | solution.py:661
  55.4 0.0 collective-permute-done.14
  55.4 1.2 %collective-permute-done.13 = bf16[1,272,128]{2,1,0:T(8,128)(2,1)S(1)} collective-permute-done((bf16[1,272,128]{2,1,0:T(8,128)(2,1)S(1)}, bf16[1,272,128]{2,1,0:T(8,128)(2,1)S(1)}, u32[]{:S(2)}, u32[]{:S(2)}) %collective-permute-start.13) | collective-permute-done | bytes 69664 | tf_op jit(solution)/shard_map/ppermute | solution.py:728
  56.6 0.2 collective-permute-done.12
  56.9 3.4 %collective-permute-start.17 = (bf16[1,272,128]{2,1,0:T(8,128)(2,1)S(1)}, bf16[1,272,128]{2,1,0:T(8,128)(2,1)S(1)}, u32[]{:S(2)}, u32[]{:S(2)}) collective-permute-start(bf16[1,272,128]{2,1,0:T(8,128)(2,1)S(1)} %add_convert_fusion.1), channel_id=1, source_target_pairs={{0,65},{1,64},{2,67},{3,66},{4,69},{5,68},{6,71},{7,70},{8,56},{9,... | collective-permute-start | bytes 208904 | tf_op jit(solution)/shard_map/ppermute | solution.py:728
  60.2 0.0 collective-permute-start.16
  60.2 0.7 collective-permute-start.15
  60.9 2.2 %spread_pass.5.out_refs_0_ = f32[64,64,256]{2,1,0:T(8,128)} custom-call(bf16[64,64,256]{2,1,0:T(8,128)(2,1)S(1)} %get-tuple-element.53.before_ref.fg_ref.after_ref, bf16[64,64,256]{2,1,0:T(8,128)(2,1)S(1)} %get-tuple-element.53.before_ref.fg_ref.after_ref, ...), custom_call_target="tpu_custom_call", output_to_operand_aliasing={{}: (12, {})} | custom-call | flops 4000000000 | bytes 4194304 | tf_op jit(solution)/shard_map/spread_pass/pallas_call | solution.py:661
  63.1 0.0 collective-permute-done.17
  63.1 1.8 %collective-permute-done.16 = bf16[1,272,128]{2,1,0:T(8,128)(2,1)S(1)} collective-permute-done((bf16[1,272,128]{2,1,0:T(8,128)(2,1)S(1)}, bf16[1,272,128]{2,1,0:T(8,128)(2,1)S(1)}, u32[]{:S(2)}, u32[]{:S(2)}) %collective-permute-start.16) | collective-permute-done | bytes 69664 | tf_op jit(solution)/shard_map/ppermute | solution.py:728
  64.9 0.0 collective-permute-done.15
  65.0 2.2 %collective-permute-start.20 = (bf16[1,272,128]{2,1,0:T(8,128)(2,1)S(1)}, bf16[1,272,128]{2,1,0:T(8,128)(2,1)S(1)}, u32[]{:S(2)}, u32[]{:S(2)}) collective-permute-start(bf16[1,272,128]{2,1,0:T(8,128)(2,1)S(1)} %add_convert_fusion.refs_0_), channel_id=1, source_target_pairs={{0,48},{1,49},{2,50},{3,51},{4,52},{5,53},{6,54},{7,55},{8,14},{9,... | collective-permute-start | bytes 208904 | tf_op jit(solution)/shard_map/ppermute | solution.py:728
  67.2 0.5 collective-permute-start.19
  67.7 0.6 collective-permute-start.18
  68.3 0.0 collective-permute-done.6.north_ref
  68.3 0.0 collective-permute-done.7.south_ref
  68.3 2.1 %spread_pass.6.out_refs_0_ = f32[64,64,256]{2,1,0:T(8,128)} custom-call(bf16[64,64,256]{2,1,0:T(8,128)(2,1)S(1)} %get-tuple-element.53.before_ref.fg_ref.after_ref, bf16[64,64,256]{2,1,0:T(8,128)(2,1)S(1)} %get-tuple-element.53.before_ref.fg_ref.after_ref, ...), custom_call_target="tpu_custom_call", output_to_operand_aliasing={{}: (12, {})} | custom-call | flops 4000000000 | bytes 4194304 | tf_op jit(solution)/shard_map/spread_pass/pallas_call | solution.py:661
  70.4 0.0 collective-permute-done.20.refs_3_
  70.4 1.4 %collective-permute-done.19.refs_2_ = bf16[1,272,128]{2,1,0:T(8,128)(2,1)S(1)} collective-permute-done((bf16[1,272,128]{2,1,0:T(8,128)(2,1)S(1)}, bf16[1,272,128]{2,1,0:T(8,128)(2,1)S(1)}, u32[]{:S(2)}, u32[]{:S(2)}) %collective-permute-start.19) | collective-permute-done | bytes 69664 | tf_op jit(solution)/shard_map/ppermute | solution.py:728
  71.9 0.0 collective-permute-done.18.refs_1_
  71.9 5.7 %collective-permute-start.21 = (bf16[4,272,128]{2,1,0:T(8,128)(2,1)S(1)}, bf16[4,272,128]{2,1,0:T(8,128)(2,1)S(1)}, u32[]{:S(2)}, u32[]{:S(2)}) collective-permute-start(bf16[4,272,128]{2,1,0:T(8,128)(2,1)S(1)} %join.1.own_ref), channel_id=1, source_target_pairs={{0,8},{1,9},{2,10},{3,11},{4,12},{5,13},{6,14},{7,15},{8,0},{9,1},... | collective-permute-start | bytes 835592 | tf_op jit(solution)/shard_map/ppermute | solution.py:728
  77.6 2.1 %spread_pass.7 = f32[64,64,256]{2,1,0:T(8,128)} custom-call(bf16[64,64,256]{2,1,0:T(8,128)(2,1)S(1)} %get-tuple-element.53.before_ref.fg_ref.after_ref, bf16[64,64,256]{2,1,0:T(8,128)(2,1)S(1)} %get-tuple-element.53.before_ref.fg_ref.after_ref, ...), custom_call_target="tpu_custom_call", output_to_operand_aliasing={{}: (12, {})} | custom-call | flops 4000000000 | bytes 4194304 | tf_op jit(solution)/shard_map/spread_pass/pallas_call | solution.py:661
  79.8 0.0 collective-permute-done.21.other_ref
  79.8 1.7 %finish.1 = (f32[49,256]{1,0:T(8,128)}, f32[1,256]{1,0:T(1,128)}, f32[1,256]{1,0:T(1,128)}, f32[1,256]{1,0:T(1,128)}, f32[256,512]{1,0:T(8,128)}, /*index=5*/f32[1,512]{1,0:T(1,128)}, f32[512,256]{1,0:T(8,128)}) custom-call(s32[2]{0:T(128)S(1)} %pad_add_fusion.refs_0_.who_ref, bf16[4,272,128]{2,1,0:T(8,128)(2,1)S(1)} %join.1.own_ref, ...), custom_call_target="tpu_custom_call" | custom-call | tf_op jit(solution)/shard_map/finish/pallas_call | solution.py:639
  (29 shorter events, 0.3 us)
Async XLA Ops:
  0.6 7.5 %copy-start.4 = (bf16[1536,147]{1,0:T(8,128)(2,1)S(1)}, bf16[1536,147]{1,0:T(8,128)(2,1)}, u32[]{:S(2)}) copy-start(bf16[1536,147]{1,0:T(8,128)(2,1)} %constant.61.clone.basis_ref) | copy-start | bytes 1354756
  0.6 10.1 %copy-start = (bf16[64,64,256]{2,1,0:T(8,128)(2,1)S(1)}, bf16[64,64,256]{2,1,0:T(8,128)(2,1)}, u32[]{:S(2)}) copy-start(bf16[64,64,256]{2,1,0:T(8,128)(2,1)} %refs_3_.3) | copy-start | bytes 6291460
  0.7 7.4 %copy-start.5 = (s32[64,64]{1,0:T(8,128)S(1)}, s32[64,64]{1,0:T(8,128)}, u32[]{:S(2)}) copy-start(s32[64,64]{1,0:T(8,128)} %wet_ref.3) | copy-start | bytes 49156
  0.7 7.4 %copy-start.11 = (bf16[512]{0:T(512)(128)(2,1)S(1)}, bf16[512]{0:T(512)(128)(2,1)}, u32[]{:S(2)}) copy-start(bf16[512]{0:T(512)(128)(2,1)} %param.23) | copy-start | bytes 3076
  0.7 7.4 %copy-start.12 = (bf16[256]{0:T(256)(128)(2,1)S(1)}, bf16[256]{0:T(256)(128)(2,1)}, u32[]{:S(2)}) copy-start(bf16[256]{0:T(256)(128)(2,1)} %param.21) | copy-start | bytes 1540
  0.7 7.4 %copy-start.13 = (bf16[256]{0:T(256)(128)(2,1)S(1)}, bf16[256]{0:T(256)(128)(2,1)}, u32[]{:S(2)}) copy-start(bf16[256]{0:T(256)(128)(2,1)} %param.20) | copy-start | bytes 1540
  0.7 7.4 %copy-start.14 = (bf16[256]{0:T(256)(128)(2,1)S(1)}, bf16[256]{0:T(256)(128)(2,1)}, u32[]{:S(2)}) copy-start(bf16[256]{0:T(256)(128)(2,1)} %param.19) | copy-start | bytes 1540
  0.7 7.4 %copy-start.6 = (bf16[49,256]{1,0:T(8,128)(2,1)S(1)}, bf16[49,256]{1,0:T(8,128)(2,1)}, u32[]{:S(2)}) copy-start(bf16[49,256]{1,0:T(8,128)(2,1)} %kernel_ref.1) | copy-start | bytes 75268
  3.1 7.6 %collective-permute-start = (bf16[12,16,256]{2,1,0:T(8,128)(2,1)}, bf16[12,16,256]{2,1,0:T(8,128)(2,1)S(1)}, u32[]{:S(2)}, u32[]{:S(2)}) collective-permute-start(bf16[12,16,256]{2,1,0:T(8,128)(2,1)} %get-tuple-element.42), channel_id=1, source_target_pairs={{0,1},{1,2},{2,3},{3,4},{4,5},{5,6},{6,7},{7,0},{8,9},{9,10},{10,1... | collective-permute-start | bytes 294920 | tf_op jit(solution)/shard_map/ppermute | solution.py:693
  5.6 5.2 %collective-permute-start.1 = (bf16[12,16,256]{2,1,0:T(8,128)(2,1)}, bf16[12,16,256]{2,1,0:T(8,128)(2,1)S(1)}, u32[]{:S(2)}, u32[]{:S(2)}) collective-permute-start(bf16[12,16,256]{2,1,0:T(8,128)(2,1)} %get-tuple-element.43), channel_id=1, source_target_pairs={{0,7},{1,0},{2,1},{3,2},{4,3},{5,4},{6,5},{7,6},{8,15},{9,8},{10,9... | collective-permute-start | bytes 294920 | tf_op jit(solution)/shard_map/ppermute | solution.py:693
  10.8 3.6 %copy-start.1 = (bf16[64,64,256]{2,1,0:T(8,128)(2,1)S(1)}, bf16[64,64,256]{2,1,0:T(8,128)(2,1)}, u32[]{:S(2)}) copy-start(bf16[64,64,256]{2,1,0:T(8,128)(2,1)} %cot_ref.7) | copy-start | bytes 6291460
  10.8 3.6 %copy-start.2 = (bf16[512,512]{1,0:T(8,128)(2,1)S(1)}, bf16[512,512]{1,0:T(8,128)(2,1)}, u32[]{:S(2)}) copy-start(bf16[512,512]{1,0:T(8,128)(2,1)} %constant.62.clone.refs_10_.place_ref) | copy-start | bytes 1572868
  10.8 3.6 %copy-start.3 = (bf16[256,512]{1,0:T(8,128)(2,1)S(1)}, bf16[256,512]{1,0:T(8,128)(2,1)}, u32[]{:S(2)}) copy-start(bf16[256,512]{1,0:T(8,128)(2,1)} %constant.64.clone.refs_12_.back_ref) | copy-start | bytes 786436
  10.8 3.6 %copy-start.7 = (bf16[256,512]{1,0:T(8,128)(2,1)S(1)}, bf16[256,512]{1,0:T(8,128)(2,1)}, u32[]{:S(2)}) copy-start(bf16[256,512]{1,0:T(8,128)(2,1)} %refs_16_.3) | copy-start | bytes 786436
  10.8 3.6 %copy-start.8 = (bf16[512,256]{1,0:T(8,128)(2,1)S(1)}, bf16[512,256]{1,0:T(8,128)(2,1)}, u32[]{:S(2)}) copy-start(bf16[512,256]{1,0:T(8,128)(2,1)} %refs_17_.3) | copy-start | bytes 786436
  10.8 3.6 %copy-start.9 = (bf16[512,256]{1,0:T(8,128)(2,1)S(1)}, bf16[512,256]{1,0:T(8,128)(2,1)}, u32[]{:S(2)}) copy-start(bf16[512,256]{1,0:T(8,128)(2,1)} %constant.63.clone.refs_11_) | copy-start | bytes 786436
  10.8 3.6 %copy-start.10 = (f32[49,768]{1,0:T(8,128)S(1)}, f32[49,768]{1,0:T(8,128)}, u32[]{:S(2)}) copy-start(f32[49,768]{1,0:T(8,128)} %constant.65.clone.refs_14_) | copy-start | bytes 451588
  10.9 13.4 %collective-permute-start.2 = (bf16[3,96,256]{2,1,0:T(8,128)(2,1)S(1)}, bf16[3,96,256]{2,1,0:T(8,128)(2,1)S(1)}, u32[]{:S(2)}, u32[]{:S(2)}) collective-permute-start(bf16[3,96,256]{2,1,0:T(8,128)(2,1)S(1)} %get-tuple-element.45), channel_id=1, source_target_pairs={{0,8},{8,16},{16,24},{24,32},{32,40},{40,48},{48,56},{56,64},{64,7... | collective-permute-start | bytes 442376 | tf_op jit(solution)/shard_map/ppermute | solution.py:697
  14.4 9.9 %collective-permute-start.3 = (bf16[3,96,256]{2,1,0:T(8,128)(2,1)S(1)}, bf16[3,96,256]{2,1,0:T(8,128)(2,1)S(1)}, u32[]{:S(2)}, u32[]{:S(2)}) collective-permute-start(bf16[3,96,256]{2,1,0:T(8,128)(2,1)S(1)} %get-tuple-element.46), channel_id=1, source_target_pairs={{0,120},{8,0},{16,8},{24,16},{32,24},{40,32},{48,40},{56,48},{64,5... | collective-permute-start | bytes 442376 | tf_op jit(solution)/shard_map/ppermute | solution.py:697
  34.7 7.9 %collective-permute-start.8 = (f32[4,272,128]{2,1,0:T(8,128)S(1)}, f32[4,272,128]{2,1,0:T(8,128)S(1)}, u32[]{:S(2)}, u32[]{:S(2)}) collective-permute-start(f32[4,272,128]{2,1,0:T(8,128)S(1)} %get-tuple-element.62), channel_id=1, source_target_pairs={{0,8},{1,9},{2,10},{3,11},{4,12},{5,13},{6,14},{7,15},{8,0},{9,1},... | collective-permute-start | bytes 1671176 | tf_op jit(solution)/shard_map/ppermute | solution.py:728
  39.1 7.6 %collective-permute-start.4 = (bf16[12,16,256]{2,1,0:T(8,128)(2,1)S(1)}, bf16[12,16,256]{2,1,0:T(8,128)(2,1)S(1)}, u32[]{:S(2)}, u32[]{:S(2)}) collective-permute-start(bf16[12,16,256]{2,1,0:T(8,128)(2,1)S(1)} %get-tuple-element.56), channel_id=1, source_target_pairs={{0,1},{1,2},{2,3},{3,4},{4,5},{5,6},{6,7},{7,0},{8,9},{9,10},{10,1... | collective-permute-start | bytes 294920 | tf_op jit(solution)/shard_map/ppermute | solution.py:693
  39.2 7.5 %collective-permute-start.5 = (bf16[12,16,256]{2,1,0:T(8,128)(2,1)S(1)}, bf16[12,16,256]{2,1,0:T(8,128)(2,1)S(1)}, u32[]{:S(2)}, u32[]{:S(2)}) collective-permute-start(bf16[12,16,256]{2,1,0:T(8,128)(2,1)S(1)} %get-tuple-element.57), channel_id=1, source_target_pairs={{0,7},{1,0},{2,1},{3,2},{4,3},{5,4},{6,5},{7,6},{8,15},{9,8},{10,9... | collective-permute-start | bytes 294920 | tf_op jit(solution)/shard_map/ppermute | solution.py:693
  42.7 5.8 %collective-permute-start.9 = (bf16[1,272,128]{2,1,0:T(8,128)(2,1)S(1)}, bf16[1,272,128]{2,1,0:T(8,128)(2,1)S(1)}, u32[]{:S(2)}, u32[]{:S(2)}) collective-permute-start(bf16[1,272,128]{2,1,0:T(8,128)(2,1)S(1)} %get-tuple-element.64), channel_id=1, source_target_pairs={{0,16},{1,17},{2,18},{3,19},{4,20},{5,21},{6,22},{7,23},{8,10},{9,... | collective-permute-start | bytes 208904 | tf_op jit(solution)/shard_map/ppermute | solution.py:728
  42.8 5.7 %collective-permute-start.10 = (bf16[1,272,128]{2,1,0:T(8,128)(2,1)S(1)}, bf16[1,272,128]{2,1,0:T(8,128)(2,1)S(1)}, u32[]{:S(2)}, u32[]{:S(2)}) collective-permute-start(bf16[1,272,128]{2,1,0:T(8,128)(2,1)S(1)} %get-tuple-element.65), channel_id=1, source_target_pairs={{0,32},{1,33},{2,34},{3,35},{4,36},{5,37},{6,38},{7,39},{8,12},{9,... | collective-permute-start | bytes 208904 | tf_op jit(solution)/shard_map/ppermute | solution.py:728
  45.1 4.4 %collective-permute-start.11 = (bf16[1,272,128]{2,1,0:T(8,128)(2,1)S(1)}, bf16[1,272,128]{2,1,0:T(8,128)(2,1)S(1)}, u32[]{:S(2)}, u32[]{:S(2)}) collective-permute-start(bf16[1,272,128]{2,1,0:T(8,128)(2,1)S(1)} %get-tuple-element.66), channel_id=1, source_target_pairs={{0,48},{1,49},{2,50},{3,51},{4,52},{5,53},{6,54},{7,55},{8,14},{9,... | collective-permute-start | bytes 208904 | tf_op jit(solution)/shard_map/ppermute | solution.py:728
  46.7 21.6 %collective-permute-start.6 = (bf16[3,96,256]{2,1,0:T(8,128)(2,1)S(1)}, bf16[3,96,256]{2,1,0:T(8,128)(2,1)S(1)}, u32[]{:S(2)}, u32[]{:S(2)}) collective-permute-start(bf16[3,96,256]{2,1,0:T(8,128)(2,1)S(1)} %get-tuple-element.58), channel_id=1, source_target_pairs={{0,8},{8,16},{16,24},{24,32},{32,40},{40,48},{48,56},{56,64},{64,7... | collective-permute-start | bytes 442376 | tf_op jit(solution)/shard_map/ppermute | solution.py:697
  46.9 21.4 %collective-permute-start.7 = (bf16[3,96,256]{2,1,0:T(8,128)(2,1)S(1)}, bf16[3,96,256]{2,1,0:T(8,128)(2,1)S(1)}, u32[]{:S(2)}, u32[]{:S(2)}) collective-permute-start(bf16[3,96,256]{2,1,0:T(8,128)(2,1)S(1)} %get-tuple-element.59), channel_id=1, source_target_pairs={{0,120},{8,0},{16,8},{24,16},{32,24},{40,32},{48,40},{56,48},{64,5... | collective-permute-start | bytes 442376 | tf_op jit(solution)/shard_map/ppermute | solution.py:697
  49.5 5.8 %collective-permute-start.14 = (bf16[1,272,128]{2,1,0:T(8,128)(2,1)S(1)}, bf16[1,272,128]{2,1,0:T(8,128)(2,1)S(1)}, u32[]{:S(2)}, u32[]{:S(2)}) collective-permute-start(bf16[1,272,128]{2,1,0:T(8,128)(2,1)S(1)} %add_convert_fusion.2), channel_id=1, source_target_pairs={{0,6},{1,7},{2,4},{3,5},{4,2},{5,3},{6,0},{7,1},{8,73},{9,72},{10,... | collective-permute-start | bytes 208904 | tf_op jit(solution)/shard_map/ppermute | solution.py:728
  51.5 5.2 %collective-permute-start.13 = (bf16[1,272,128]{2,1,0:T(8,128)(2,1)S(1)}, bf16[1,272,128]{2,1,0:T(8,128)(2,1)S(1)}, u32[]{:S(2)}, u32[]{:S(2)}) collective-permute-start(bf16[1,272,128]{2,1,0:T(8,128)(2,1)S(1)} %add_convert_fusion.2), channel_id=1, source_target_pairs={{0,4},{1,5},{2,6},{3,7},{4,0},{5,1},{6,2},{7,3},{8,72},{9,73},{10,... | collective-permute-start | bytes 208904 | tf_op jit(solution)/shard_map/ppermute | solution.py:728
  53.2 3.6 %collective-permute-start.12 = (bf16[1,272,128]{2,1,0:T(8,128)(2,1)S(1)}, bf16[1,272,128]{2,1,0:T(8,128)(2,1)S(1)}, u32[]{:S(2)}, u32[]{:S(2)}) collective-permute-start(bf16[1,272,128]{2,1,0:T(8,128)(2,1)S(1)} %add_convert_fusion.2), channel_id=1, source_target_pairs={{0,2},{1,3},{2,0},{3,1},{4,6},{5,7},{6,4},{7,5},{8,9},{9,8},{10,11... | collective-permute-start | bytes 208904 | tf_op jit(solution)/shard_map/ppermute | solution.py:728
  56.9 6.2 %collective-permute-start.17 = (bf16[1,272,128]{2,1,0:T(8,128)(2,1)S(1)}, bf16[1,272,128]{2,1,0:T(8,128)(2,1)S(1)}, u32[]{:S(2)}, u32[]{:S(2)}) collective-permute-start(bf16[1,272,128]{2,1,0:T(8,128)(2,1)S(1)} %add_convert_fusion.1), channel_id=1, source_target_pairs={{0,65},{1,64},{2,67},{3,66},{4,69},{5,68},{6,71},{7,70},{8,56},{9,... | collective-permute-start | bytes 208904 | tf_op jit(solution)/shard_map/ppermute | solution.py:728
  60.2 4.7 %collective-permute-start.16 = (bf16[1,272,128]{2,1,0:T(8,128)(2,1)S(1)}, bf16[1,272,128]{2,1,0:T(8,128)(2,1)S(1)}, u32[]{:S(2)}, u32[]{:S(2)}) collective-permute-start(bf16[1,272,128]{2,1,0:T(8,128)(2,1)S(1)} %add_convert_fusion.1), channel_id=1, source_target_pairs={{0,64},{1,65},{2,66},{3,67},{4,68},{5,69},{6,70},{7,71},{8,40},{9,... | collective-permute-start | bytes 208904 | tf_op jit(solution)/shard_map/ppermute | solution.py:728
  60.2 4.7 %collective-permute-start.15 = (bf16[1,272,128]{2,1,0:T(8,128)(2,1)S(1)}, bf16[1,272,128]{2,1,0:T(8,128)(2,1)S(1)}, u32[]{:S(2)}, u32[]{:S(2)}) collective-permute-start(bf16[1,272,128]{2,1,0:T(8,128)(2,1)S(1)} %add_convert_fusion.1), channel_id=1, source_target_pairs={{0,1},{1,0},{2,3},{3,2},{4,5},{5,4},{6,7},{7,6},{8,24},{9,25},{10,... | collective-permute-start | bytes 208904 | tf_op jit(solution)/shard_map/ppermute | solution.py:728
  65.0 5.5 %collective-permute-start.20 = (bf16[1,272,128]{2,1,0:T(8,128)(2,1)S(1)}, bf16[1,272,128]{2,1,0:T(8,128)(2,1)S(1)}, u32[]{:S(2)}, u32[]{:S(2)}) collective-permute-start(bf16[1,272,128]{2,1,0:T(8,128)(2,1)S(1)} %add_convert_fusion.refs_0_), channel_id=1, source_target_pairs={{0,48},{1,49},{2,50},{3,51},{4,52},{5,53},{6,54},{7,55},{8,14},{9,... | collective-permute-start | bytes 208904 | tf_op jit(solution)/shard_map/ppermute | solution.py:728
  67.2 4.7 %collective-permute-start.19 = (bf16[1,272,128]{2,1,0:T(8,128)(2,1)S(1)}, bf16[1,272,128]{2,1,0:T(8,128)(2,1)S(1)}, u32[]{:S(2)}, u32[]{:S(2)}) collective-permute-start(bf16[1,272,128]{2,1,0:T(8,128)(2,1)S(1)} %add_convert_fusion.refs_0_), channel_id=1, source_target_pairs={{0,32},{1,33},{2,34},{3,35},{4,36},{5,37},{6,38},{7,39},{8,12},{9,... | collective-permute-start | bytes 208904 | tf_op jit(solution)/shard_map/ppermute | solution.py:728
  67.7 4.2 %collective-permute-start.18 = (bf16[1,272,128]{2,1,0:T(8,128)(2,1)S(1)}, bf16[1,272,128]{2,1,0:T(8,128)(2,1)S(1)}, u32[]{:S(2)}, u32[]{:S(2)}) collective-permute-start(bf16[1,272,128]{2,1,0:T(8,128)(2,1)S(1)} %add_convert_fusion.refs_0_), channel_id=1, source_target_pairs={{0,16},{1,17},{2,18},{3,19},{4,20},{5,21},{6,22},{7,23},{8,10},{9,... | collective-permute-start | bytes 208904 | tf_op jit(solution)/shard_map/ppermute | solution.py:728
  71.9 7.9 %collective-permute-start.21 = (bf16[4,272,128]{2,1,0:T(8,128)(2,1)S(1)}, bf16[4,272,128]{2,1,0:T(8,128)(2,1)S(1)}, u32[]{:S(2)}, u32[]{:S(2)}) collective-permute-start(bf16[4,272,128]{2,1,0:T(8,128)(2,1)S(1)} %join.1.own_ref), channel_id=1, source_target_pairs={{0,8},{1,9},{2,10},{3,11},{4,12},{5,13},{6,14},{7,15},{8,0},{9,1},... | collective-permute-start | bytes 835592 | tf_op jit(solution)/shard_map/ppermute | solution.py:728
